TPU v7x, 32 devices: a whole 2x2x4 slice. The times are simulated.
32 devices in a mesh: gx: 8 (over z, y), gy: 4 (over x, core).
Axes of the slice: x: 2, y: 2, z: 4, core: 2. Of those that a mesh axis runs over, the one named last changes fastest.
Arguments:
- delta: float32 [4, 128, 64, 128], P(None, 'gx', 'gy'), may hold values from -6 to 6
- alpha: float32 [8, 16, 4, 128], P('gx', 'gy'), may hold values from -6 to 6
- eddy: float32 [128, 64, 128], P('gx', 'gy'), may hold values from 0.02 to 0.2
- courant: float32 [2, 128, 64, 128], P(None, 'gx', 'gy'), may hold values from -0.4 to 0.4
- tile_map: int32 [128, 64], P('gx', 'gy'), may hold values from 0 to 15
- obs_rows: float32 [256, 3, 128], P(('gx', 'gy')), may hold values from -6 to 6
- gate_beam: int32 [8, 4, 256], P('gx', 'gy'), may hold values from 0 to 63
- gate_index: int32 [8, 4, 256], P('gx', 'gy'), may hold values from 0 to 127
- gate_column: int32 [8, 4, 256], P('gx', 'gy'), may hold values from 0 to 255
- gate_live: int32 [8, 4, 256], P('gx', 'gy'), may hold values 0 or 1
- obs_weight: float32 [8, 4, 256, 4, 128], P('gx', 'gy'), may hold values from -0.25 to 0.25
- obs_precision: float32 [8, 4, 256], P('gx', 'gy'), may hold values from 4 to 64
Outputs:
- grad_delta: float32 [4, 128, 64, 128], P(None, 'gx', 'gy')
- grad_alpha: float32 [8, 16, 4, 128], P('gx', 'gy')
Inputs may be any that keep to these rules, and one draw needn't show every extreme that they name: `gate_beam`: a slot's beam is numbered within its own north-south row of tiles as the east-west index of the beam's owner times 8 plus its place among that owner's beams. `gate_column`: column index within the tile is east-west offset times 16 plus north-south offset.
All inputs are finite; a program needn't handle non-finite values. No bound on the sum of `gate_live` on one device may be relied on, other than what follows from the above.
Results may differ from a plain program's by a relative error of at most 0.00011.
Values sent between devices are 32-bit elements; how exact they have to be, the bound alone decides.
No kernel may reach another device: no remote copies, remote signals or barrier semaphores. Data moves between devices by JAX's collectives and lax.ppermute only.
A program may use at most 64 MiB of HBM per device.

v0:
```python
import jax
import jax.numpy as jnp
from jax import lax
from jax.sharding import PartitionSpec as P

STEPS = 3


profile_weight = 0.125
highest = lax.Precision.HIGHEST


def padded_2(block, sides, width):
    for axis, dim in sides:
        count = lax.axis_size(axis)
        forward = [(i, i + 1) for i in range(count - 1)]
        backward = [(target, source) for source, target in forward]
        low = lax.ppermute(
            lax.slice_in_dim(block, block.shape[dim] - width, None, axis=dim), axis, forward
        )
        high = lax.ppermute(lax.slice_in_dim(block, 0, width, axis=dim), axis, backward)
        block = jnp.concatenate([low, block, high], axis=dim)
    return block


def advance(padded, coefs):
    centre = padded[:, 1:-1, 1:-1]
    east_side = padded[:, 2:, 1:-1]
    west_side = padded[:, :-2, 1:-1]
    north_side = padded[:, 1:-1, 2:]
    south_side = padded[:, 1:-1, :-2]
    return (
        centre
        + coefs[0] * (east_side + west_side + north_side + south_side - 4.0 * centre)
        - 0.5 * coefs[1] * (east_side - west_side)
        - 0.5 * coefs[2] * (north_side - south_side)
    )


def trimmed(padded_coefs, margin, rows, columns):
    first = STEPS - margin
    return padded_coefs[:, first : first + rows + 2 * margin, first : first + columns + 2 * margin]


def transpose_step(padded, coefs):
    viscous = coefs[0]
    along_x = coefs[1]
    along_y = coefs[2]
    centre = padded[:, 1:-1, 1:-1]
    result = (1.0 - 4.0 * viscous[1:-1, 1:-1]) * centre
    result = result + (viscous[:-2, 1:-1] - 0.5 * along_x[:-2, 1:-1]) * padded[:, :-2, 1:-1]
    result = result + (viscous[2:, 1:-1] + 0.5 * along_x[2:, 1:-1]) * padded[:, 2:, 1:-1]
    result = result + (viscous[1:-1, :-2] - 0.5 * along_y[1:-1, :-2]) * padded[:, 1:-1, :-2]
    result = result + (viscous[1:-1, 2:] + 0.5 * along_y[1:-1, 2:]) * padded[:, 1:-1, 2:]
    return result


def retreat(adjoint, padded_coefs, rows, columns):
    padded = padded_2(adjoint, (("gx", 1), ("gy", 2)), 1)
    return transpose_step(padded, trimmed(padded_coefs, 1, rows, columns))


def observed_values(obs_rows, beams, gates):
    ngates = obs_rows.shape[2]
    values = []
    for step in range(STEPS):
        gathered = lax.all_gather(obs_rows[:, step, :], "gx", axis=0, tiled=True)
        values.append(gathered.reshape(-1)[beams * ngates + gates])
    return values


def on_device(
    delta,
    alpha,
    eddy,
    courant,
    tile_map,
    obs_rows,
    gate_beam,
    gate_index,
    gate_column,
    gate_live,
    obs_weight,
    obs_precision,
):
    rows, columns, levels = (delta.shape[1], delta.shape[2], delta.shape[3])
    owned_tiles = alpha.shape[1]
    strip_tiles = owned_tiles * lax.axis_size("gy")
    coefs = jnp.concatenate([eddy[None], courant], axis=0)
    padded_coefs = padded_2(coefs, (("gx", 1), ("gy", 2)), STEPS)
    selector = (tile_map.reshape(-1)[:, None] == lax.iota(jnp.int32, strip_tiles)[None, :]).astype(
        jnp.float32
    )
    piece = lax.all_gather(alpha, "gy", axis=1, tiled=True)
    profiles = jnp.dot(selector, piece[0].reshape(piece.shape[1], 4 * levels), precision=highest)
    profiles = jnp.transpose(profiles.reshape(rows, columns, 4, levels), (2, 0, 1, 3))
    state = delta + profile_weight * profiles
    beams = gate_beam[0, 0]
    gates = gate_index[0, 0]
    slots = gate_column[0, 0]
    weights = obs_weight[0, 0]
    scaled = gate_live[0, 0].astype(jnp.float32) * obs_precision[0, 0]
    observed = observed_values(obs_rows, beams, gates)
    states = []
    for step in range(STEPS):
        padded = padded_2(state, (("gx", 1), ("gy", 2)), 1)
        state = advance(padded, trimmed(padded_coefs, 0, rows, columns))
        states.append(state)
    forcings = []
    for step in range(STEPS):
        picked = jnp.take(states[step].reshape(4, rows * columns, levels), slots, axis=1)
        seen = jnp.einsum("cgz,gcz->g", picked, weights, precision=highest)
        misfit = scaled * (seen - observed[step])
        pushed = jax.ops.segment_sum(
            misfit[:, None, None] * weights, slots, num_segments=rows * columns
        )
        forcings.append(jnp.transpose(pushed.reshape(rows, columns, 4, levels), (2, 0, 1, 3)))
    adjoint = forcings[STEPS - 1]
    for step in range(STEPS - 1, -1, -1):
        adjoint = retreat(adjoint, padded_coefs, rows, columns)
        if step > 0:
            adjoint = adjoint + forcings[step - 1]
    flat_adjoint = jnp.transpose(adjoint, (1, 2, 0, 3)).reshape(rows * columns, 4 * levels)
    picked = selector
    sums = lax.psum_scatter(
        lax.dot_general(picked, flat_adjoint, (((0,), (0,)), ((), ())), precision=highest),
        "gy",
        scatter_dimension=0,
        tiled=True,
    )
    grad_alpha = alpha + profile_weight * sums.reshape(1, owned_tiles, 4, levels)
    return (delta + adjoint, grad_alpha)


def solution(mesh):
    return jax.shard_map(
        on_device,
        mesh=mesh,
        in_specs=(
            P(None, "gx", "gy", None),
            P("gx", "gy", None, None),
            P("gx", "gy", None),
            P(None, "gx", "gy", None),
            P("gx", "gy"),
            P(("gx", "gy"), None, None),
            P("gx", "gy", None),
            P("gx", "gy", None),
            P("gx", "gy", None),
            P("gx", "gy", None),
            P("gx", "gy", None, None, None),
            P("gx", "gy", None),
        ),
        out_specs=(P(None, "gx", "gy", None), P("gx", "gy", None, None)),
        check_vma=False,
    )
```

profile of v0, /device:TPU:0, one launch (start us, length us, event | category | flops | bytes accessed | tf_op | source)
XLA Modules:
  0.0 257.9 jit_solution(1502923572777781767)
XLA Ops:
  0.6 6.4 %all_gather.12 = f32[1,16,4,128]{3,2,0,1:T(4,128)S(1)} all-gather(f32[1,4,4,128]{3,2,0,1:T(4,128)} %bitcast.108), channel_id=1, replica_groups=mesh['gx'=8,'gy'=4] {'gy'}, dimensions={1}, use_global_device_ids=true | all-gather | bytes 40960 | tf_op jit(solution)/shard_map/all_gather | solution.py:94
  7.0 1.5 fusion.1
  8.6 1.4 collective-permute-start.4
  10.0 4.5 %collective-permute-start.5 = (f32[4,1,16,128]{3,2,0,1:T(8,128)S(1)}, f32[4,1,16,128]{3,2,0,1:T(8,128)S(1)}, u32[]{:S(2)}, u32[]{:S(2)}) collective-permute-start(f32[4,1,16,128]{3,2,0,1:T(8,128)S(1)} %get-tuple-element.38), channel_id=1, source_target_pairs={{0,4},{4,8},{8,12},{12,16},{16,20},{20,24},{24,28},{1,5},{5,9},{9,... | collective-permute-start | bytes 98312 | tf_op jit(solution)/shard_map/ppermute | solution.py:18
  14.6 4.8 %collective-permute-start = (f32[3,3,16,128]{3,2,1,0:T(8,128)S(1)}, f32[3,3,16,128]{3,2,1,0:T(8,128)S(1)}, u32[]{:S(2)}, u32[]{:S(2)}) collective-permute-start(f32[3,3,16,128]{3,2,1,0:T(8,128)S(1)} %get-tuple-element.44), channel_id=1, source_target_pairs={{0,4},{4,8},{8,12},{12,16},{16,20},{20,24},{24,28},{1,5},{5,9},{9,... | collective-permute-start | bytes 221192 | tf_op jit(solution)/shard_map/ppermute | solution.py:18
  19.4 1.3 collective-permute-start.1
  20.8 0.6 copy-done.8
  21.5 0.7 copy-done.10
  22.1 0.7 copy-done.6
  22.9 1.3 collective-permute-start.6
  24.2 3.0 %collective-permute-start.7 = (f32[4,18,1,128]{3,2,0,1:T(1,128)S(1)}, f32[4,18,1,128]{3,2,0,1:T(1,128)S(1)}, u32[]{:S(2)}, u32[]{:S(2)}) collective-permute-start(f32[4,18,1,128]{3,2,0,1:T(1,128)S(1)} %get-tuple-element.22), channel_id=1, source_target_pairs={{0,1},{1,2},{2,3},{4,5},{5,6},{6,7},{8,9},{9,10},{10,11},{12,13},{... | collective-permute-start | bytes 110600 | tf_op jit(solution)/shard_map/ppermute | solution.py:18
  27.3 0.8 collective-permute-done.7
  28.1 0.4 multiply_subtract_fusion.2
  28.5 1.3 collective-permute-start.8
  29.8 5.2 %collective-permute-start.9 = (f32[4,1,16,128]{3,2,0,1:T(8,128)S(1)}, f32[4,1,16,128]{3,2,0,1:T(8,128)S(1)}, u32[]{:S(2)}, u32[]{:S(2)}) collective-permute-start(f32[4,1,16,128]{3,2,0,1:T(8,128)S(1)} %get-tuple-element.36), channel_id=1, source_target_pairs={{0,4},{4,8},{8,12},{12,16},{16,20},{20,24},{24,28},{1,5},{5,9},{9,... | collective-permute-start | bytes 98312 | tf_op jit(solution)/shard_map/ppermute | solution.py:18
  35.0 1.6 collective-permute-done.9
  36.6 1.3 collective-permute-start.10
  37.9 3.0 %collective-permute-start.11 = (f32[4,18,1,128]{3,2,0,1:T(1,128)S(1)}, f32[4,18,1,128]{3,2,0,1:T(1,128)S(1)}, u32[]{:S(2)}, u32[]{:S(2)}) collective-permute-start(f32[4,18,1,128]{3,2,0,1:T(1,128)S(1)} %get-tuple-element.20), channel_id=1, source_target_pairs={{0,1},{1,2},{2,3},{4,5},{5,6},{6,7},{8,9},{9,10},{10,11},{12,13},{... | collective-permute-start | bytes 110600 | tf_op jit(solution)/shard_map/ppermute | solution.py:18
  40.9 0.8 collective-permute-done.11
  42.1 1.3 collective-permute-start.12
  43.4 5.6 %collective-permute-start.13 = (f32[4,1,16,128]{3,2,0,1:T(8,128)S(1)}, f32[4,1,16,128]{3,2,0,1:T(8,128)S(1)}, u32[]{:S(2)}, u32[]{:S(2)}) collective-permute-start(f32[4,1,16,128]{3,2,0,1:T(8,128)S(1)} %get-tuple-element.34), channel_id=1, source_target_pairs={{0,4},{4,8},{8,12},{12,16},{16,20},{20,24},{24,28},{1,5},{5,9},{9,... | collective-permute-start | bytes 98312 | tf_op jit(solution)/shard_map/ppermute | solution.py:18
  49.0 33.1 %all-gather = f32[64,1,128]{2,0,1:T(8,128)S(1)} all-gather(f32[8,1,128]{2,0,1:T(8,128)S(1)} %get-tuple-element.53), channel_id=2, replica_groups=mesh['gx'=8,'gy'=4] {'gx'}, dimensions={0}, use_global_device_ids=true | all-gather | bytes 36864 | tf_op jit(solution)/shard_map/all_gather | solution.py:67
  82.1 1.7 gather_fusion
  83.8 30.4 %all-gather.1 = f32[64,1,128]{2,0,1:T(8,128)S(1)} all-gather(f32[8,1,128]{2,0,1:T(8,128)S(1)} %get-tuple-element.54), channel_id=3, replica_groups=mesh['gx'=8,'gy'=4] {'gx'}, dimensions={0}, use_global_device_ids=true | all-gather | bytes 36864 | tf_op jit(solution)/shard_map/all_gather | solution.py:67
  114.3 1.7 gather_fusion.1
  116.0 30.4 %all-gather.2 = f32[64,1,128]{2,0,1:T(8,128)S(1)} all-gather(f32[8,1,128]{2,0,1:T(8,128)S(1)} %get-tuple-element.52), channel_id=4, replica_groups=mesh['gx'=8,'gy'=4] {'gx'}, dimensions={0}, use_global_device_ids=true | all-gather | bytes 36864 | tf_op jit(solution)/shard_map/all_gather | solution.py:67
  146.4 1.7 gather_fusion.2
  148.5 1.0 gather_fusion.5
  149.6 1.3 collective-permute-start.14
  150.9 3.0 %collective-permute-start.15 = (f32[4,18,1,128]{3,2,0,1:T(1,128)S(1)}, f32[4,18,1,128]{3,2,0,1:T(1,128)S(1)}, u32[]{:S(2)}, u32[]{:S(2)}) collective-permute-start(f32[4,18,1,128]{3,2,0,1:T(1,128)S(1)} %get-tuple-element.18), channel_id=1, source_target_pairs={{0,1},{1,2},{2,3},{4,5},{5,6},{6,7},{8,9},{9,10},{10,11},{12,13},{... | collective-permute-start | bytes 110600 | tf_op jit(solution)/shard_map/ppermute | solution.py:18
  154.0 0.8 pad_maximum_fusion.56
  154.7 7.4 %collective-permute-start.2 = (f32[3,22,3,128]{3,2,1,0:T(4,128)}, f32[3,22,3,128]{3,2,1,0:T(4,128)}, u32[]{:S(2)}, u32[]{:S(2)}) collective-permute-start(f32[3,22,3,128]{3,2,1,0:T(4,128)} %get-tuple-element.23), channel_id=1, source_target_pairs={{0,1},{1,2},{2,3},{4,5},{5,6},{6,7},{8,9},{9,10},{10,11},{12,13},{... | collective-permute-start | bytes 304136 | tf_op jit(solution)/shard_map/ppermute | solution.py:18
  162.1 1.3 collective-permute-start.3
  163.8 1.0 gather_fusion.4
  164.8 0.4 multiply_subtract_fusion
  165.6 1.0 gather_fusion.3
  166.6 4.4 %fusion.33 = (f32[256]{0:T(256)S(1)}, f32[256]{0:T(256)S(1)}, f32[256]{0:T(256)S(1)}) fusion(f32[1,1,256,4,128]{4,3,2,1,0:T(4,128)S(1)} %copy-done.2, f32[256,4,128]{2,1,0:T(4,128)S(1)} %gather_fusion.5, pred[256]{0:T(512)(128)(4,1)S(1)} %compare_and_fusion, f32[256,4,128]{2,1,0:T(4,128)S(1)} %gather_fusion.4, f32[256,4,128]{2,1,0:T(4,128)S(1)} %gather_fusion.3), kind=kLoop, calls=%fused_computation.97 | loop fusion | flops 1178880 | bytes 2100480 | tf_op jit(solution)/shard_map/cgz,gcz->g/dot_general | solution.py:112
  171.1 1.1 bitcast_multiply_fusion
  172.3 8.3 %scatter_fusion = f32[256,4,128]{2,1,0:T(4,128)S(1)} fusion(f32[256,4,128]{2,1,0:T(4,128)S(1)} %broadcast.96.clone, s32[256]{0:T(256)S(1)} %bitcast.111, f32[256,4,128]{2,1,0:T(4,128)S(1)} %get-tuple-element.29), kind=kCustom, calls=%fused_computation.6 | custom fusion | flops 131072 | bytes 1573888 | tf_op jit(solution)/shard_map/scatter-add | solution.py:114
  180.7 1.3 collective-permute-start.16
  182.0 1.3 collective-permute-start.17
  183.3 1.0 maximum_bitcast_fusion
  184.3 3.7 %collective-permute-done.17 = f32[4,1,16,128]{3,2,1,0:T(8,128)S(1)} collective-permute-done((f32[4,1,16,128]{3,2,1,0:T(8,128)S(1)}, f32[4,1,16,128]{3,2,1,0:T(8,128)S(1)}, u32[]{:S(2)}, u32[]{:S(2)}) %collective-permute-start.17) | collective-permute-done | bytes 32800 | tf_op jit(solution)/shard_map/ppermute | solution.py:21
  188.1 2.0 collective-permute-start.18
  190.1 1.3 collective-permute-start.19
  191.6 8.3 %scatter_fusion.1 = f32[256,4,128]{2,1,0:T(4,128)S(1)} fusion(f32[256,4,128]{2,1,0:T(4,128)S(1)} %broadcast.96.clone.1, s32[256]{0:T(256)S(1)} %bitcast.112, f32[256,4,128]{2,1,0:T(4,128)S(1)} %get-tuple-element.28), kind=kCustom, calls=%fused_computation.7 | custom fusion | flops 131072 | bytes 1573888 | tf_op jit(solution)/shard_map/scatter-add | solution.py:114
  200.2 3.5 %collective-permute-start.20 = (f32[4,1,16,128]{3,2,1,0:T(8,128)S(1)}, f32[4,1,16,128]{3,2,1,0:T(8,128)S(1)}, u32[]{:S(2)}, u32[]{:S(2)}) collective-permute-start(f32[4,1,16,128]{3,2,1,0:T(8,128)S(1)} %get-tuple-element.30), channel_id=1, source_target_pairs={{0,4},{4,8},{8,12},{12,16},{16,20},{20,24},{24,28},{1,5},{5,9},{9,... | collective-permute-start | bytes 98312 | tf_op jit(solution)/shard_map/ppermute | solution.py:18
  203.8 1.3 collective-permute-start.21
  205.4 4.2 %collective-permute-done.21 = f32[4,1,16,128]{3,2,1,0:T(8,128)S(1)} collective-permute-done((f32[4,1,16,128]{3,2,1,0:T(8,128)S(1)}, f32[4,1,16,128]{3,2,1,0:T(8,128)S(1)}, u32[]{:S(2)}, u32[]{:S(2)}) %collective-permute-start.21) | collective-permute-done | bytes 32800 | tf_op jit(solution)/shard_map/ppermute | solution.py:21
  209.7 3.1 %collective-permute-start.22 = (f32[4,18,1,128]{3,2,1,0:T(1,128)S(1)}, f32[4,18,1,128]{3,2,1,0:T(1,128)S(1)}, u32[]{:S(2)}, u32[]{:S(2)}) collective-permute-start(f32[4,18,1,128]{3,2,1,0:T(1,128)S(1)} %get-tuple-element.13), channel_id=1, source_target_pairs={{0,1},{1,2},{2,3},{4,5},{5,6},{6,7},{8,9},{9,10},{10,11},{12,13},{... | collective-permute-start | bytes 110600 | tf_op jit(solution)/shard_map/ppermute | solution.py:18
  212.8 1.5 collective-permute-start.23
  214.4 8.3 %scatter_fusion.2 = f32[256,4,128]{2,1,0:T(4,128)S(1)} fusion(f32[256,4,128]{2,1,0:T(4,128)S(1)} %broadcast.96.clone.2, s32[256]{0:T(256)S(1)} %bitcast.113, f32[256,4,128]{2,1,0:T(4,128)S(1)} %get-tuple-element.27), kind=kCustom, calls=%fused_computation.8 | custom fusion | flops 131072 | bytes 1573888 | tf_op jit(solution)/shard_map/scatter-add | solution.py:114
  223.1 3.2 %collective-permute-start.24 = (f32[4,1,16,128]{3,2,1,0:T(8,128)S(1)}, f32[4,1,16,128]{3,2,1,0:T(8,128)S(1)}, u32[]{:S(2)}, u32[]{:S(2)}) collective-permute-start(f32[4,1,16,128]{3,2,1,0:T(8,128)S(1)} %get-tuple-element.25), channel_id=1, source_target_pairs={{0,4},{4,8},{8,12},{12,16},{16,20},{20,24},{24,28},{1,5},{5,9},{9,... | collective-permute-start | bytes 98312 | tf_op jit(solution)/shard_map/ppermute | solution.py:18
  226.3 1.3 collective-permute-start.25
  227.9 4.2 %collective-permute-done.25 = f32[4,1,16,128]{3,2,1,0:T(8,128)S(1)} collective-permute-done((f32[4,1,16,128]{3,2,1,0:T(8,128)S(1)}, f32[4,1,16,128]{3,2,1,0:T(8,128)S(1)}, u32[]{:S(2)}, u32[]{:S(2)}) %collective-permute-start.25) | collective-permute-done | bytes 32800 | tf_op jit(solution)/shard_map/ppermute | solution.py:21
  232.2 4.0 %collective-permute-start.26 = (f32[4,18,1,128]{3,2,1,0:T(1,128)S(1)}, f32[4,18,1,128]{3,2,1,0:T(1,128)S(1)}, u32[]{:S(2)}, u32[]{:S(2)}) collective-permute-start(f32[4,18,1,128]{3,2,1,0:T(1,128)S(1)} %get-tuple-element.11), channel_id=1, source_target_pairs={{0,1},{1,2},{2,3},{4,5},{5,6},{6,7},{8,9},{9,10},{10,11},{12,13},{... | collective-permute-start | bytes 110600 | tf_op jit(solution)/shard_map/ppermute | solution.py:18
  236.2 1.3 collective-permute-start.27
  237.5 0.7 copy-done.12
  238.2 0.6 dynamic-slice
  239.4 2.5 collective-permute-done.27
  241.9 1.1 fusion.45
  243.7 12.8 %all-reduce = f32[16,512]{1,0:T(8,128)S(1)} all-reduce(f32[16,512]{1,0:T(8,128)S(1)} %fusion.2), channel_id=5, replica_groups=mesh['gx'=8,'gy'=4] {'gy'}, use_global_device_ids=true, to_apply=%region_3.5.clone | all-reduce | flops 8192 | bytes 65536
  256.6 0.7 copy-done.5
  257.3 0.6 add.171
  (83 shorter events, 4.4 us)
Async XLA Ops:
  0.6 6.4 %copy-start.4 = (s32[16,16]{1,0:T(8,128)S(1)}, s32[16,16]{1,0:T(8,128)}, u32[]{:S(2)}) copy-start(s32[16,16]{1,0:T(8,128)} %param.18) | copy-start | bytes 3076
  7.0 7.5 %copy-start.1 = (f32[2,16,16,128]{3,2,1,0:T(8,128)S(1)}, f32[2,16,16,128]{3,2,1,0:T(8,128)}, u32[]{:S(2)}) copy-start(f32[2,16,16,128]{3,2,1,0:T(8,128)} %param.17) | copy-start | bytes 786436
  8.5 6.0 %copy-start = (f32[16,16,128]{2,1,0:T(8,128)S(1)}, f32[16,16,128]{2,1,0:T(8,128)}, u32[]{:S(2)}) copy-start(f32[16,16,128]{2,1,0:T(8,128)} %param.16) | copy-start | bytes 393220
  8.6 14.3 %collective-permute-start.4 = (f32[4,1,16,128]{3,2,0,1:T(8,128)S(1)}, f32[4,1,16,128]{3,2,0,1:T(8,128)S(1)}, u32[]{:S(2)}, u32[]{:S(2)}) collective-permute-start(f32[4,1,16,128]{3,2,0,1:T(8,128)S(1)} %get-tuple-element.39), channel_id=1, source_target_pairs={{4,0},{8,4},{12,8},{16,12},{20,16},{24,20},{28,24},{5,1},{9,5},{13... | collective-permute-start | bytes 98312 | tf_op jit(solution)/shard_map/ppermute | solution.py:21
  10.0 12.8 %collective-permute-start.5 = (f32[4,1,16,128]{3,2,0,1:T(8,128)S(1)}, f32[4,1,16,128]{3,2,0,1:T(8,128)S(1)}, u32[]{:S(2)}, u32[]{:S(2)}) collective-permute-start(f32[4,1,16,128]{3,2,0,1:T(8,128)S(1)} %get-tuple-element.38), channel_id=1, source_target_pairs={{0,4},{4,8},{8,12},{12,16},{16,20},{20,24},{24,28},{1,5},{5,9},{9,... | collective-permute-start | bytes 98312 | tf_op jit(solution)/shard_map/ppermute | solution.py:18
  14.6 139.4 %collective-permute-start = (f32[3,3,16,128]{3,2,1,0:T(8,128)S(1)}, f32[3,3,16,128]{3,2,1,0:T(8,128)S(1)}, u32[]{:S(2)}, u32[]{:S(2)}) collective-permute-start(f32[3,3,16,128]{3,2,1,0:T(8,128)S(1)} %get-tuple-element.44), channel_id=1, source_target_pairs={{0,4},{4,8},{8,12},{12,16},{16,20},{20,24},{24,28},{1,5},{5,9},{9,... | collective-permute-start | bytes 221192 | tf_op jit(solution)/shard_map/ppermute | solution.py:18
  19.4 1.3 copy-start.7
  19.4 134.6 %collective-permute-start.1 = (f32[3,3,16,128]{3,2,1,0:T(8,128)S(1)}, f32[3,3,16,128]{3,2,1,0:T(8,128)S(1)}, u32[]{:S(2)}, u32[]{:S(2)}) collective-permute-start(f32[3,3,16,128]{3,2,1,0:T(8,128)S(1)} %get-tuple-element.45), channel_id=1, source_target_pairs={{4,0},{8,4},{12,8},{16,12},{20,16},{24,20},{28,24},{5,1},{9,5},{13... | collective-permute-start | bytes 221192 | tf_op jit(solution)/shard_map/ppermute | solution.py:21
  20.7 0.7 copy-start.8
  20.8 0.7 copy-start.9
  21.4 0.7 copy-start.10
  21.4 0.7 copy-start.11
  22.1 0.7 copy-start.6
  22.9 4.4 %collective-permute-start.6 = (f32[4,18,1,128]{3,2,0,1:T(1,128)S(1)}, f32[4,18,1,128]{3,2,0,1:T(1,128)S(1)}, u32[]{:S(2)}, u32[]{:S(2)}) collective-permute-start(f32[4,18,1,128]{3,2,0,1:T(1,128)S(1)} %get-tuple-element.21), channel_id=1, source_target_pairs={{1,0},{2,1},{3,2},{5,4},{6,5},{7,6},{9,8},{10,9},{11,10},{13,12},{... | collective-permute-start | bytes 110600 | tf_op jit(solution)/shard_map/ppermute | solution.py:21
  24.2 3.9 %collective-permute-start.7 = (f32[4,18,1,128]{3,2,0,1:T(1,128)S(1)}, f32[4,18,1,128]{3,2,0,1:T(1,128)S(1)}, u32[]{:S(2)}, u32[]{:S(2)}) collective-permute-start(f32[4,18,1,128]{3,2,0,1:T(1,128)S(1)} %get-tuple-element.22), channel_id=1, source_target_pairs={{0,1},{1,2},{2,3},{4,5},{5,6},{6,7},{8,9},{9,10},{10,11},{12,13},{... | collective-permute-start | bytes 110600 | tf_op jit(solution)/shard_map/ppermute | solution.py:18
  28.5 6.5 %collective-permute-start.8 = (f32[4,1,16,128]{3,2,0,1:T(8,128)S(1)}, f32[4,1,16,128]{3,2,0,1:T(8,128)S(1)}, u32[]{:S(2)}, u32[]{:S(2)}) collective-permute-start(f32[4,1,16,128]{3,2,0,1:T(8,128)S(1)} %get-tuple-element.37), channel_id=1, source_target_pairs={{4,0},{8,4},{12,8},{16,12},{20,16},{24,20},{28,24},{5,1},{9,5},{13... | collective-permute-start | bytes 98312 | tf_op jit(solution)/shard_map/ppermute | solution.py:21
  29.8 6.8 %collective-permute-start.9 = (f32[4,1,16,128]{3,2,0,1:T(8,128)S(1)}, f32[4,1,16,128]{3,2,0,1:T(8,128)S(1)}, u32[]{:S(2)}, u32[]{:S(2)}) collective-permute-start(f32[4,1,16,128]{3,2,0,1:T(8,128)S(1)} %get-tuple-element.36), channel_id=1, source_target_pairs={{0,4},{4,8},{8,12},{12,16},{16,20},{20,24},{24,28},{1,5},{5,9},{9,... | collective-permute-start | bytes 98312 | tf_op jit(solution)/shard_map/ppermute | solution.py:18
  36.6 4.4 %collective-permute-start.10 = (f32[4,18,1,128]{3,2,0,1:T(1,128)S(1)}, f32[4,18,1,128]{3,2,0,1:T(1,128)S(1)}, u32[]{:S(2)}, u32[]{:S(2)}) collective-permute-start(f32[4,18,1,128]{3,2,0,1:T(1,128)S(1)} %get-tuple-element.19), channel_id=1, source_target_pairs={{1,0},{2,1},{3,2},{5,4},{6,5},{7,6},{9,8},{10,9},{11,10},{13,12},{... | collective-permute-start | bytes 110600 | tf_op jit(solution)/shard_map/ppermute | solution.py:21
  37.9 3.9 %collective-permute-start.11 = (f32[4,18,1,128]{3,2,0,1:T(1,128)S(1)}, f32[4,18,1,128]{3,2,0,1:T(1,128)S(1)}, u32[]{:S(2)}, u32[]{:S(2)}) collective-permute-start(f32[4,18,1,128]{3,2,0,1:T(1,128)S(1)} %get-tuple-element.20), channel_id=1, source_target_pairs={{0,1},{1,2},{2,3},{4,5},{5,6},{6,7},{8,9},{9,10},{10,11},{12,13},{... | collective-permute-start | bytes 110600 | tf_op jit(solution)/shard_map/ppermute | solution.py:18
  42.1 107.4 %collective-permute-start.12 = (f32[4,1,16,128]{3,2,0,1:T(8,128)S(1)}, f32[4,1,16,128]{3,2,0,1:T(8,128)S(1)}, u32[]{:S(2)}, u32[]{:S(2)}) collective-permute-start(f32[4,1,16,128]{3,2,0,1:T(8,128)S(1)} %get-tuple-element.35), channel_id=1, source_target_pairs={{4,0},{8,4},{12,8},{16,12},{20,16},{24,20},{28,24},{5,1},{9,5},{13... | collective-permute-start | bytes 98312 | tf_op jit(solution)/shard_map/ppermute | solution.py:21
  43.4 106.1 %collective-permute-start.13 = (f32[4,1,16,128]{3,2,0,1:T(8,128)S(1)}, f32[4,1,16,128]{3,2,0,1:T(8,128)S(1)}, u32[]{:S(2)}, u32[]{:S(2)}) collective-permute-start(f32[4,1,16,128]{3,2,0,1:T(8,128)S(1)} %get-tuple-element.34), channel_id=1, source_target_pairs={{0,4},{4,8},{8,12},{12,16},{16,20},{20,24},{24,28},{1,5},{5,9},{9,... | collective-permute-start | bytes 98312 | tf_op jit(solution)/shard_map/ppermute | solution.py:18
  149.6 15.2 %collective-permute-start.14 = (f32[4,18,1,128]{3,2,0,1:T(1,128)S(1)}, f32[4,18,1,128]{3,2,0,1:T(1,128)S(1)}, u32[]{:S(2)}, u32[]{:S(2)}) collective-permute-start(f32[4,18,1,128]{3,2,0,1:T(1,128)S(1)} %get-tuple-element.17), channel_id=1, source_target_pairs={{1,0},{2,1},{3,2},{5,4},{6,5},{7,6},{9,8},{10,9},{11,10},{13,12},{... | collective-permute-start | bytes 110600 | tf_op jit(solution)/shard_map/ppermute | solution.py:21
  150.9 13.9 %collective-permute-start.15 = (f32[4,18,1,128]{3,2,0,1:T(1,128)S(1)}, f32[4,18,1,128]{3,2,0,1:T(1,128)S(1)}, u32[]{:S(2)}, u32[]{:S(2)}) collective-permute-start(f32[4,18,1,128]{3,2,0,1:T(1,128)S(1)} %get-tuple-element.18), channel_id=1, source_target_pairs={{0,1},{1,2},{2,3},{4,5},{5,6},{6,7},{8,9},{9,10},{10,11},{12,13},{... | collective-permute-start | bytes 110600 | tf_op jit(solution)/shard_map/ppermute | solution.py:18
  154.7 28.6 %collective-permute-start.2 = (f32[3,22,3,128]{3,2,1,0:T(4,128)}, f32[3,22,3,128]{3,2,1,0:T(4,128)}, u32[]{:S(2)}, u32[]{:S(2)}) collective-permute-start(f32[3,22,3,128]{3,2,1,0:T(4,128)} %get-tuple-element.23), channel_id=1, source_target_pairs={{0,1},{1,2},{2,3},{4,5},{5,6},{6,7},{8,9},{9,10},{10,11},{12,13},{... | collective-permute-start | bytes 304136 | tf_op jit(solution)/shard_map/ppermute | solution.py:18
  162.1 21.2 %collective-permute-start.3 = (f32[3,22,3,128]{3,2,1,0:T(4,128)}, f32[3,22,3,128]{3,2,1,0:T(4,128)}, u32[]{:S(2)}, u32[]{:S(2)}) collective-permute-start(f32[3,22,3,128]{3,2,1,0:T(4,128)} %get-tuple-element.24), channel_id=1, source_target_pairs={{1,0},{2,1},{3,2},{5,4},{6,5},{7,6},{9,8},{10,9},{11,10},{13,12},{... | collective-permute-start | bytes 304136 | tf_op jit(solution)/shard_map/ppermute | solution.py:21
  165.6 1.0 copy-start.2
  180.7 3.6 %collective-permute-start.16 = (f32[4,1,16,128]{3,2,1,0:T(8,128)S(1)}, f32[4,1,16,128]{3,2,1,0:T(8,128)S(1)}, u32[]{:S(2)}, u32[]{:S(2)}) collective-permute-start(f32[4,1,16,128]{3,2,1,0:T(8,128)S(1)} %get-tuple-element.32), channel_id=1, source_target_pairs={{0,4},{4,8},{8,12},{12,16},{16,20},{20,24},{24,28},{1,5},{5,9},{9,... | collective-permute-start | bytes 98312 | tf_op jit(solution)/shard_map/ppermute | solution.py:18
  182.0 6.0 %collective-permute-start.17 = (f32[4,1,16,128]{3,2,1,0:T(8,128)S(1)}, f32[4,1,16,128]{3,2,1,0:T(8,128)S(1)}, u32[]{:S(2)}, u32[]{:S(2)}) collective-permute-start(f32[4,1,16,128]{3,2,1,0:T(8,128)S(1)} %get-tuple-element.33), channel_id=1, source_target_pairs={{4,0},{8,4},{12,8},{16,12},{20,16},{24,20},{28,24},{5,1},{9,5},{13... | collective-permute-start | bytes 98312 | tf_op jit(solution)/shard_map/ppermute | solution.py:21
  188.1 11.9 %collective-permute-start.18 = (f32[4,18,1,128]{3,2,1,0:T(1,128)S(1)}, f32[4,18,1,128]{3,2,1,0:T(1,128)S(1)}, u32[]{:S(2)}, u32[]{:S(2)}) collective-permute-start(f32[4,18,1,128]{3,2,1,0:T(1,128)S(1)} %get-tuple-element.15), channel_id=1, source_target_pairs={{0,1},{1,2},{2,3},{4,5},{5,6},{6,7},{8,9},{9,10},{10,11},{12,13},{... | collective-permute-start | bytes 110600 | tf_op jit(solution)/shard_map/ppermute | solution.py:18
  190.1 9.8 %collective-permute-start.19 = (f32[4,18,1,128]{3,2,1,0:T(1,128)S(1)}, f32[4,18,1,128]{3,2,1,0:T(1,128)S(1)}, u32[]{:S(2)}, u32[]{:S(2)}) collective-permute-start(f32[4,18,1,128]{3,2,1,0:T(1,128)S(1)} %get-tuple-element.16), channel_id=1, source_target_pairs={{1,0},{2,1},{3,2},{5,4},{6,5},{7,6},{9,8},{10,9},{11,10},{13,12},{... | collective-permute-start | bytes 110600 | tf_op jit(solution)/shard_map/ppermute | solution.py:21
  200.2 5.1 %collective-permute-start.20 = (f32[4,1,16,128]{3,2,1,0:T(8,128)S(1)}, f32[4,1,16,128]{3,2,1,0:T(8,128)S(1)}, u32[]{:S(2)}, u32[]{:S(2)}) collective-permute-start(f32[4,1,16,128]{3,2,1,0:T(8,128)S(1)} %get-tuple-element.30), channel_id=1, source_target_pairs={{0,4},{4,8},{8,12},{12,16},{16,20},{20,24},{24,28},{1,5},{5,9},{9,... | collective-permute-start | bytes 98312 | tf_op jit(solution)/shard_map/ppermute | solution.py:18
  203.8 5.8 %collective-permute-start.21 = (f32[4,1,16,128]{3,2,1,0:T(8,128)S(1)}, f32[4,1,16,128]{3,2,1,0:T(8,128)S(1)}, u32[]{:S(2)}, u32[]{:S(2)}) collective-permute-start(f32[4,1,16,128]{3,2,1,0:T(8,128)S(1)} %get-tuple-element.31), channel_id=1, source_target_pairs={{4,0},{8,4},{12,8},{16,12},{20,16},{24,20},{28,24},{5,1},{9,5},{13... | collective-permute-start | bytes 98312 | tf_op jit(solution)/shard_map/ppermute | solution.py:21
  209.7 13.0 %collective-permute-start.22 = (f32[4,18,1,128]{3,2,1,0:T(1,128)S(1)}, f32[4,18,1,128]{3,2,1,0:T(1,128)S(1)}, u32[]{:S(2)}, u32[]{:S(2)}) collective-permute-start(f32[4,18,1,128]{3,2,1,0:T(1,128)S(1)} %get-tuple-element.13), channel_id=1, source_target_pairs={{0,1},{1,2},{2,3},{4,5},{5,6},{6,7},{8,9},{9,10},{10,11},{12,13},{... | collective-permute-start | bytes 110600 | tf_op jit(solution)/shard_map/ppermute | solution.py:18
  212.8 9.9 %collective-permute-start.23 = (f32[4,18,1,128]{3,2,1,0:T(1,128)S(1)}, f32[4,18,1,128]{3,2,1,0:T(1,128)S(1)}, u32[]{:S(2)}, u32[]{:S(2)}) collective-permute-start(f32[4,18,1,128]{3,2,1,0:T(1,128)S(1)} %get-tuple-element.14), channel_id=1, source_target_pairs={{1,0},{2,1},{3,2},{5,4},{6,5},{7,6},{9,8},{10,9},{11,10},{13,12},{... | collective-permute-start | bytes 110600 | tf_op jit(solution)/shard_map/ppermute | solution.py:21
  223.0 18.9 %copy-start.3 = (f32[4,16,16,128]{3,2,1,0:T(8,128)S(1)}, f32[4,16,16,128]{3,2,1,0:T(8,128)}, u32[]{:S(2)}) copy-start(f32[4,16,16,128]{3,2,1,0:T(8,128)} %param.14) | copy-start | bytes 1572868
  223.1 4.8 %collective-permute-start.24 = (f32[4,1,16,128]{3,2,1,0:T(8,128)S(1)}, f32[4,1,16,128]{3,2,1,0:T(8,128)S(1)}, u32[]{:S(2)}, u32[]{:S(2)}) collective-permute-start(f32[4,1,16,128]{3,2,1,0:T(8,128)S(1)} %get-tuple-element.25), channel_id=1, source_target_pairs={{0,4},{4,8},{8,12},{12,16},{16,20},{20,24},{24,28},{1,5},{5,9},{9,... | collective-permute-start | bytes 98312 | tf_op jit(solution)/shard_map/ppermute | solution.py:18
  226.3 5.8 %collective-permute-start.25 = (f32[4,1,16,128]{3,2,1,0:T(8,128)S(1)}, f32[4,1,16,128]{3,2,1,0:T(8,128)S(1)}, u32[]{:S(2)}, u32[]{:S(2)}) collective-permute-start(f32[4,1,16,128]{3,2,1,0:T(8,128)S(1)} %get-tuple-element.26), channel_id=1, source_target_pairs={{4,0},{8,4},{12,8},{16,12},{20,16},{24,20},{28,24},{5,1},{9,5},{13... | collective-permute-start | bytes 98312 | tf_op jit(solution)/shard_map/ppermute | solution.py:21
  232.2 7.3 %collective-permute-start.26 = (f32[4,18,1,128]{3,2,1,0:T(1,128)S(1)}, f32[4,18,1,128]{3,2,1,0:T(1,128)S(1)}, u32[]{:S(2)}, u32[]{:S(2)}) collective-permute-start(f32[4,18,1,128]{3,2,1,0:T(1,128)S(1)} %get-tuple-element.11), channel_id=1, source_target_pairs={{0,1},{1,2},{2,3},{4,5},{5,6},{6,7},{8,9},{9,10},{10,11},{12,13},{... | collective-permute-start | bytes 110600 | tf_op jit(solution)/shard_map/ppermute | solution.py:18
  236.2 5.8 %collective-permute-start.27 = (f32[4,18,1,128]{3,2,1,0:T(1,128)S(1)}, f32[4,18,1,128]{3,2,1,0:T(1,128)S(1)}, u32[]{:S(2)}, u32[]{:S(2)}) collective-permute-start(f32[4,18,1,128]{3,2,1,0:T(1,128)S(1)} %get-tuple-element.12), channel_id=1, source_target_pairs={{1,0},{2,1},{3,2},{5,4},{6,5},{7,6},{9,8},{10,9},{11,10},{13,12},{... | collective-permute-start | bytes 110600 | tf_op jit(solution)/shard_map/ppermute | solution.py:21
  237.5 0.7 copy-start.12
  256.6 0.7 copy-start.5
where the time goes:
time: 259 us; the launch traced here: 258 us
  blocking collectives  113 us (44%)
  starting transfers between devices  72.2 us (28%)
  other arithmetic  36.2 us (14%)
  waiting for transfers between devices  18.5 us (7%)
  local copies, waits for them, and re-layouts  14 us (5%)
    all_gather x3, blocking collectives, observed_values(): gathered = lax.all_gather(obs_rows[:, step, :], 'gx', axis=0, tiled=True)  93.9 us
    ppermute x14, starting transfers between devices, padded_2(): lax.ppermute(lax.slice_in_dim(block, block.shape[dim] - width, None, axis...  53.8 us
    scatter-add x3, other arithmetic, on_device(): jax.ops.segment_sum(misfit[:, None, None] * weights, slots, num_segments=...  25 us
    ppermute x14, starting transfers between devices, padded_2(): lax.ppermute(lax.slice_in_dim(block, 0, width, axis=dim), axis, backward)  18.4 us
    ppermute x14, waiting for transfers between devices, padded_2(): lax.ppermute(lax.slice_in_dim(block, 0, width, axis=dim), axis, backward)  14.7 us
    unnamed x1, blocking collectives  12.8 us
    all_gather x1, blocking collectives, on_device(): piece = lax.all_gather(alpha, 'gy', axis=1, tiled=True)  6.39 us
  transfers between devices with their start and end apart: 28, of which 9 were waited for; matrix products, arithmetic and copies ran while one was open for 17% of the time, Pallas kernels for 0%

commit v1 on v0

v1 whole, which is shorter than its diff:
```python
import jax
import jax.numpy as jnp
from jax import lax
from jax.experimental import pallas as pl
from jax.experimental.pallas import tpu as pltpu
from jax.sharding import PartitionSpec as P

STEPS = 3
RIM = 3
INNER = RIM - 1
NC = 4
CX = 16
CY = 16
BLOCKS = CX + 8
PITCH = CY + 8
FIRST = 4
FIELD = BLOCKS * PITCH
NORTH = CY
SOUTH = PITCH - RIM

X_COEF = NC * RIM * CY
X_ALPHA = X_COEF + 3 * INNER * CY
Y_COEF = NC * RIM * BLOCKS
Y_ALPHA = Y_COEF + 3 * INNER * BLOCKS

profile_weight = 0.125
f32 = jnp.float32
bf16 = jnp.bfloat16

VMEM = pl.BlockSpec(memory_space=pltpu.VMEM)
ANY = pl.BlockSpec(memory_space=pl.ANY)


def call(body, outs, ins, scratch=(), in_specs=None, aliases=None, flops=1000000, limit=40 * 2**20):
    single = not isinstance(outs, list)
    shapes = [jax.ShapeDtypeStruct(shape, f32) for shape in ([outs] if single else outs)]
    size = sum(4 * value.size for value in ins)
    got = pl.pallas_call(
        body,
        out_shape=shapes,
        in_specs=in_specs or [VMEM] * len(ins),
        out_specs=[VMEM] * len(shapes),
        scratch_shapes=list(scratch),
        input_output_aliases=aliases or {},
        compiler_params=pltpu.CompilerParams(vmem_limit_bytes=limit),
        cost_estimate=pl.CostEstimate(flops=flops, bytes_accessed=size, transcendentals=0),
    )(*ins)
    return got[0] if single else got


def parity(axis):
    return lax.rem(lax.axis_index(axis), 2) == 0


def pair_a(block, axis):
    count = lax.axis_size(axis)
    return lax.ppermute(block, axis, [(i, i ^ 1) for i in range(count)])


def pair_b(block, axis, wrap):
    count = lax.axis_size(axis)
    pairs = []
    for low in range(1, count, 2):
        other = (low + 1) % count
        if other or wrap:
            pairs += [(low, other), (other, low)]
    return lax.ppermute(block, axis, pairs)


def partner(axis, xor):
    return [(i, i ^ xor) for i in range(lax.axis_size(axis))]


def split(value):
    top = value.astype(bf16)
    return top, (value - top.astype(f32)).astype(bf16)


def pack_x(delta, eddy, courant, alpha, tiles, out_a, out_b):
    even = parity("gx")

    def put(at, count, east_side, west_side):
        out_a[at : at + count] = jnp.where(even, east_side, west_side)
        out_b[at : at + count] = jnp.where(even, west_side, east_side)

    wide = RIM * CY
    for c in range(NC):
        put(c * wide, wide, delta[c, CX * CY - wide :], delta[c, :wide])
    slim = INNER * CY
    for f in range(3):
        field = eddy if f == 0 else courant.at[f - 1]
        put(X_COEF + f * slim, slim, field[CX * CY - slim :], field[:slim])
    own = alpha[...]
    put(X_ALPHA, own.shape[0], own, own)
    at = X_ALPHA + own.shape[0]
    for out in (out_a, out_b):
        out[at : at + CX] = jnp.full((CX, 128), -1.0, f32)
        out[at : at + CX, 0:CY] = tiles[...].astype(f32)


def pack_y(delta, eddy, courant, alpha, tiles, got_a, got_b, out_a, out_b, shared):
    even = parity("gy")
    even_x = parity("gx")
    owned = alpha.shape[0]
    out_a[...] = jnp.zeros(out_a.shape, f32)
    out_b[...] = jnp.zeros(out_b.shape, f32)

    def sides(rows):
        first, second = got_a[rows], got_b[rows]
        return jnp.where(even_x, second, first), jnp.where(even_x, first, second)

    def put(at, count, north_side, south_side):
        out_a[at : at + count] = jnp.where(even, north_side, south_side)
        out_b[at : at + count] = jnp.where(even, south_side, north_side)

    def edge(at, own, base, layers, north_y, south_y):
        north_w, north_e = sides(pl.ds(base + north_y, layers, stride=CY))
        south_w, south_e = sides(pl.ds(base + south_y, layers, stride=CY))
        put(at + FIRST - layers, layers, north_w, south_w)
        put(
            at + FIRST,
            CX,
            own[pl.ds(north_y, CX, stride=CY)],
            own[pl.ds(south_y, CX, stride=CY)],
        )
        put(at + FIRST + CX, layers, north_e, south_e)

    for c in range(NC):
        for d in range(RIM):
            edge((c * RIM + d) * BLOCKS, delta.at[c], c * RIM * CY, RIM, CY - RIM + d, d)
    for f in range(3):
        for d in range(INNER):
            edge(
                Y_COEF + (f * INNER + d) * BLOCKS,
                eddy if f == 0 else courant.at[f - 1],
                X_COEF + f * INNER * CY,
                INNER,
                CY - INNER + d,
                d,
            )
    west, east = sides(pl.ds(X_ALPHA, owned))
    shared[0:owned] = west
    shared[owned : 2 * owned] = alpha[...]
    shared[2 * owned : 3 * owned] = east
    west, east = sides(pl.ds(X_ALPHA + owned, CX))
    at = 3 * owned
    shared[at : at + BLOCKS] = jnp.full((BLOCKS, 128), -1.0, f32)
    shared[at + FIRST - RIM : at + FIRST] = west[CX - RIM :]
    shared[at + FIRST : at + FIRST + CX, 0:CY] = tiles[...].astype(f32)
    shared[at + FIRST + CX : at + FIRST + CX + RIM] = east[:RIM]
    whole = shared[...]
    for out in (out_a, out_b):
        out[Y_ALPHA:] = whole


def main(
    ny,
    parts,
    delta,
    eddy,
    courant,
    gate_beam,
    gate_index,
    gate_column,
    gate_live,
    precision,
    weights,
    x_a,
    x_b,
    shared,
    y_a,
    y_b,
    *rest,
):
    others = rest[: ny - 3]
    beams = rest[ny - 3 : ny - 3 + parts]
    out_a, out_b, out_sums, out_adjoint = rest[ny - 3 + parts : ny + 1 + parts]
    (state_0, state_1, coef, forcing, known, picks, meta, tiles, table, sums) = rest[
        ny + 1 + parts :
    ]
    per_slot = shared.shape[0] - BLOCKS
    group = per_slot // NC
    owned = group // 3
    total = ny * group
    me = lax.axis_index("gy")
    me_x = lax.axis_index("gx")
    even = parity("gy")
    even_x = parity("gx")
    has_south = me > 0
    has_north = me < ny - 1

    def x_sides(rows):
        first, second = x_a[rows], x_b[rows]
        return jnp.where(even_x, second, first), jnp.where(even_x, first, second)

    def y_sides(rows):
        first, second = y_a[rows], y_b[rows]
        north, south = jnp.where(even, first, second), jnp.where(even, second, first)
        return jnp.where(has_north, north, 0.0), jnp.where(has_south, south, 0.0)

    coef[...] = jnp.zeros(coef.shape, f32)
    state_0[...] = jnp.zeros(state_0.shape, f32)
    state_1[...] = jnp.zeros(state_1.shape, f32)

    def place(ref, base, own, x_base, layers, y_base, south_row):
        for x in range(CX):
            at = base + (FIRST + x) * PITCH
            ref[at : at + CY] = own[x * CY : (x + 1) * CY]
        for h in range(layers):
            west, east = x_sides(pl.ds(x_base + h * CY, CY))
            at = base + (FIRST - layers + h) * PITCH
            ref[at : at + CY] = west
            at = base + (FIRST + CX + h) * PITCH
            ref[at : at + CY] = east
        for d in range(layers):
            north, south = y_sides(pl.ds(y_base + d * BLOCKS, BLOCKS))
            ref[pl.ds(base + NORTH + d, BLOCKS, stride=PITCH)] = north
            ref[pl.ds(base + south_row + d, BLOCKS, stride=PITCH)] = south

    for c in range(NC):
        place(
            state_0,
            c * FIELD,
            delta.at[c],
            c * RIM * CY,
            RIM,
            c * RIM * BLOCKS,
            SOUTH,
        )
    for f in range(3):
        place(
            coef,
            f * FIELD,
            eddy if f == 0 else courant.at[f - 1],
            X_COEF + f * INNER * CY,
            INNER,
            Y_COEF + f * INNER * BLOCKS,
            SOUTH + 1,
        )

    def combine(b, carry):
        at = pl.multiple_of(b * PITCH, 8)
        viscous = coef[pl.ds(at, PITCH)]
        along_x = 0.5 * coef[pl.ds(FIELD + at, PITCH)]
        along_y = 0.5 * coef[pl.ds(2 * FIELD + at, PITCH)]
        coef[pl.ds(at, PITCH)] = 1.0 - 4.0 * viscous
        coef[pl.ds(FIELD + at, PITCH)] = viscous - along_x
        coef[pl.ds(2 * FIELD + at, PITCH)] = viscous + along_x
        coef[pl.ds(3 * FIELD + at, PITCH)] = viscous - along_y
        coef[pl.ds(4 * FIELD + at, PITCH)] = viscous + along_y
        return carry

    lax.fori_loop(0, BLOCKS, combine, 0)

    known[0:per_slot] = shared[0:per_slot]
    known[per_slot : 2 * per_slot] = y_a[Y_ALPHA : Y_ALPHA + per_slot]
    known[2 * per_slot : 3 * per_slot] = y_b[Y_ALPHA : Y_ALPHA + per_slot]
    for s, other in enumerate(others):
        known[(3 + s) * per_slot : (4 + s) * per_slot] = other[0:per_slot]
    lane = lax.broadcasted_iota(jnp.int32, (1, total), 1)
    partner_a = jnp.where(even, me + 1, me - 1)
    partner_b = lax.rem(jnp.where(even, me - 1, me + 1) + ny, ny)
    owner = [me, partner_a, partner_b] + [lax.rem(me - s + ny, ny) for s in range(2, ny - 1)]
    tile_ids = []
    for strip in range(3):
        ids = jnp.full((1, total), -2, jnp.int32)
        for s in range(ny):
            base = s * group + strip * owned
            ids = jnp.where(
                (lane >= base) & (lane < base + owned), owner[s] * owned + lane - base, ids
            )
        tile_ids.append(ids.astype(f32))
    spot = lax.broadcasted_iota(jnp.int32, (BLOCKS, 128), 1)
    from_north, from_south = y_sides(pl.ds(Y_ALPHA + per_slot, BLOCKS))
    near = jnp.where(
        (spot >= NORTH) & (spot < NORTH + RIM) & has_north,
        pltpu.roll(from_north, NORTH, 1),
        jnp.where(
            (spot >= SOUTH) & (spot < PITCH) & has_south,
            pltpu.roll(from_south, PITCH - CY, 1),
            -1.0,
        ),
    )
    tiles[...] = jnp.full(tiles.shape, -1.0, f32)
    tiles[0:BLOCKS] = jnp.where(spot < CY, shared[per_slot:], near)
    turned = jnp.transpose(tiles[...])[0:PITCH]
    for b in range(BLOCKS):
        strip = 0 if b < FIRST else 1 if b < FIRST + CX else 2
        picks[b * PITCH : (b + 1) * PITCH] = (turned[:, b : b + 1] == tile_ids[strip]).astype(f32)

    def by_variable(ref, count):
        return jnp.concatenate([ref[pl.ds(c, count, stride=NC)] for c in range(NC)], axis=1)

    def two_part_dot(left, value):
        top, low = split(value)
        return jnp.dot(left, top, preferred_element_type=f32) + jnp.dot(
            left, low, preferred_element_type=f32
        )

    profiles = two_part_dot(picks[...].astype(bf16), by_variable(known, total))
    for c in range(NC):
        state_0[c * FIELD : (c + 1) * FIELD] += (
            profile_weight * profiles[:, c * 128 : (c + 1) * 128]
        )

    slots = gate_column.shape[1]
    per_beam = table.shape[0] // STEPS
    beam = gate_beam[...]
    block = beams[0].shape[0] // STEPS
    relative = jnp.bitwise_xor(beam >> 3, me_x) * 8 + (beam & 7)
    meta[...] = jnp.zeros(meta.shape, f32)
    meta[0:1] = gate_column[...].astype(f32)
    meta[1:2] = relative.astype(f32)
    meta[2:3] = gate_index[...].astype(f32)
    meta[3:4] = gate_live[...].astype(f32) * precision[...]
    columns = jnp.transpose(meta[...])
    scaled = columns[:, 3:4]
    slot_lane = lax.broadcasted_iota(jnp.int32, (slots, CX * CY), 1).astype(f32)
    slot_pick = (slot_lane == columns[:, 0:1]).astype(f32).astype(bf16)
    column_row = lax.broadcasted_iota(jnp.int32, (CX * CY, slots), 0)
    slot_push = (column_row == gate_column[...]).astype(f32).astype(bf16)
    beam_lane = lax.broadcasted_iota(jnp.int32, (slots, per_beam), 1).astype(f32)
    beam_pick = (beam_lane == columns[:, 1:2]).astype(f32).astype(bf16)
    gate_lane = lax.broadcasted_iota(jnp.int32, (slots, 128), 1).astype(f32)
    gate_here = gate_lane == columns[:, 2:3]
    for p, part in enumerate(beams):
        table[p * block * STEPS : (p + 1) * block * STEPS] = part[...]

    def forward(source, target, low, high):
        def body(b, carry):
            at = pl.multiple_of(b * PITCH, 8)
            k = [coef[pl.ds(f * FIELD + at, PITCH)] for f in range(5)]
            for c in range(NC):
                base = c * FIELD + at
                here = source[pl.ds(base, PITCH)]
                target[pl.ds(base, PITCH)] = (
                    k[0] * here
                    + k[1] * source[pl.ds(base + PITCH, PITCH)]
                    + k[2] * source[pl.ds(base - PITCH, PITCH)]
                    + k[3] * pltpu.roll(here, PITCH - 1, 0)
                    + k[4] * pltpu.roll(here, 1, 0)
                )
            return carry

        lax.fori_loop(low, high, body, 0)

    buffers = [state_0, state_1]
    for step in range(STEPS):
        source, target = buffers[step % 2], buffers[(step + 1) % 2]
        forward(source, target, 2 + step, BLOCKS - 2 - step)
        own = jnp.concatenate(
            [
                jnp.concatenate(
                    [
                        target[c * FIELD + b * PITCH : c * FIELD + b * PITCH + CY]
                        for b in range(FIRST, FIRST + CX)
                    ],
                    axis=0,
                )
                for c in range(NC)
            ],
            axis=1,
        )
        picked = two_part_dot(slot_pick, own)
        rows = two_part_dot(beam_pick, table[pl.ds(step, per_beam, stride=STEPS)])
        tally = -jnp.where(gate_here, rows, 0.0)
        for c in range(NC):
            tally = tally + picked[:, c * 128 : (c + 1) * 128] * weights[pl.ds(c, slots, stride=NC)]
        misfit = scaled * jnp.sum(tally, axis=1, keepdims=True)
        pushed = jnp.concatenate(
            [misfit * weights[pl.ds(c, slots, stride=NC)] for c in range(NC)], axis=1
        )
        forcing[step * CX * CY : (step + 1) * CX * CY] = two_part_dot(slot_push, pushed)

    state_0[...] = jnp.zeros(state_0.shape, f32)
    state_1[...] = jnp.zeros(state_1.shape, f32)

    def add_forcing(ref, step):
        for c in range(NC):
            for x in range(CX):
                at = c * FIELD + (FIRST + x) * PITCH
                first = step * CX * CY + x * CY
                ref[at : at + CY] += forcing[first : first + CY, c * 128 : (c + 1) * 128]

    def backward(source, target, low, high):
        def body(b, carry):
            at = pl.multiple_of(b * PITCH, 8)
            k = [
                coef[pl.ds(at, PITCH)],
                coef[pl.ds(FIELD + at - PITCH, PITCH)],
                coef[pl.ds(2 * FIELD + at + PITCH, PITCH)],
                coef[pl.ds(3 * FIELD + at, PITCH)],
                coef[pl.ds(4 * FIELD + at, PITCH)],
            ]
            for c in range(NC):
                base = c * FIELD + at
                here = source[pl.ds(base, PITCH)]
                target[pl.ds(base, PITCH)] = (
                    k[0] * here
                    + k[1] * source[pl.ds(base - PITCH, PITCH)]
                    + k[2] * source[pl.ds(base + PITCH, PITCH)]
                    + pltpu.roll(k[3] * here, 1, 0)
                    + pltpu.roll(k[4] * here, PITCH - 1, 0)
                )
            return carry

        lax.fori_loop(low, high, body, 0)

    for step in range(STEPS):
        source, target = buffers[step % 2], buffers[(step + 1) % 2]
        add_forcing(source, STEPS - 1 - step)
        backward(source, target, FIRST - 1 - step, FIRST + CX + 1 + step)
    final = buffers[STEPS % 2]

    adjoint = jnp.concatenate([final[c * FIELD : (c + 1) * FIELD] for c in range(NC)], axis=1)
    top, low = split(adjoint)
    turned = jnp.transpose(picks[...]).astype(bf16)
    tile_sums = jnp.dot(turned, top, preferred_element_type=f32) + jnp.dot(
        turned, low, preferred_element_type=f32
    )
    for c in range(NC):
        sums[pl.ds(c, total, stride=NC)] = tile_sums[:, c * 128 : (c + 1) * 128]
    edge_rows = NC * RIM * BLOCKS
    for c in range(NC):
        for d in range(RIM):
            north = final[pl.ds(c * FIELD + NORTH + d, BLOCKS, stride=PITCH)]
            south = final[pl.ds(c * FIELD + SOUTH + d, BLOCKS, stride=PITCH)]
            at = (c * RIM + d) * BLOCKS
            out_a[at : at + BLOCKS] = jnp.where(even, north, south)
            out_b[at : at + BLOCKS] = jnp.where(even, south, north)
    out_a[edge_rows:] = sums[per_slot : 2 * per_slot]
    out_b[edge_rows:] = sums[2 * per_slot : 3 * per_slot]
    out_sums[0:per_slot] = sums[0:per_slot]
    out_sums[per_slot:] = sums[3 * per_slot :]
    for c in range(NC):
        for b in range(BLOCKS):
            at = (c * BLOCKS + b) * CY
            first = c * FIELD + b * PITCH
            out_adjoint[at : at + CY] = final[first : first + CY]


def add_y(ny, delta, alpha, sums, adjoint, got_a, got_b, *rest):
    others = rest[: ny - 3]
    out_a, out_b, out_delta, out_alpha, field = rest[ny - 3 :]
    owned = alpha.shape[0]
    even = parity("gy")
    even_x = parity("gx")
    me = lax.axis_index("gy")
    field[...] = adjoint[...]
    for c in range(NC):
        for d in range(RIM):
            rows = pl.ds((c * RIM + d) * BLOCKS, BLOCKS)
            first, second = got_a[rows], got_b[rows]
            north = jnp.where(me < ny - 1, jnp.where(even, first, second), 0.0)
            south = jnp.where(me > 0, jnp.where(even, second, first), 0.0)
            low = pl.ds(c * BLOCKS * CY + d, BLOCKS, stride=CY)
            high = pl.ds(c * BLOCKS * CY + CY - RIM + d, BLOCKS, stride=CY)
            field[low] = field[low] + south
            field[high] = field[high] + north
    tail = NC * RIM * BLOCKS
    total = sums[0 : 3 * owned] + got_a[tail:] + got_b[tail:]
    for other in others:
        total = total + other[...]
    wide = RIM * CY
    for c in range(NC):
        base = c * BLOCKS * CY
        west = field[base + CY : base + CY + wide]
        at = base + (FIRST + CX) * CY
        east = field[at : at + wide]
        out_a[c * wide : (c + 1) * wide] = jnp.where(even_x, east, west)
        out_b[c * wide : (c + 1) * wide] = jnp.where(even_x, west, east)
        at = base + FIRST * CY
        out_delta[c] = delta[c] + field[at : at + CX * CY]
    west, east = total[0:owned], total[2 * owned :]
    out_a[NC * wide :] = jnp.where(even_x, east, west)
    out_b[NC * wide :] = jnp.where(even_x, west, east)
    out_alpha[...] = alpha[...] + profile_weight * total[owned : 2 * owned]


def add_x(near_delta, near_alpha, got_a, got_b, out_delta, out_alpha):
    even_x = parity("gx")
    wide = RIM * CY
    out_delta[...] = near_delta[...]
    for c in range(NC):
        rows = pl.ds(c * wide, wide)
        first, second = got_a[rows], got_b[rows]
        out_delta[c, 0:wide] += jnp.where(even_x, second, first)
        out_delta[c, CX * CY - wide :] += jnp.where(even_x, first, second)
    out_alpha[...] = near_alpha[...] + profile_weight * (
        got_a[NC * wide :] + got_b[NC * wide :]
    )


def on_device(
    delta,
    alpha,
    eddy,
    courant,
    tile_map,
    obs_rows,
    gate_beam,
    gate_index,
    gate_column,
    gate_live,
    obs_weight,
    obs_precision,
):
    nx = lax.axis_size("gx")
    ny = lax.axis_size("gy")
    owned = alpha.shape[1]
    slots = gate_column.shape[2]
    fine = delta.reshape(NC, CX * CY, 128)
    eddy = eddy.reshape(CX * CY, 128)
    courant = courant.reshape(2, CX * CY, 128)
    control = alpha.reshape(owned * NC, 128)
    weights = obs_weight.reshape(slots * NC, 128)
    gates = [
        value.reshape(1, slots)
        for value in (gate_beam, gate_index, gate_column, gate_live, obs_precision)
    ]
    beam_rows = obs_rows.reshape(-1, 128)

    x_rows = X_ALPHA + owned * NC + CX
    pieces = call(pack_x, [(x_rows, 128)] * 2, [fine, eddy, courant, control, tile_map])
    x_a = pair_a(pieces[0], "gx")
    x_b = pair_b(pieces[1], "gx", False)
    beam_pair = jnp.concatenate([beam_rows, pair_a(beam_rows, "gx")])

    shared_rows = 3 * owned * NC + BLOCKS
    y_rows = Y_ALPHA + shared_rows
    piece_a, piece_b, shared = call(
        pack_y,
        [(y_rows, 128), (y_rows, 128), (shared_rows, 128)],
        [fine, eddy, courant, control, tile_map, x_a, x_b],
    )
    y_a = pair_a(piece_a, "gy")
    y_b = pair_b(piece_b, "gy", True)
    others = [
        lax.ppermute(shared, "gy", [(i, (i + s) % ny) for i in range(ny)])
        for s in range(2, ny - 1)
    ]
    beams = [beam_pair] + [
        lax.ppermute(beam_pair, "gx", partner("gx", xor)) for xor in range(2, nx, 2)
    ]

    per_slot = 3 * owned * NC
    total = ny * 3 * owned
    edge_rows = NC * RIM * BLOCKS
    back_a, back_b, sums, adjoint = call(
        lambda *refs: main(ny, len(beams), *refs),
        [
            (edge_rows + per_slot, 128),
            (edge_rows + per_slot, 128),
            ((ny - 2) * per_slot, 128),
            (NC * BLOCKS * CY, 128),
        ],
        [fine, eddy, courant, *gates, weights, x_a, x_b, shared, y_a, y_b, *others, *beams],
        [
            pltpu.VMEM((NC * FIELD, 128), f32),
            pltpu.VMEM((NC * FIELD, 128), f32),
            pltpu.VMEM((5 * FIELD, 128), f32),
            pltpu.VMEM((STEPS * CX * CY, NC * 128), f32),
            pltpu.VMEM((ny * per_slot, 128), f32),
            pltpu.VMEM((FIELD, total), f32),
            pltpu.VMEM((8, slots), f32),
            pltpu.VMEM((128, 128), f32),
            pltpu.VMEM((nx * beam_rows.shape[0], 128), f32),
            pltpu.VMEM((ny * per_slot, 128), f32),
        ],
        flops=30000000,
    )
    got_a = pair_a(back_a, "gy")
    got_b = pair_b(back_b, "gy", True)
    got_others = [
        lax.ppermute(
            sums[(s - 1) * per_slot : s * per_slot], "gy", [(i, (i - s) % ny) for i in range(ny)]
        )
        for s in range(2, ny - 1)
    ]
    home_rows = NC * RIM * CY + owned * NC
    home_a, home_b, near_delta, near_alpha = call(
        lambda *refs: add_y(ny, *refs),
        [(home_rows, 128), (home_rows, 128), fine.shape, control.shape],
        [fine, control, sums, adjoint, got_a, got_b, *got_others],
        [pltpu.VMEM((NC * BLOCKS * CY, 128), f32)],
    )
    grad_delta, grad_alpha = call(
        add_x,
        [fine.shape, control.shape],
        [near_delta, near_alpha, pair_a(home_a, "gx"), pair_b(home_b, "gx", False)],
    )
    return grad_delta.reshape(delta.shape), grad_alpha.reshape(alpha.shape)


def solution(mesh):
    return jax.shard_map(
        on_device,
        mesh=mesh,
        in_specs=(
            P(None, "gx", "gy", None),
            P("gx", "gy", None, None),
            P("gx", "gy", None),
            P(None, "gx", "gy", None),
            P("gx", "gy"),
            P(("gx", "gy"), None, None),
            P("gx", "gy", None),
            P("gx", "gy", None),
            P("gx", "gy", None),
            P("gx", "gy", None),
            P("gx", "gy", None, None, None),
            P("gx", "gy", None),
        ),
        out_specs=(P(None, "gx", "gy", None), P("gx", "gy", None, None)),
        check_vma=False,
    )
```

time: 259 us -> 51.6 us (0.20)
  the two profiles are of different devices: /device:TPU:0 before, /device:TPU:4 now
where the time goes in v1:
time: 51.6 us; the launch traced here: 51.2 us
  waiting for transfers between devices  20.4 us (40%)
  starting transfers between devices  16 us (31%)
  Pallas kernels  8.97 us (17%)
  local copies, waits for them, and re-layouts  4.98 us (10%)
  between operations  0.89 us (2%)
    ppermute x4, starting transfers between devices, pair_b(): return lax.ppermute(block, axis, pairs)  9.78 us
    pallas_call x5, Pallas kernels, call(): pl.pallas_call(body, out_shape=shapes, in_specs=in_specs or [VMEM] * len(...  8.97 us
    ppermute x3, waiting for transfers between devices, on_device(): lax.ppermute(beam_pair, 'gx', partner('gx', xor))  5.89 us
    ppermute x5, waiting for transfers between devices, pair_a(): return lax.ppermute(block, axis, [(i, i ^ 1) for i in range(count)])  5.83 us
    ppermute x1, waiting for transfers between devices, on_device(): lax.ppermute(sums[(s - 1) * per_slot:s * per_slot], 'gy', [(i, (i - s) %...  5.12 us
    unnamed x36, local copies, waits for them, and re-layouts  4.97 us
    ppermute x4, waiting for transfers between devices, pair_b(): return lax.ppermute(block, axis, pairs)  3.54 us
    ppermute x3, starting transfers between devices, on_device(): lax.ppermute(beam_pair, 'gx', partner('gx', xor))  3.11 us
  transfers between devices with their start and end apart: 14, of which 6 were waited for; matrix products, arithmetic and copies ran while one was open for 0% of the time, Pallas kernels for 0%

profile of v1, /device:TPU:4, one launch (start us, length us, event | category | flops | bytes accessed | tf_op | source)
XLA Modules:
  0.0 51.2 jit_solution(7508201551366113198)
XLA Ops:
  0.6 0.0 copy-start
  0.6 1.0 %copy-done = f32[4,16,16,128]{3,2,1,0:T(8,128)S(1)} copy-done((f32[4,16,16,128]{3,2,1,0:T(8,128)S(1)}, f32[4,16,16,128]{3,2,1,0:T(8,128)}, u32[]{:S(2)}) %copy-start) | copy-done | bytes 524312
  1.7 0.0 copy-start.2
  1.7 0.9 %copy-done.2 = f32[2,16,16,128]{3,2,1,0:T(8,128)S(1)} copy-done((f32[2,16,16,128]{3,2,1,0:T(8,128)S(1)}, f32[2,16,16,128]{3,2,1,0:T(8,128)}, u32[]{:S(2)}) %copy-start.2) | copy-done | bytes 262168
  2.6 0.0 copy-start.4
  2.6 0.9 %copy-done.4 = f32[16,16,128]{2,1,0:T(8,128)S(1)} copy-done((f32[16,16,128]{2,1,0:T(8,128)S(1)}, f32[16,16,128]{2,1,0:T(8,128)}, u32[]{:S(2)}) %copy-start.4) | copy-done | bytes 131096
  3.5 0.0 copy-start.7
  3.5 0.7 %copy-done.7 = f32[1,4,4,128]{3,2,1,0:T(4,128)S(1)} copy-done((f32[1,4,4,128]{3,2,1,0:T(4,128)S(1)}, f32[1,4,4,128]{3,2,1,0:T(4,128)}, u32[]{:S(2)}) %copy-start.7) | copy-done | bytes 8216
  4.2 0.0 copy-start.9
  4.2 0.7 %copy-done.9 = s32[16,16]{1,0:T(8,128)S(1)} copy-done((s32[16,16]{1,0:T(8,128)S(1)}, s32[16,16]{1,0:T(8,128)}, u32[]{:S(2)}) %copy-start.9) | copy-done | bytes 1048
  4.9 0.0 copy-start.16
  4.9 0.0 copy-start.1
  4.9 0.0 copy-start.3
  4.9 0.0 copy-start.5
  5.0 0.1 collective-permute-start
  5.1 4.9 %collective-permute-start.1 = (f32[320,128]{1,0:T(8,128)S(1)}, f32[320,128]{1,0:T(8,128)S(1)}, u32[]{:S(2)}, u32[]{:S(2)}) collective-permute-start(f32[320,128]{1,0:T(8,128)S(1)} %get-tuple-element.18), channel_id=1, source_target_pairs={{4,8},{8,4},{12,16},{16,12},{20,24},{24,20},{5,9},{9,5},{13,17},{1... | collective-permute-start | bytes 491528 | tf_op jit(solution)/shard_map/ppermute | solution.py:67
  10.0 0.0 copy-done.16
  10.0 0.0 copy-start.8
  10.0 0.0 copy-start.10
  10.1 0.0 copy-start.6
  10.1 0.1 collective-permute-start.5
  10.1 4.5 %collective-permute-done.got_a.refs_9_ = f32[320,128]{1,0:T(8,128)S(1)} collective-permute-done((f32[320,128]{1,0:T(8,128)S(1)}, f32[320,128]{1,0:T(8,128)S(1)}, u32[]{:S(2)}, u32[]{:S(2)}) %collective-permute-start) | collective-permute-done | bytes 163872 | tf_op jit(solution)/shard_map/ppermute | solution.py:57
  14.6 0.0 collective-permute-done.1.got_b.refs_10_
  14.6 0.0 copy-done.1
  14.6 0.0 copy-done.3
  14.6 0.0 copy-done.5
  14.6 0.0 copy-done.8
  14.7 0.0 copy-done.10
  14.7 0.2 shard_map.132
  14.8 0.1 collective-permute-start.2
  14.9 1.6 %collective-permute-start.3 = (f32[504,128]{1,0:T(8,128)S(1)}, f32[504,128]{1,0:T(8,128)S(1)}, u32[]{:S(2)}, u32[]{:S(2)}) collective-permute-start(f32[504,128]{1,0:T(8,128)S(1)} %get-tuple-element.21), channel_id=1, source_target_pairs={{1,2},{2,1},{3,0},{0,3},{5,6},{6,5},{7,4},{4,7},{9,10},{10,9},{11,... | collective-permute-start | bytes 774152 | tf_op jit(solution)/shard_map/ppermute | solution.py:67
  16.5 0.0 collective-permute-done.5
  16.5 0.0 copy-start.14
  16.6 0.0 copy-start.15
  16.6 0.2 collective-permute-start.8
  16.7 0.5 %collective-permute-start.4 = (f32[72,128]{1,0:T(8,128)S(1)}, f32[72,128]{1,0:T(8,128)S(1)}, u32[]{:S(2)}, u32[]{:S(2)}) collective-permute-start(f32[72,128]{1,0:T(8,128)S(1)} %get-tuple-element.19.refs_11_), channel_id=1, source_target_pairs={{0,2},{1,3},{2,0},{3,1},{4,6},{5,7},{6,4},{7,5},{8,10},{9,11},{10,... | collective-permute-start | bytes 110600 | tf_op jit(solution)/shard_map/ppermute | solution.py:539
  17.3 2.9 %collective-permute-start.7 = (f32[48,128]{1,0:T(8,128)S(1)}, f32[48,128]{1,0:T(8,128)S(1)}, u32[]{:S(2)}, u32[]{:S(2)}) collective-permute-start(f32[48,128]{1,0:T(8,128)S(1)} %constant_dynamic-update-slice_fusion.refs_15_), channel_id=1, source_target_pairs={{0,16},{4,20},{8,24},{12,28},{16,0},{20,4},{24,8},{28,12},{1,17},{... | collective-permute-start | bytes 73736 | tf_op jit(solution)/shard_map/ppermute | solution.py:543
  20.2 2.1 %collective-permute-done.8.refs_18_ = f32[48,128]{1,0:T(8,128)S(1)} collective-permute-done((f32[48,128]{1,0:T(8,128)S(1)}, f32[48,128]{1,0:T(8,128)S(1)}, u32[]{:S(2)}, u32[]{:S(2)}) %collective-permute-start.8) | collective-permute-done | bytes 24608 | tf_op jit(solution)/shard_map/ppermute | solution.py:543
  22.3 0.0 collective-permute-start.6
  22.3 0.0 collective-permute-done.7.refs_17_
  22.3 3.8 %collective-permute-done.6.refs_16_ = f32[48,128]{1,0:T(8,128)S(1)} collective-permute-done((f32[48,128]{1,0:T(8,128)S(1)}, f32[48,128]{1,0:T(8,128)S(1)}, u32[]{:S(2)}, u32[]{:S(2)}) %collective-permute-start.6) | collective-permute-done | bytes 24608 | tf_op jit(solution)/shard_map/ppermute | solution.py:543
  26.1 0.0 collective-permute-done.4.refs_14_
  26.1 0.0 collective-permute-done.2.refs_12_
  26.1 0.0 collective-permute-done.3.refs_13_
  26.1 0.0 copy-start.11
  26.1 0.0 copy-done.6
  26.1 0.0 copy-done.12
  26.2 0.0 copy-done.13
  26.2 0.0 copy-done.14
  26.2 0.0 copy-done.15
  26.2 0.6 %copy-done.11 = s32[1,1,256]{2,1,0:T(1,128)S(1)} copy-done((s32[1,1,256]{2,1,0:T(1,128)S(1)}, s32[1,1,256]{2,1,0:T(1,128)}, u32[]{:S(2)}) %copy-start.11) | copy-done | bytes 1048
  26.8 7.6 %shard_map.133 = (f32[336,128]{1,0:T(8,128)S(1)}, f32[336,128]{1,0:T(8,128)S(1)}, f32[96,128]{1,0:T(8,128)S(1)}, f32[1536,128]{1,0:T(8,128)S(1)}) custom-call(f32[4,256,128]{2,1,0:T(8,128)S(1)} %bitcast.14, f32[256,128]{1,0:T(8,128)S(1)} %bitcast.21, f32[2,256,128]{2,1,0:T(8,128)S(1)} %bitcast.18, s32[1,256]{1,0:T(1,128)S(1)} %bitcast.26, ...), custom_call_target="tpu_custom_call" | custom-call | flops 30000000 | bytes 2462720 | tf_op jit(solution)/shard_map/pallas_call | solution.py:38
  34.4 0.1 collective-permute-start.9
  34.5 0.6 %collective-permute-start.10 = (f32[336,128]{1,0:T(8,128)S(1)}, f32[336,128]{1,0:T(8,128)S(1)}, u32[]{:S(2)}, u32[]{:S(2)}) collective-permute-start(f32[336,128]{1,0:T(8,128)S(1)} %get-tuple-element.25), channel_id=1, source_target_pairs={{1,2},{2,1},{3,0},{0,3},{5,6},{6,5},{7,4},{4,7},{9,10},{10,9},{11,... | collective-permute-start | bytes 516104 | tf_op jit(solution)/shard_map/ppermute | solution.py:67
  35.2 1.5 %collective-permute-start.11 = (f32[48,128]{1,0:T(8,128)S(1)}, f32[48,128]{1,0:T(8,128)S(1)}, u32[]{:S(2)}, u32[]{:S(2)}) collective-permute-start(f32[48,128]{1,0:T(8,128)S(1)} %slice.3), channel_id=1, source_target_pairs={{0,2},{1,3},{2,0},{3,1},{4,6},{5,7},{6,4},{7,5},{8,10},{9,11},{10,... | collective-permute-start | bytes 73736 | tf_op jit(solution)/shard_map/ppermute | solution.py:575
  36.7 5.1 %collective-permute-done.11.refs_6_ = f32[48,128]{1,0:T(8,128)S(1)} collective-permute-done((f32[48,128]{1,0:T(8,128)S(1)}, f32[48,128]{1,0:T(8,128)S(1)}, u32[]{:S(2)}, u32[]{:S(2)}) %collective-permute-start.11) | collective-permute-done | bytes 24608 | tf_op jit(solution)/shard_map/ppermute | solution.py:575
  41.8 0.0 collective-permute-done.9.refs_4_
  41.8 0.0 collective-permute-done.10.refs_5_
  41.8 0.3 shard_map.134
  42.1 0.8 %collective-permute-start.12 = (f32[208,128]{1,0:T(8,128)S(1)}, f32[208,128]{1,0:T(8,128)S(1)}, u32[]{:S(2)}, u32[]{:S(2)}) collective-permute-start(f32[208,128]{1,0:T(8,128)S(1)} %get-tuple-element.28), channel_id=1, source_target_pairs={{0,4},{4,0},{8,12},{12,8},{16,20},{20,16},{24,28},{28,24},{1,5},{5... | collective-permute-start | bytes 319496 | tf_op jit(solution)/shard_map/ppermute | solution.py:57
  42.9 2.6 %collective-permute-start.13 = (f32[208,128]{1,0:T(8,128)S(1)}, f32[208,128]{1,0:T(8,128)S(1)}, u32[]{:S(2)}, u32[]{:S(2)}) collective-permute-start(f32[208,128]{1,0:T(8,128)S(1)} %get-tuple-element.29), channel_id=1, source_target_pairs={{4,8},{8,4},{12,16},{16,12},{20,24},{24,20},{5,9},{9,5},{13,17},{1... | collective-permute-start | bytes 319496 | tf_op jit(solution)/shard_map/ppermute | solution.py:67
  45.5 1.3 %collective-permute-done.12.got_a = f32[208,128]{1,0:T(8,128)S(1)} collective-permute-done((f32[208,128]{1,0:T(8,128)S(1)}, f32[208,128]{1,0:T(8,128)S(1)}, u32[]{:S(2)}, u32[]{:S(2)}) %collective-permute-start.12) | collective-permute-done | bytes 106528 | tf_op jit(solution)/shard_map/ppermute | solution.py:57
  46.9 3.5 %collective-permute-done.13.got_b = f32[208,128]{1,0:T(8,128)S(1)} collective-permute-done((f32[208,128]{1,0:T(8,128)S(1)}, f32[208,128]{1,0:T(8,128)S(1)}, u32[]{:S(2)}, u32[]{:S(2)}) %collective-permute-start.13) | collective-permute-done | bytes 106528 | tf_op jit(solution)/shard_map/ppermute | solution.py:67
  50.4 0.8 %shard_map.135 = (f32[4,256,128]{2,1,0:T(8,128)}, f32[16,128]{1,0:T(8,128)}) custom-call(f32[4,256,128]{2,1,0:T(8,128)S(1)} %get-tuple-element.26.near_delta, f32[16,128]{1,0:T(8,128)S(1)} %get-tuple-element.27.near_alpha, f32[208,128]{1,0:T(8,128)S(1)} %collective-permute-done.12.got_a, f32[208,128]{1,0:T(8,128)S(1)} %collective-permute-done.13.got_b), custom_call_target="tpu_custom_call" | custom-call | flops 1000000 | bytes 745472 | tf_op jit(solution)/shard_map/pallas_call | solution.py:38
  (8 shorter events, 0.1 us)
Async XLA Ops:
  0.6 1.0 %copy-start = (f32[4,16,16,128]{3,2,1,0:T(8,128)S(1)}, f32[4,16,16,128]{3,2,1,0:T(8,128)}, u32[]{:S(2)}) copy-start(f32[4,16,16,128]{3,2,1,0:T(8,128)} %param.12) | copy-start | bytes 1572868
  1.7 0.9 %copy-start.2 = (f32[2,16,16,128]{3,2,1,0:T(8,128)S(1)}, f32[2,16,16,128]{3,2,1,0:T(8,128)}, u32[]{:S(2)}) copy-start(f32[2,16,16,128]{3,2,1,0:T(8,128)} %param.15) | copy-start | bytes 786436
  2.6 0.9 %copy-start.4 = (f32[16,16,128]{2,1,0:T(8,128)S(1)}, f32[16,16,128]{2,1,0:T(8,128)}, u32[]{:S(2)}) copy-start(f32[16,16,128]{2,1,0:T(8,128)} %param.14) | copy-start | bytes 393220
  3.5 0.7 %copy-start.7 = (f32[1,4,4,128]{3,2,1,0:T(4,128)S(1)}, f32[1,4,4,128]{3,2,1,0:T(4,128)}, u32[]{:S(2)}) copy-start(f32[1,4,4,128]{3,2,1,0:T(4,128)} %param.13) | copy-start | bytes 24580
  4.2 0.7 %copy-start.9 = (s32[16,16]{1,0:T(8,128)S(1)}, s32[16,16]{1,0:T(8,128)}, u32[]{:S(2)}) copy-start(s32[16,16]{1,0:T(8,128)} %tiles.3) | copy-start | bytes 3076
  4.9 5.1 %copy-start.16 = (f32[8,3,128]{2,0,1:T(8,128)S(1)}, f32[8,3,128]{2,0,1:T(8,128)}, u32[]{:S(2)}) copy-start(f32[8,3,128]{2,0,1:T(8,128)} %param.17) | copy-start | bytes 36868
  4.9 9.7 %copy-start.1 = (f32[4,16,16,128]{3,2,1,0:T(8,128)S(1)}, f32[4,16,16,128]{3,2,1,0:T(8,128)}, u32[]{:S(2)}) copy-start(f32[4,16,16,128]{3,2,1,0:T(8,128)} %param.12) | copy-start | bytes 1572868
  4.9 9.7 %copy-start.3 = (f32[2,16,16,128]{3,2,1,0:T(8,128)S(1)}, f32[2,16,16,128]{3,2,1,0:T(8,128)}, u32[]{:S(2)}) copy-start(f32[2,16,16,128]{3,2,1,0:T(8,128)} %param.15) | copy-start | bytes 786436
  4.9 9.7 %copy-start.5 = (f32[16,16,128]{2,1,0:T(8,128)S(1)}, f32[16,16,128]{2,1,0:T(8,128)}, u32[]{:S(2)}) copy-start(f32[16,16,128]{2,1,0:T(8,128)} %param.14) | copy-start | bytes 393220
  5.0 9.6 %collective-permute-start = (f32[320,128]{1,0:T(8,128)S(1)}, f32[320,128]{1,0:T(8,128)S(1)}, u32[]{:S(2)}, u32[]{:S(2)}) collective-permute-start(f32[320,128]{1,0:T(8,128)S(1)} %get-tuple-element.17), channel_id=1, source_target_pairs={{0,4},{4,0},{8,12},{12,8},{16,20},{20,16},{24,28},{28,24},{1,5},{5... | collective-permute-start | bytes 491528 | tf_op jit(solution)/shard_map/ppermute | solution.py:57
  5.1 9.6 %collective-permute-start.1 = (f32[320,128]{1,0:T(8,128)S(1)}, f32[320,128]{1,0:T(8,128)S(1)}, u32[]{:S(2)}, u32[]{:S(2)}) collective-permute-start(f32[320,128]{1,0:T(8,128)S(1)} %get-tuple-element.18), channel_id=1, source_target_pairs={{4,8},{8,4},{12,16},{16,12},{20,24},{24,20},{5,9},{9,5},{13,17},{1... | collective-permute-start | bytes 491528 | tf_op jit(solution)/shard_map/ppermute | solution.py:67
  10.0 4.6 %copy-start.8 = (f32[1,4,4,128]{3,2,1,0:T(4,128)S(1)}, f32[1,4,4,128]{3,2,1,0:T(4,128)}, u32[]{:S(2)}) copy-start(f32[1,4,4,128]{3,2,1,0:T(4,128)} %param.13) | copy-start | bytes 24580
  10.0 4.6 %copy-start.10 = (s32[16,16]{1,0:T(8,128)S(1)}, s32[16,16]{1,0:T(8,128)}, u32[]{:S(2)}) copy-start(s32[16,16]{1,0:T(8,128)} %tiles.3) | copy-start | bytes 3076
  10.1 16.1 %copy-start.6 = (f32[1,1,256,4,128]{4,3,2,1,0:T(4,128)S(1)}, f32[1,1,256,4,128]{4,3,2,1,0:T(4,128)}, u32[]{:S(2)}) copy-start(f32[1,1,256,4,128]{4,3,2,1,0:T(4,128)} %param.22) | copy-start | bytes 1572868
  10.1 6.5 %collective-permute-start.5 = (f32[24,128]{1,0:T(8,128)S(1)}, f32[24,128]{1,0:T(8,128)S(1)}, u32[]{:S(2)}, u32[]{:S(2)}) collective-permute-start(f32[24,128]{1,0:T(8,128)S(1)} %reshape.53), channel_id=1, source_target_pairs={{0,4},{4,0},{8,12},{12,8},{16,20},{20,16},{24,28},{28,24},{1,5},{5... | collective-permute-start | bytes 36872 | tf_op jit(solution)/shard_map/ppermute | solution.py:57
  14.8 11.3 %collective-permute-start.2 = (f32[504,128]{1,0:T(8,128)S(1)}, f32[504,128]{1,0:T(8,128)S(1)}, u32[]{:S(2)}, u32[]{:S(2)}) collective-permute-start(f32[504,128]{1,0:T(8,128)S(1)} %get-tuple-element.20), channel_id=1, source_target_pairs={{0,1},{1,0},{2,3},{3,2},{4,5},{5,4},{6,7},{7,6},{8,9},{9,8},{10,11... | collective-permute-start | bytes 774152 | tf_op jit(solution)/shard_map/ppermute | solution.py:57
  14.9 11.2 %collective-permute-start.3 = (f32[504,128]{1,0:T(8,128)S(1)}, f32[504,128]{1,0:T(8,128)S(1)}, u32[]{:S(2)}, u32[]{:S(2)}) collective-permute-start(f32[504,128]{1,0:T(8,128)S(1)} %get-tuple-element.21), channel_id=1, source_target_pairs={{1,2},{2,1},{3,0},{0,3},{5,6},{6,5},{7,4},{4,7},{9,10},{10,9},{11,... | collective-permute-start | bytes 774152 | tf_op jit(solution)/shard_map/ppermute | solution.py:67
  16.5 9.6 %copy-start.12 = (s32[1,1,256]{2,1,0:T(1,128)S(1)}, s32[1,1,256]{2,1,0:T(1,128)}, u32[]{:S(2)}) copy-start(s32[1,1,256]{2,1,0:T(1,128)} %param.19) | copy-start | bytes 3076
  16.5 9.6 %copy-start.13 = (s32[1,1,256]{2,1,0:T(1,128)S(1)}, s32[1,1,256]{2,1,0:T(1,128)}, u32[]{:S(2)}) copy-start(s32[1,1,256]{2,1,0:T(1,128)} %param.20) | copy-start | bytes 3076
  16.5 9.6 %copy-start.14 = (s32[1,1,256]{2,1,0:T(1,128)S(1)}, s32[1,1,256]{2,1,0:T(1,128)}, u32[]{:S(2)}) copy-start(s32[1,1,256]{2,1,0:T(1,128)} %param.21) | copy-start | bytes 3076
  16.6 9.6 %copy-start.15 = (f32[1,1,256]{2,1,0:T(1,128)S(1)}, f32[1,1,256]{2,1,0:T(1,128)}, u32[]{:S(2)}) copy-start(f32[1,1,256]{2,1,0:T(1,128)} %param.23) | copy-start | bytes 3076
  16.6 5.7 %collective-permute-start.8 = (f32[48,128]{1,0:T(8,128)S(1)}, f32[48,128]{1,0:T(8,128)S(1)}, u32[]{:S(2)}, u32[]{:S(2)}) collective-permute-start(f32[48,128]{1,0:T(8,128)S(1)} %constant_dynamic-update-slice_fusion.refs_15_), channel_id=1, source_target_pairs={{0,24},{4,28},{8,16},{12,20},{16,8},{20,12},{24,0},{28,4},{1,25},{... | collective-permute-start | bytes 73736 | tf_op jit(solution)/shard_map/ppermute | solution.py:543
  16.7 9.4 %collective-permute-start.4 = (f32[72,128]{1,0:T(8,128)S(1)}, f32[72,128]{1,0:T(8,128)S(1)}, u32[]{:S(2)}, u32[]{:S(2)}) collective-permute-start(f32[72,128]{1,0:T(8,128)S(1)} %get-tuple-element.19.refs_11_), channel_id=1, source_target_pairs={{0,2},{1,3},{2,0},{3,1},{4,6},{5,7},{6,4},{7,5},{8,10},{9,11},{10,... | collective-permute-start | bytes 110600 | tf_op jit(solution)/shard_map/ppermute | solution.py:539
  17.3 5.0 %collective-permute-start.7 = (f32[48,128]{1,0:T(8,128)S(1)}, f32[48,128]{1,0:T(8,128)S(1)}, u32[]{:S(2)}, u32[]{:S(2)}) collective-permute-start(f32[48,128]{1,0:T(8,128)S(1)} %constant_dynamic-update-slice_fusion.refs_15_), channel_id=1, source_target_pairs={{0,16},{4,20},{8,24},{12,28},{16,0},{20,4},{24,8},{28,12},{1,17},{... | collective-permute-start | bytes 73736 | tf_op jit(solution)/shard_map/ppermute | solution.py:543
  22.3 3.8 %collective-permute-start.6 = (f32[48,128]{1,0:T(8,128)S(1)}, f32[48,128]{1,0:T(8,128)S(1)}, u32[]{:S(2)}, u32[]{:S(2)}) collective-permute-start(f32[48,128]{1,0:T(8,128)S(1)} %constant_dynamic-update-slice_fusion.refs_15_), channel_id=1, source_target_pairs={{0,8},{4,12},{8,0},{12,4},{16,24},{20,28},{24,16},{28,20},{1,9},{5... | collective-permute-start | bytes 73736 | tf_op jit(solution)/shard_map/ppermute | solution.py:543
  26.1 0.7 %copy-start.11 = (s32[1,1,256]{2,1,0:T(1,128)S(1)}, s32[1,1,256]{2,1,0:T(1,128)}, u32[]{:S(2)}) copy-start(s32[1,1,256]{2,1,0:T(1,128)} %param.18) | copy-start | bytes 3076
  34.4 7.3 %collective-permute-start.9 = (f32[336,128]{1,0:T(8,128)S(1)}, f32[336,128]{1,0:T(8,128)S(1)}, u32[]{:S(2)}, u32[]{:S(2)}) collective-permute-start(f32[336,128]{1,0:T(8,128)S(1)} %get-tuple-element.24), channel_id=1, source_target_pairs={{0,1},{1,0},{2,3},{3,2},{4,5},{5,4},{6,7},{7,6},{8,9},{9,8},{10,11... | collective-permute-start | bytes 516104 | tf_op jit(solution)/shard_map/ppermute | solution.py:57
  34.5 7.3 %collective-permute-start.10 = (f32[336,128]{1,0:T(8,128)S(1)}, f32[336,128]{1,0:T(8,128)S(1)}, u32[]{:S(2)}, u32[]{:S(2)}) collective-permute-start(f32[336,128]{1,0:T(8,128)S(1)} %get-tuple-element.25), channel_id=1, source_target_pairs={{1,2},{2,1},{3,0},{0,3},{5,6},{6,5},{7,4},{4,7},{9,10},{10,9},{11,... | collective-permute-start | bytes 516104 | tf_op jit(solution)/shard_map/ppermute | solution.py:67
  35.2 6.6 %collective-permute-start.11 = (f32[48,128]{1,0:T(8,128)S(1)}, f32[48,128]{1,0:T(8,128)S(1)}, u32[]{:S(2)}, u32[]{:S(2)}) collective-permute-start(f32[48,128]{1,0:T(8,128)S(1)} %slice.3), channel_id=1, source_target_pairs={{0,2},{1,3},{2,0},{3,1},{4,6},{5,7},{6,4},{7,5},{8,10},{9,11},{10,... | collective-permute-start | bytes 73736 | tf_op jit(solution)/shard_map/ppermute | solution.py:575
  42.1 4.8 %collective-permute-start.12 = (f32[208,128]{1,0:T(8,128)S(1)}, f32[208,128]{1,0:T(8,128)S(1)}, u32[]{:S(2)}, u32[]{:S(2)}) collective-permute-start(f32[208,128]{1,0:T(8,128)S(1)} %get-tuple-element.28), channel_id=1, source_target_pairs={{0,4},{4,0},{8,12},{12,8},{16,20},{20,16},{24,28},{28,24},{1,5},{5... | collective-permute-start | bytes 319496 | tf_op jit(solution)/shard_map/ppermute | solution.py:57
  42.9 7.5 %collective-permute-start.13 = (f32[208,128]{1,0:T(8,128)S(1)}, f32[208,128]{1,0:T(8,128)S(1)}, u32[]{:S(2)}, u32[]{:S(2)}) collective-permute-start(f32[208,128]{1,0:T(8,128)S(1)} %get-tuple-element.29), channel_id=1, source_target_pairs={{4,8},{8,4},{12,16},{16,12},{20,24},{24,20},{5,9},{9,5},{13,17},{1... | collective-permute-start | bytes 319496 | tf_op jit(solution)/shard_map/ppermute | solution.py:67

commit v2 on v1

v2 whole, which is shorter than its diff:
```python
import jax
import jax.numpy as jnp
from jax import lax
from jax.experimental import pallas as pl
from jax.experimental.pallas import tpu as pltpu
from jax.sharding import PartitionSpec as P

STEPS = 3
RIM = 3
INNER = RIM - 1
NC = 4
CX = 16
CY = 16
BLOCKS = CX + 8
PITCH = CY + 8
FIRST = 4
FIELD = BLOCKS * PITCH

BULK_COEF = NC * RIM * CY
BULK = BULK_COEF + 3 * INNER * CY

profile_weight = 0.125
f32 = jnp.float32
bf16 = jnp.bfloat16

VMEM = pl.BlockSpec(memory_space=pltpu.VMEM)
ANY = pl.BlockSpec(memory_space=pl.ANY)


def call(body, outs, ins, scratch=(), in_specs=None, flops=1000000, limit=40 * 2**20):
    shapes = [jax.ShapeDtypeStruct(shape, f32) for shape in outs]
    size = sum(4 * value.size for value in ins)
    return pl.pallas_call(
        body,
        out_shape=shapes,
        in_specs=in_specs or [VMEM] * len(ins),
        out_specs=[VMEM] * len(shapes),
        scratch_shapes=list(scratch),
        compiler_params=pltpu.CompilerParams(vmem_limit_bytes=limit),
        cost_estimate=pl.CostEstimate(flops=flops, bytes_accessed=size, transcendentals=0),
    )(*ins)


def parity(axis):
    return lax.rem(lax.axis_index(axis), 2) == 0


def swap(block, axis, xor):
    return lax.ppermute(block, axis, [(i, i ^ xor) for i in range(lax.axis_size(axis))])


def pair_b(block, axis):
    pairs = []
    for low in range(1, lax.axis_size(axis) - 1, 2):
        pairs += [(low, low + 1), (low + 1, low)]
    return lax.ppermute(block, axis, pairs)


def split(value):
    top = value.astype(bf16)
    return top, (value - top.astype(f32)).astype(bf16)


def layers(reach):
    found, at = [], 0
    for away in range(1, reach + 1):
        count = CX + 2 * (reach - away)
        found.append((away, at, FIRST - (reach - away), count))
        at += count
    return found, at


WIDE, WIDE_ROWS = layers(RIM)
SLIM, SLIM_ROWS = layers(INNER)
Y_COEF = NC * WIDE_ROWS
Y_HALO = Y_COEF + 3 * SLIM_ROWS

CORNER = sum(RIM - away for away in range(1, RIM + 1))
COEF_CORNER = sum(INNER - away for away in range(1, INNER + 1))


def small_places(profile_rows):
    tile = profile_rows
    corner = tile + 8
    coef_corner = corner + 2 * NC * CORNER
    beams = coef_corner + 8
    return tile, corner, coef_corner, beams


def pack_x(
    delta,
    eddy,
    courant,
    alpha,
    tile_map,
    beam_rows,
    bulk_a,
    bulk_b,
    small_a,
    small_b,
    east,
    west,
    own,
    tiles,
    beams,
    sems,
):
    even = parity("gx")
    wide, slim = RIM * CY, INNER * CY
    copies = []

    def copy(source, target):
        move = pltpu.make_async_copy(source, target, sems.at[len(copies)])
        move.start()
        copies.append(move)

    last = CX * CY
    for c in range(NC):
        rows = pl.ds(c * wide, wide)
        copy(delta.at[c, pl.ds(last - wide, wide)], east.at[rows])
        copy(delta.at[c, pl.ds(0, wide)], west.at[rows])
    for f in range(3):
        field = eddy if f == 0 else courant.at[f - 1]
        rows = pl.ds(BULK_COEF + f * slim, slim)
        copy(field.at[pl.ds(last - slim, slim)], east.at[rows])
        copy(field.at[pl.ds(0, slim)], west.at[rows])
    copy(alpha, own)
    copy(tile_map, tiles)
    copy(beam_rows, beams)
    for move in copies:
        move.wait()

    bulk_a[...] = jnp.where(even, east[...], west[...])
    bulk_b[...] = jnp.where(even, west[...], east[...])
    count = own.shape[0]
    tile, corner, coef_corner, beam = small_places(count)

    def put(at, size, east_side, west_side):
        small_a[at : at + size] = jnp.where(even, east_side, west_side)
        small_b[at : at + size] = jnp.where(even, west_side, east_side)

    small_a[0:count] = own[...]
    small_b[0:count] = own[...]
    numbers = tiles[...].astype(f32)
    put(tile, 8, jnp.zeros((8, 128), f32), jnp.zeros((8, 128), f32))
    for out in (small_a, small_b):
        out[coef_corner : coef_corner + 8] = jnp.zeros((8, 128), f32)
    small_a[tile : tile + RIM, 0:CY] = jnp.where(even, numbers[CX - RIM :], numbers[:RIM])
    small_b[tile : tile + RIM, 0:CY] = jnp.where(even, numbers[:RIM], numbers[CX - RIM :])

    def corners(at, base, reach, side):
        for away in range(1, reach):
            y = CY - away if side == 0 else away - 1
            width = reach - away
            for i in range(width):
                put(
                    at,
                    1,
                    east[pl.ds(base + (reach - width + i) * CY + y, 1)],
                    west[pl.ds(base + i * CY + y, 1)],
                )
                at += 1

    for side in range(2):
        for c in range(NC):
            corners(corner + (side * NC + c) * CORNER, c * wide, RIM, side)
        for f in range(3):
            corners(
                coef_corner + (side * 3 + f) * COEF_CORNER, BULK_COEF + f * slim, INNER, side
            )
    small_a[beam:] = beams[...]


def pack_y(
    delta,
    eddy,
    courant,
    alpha,
    tiles,
    beam_rows,
    got_a,
    got_b,
    out_a,
    out_b,
    profiles,
    near_tiles,
    beam_pair,
):
    even = parity("gy")
    even_x = parity("gx")
    count = alpha.shape[0]
    tile, corner, coef_corner, beam = small_places(count)

    def sides(at, size):
        first, second = got_a[at : at + size], got_b[at : at + size]
        return jnp.where(even_x, second, first), jnp.where(even_x, first, second)

    def put(at, size, north_side, south_side):
        out_a[at : at + size] = jnp.where(even, north_side, south_side)
        out_b[at : at + size] = jnp.where(even, south_side, north_side)

    def edge(at, found, own, north_corner, south_corner):
        for away, start, _, size in found:
            here = at + start
            width = (size - CX) // 2
            if width:
                north_w, north_e = sides(north_corner, width)
                south_w, south_e = sides(south_corner, width)
                put(here, width, north_w, south_w)
                put(here + width + CX, width, north_e, south_e)
                north_corner += width
                south_corner += width
            put(
                here + width,
                CX,
                own[pl.ds(CY - away, CX, stride=CY)],
                own[pl.ds(away - 1, CX, stride=CY)],
            )

    for c in range(NC):
        edge(
            c * WIDE_ROWS,
            WIDE,
            delta.at[c],
            corner + c * CORNER,
            corner + (NC + c) * CORNER,
        )
    for f in range(3):
        edge(
            Y_COEF + f * SLIM_ROWS,
            SLIM,
            eddy if f == 0 else courant.at[f - 1],
            coef_corner + f * COEF_CORNER,
            coef_corner + (3 + f) * COEF_CORNER,
        )
    west, east = sides(0, count)
    profiles[0:count] = west
    profiles[count : 2 * count] = alpha[...]
    profiles[2 * count :] = east
    west, east = sides(tile, RIM)
    near_tiles[...] = jnp.full(near_tiles.shape, -1.0, f32)
    near_tiles[FIRST - RIM : FIRST] = west
    near_tiles[FIRST : FIRST + CX, 0:CY] = tiles[...].astype(f32)
    near_tiles[FIRST + CX : FIRST + CX + RIM] = east
    out_a[Y_HALO : Y_HALO + BLOCKS] = near_tiles[...]
    out_b[Y_HALO : Y_HALO + BLOCKS] = near_tiles[...]
    out_a[Y_HALO + BLOCKS :] = profiles[...]
    beam_pair[0 : beam_rows.shape[0]] = beam_rows[...]
    beam_pair[beam_rows.shape[0] :] = got_a[beam:]


def main(
    ny,
    parts,
    delta,
    eddy,
    courant,
    gate_beam,
    gate_index,
    gate_column,
    gate_live,
    precision,
    weights,
    x_a,
    x_b,
    profiles,
    near_tiles,
    y_a,
    y_b,
    *rest,
):
    others = rest[: ny - 2]
    beams = rest[ny - 2 : ny - 2 + parts]
    outs = rest[ny - 2 + parts : 2 * ny + 2 + parts]
    out_a, out_b, bulk_a, bulk_b, out_near, out_sums = outs[:6]
    out_others = outs[6:]
    (state_0, state_1, coef, forcing, known, picks, meta, tiles, table, sums) = rest[
        2 * ny + 2 + parts :
    ]
    per_slot = profiles.shape[0]
    group = per_slot // NC
    owned = group // 3
    total = ny * group
    me = lax.axis_index("gy")
    me_x = lax.axis_index("gx")
    even = parity("gy")
    even_x = parity("gx")
    has_south = me > 0
    has_north = me < ny - 1

    def x_sides(rows):
        first, second = x_a[rows], x_b[rows]
        return jnp.where(even_x, second, first), jnp.where(even_x, first, second)

    def y_sides(rows):
        first, second = y_a[rows], y_b[rows]
        return jnp.where(even, first, second), jnp.where(even, second, first)

    coef[...] = jnp.zeros(coef.shape, f32)
    state_0[...] = jnp.zeros(state_0.shape, f32)
    state_1[...] = jnp.zeros(state_1.shape, f32)

    def place(ref, base, own, x_base, reach, y_base, found):
        for x in range(CX):
            at = base + (FIRST + x) * PITCH
            ref[at : at + CY] = own[x * CY : (x + 1) * CY]
        for h in range(reach):
            west, east = x_sides(pl.ds(x_base + h * CY, CY))
            at = base + (FIRST - reach + h) * PITCH
            ref[at : at + CY] = west
            at = base + (FIRST + CX + h) * PITCH
            ref[at : at + CY] = east
        for away, start, block, size in found:
            north, south = y_sides(pl.ds(y_base + start, size))
            at = base + block * PITCH
            ref[pl.ds(at + CY - 1 + away, size, stride=PITCH)] = north
            ref[pl.ds(at + PITCH - away, size, stride=PITCH)] = south

    for c in range(NC):
        place(state_0, c * FIELD, delta.at[c], c * RIM * CY, RIM, c * WIDE_ROWS, WIDE)
    for f in range(3):
        place(
            coef,
            f * FIELD,
            eddy if f == 0 else courant.at[f - 1],
            BULK_COEF + f * INNER * CY,
            INNER,
            Y_COEF + f * SLIM_ROWS,
            SLIM,
        )

    def combine(b, carry):
        at = pl.multiple_of(b * PITCH, 8)
        viscous = coef[pl.ds(at, PITCH)]
        along_x = 0.5 * coef[pl.ds(FIELD + at, PITCH)]
        along_y = 0.5 * coef[pl.ds(2 * FIELD + at, PITCH)]
        coef[pl.ds(at, PITCH)] = 1.0 - 4.0 * viscous
        coef[pl.ds(FIELD + at, PITCH)] = viscous - along_x
        coef[pl.ds(2 * FIELD + at, PITCH)] = viscous + along_x
        coef[pl.ds(3 * FIELD + at, PITCH)] = viscous - along_y
        coef[pl.ds(4 * FIELD + at, PITCH)] = viscous + along_y
        return carry

    lax.fori_loop(0, BLOCKS, combine, 0)

    known[0:per_slot] = profiles[...]
    known[per_slot : 2 * per_slot] = y_a[Y_HALO + BLOCKS :]
    for s, other in enumerate(others):
        known[(2 + s) * per_slot : (3 + s) * per_slot] = other[...]
    lane = lax.broadcasted_iota(jnp.int32, (1, total), 1)
    tile_ids = []
    for strip in range(3):
        ids = jnp.full((1, total), -2, jnp.int32)
        for s in range(ny):
            base = s * group + strip * owned
            ids = jnp.where(
                (lane >= base) & (lane < base + owned),
                jnp.bitwise_xor(me, s) * owned + lane - base,
                ids,
            )
        tile_ids.append(ids.astype(f32))
    spot = lax.broadcasted_iota(jnp.int32, (BLOCKS, 128), 1)
    from_north, from_south = y_sides(pl.ds(Y_HALO, BLOCKS))
    near = jnp.where(
        (spot >= CY) & (spot < CY + RIM) & has_north,
        pltpu.roll(from_north, CY, 1),
        jnp.where(
            (spot >= PITCH - RIM) & (spot < PITCH) & has_south,
            pltpu.roll(from_south, PITCH - CY, 1),
            -1.0,
        ),
    )
    tiles[...] = jnp.full(tiles.shape, -1.0, f32)
    tiles[0:BLOCKS] = jnp.where(spot < CY, near_tiles[...], near)
    turned = jnp.transpose(tiles[...])[0:PITCH]
    for b in range(BLOCKS):
        strip = 0 if b < FIRST else 1 if b < FIRST + CX else 2
        picks[b * PITCH : (b + 1) * PITCH] = (turned[:, b : b + 1] == tile_ids[strip]).astype(f32)

    def by_variable(ref, count):
        return jnp.concatenate([ref[pl.ds(c, count, stride=NC)] for c in range(NC)], axis=1)

    def two_part_dot(left, value):
        top, low = split(value)
        return jnp.dot(left, top, preferred_element_type=f32) + jnp.dot(
            left, low, preferred_element_type=f32
        )

    fine = two_part_dot(picks[...].astype(bf16), by_variable(known, total))
    for c in range(NC):
        state_0[c * FIELD : (c + 1) * FIELD] += profile_weight * fine[:, c * 128 : (c + 1) * 128]

    slots = gate_column.shape[1]
    per_beam = table.shape[0] // STEPS
    beam = gate_beam[...]
    pair = beams[0].shape[0]
    relative = jnp.bitwise_xor(beam >> 3, me_x) * 8 + (beam & 7)
    meta[...] = jnp.zeros(meta.shape, f32)
    meta[0:1] = gate_column[...].astype(f32)
    meta[1:2] = relative.astype(f32)
    meta[2:3] = gate_index[...].astype(f32)
    meta[3:4] = gate_live[...].astype(f32) * precision[...]
    columns = jnp.transpose(meta[...])
    scaled = columns[:, 3:4]
    slot_lane = lax.broadcasted_iota(jnp.int32, (slots, CX * CY), 1).astype(f32)
    slot_pick = (slot_lane == columns[:, 0:1]).astype(f32).astype(bf16)
    column_row = lax.broadcasted_iota(jnp.int32, (CX * CY, slots), 0)
    slot_push = (column_row == gate_column[...]).astype(f32).astype(bf16)
    beam_lane = lax.broadcasted_iota(jnp.int32, (slots, per_beam), 1).astype(f32)
    beam_pick = (beam_lane == columns[:, 1:2]).astype(f32).astype(bf16)
    gate_lane = lax.broadcasted_iota(jnp.int32, (slots, 128), 1).astype(f32)
    gate_here = gate_lane == columns[:, 2:3]
    for p, part in enumerate(beams):
        table[p * pair : (p + 1) * pair] = part[...]

    def forward(source, target, low, high):
        def body(b, carry):
            at = pl.multiple_of(b * PITCH, 8)
            k = [coef[pl.ds(f * FIELD + at, PITCH)] for f in range(5)]
            for c in range(NC):
                base = c * FIELD + at
                here = source[pl.ds(base, PITCH)]
                target[pl.ds(base, PITCH)] = (
                    k[0] * here
                    + k[1] * source[pl.ds(base + PITCH, PITCH)]
                    + k[2] * source[pl.ds(base - PITCH, PITCH)]
                    + k[3] * pltpu.roll(here, PITCH - 1, 0)
                    + k[4] * pltpu.roll(here, 1, 0)
                )
            return carry

        lax.fori_loop(low, high, body, 0)

    buffers = [state_0, state_1]
    for step in range(STEPS):
        source, target = buffers[step % 2], buffers[(step + 1) % 2]
        forward(source, target, 2 + step, BLOCKS - 2 - step)
        own = jnp.concatenate(
            [
                jnp.concatenate(
                    [
                        target[c * FIELD + b * PITCH : c * FIELD + b * PITCH + CY]
                        for b in range(FIRST, FIRST + CX)
                    ],
                    axis=0,
                )
                for c in range(NC)
            ],
            axis=1,
        )
        picked = two_part_dot(slot_pick, own)
        rows = two_part_dot(beam_pick, table[pl.ds(step, per_beam, stride=STEPS)])
        tally = -jnp.where(gate_here, rows, 0.0)
        for c in range(NC):
            tally = tally + picked[:, c * 128 : (c + 1) * 128] * weights[pl.ds(c, slots, stride=NC)]
        misfit = scaled * jnp.sum(tally, axis=1, keepdims=True)
        pushed = jnp.concatenate(
            [misfit * weights[pl.ds(c, slots, stride=NC)] for c in range(NC)], axis=1
        )
        forcing[step * CX * CY : (step + 1) * CX * CY] = two_part_dot(slot_push, pushed)

    state_0[...] = jnp.zeros(state_0.shape, f32)
    state_1[...] = jnp.zeros(state_1.shape, f32)

    def add_forcing(ref, step):
        for c in range(NC):
            for x in range(CX):
                at = c * FIELD + (FIRST + x) * PITCH
                first = step * CX * CY + x * CY
                ref[at : at + CY] += forcing[first : first + CY, c * 128 : (c + 1) * 128]

    def backward(source, target, low, high):
        def body(b, carry):
            at = pl.multiple_of(b * PITCH, 8)
            k = [
                coef[pl.ds(at, PITCH)],
                coef[pl.ds(FIELD + at - PITCH, PITCH)],
                coef[pl.ds(2 * FIELD + at + PITCH, PITCH)],
                coef[pl.ds(3 * FIELD + at, PITCH)],
                coef[pl.ds(4 * FIELD + at, PITCH)],
            ]
            for c in range(NC):
                base = c * FIELD + at
                here = source[pl.ds(base, PITCH)]
                target[pl.ds(base, PITCH)] = (
                    k[0] * here
                    + k[1] * source[pl.ds(base - PITCH, PITCH)]
                    + k[2] * source[pl.ds(base + PITCH, PITCH)]
                    + pltpu.roll(k[3] * here, 1, 0)
                    + pltpu.roll(k[4] * here, PITCH - 1, 0)
                )
            return carry

        lax.fori_loop(low, high, body, 0)

    for step in range(STEPS):
        source, target = buffers[step % 2], buffers[(step + 1) % 2]
        add_forcing(source, STEPS - 1 - step)
        backward(source, target, FIRST - 1 - step, FIRST + CX + 1 + step)
    final = buffers[STEPS % 2]

    for c in range(NC):
        for h in range(RIM):
            at = c * FIELD + (FIRST - RIM + h) * PITCH
            west = final[at : at + CY]
            at = c * FIELD + (FIRST + CX + h) * PITCH
            east = final[at : at + CY]
            at = (c * RIM + h) * CY
            bulk_a[at : at + CY] = jnp.where(even_x, east, west)
            bulk_b[at : at + CY] = jnp.where(even_x, west, east)
        for away, start, block, size in WIDE:
            at = c * FIELD + block * PITCH
            north = final[pl.ds(at + CY - 1 + away, size, stride=PITCH)]
            south = final[pl.ds(at + PITCH - away, size, stride=PITCH)]
            at = c * WIDE_ROWS + start
            out_a[at : at + size] = jnp.where(even, north, south)
            out_b[at : at + size] = jnp.where(even, south, north)
        for x in range(CX):
            at = c * FIELD + (FIRST + x) * PITCH
            rows = slice(x * CY, (x + 1) * CY)
            out_near[c, rows] = delta[c, rows] + final[at : at + CY]

    adjoint = jnp.concatenate([final[c * FIELD : (c + 1) * FIELD] for c in range(NC)], axis=1)
    tile_sums = two_part_dot(jnp.transpose(picks[...]).astype(bf16), adjoint)
    for c in range(NC):
        sums[pl.ds(c, total, stride=NC)] = tile_sums[:, c * 128 : (c + 1) * 128]
    out_sums[...] = sums[0:per_slot]
    out_a[NC * WIDE_ROWS :] = sums[per_slot : 2 * per_slot]
    for s, other in enumerate(out_others):
        other[...] = sums[(2 + s) * per_slot : (3 + s) * per_slot]


def pack_home(sums, got_a, got_b, *rest):
    others = rest[:-3]
    out_a, out_b, out_sum = rest[-3:]
    owned = sums.shape[0] // 3
    even = parity("gy")
    even_x = parity("gx")
    total = sums[...] + got_a[NC * WIDE_ROWS :]
    for other in others:
        total = total + other[...]

    def put(at, size, west, east):
        out_a[at : at + size] = jnp.where(even_x, east, west)
        out_b[at : at + size] = jnp.where(even_x, west, east)

    put(0, owned, total[0:owned], total[2 * owned :])
    out_sum[...] = total[owned : 2 * owned]
    at = owned
    for c in range(NC):
        for away, start, _, size in WIDE:
            width = (size - CX) // 2
            first = c * WIDE_ROWS + start
            for side in range(2):
                if width:
                    pieces = []
                    for rows in (
                        slice(first, first + width),
                        slice(first + size - width, first + size),
                    ):
                        north = jnp.where(even, got_a[rows], got_b[rows])
                        south = jnp.where(even, got_b[rows], got_a[rows])
                        pieces.append((north, south)[side])
                    put(at, width, *pieces)
                    at += width


def finish(alpha, near, own_sum, y_a, y_b, bulk_a, bulk_b, small_a, small_b, out_delta, out_alpha):
    even = parity("gy")
    even_x = parity("gx")
    owned = own_sum.shape[0]
    wide = RIM * CY
    out_delta[...] = near[...]
    at = owned
    for c in range(NC):
        rows = pl.ds(c * wide, wide)
        first, second = bulk_a[rows], bulk_b[rows]
        out_delta[c, 0:wide] += jnp.where(even_x, second, first)
        out_delta[c, CX * CY - wide :] += jnp.where(even_x, first, second)
        for away, start, _, size in WIDE:
            width = (size - CX) // 2
            rows = pl.ds(c * WIDE_ROWS + start + width, CX)
            first, second = y_a[rows], y_b[rows]
            high = pl.ds(CY - away, CX, stride=CY)
            low = pl.ds(away - 1, CX, stride=CY)
            out_delta[c, high] = out_delta[c, high] + jnp.where(even, first, second)
            out_delta[c, low] = out_delta[c, low] + jnp.where(even, second, first)
            for y in (CY - away, away - 1):
                for i in range(width):
                    first, second = small_a[at + i : at + i + 1], small_b[at + i : at + i + 1]
                    out_delta[c, pl.ds((CX - width + i) * CY + y, 1)] += jnp.where(
                        even_x, first, second
                    )
                    out_delta[c, pl.ds(i * CY + y, 1)] += jnp.where(even_x, second, first)
                at += width
    out_alpha[...] = alpha[...] + profile_weight * (
        own_sum[...] + small_a[0:owned] + small_b[0:owned]
    )


def on_device(
    delta,
    alpha,
    eddy,
    courant,
    tile_map,
    obs_rows,
    gate_beam,
    gate_index,
    gate_column,
    gate_live,
    obs_weight,
    obs_precision,
):
    nx = lax.axis_size("gx")
    ny = lax.axis_size("gy")
    owned = alpha.shape[1]
    slots = gate_column.shape[2]
    fine = delta.reshape(NC, CX * CY, 128)
    eddy = eddy.reshape(CX * CY, 128)
    courant = courant.reshape(2, CX * CY, 128)
    control = alpha.reshape(owned * NC, 128)
    weights = obs_weight.reshape(slots * NC, 128)
    gates = [
        value.reshape(1, slots)
        for value in (gate_beam, gate_index, gate_column, gate_live, obs_precision)
    ]
    beam_rows = obs_rows.reshape(-1, 128)
    profile_rows = owned * NC
    per_slot = 3 * profile_rows
    total = ny * 3 * owned
    beam_at = small_places(profile_rows)[-1]

    bulk_a, bulk_b, small_a, small_b = call(
        pack_x,
        [(BULK, 128), (BULK, 128), (beam_at + beam_rows.shape[0], 128), (beam_at, 128)],
        [fine, eddy, courant, control, tile_map, beam_rows],
        [
            pltpu.VMEM((BULK, 128), f32),
            pltpu.VMEM((BULK, 128), f32),
            pltpu.VMEM(control.shape, f32),
            pltpu.VMEM(tile_map.shape, jnp.int32),
            pltpu.VMEM(beam_rows.shape, f32),
            pltpu.SemaphoreType.DMA((2 * NC + 9,)),
        ],
        in_specs=[ANY] * 6,
    )
    small_a = swap(small_a, "gx", 1)
    small_b = pair_b(small_b, "gx")
    bulk_a = swap(bulk_a, "gx", 1)
    bulk_b = pair_b(bulk_b, "gx")

    y_a, y_b, profiles, near_tiles, beam_pair = call(
        pack_y,
        [
            (Y_HALO + BLOCKS + per_slot, 128),
            (Y_HALO + BLOCKS, 128),
            (per_slot, 128),
            (BLOCKS, 128),
            (2 * beam_rows.shape[0], 128),
        ],
        [fine, eddy, courant, control, tile_map, beam_rows, small_a, small_b],
    )
    y_a = swap(y_a, "gy", 1)
    y_b = pair_b(y_b, "gy")
    others = [swap(profiles, "gy", xor) for xor in range(2, ny)]
    beams = [beam_pair] + [swap(beam_pair, "gx", xor) for xor in range(2, nx, 2)]

    edge_rows = NC * WIDE_ROWS
    back_a, back_b, bulk_a, bulk_b, near, sums, *back = call(
        lambda *refs: main(ny, len(beams), *refs),
        [
            (edge_rows + per_slot, 128),
            (edge_rows, 128),
            (BULK_COEF, 128),
            (BULK_COEF, 128),
            fine.shape,
            (per_slot, 128),
        ]
        + [(per_slot, 128)] * (ny - 2),
        [
            fine,
            eddy,
            courant,
            *gates,
            weights,
            bulk_a,
            bulk_b,
            profiles,
            near_tiles,
            y_a,
            y_b,
            *others,
            *beams,
        ],
        [
            pltpu.VMEM((NC * FIELD, 128), f32),
            pltpu.VMEM((NC * FIELD, 128), f32),
            pltpu.VMEM((5 * FIELD, 128), f32),
            pltpu.VMEM((STEPS * CX * CY, NC * 128), f32),
            pltpu.VMEM((ny * per_slot, 128), f32),
            pltpu.VMEM((FIELD, total), f32),
            pltpu.VMEM((8, slots), f32),
            pltpu.VMEM((128, 128), f32),
            pltpu.VMEM((nx * beam_rows.shape[0], 128), f32),
            pltpu.VMEM((ny * per_slot, 128), f32),
        ],
        flops=30000000,
    )
    y_a = swap(back_a, "gy", 1)
    y_b = pair_b(back_b, "gy")
    others = [swap(value, "gy", xor) for xor, value in zip(range(2, ny), back)]
    bulk_a = swap(bulk_a, "gx", 1)
    bulk_b = pair_b(bulk_b, "gx")
    home_rows = profile_rows + 2 * NC * CORNER
    small_a, small_b, own_sum = call(
        pack_home,
        [(home_rows, 128), (home_rows, 128), control.shape],
        [sums, y_a, y_b, *others],
    )
    small_a = swap(small_a, "gx", 1)
    small_b = pair_b(small_b, "gx")
    grad_delta, grad_alpha = call(
        finish,
        [fine.shape, control.shape],
        [control, near, own_sum, y_a, y_b, bulk_a, bulk_b, small_a, small_b],
    )
    return grad_delta.reshape(delta.shape), grad_alpha.reshape(alpha.shape)


def solution(mesh):
    return jax.shard_map(
        on_device,
        mesh=mesh,
        in_specs=(
            P(None, "gx", "gy", None),
            P("gx", "gy", None, None),
            P("gx", "gy", None),
            P(None, "gx", "gy", None),
            P("gx", "gy"),
            P(("gx", "gy"), None, None),
            P("gx", "gy", None),
            P("gx", "gy", None),
            P("gx", "gy", None),
            P("gx", "gy", None),
            P("gx", "gy", None, None, None),
            P("gx", "gy", None),
        ),
        out_specs=(P(None, "gx", "gy", None), P("gx", "gy", None, None)),
        check_vma=False,
    )
```

time: 51.6 us -> 73 us (1.41)
  the two profiles are of different devices: /device:TPU:4 before, /device:TPU:18 now
where the time goes in v2:
time: 73 us; the launch traced here: 72.5 us
  waiting for transfers between devices  30.4 us (42%)
  starting transfers between devices  26.8 us (37%)
  Pallas kernels  9.48 us (13%)
  local copies, waits for them, and re-layouts  4.97 us (7%)
  between operations  0.88 us (1%)
    ppermute x13, waiting for transfers between devices, swap(): lax.ppermute(block, axis, [(i, i ^ xor) for i in range(lax.axis_size(axis...  22 us
    ppermute x6, starting transfers between devices, pair_b(): return lax.ppermute(block, axis, pairs)  16.8 us
    ppermute x13, starting transfers between devices, swap(): lax.ppermute(block, axis, [(i, i ^ xor) for i in range(lax.axis_size(axis...  9.94 us
    pallas_call x5, Pallas kernels, call(): pl.pallas_call(body, out_shape=shapes, in_specs=in_specs or [VMEM] * len(...  9.48 us
    ppermute x6, waiting for transfers between devices, pair_b(): return lax.ppermute(block, axis, pairs)  8.44 us
    unnamed x23, local copies, waits for them, and re-layouts  4.96 us
  transfers between devices with their start and end apart: 19, of which 9 were waited for; matrix products, arithmetic and copies ran while one was open for 0% of the time, Pallas kernels for 0%

profile of v2, /device:TPU:18, one launch (start us, length us, event | category | flops | bytes accessed | tf_op | source)
XLA Modules:
  0.0 72.5 jit_solution(13516777076551138132)
XLA Ops:
  0.6 0.7 copy.15
  1.3 0.0 copy-start.4
  1.3 0.0 copy-start.5
  1.4 0.7 copy-done.4
  2.0 0.0 copy-done.5
  2.1 0.0 copy-start
  2.1 1.0 %copy-done = f32[4,16,16,128]{3,2,1,0:T(8,128)S(1)} copy-done((f32[4,16,16,128]{3,2,1,0:T(8,128)S(1)}, f32[4,16,16,128]{3,2,1,0:T(8,128)}, u32[]{:S(2)}) %copy-start) | copy-done | bytes 524312
  3.1 0.0 copy-start.1
  3.1 0.9 %copy-done.1 = f32[2,16,16,128]{3,2,1,0:T(8,128)S(1)} copy-done((f32[2,16,16,128]{3,2,1,0:T(8,128)S(1)}, f32[2,16,16,128]{3,2,1,0:T(8,128)}, u32[]{:S(2)}) %copy-start.1) | copy-done | bytes 262168
  4.1 0.9 %copy-done.2 = f32[16,16,128]{2,1,0:T(8,128)S(1)} copy-done((f32[16,16,128]{2,1,0:T(8,128)S(1)}, f32[16,16,128]{2,1,0:T(8,128)}, u32[]{:S(2)}) %copy-start.2) | copy-done | bytes 131096
  5.0 0.6 shard_map.131
  5.6 0.0 copy-start.3
  5.6 1.6 %collective-permute-start.2 = (f32[80,128]{1,0:T(8,128)S(1)}, f32[80,128]{1,0:T(8,128)S(1)}, u32[]{:S(2)}, u32[]{:S(2)}) collective-permute-start(f32[80,128]{1,0:T(8,128)S(1)} %get-tuple-element.26), channel_id=1, source_target_pairs={{0,4},{4,0},{8,12},{12,8},{16,20},{20,16},{24,28},{28,24},{1,5},{5... | collective-permute-start | bytes 122888 | tf_op jit(solution)/shard_map/ppermute | solution.py:49
  7.2 2.3 %collective-permute-start.3 = (f32[56,128]{1,0:T(8,128)S(1)}, f32[56,128]{1,0:T(8,128)S(1)}, u32[]{:S(2)}, u32[]{:S(2)}) collective-permute-start(f32[56,128]{1,0:T(8,128)S(1)} %get-tuple-element.27), channel_id=1, source_target_pairs={{4,8},{8,4},{12,16},{16,12},{20,24},{24,20},{5,9},{9,5},{13,17},{1... | collective-permute-start | bytes 86024 | tf_op jit(solution)/shard_map/ppermute | solution.py:56
  9.5 4.4 %collective-permute-done.3.got_b = f32[56,128]{1,0:T(8,128)S(1)} collective-permute-done((f32[56,128]{1,0:T(8,128)S(1)}, f32[56,128]{1,0:T(8,128)S(1)}, u32[]{:S(2)}, u32[]{:S(2)}) %collective-permute-start.3) | collective-permute-done | bytes 28704 | tf_op jit(solution)/shard_map/ppermute | solution.py:56
  13.8 0.0 collective-permute-done.2.got_a
  13.8 0.1 shard_map.132
  13.9 0.1 collective-permute-start.4
  14.0 0.0 copy-start.7
  14.0 0.0 copy-start.8
  14.1 0.0 copy-start.9
  14.1 0.0 copy-start.10
  14.1 2.6 %collective-permute-start.5 = (f32[342,128]{1,0:T(8,128)S(1)}, f32[342,128]{1,0:T(8,128)S(1)}, u32[]{:S(2)}, u32[]{:S(2)}) collective-permute-start(f32[342,128]{1,0:T(8,128)S(1)} %get-tuple-element.31), channel_id=1, source_target_pairs={{1,2},{2,1},{5,6},{6,5},{9,10},{10,9},{13,14},{14,13},{17,18},{18,... | collective-permute-start | bytes 525320 | tf_op jit(solution)/shard_map/ppermute | solution.py:56
  16.7 0.6 collective-permute-start
  17.3 3.3 %collective-permute-start.1 = (f32[288,128]{1,0:T(8,128)S(1)}, f32[288,128]{1,0:T(8,128)S(1)}, u32[]{:S(2)}, u32[]{:S(2)}) collective-permute-start(f32[288,128]{1,0:T(8,128)S(1)} %get-tuple-element.25), channel_id=1, source_target_pairs={{4,8},{8,4},{12,16},{16,12},{20,24},{24,20},{5,9},{9,5},{13,17},{1... | collective-permute-start | bytes 442376 | tf_op jit(solution)/shard_map/ppermute | solution.py:56
  20.6 0.7 collective-permute-start.7
  21.3 2.7 %collective-permute-done.7.refs_16_ = f32[48,128]{1,0:T(8,128)S(1)} collective-permute-done((f32[48,128]{1,0:T(8,128)S(1)}, f32[48,128]{1,0:T(8,128)S(1)}, u32[]{:S(2)}, u32[]{:S(2)}) %collective-permute-start.7) | collective-permute-done | bytes 24608 | tf_op jit(solution)/shard_map/ppermute | solution.py:49
  23.9 0.0 collective-permute-start.6
  23.9 3.8 %collective-permute-done.6.refs_15_ = f32[48,128]{1,0:T(8,128)S(1)} collective-permute-done((f32[48,128]{1,0:T(8,128)S(1)}, f32[48,128]{1,0:T(8,128)S(1)}, u32[]{:S(2)}, u32[]{:S(2)}) %collective-permute-start.6) | collective-permute-done | bytes 24608 | tf_op jit(solution)/shard_map/ppermute | solution.py:49
  27.7 0.0 collective-permute-start.10
  27.8 3.8 %collective-permute-done.10.refs_20_ = f32[48,128]{1,0:T(8,128)S(1)} collective-permute-done((f32[48,128]{1,0:T(8,128)S(1)}, f32[48,128]{1,0:T(8,128)S(1)}, u32[]{:S(2)}, u32[]{:S(2)}) %collective-permute-start.10) | collective-permute-done | bytes 24608 | tf_op jit(solution)/shard_map/ppermute | solution.py:49
  31.6 1.9 %collective-permute-start.9 = (f32[48,128]{1,0:T(8,128)S(1)}, f32[48,128]{1,0:T(8,128)S(1)}, u32[]{:S(2)}, u32[]{:S(2)}) collective-permute-start(f32[48,128]{1,0:T(8,128)S(1)} %get-tuple-element.32.refs_17_), channel_id=1, source_target_pairs={{0,16},{4,20},{8,24},{12,28},{16,0},{20,4},{24,8},{28,12},{1,17},{... | collective-permute-start | bytes 73736 | tf_op jit(solution)/shard_map/ppermute | solution.py:49
  33.5 2.8 %collective-permute-done.9.refs_19_ = f32[48,128]{1,0:T(8,128)S(1)} collective-permute-done((f32[48,128]{1,0:T(8,128)S(1)}, f32[48,128]{1,0:T(8,128)S(1)}, u32[]{:S(2)}, u32[]{:S(2)}) %collective-permute-start.9) | collective-permute-done | bytes 24608 | tf_op jit(solution)/shard_map/ppermute | solution.py:49
  36.3 3.4 %collective-permute-start.8 = (f32[48,128]{1,0:T(8,128)S(1)}, f32[48,128]{1,0:T(8,128)S(1)}, u32[]{:S(2)}, u32[]{:S(2)}) collective-permute-start(f32[48,128]{1,0:T(8,128)S(1)} %get-tuple-element.32.refs_17_), channel_id=1, source_target_pairs={{0,8},{4,12},{8,0},{12,4},{16,24},{20,28},{24,16},{28,20},{1,9},{5... | collective-permute-start | bytes 73736 | tf_op jit(solution)/shard_map/ppermute | solution.py:49
  39.7 1.8 %collective-permute-done.8.refs_18_ = f32[48,128]{1,0:T(8,128)S(1)} collective-permute-done((f32[48,128]{1,0:T(8,128)S(1)}, f32[48,128]{1,0:T(8,128)S(1)}, u32[]{:S(2)}, u32[]{:S(2)}) %collective-permute-start.8) | collective-permute-done | bytes 24608 | tf_op jit(solution)/shard_map/ppermute | solution.py:49
  41.5 0.0 collective-permute-done.refs_9_
  41.5 0.0 collective-permute-done.1.refs_10_
  41.5 0.0 collective-permute-done.5.refs_14_
  41.5 0.0 collective-permute-done.4.refs_13_
  41.5 0.0 copy-start.6
  41.5 0.0 copy-done.3
  41.5 0.0 copy-done.7
  41.5 0.0 copy-done.8
  41.5 0.0 copy-done.9
  41.6 0.0 copy-done.10
  41.6 0.6 copy-done.6
  42.2 7.7 %shard_map.133 = (f32[264,128]{1,0:T(8,128)S(1)}, f32[216,128]{1,0:T(8,128)S(1)}, f32[192,128]{1,0:T(8,128)S(1)}, f32[192,128]{1,0:T(8,128)S(1)}, f32[4,256,128]...) custom-call(f32[4,256,128]{2,1,0:T(8,128)S(1)} %bitcast.14, ...), custom_call_target="tpu_custom_call" | custom-call | flops 30000000 | bytes 2300928 | tf_op jit(solution)/shard_map/pallas_call | solution.py:33
  49.9 0.1 collective-permute-start.11
  50.0 2.2 %collective-permute-start.12 = (f32[216,128]{1,0:T(8,128)S(1)}, f32[216,128]{1,0:T(8,128)S(1)}, u32[]{:S(2)}, u32[]{:S(2)}) collective-permute-start(f32[216,128]{1,0:T(8,128)S(1)} %get-tuple-element.36), channel_id=1, source_target_pairs={{1,2},{2,1},{5,6},{6,5},{9,10},{10,9},{13,14},{14,13},{17,18},{18,... | collective-permute-start | bytes 331784 | tf_op jit(solution)/shard_map/ppermute | solution.py:56
  52.2 0.1 collective-permute-start.15
  52.3 3.9 %collective-permute-start.16 = (f32[192,128]{1,0:T(8,128)S(1)}, f32[192,128]{1,0:T(8,128)S(1)}, u32[]{:S(2)}, u32[]{:S(2)}) collective-permute-start(f32[192,128]{1,0:T(8,128)S(1)} %get-tuple-element.41), channel_id=1, source_target_pairs={{4,8},{8,4},{12,16},{16,12},{20,24},{24,20},{5,9},{9,5},{13,17},{1... | collective-permute-start | bytes 294920 | tf_op jit(solution)/shard_map/ppermute | solution.py:56
  56.2 0.1 collective-permute-start.13
  56.3 3.8 %collective-permute-done.13.rest_0_ = f32[48,128]{1,0:T(8,128)S(1)} collective-permute-done((f32[48,128]{1,0:T(8,128)S(1)}, f32[48,128]{1,0:T(8,128)S(1)}, u32[]{:S(2)}, u32[]{:S(2)}) %collective-permute-start.13) | collective-permute-done | bytes 24608 | tf_op jit(solution)/shard_map/ppermute | solution.py:49
  60.1 0.0 collective-permute-start.14
  60.1 3.2 %collective-permute-done.14.rest_1_ = f32[48,128]{1,0:T(8,128)S(1)} collective-permute-done((f32[48,128]{1,0:T(8,128)S(1)}, f32[48,128]{1,0:T(8,128)S(1)}, u32[]{:S(2)}, u32[]{:S(2)}) %collective-permute-start.14) | collective-permute-done | bytes 24608 | tf_op jit(solution)/shard_map/ppermute | solution.py:49
  63.4 0.0 collective-permute-done.12.got_b.y_b
  63.4 0.0 collective-permute-done.11.got_a.y_a
  63.4 1.5 %collective-permute-start.17 = (f32[40,128]{1,0:T(8,128)S(1)}, f32[40,128]{1,0:T(8,128)S(1)}, u32[]{:S(2)}, u32[]{:S(2)}) collective-permute-start(f32[40,128]{1,0:T(8,128)S(1)} %get-tuple-element.42), channel_id=1, source_target_pairs={{0,4},{4,0},{8,12},{12,8},{16,20},{20,16},{24,28},{28,24},{1,5},{5... | collective-permute-start | bytes 61448 | tf_op jit(solution)/shard_map/ppermute | solution.py:49
  65.0 2.5 %collective-permute-start.18 = (f32[40,128]{1,0:T(8,128)S(1)}, f32[40,128]{1,0:T(8,128)S(1)}, u32[]{:S(2)}, u32[]{:S(2)}) collective-permute-start(f32[40,128]{1,0:T(8,128)S(1)} %get-tuple-element.43), channel_id=1, source_target_pairs={{4,8},{8,4},{12,16},{16,12},{20,24},{24,20},{5,9},{9,5},{13,17},{1... | collective-permute-start | bytes 61448 | tf_op jit(solution)/shard_map/ppermute | solution.py:56
  67.4 0.0 collective-permute-done.15.bulk_a
  67.4 0.0 collective-permute-done.16.bulk_b
  67.4 0.0 collective-permute-done.17.small_a
  67.5 4.1 %collective-permute-done.18.small_b = f32[40,128]{1,0:T(8,128)S(1)} collective-permute-done((f32[40,128]{1,0:T(8,128)S(1)}, f32[40,128]{1,0:T(8,128)S(1)}, u32[]{:S(2)}, u32[]{:S(2)}) %collective-permute-start.18) | collective-permute-done | bytes 20512 | tf_op jit(solution)/shard_map/ppermute | solution.py:56
  71.5 1.0 %shard_map.135 = (f32[4,256,128]{2,1,0:T(8,128)}, f32[16,128]{1,0:T(8,128)}) custom-call(f32[16,128]{1,0:T(8,128)S(1)} %bitcast.24, f32[4,256,128]{2,1,0:T(8,128)S(1)} %get-tuple-element.33.near, f32[16,128]{1,0:T(8,128)S(1)} %get-tuple-element.39.own_sum, f32[264,128]{1,0:T(8,128)S(1)} %collective-permute-done.11.got_a.y_a, ...), custom_call_target="tpu_custom_call" | custom-call | flops 1000000 | bytes 1024000 | tf_op jit(solution)/shard_map/pallas_call | solution.py:33
  (3 shorter events, 0.0 us)
Async XLA Ops:
  1.3 0.7 copy-start.4
  1.3 0.7 copy-start.5
  2.1 1.0 %copy-start = (f32[4,16,16,128]{3,2,1,0:T(8,128)S(1)}, f32[4,16,16,128]{3,2,1,0:T(8,128)}, u32[]{:S(2)}) copy-start(f32[4,16,16,128]{3,2,1,0:T(8,128)} %param.12) | copy-start | bytes 1572868
  3.1 0.9 %copy-start.1 = (f32[2,16,16,128]{3,2,1,0:T(8,128)S(1)}, f32[2,16,16,128]{3,2,1,0:T(8,128)}, u32[]{:S(2)}) copy-start(f32[2,16,16,128]{3,2,1,0:T(8,128)} %param.15) | copy-start | bytes 786436
  4.0 0.9 %copy-start.2 = (f32[16,16,128]{2,1,0:T(8,128)S(1)}, f32[16,16,128]{2,1,0:T(8,128)}, u32[]{:S(2)}) copy-start(f32[16,16,128]{2,1,0:T(8,128)} %param.14) | copy-start | bytes 393220
  5.6 35.9 %copy-start.3 = (f32[1,1,256,4,128]{4,3,2,1,0:T(4,128)S(1)}, f32[1,1,256,4,128]{4,3,2,1,0:T(4,128)}, u32[]{:S(2)}) copy-start(f32[1,1,256,4,128]{4,3,2,1,0:T(4,128)} %param.22) | copy-start | bytes 1572868
  5.6 8.2 %collective-permute-start.2 = (f32[80,128]{1,0:T(8,128)S(1)}, f32[80,128]{1,0:T(8,128)S(1)}, u32[]{:S(2)}, u32[]{:S(2)}) collective-permute-start(f32[80,128]{1,0:T(8,128)S(1)} %get-tuple-element.26), channel_id=1, source_target_pairs={{0,4},{4,0},{8,12},{12,8},{16,20},{20,16},{24,28},{28,24},{1,5},{5... | collective-permute-start | bytes 122888 | tf_op jit(solution)/shard_map/ppermute | solution.py:49
  7.2 6.7 %collective-permute-start.3 = (f32[56,128]{1,0:T(8,128)S(1)}, f32[56,128]{1,0:T(8,128)S(1)}, u32[]{:S(2)}, u32[]{:S(2)}) collective-permute-start(f32[56,128]{1,0:T(8,128)S(1)} %get-tuple-element.27), channel_id=1, source_target_pairs={{4,8},{8,4},{12,16},{16,12},{20,24},{24,20},{5,9},{9,5},{13,17},{1... | collective-permute-start | bytes 86024 | tf_op jit(solution)/shard_map/ppermute | solution.py:56
  13.9 27.5 %collective-permute-start.4 = (f32[390,128]{1,0:T(8,128)S(1)}, f32[390,128]{1,0:T(8,128)S(1)}, u32[]{:S(2)}, u32[]{:S(2)}) collective-permute-start(f32[390,128]{1,0:T(8,128)S(1)} %get-tuple-element.30), channel_id=1, source_target_pairs={{0,1},{1,0},{2,3},{3,2},{4,5},{5,4},{6,7},{7,6},{8,9},{9,8},{10,11... | collective-permute-start | bytes 599048 | tf_op jit(solution)/shard_map/ppermute | solution.py:49
  14.0 27.5 %copy-start.7 = (s32[1,1,256]{2,1,0:T(1,128)S(1)}, s32[1,1,256]{2,1,0:T(1,128)}, u32[]{:S(2)}) copy-start(s32[1,1,256]{2,1,0:T(1,128)} %param.19) | copy-start | bytes 3076
  14.0 27.5 %copy-start.8 = (s32[1,1,256]{2,1,0:T(1,128)S(1)}, s32[1,1,256]{2,1,0:T(1,128)}, u32[]{:S(2)}) copy-start(s32[1,1,256]{2,1,0:T(1,128)} %param.20) | copy-start | bytes 3076
  14.1 27.5 %copy-start.9 = (s32[1,1,256]{2,1,0:T(1,128)S(1)}, s32[1,1,256]{2,1,0:T(1,128)}, u32[]{:S(2)}) copy-start(s32[1,1,256]{2,1,0:T(1,128)} %param.21) | copy-start | bytes 3076
  14.1 27.5 %copy-start.10 = (f32[1,1,256]{2,1,0:T(1,128)S(1)}, f32[1,1,256]{2,1,0:T(1,128)}, u32[]{:S(2)}) copy-start(f32[1,1,256]{2,1,0:T(1,128)} %param.23) | copy-start | bytes 3076
  14.1 27.4 %collective-permute-start.5 = (f32[342,128]{1,0:T(8,128)S(1)}, f32[342,128]{1,0:T(8,128)S(1)}, u32[]{:S(2)}, u32[]{:S(2)}) collective-permute-start(f32[342,128]{1,0:T(8,128)S(1)} %get-tuple-element.31), channel_id=1, source_target_pairs={{1,2},{2,1},{5,6},{6,5},{9,10},{10,9},{13,14},{14,13},{17,18},{18,... | collective-permute-start | bytes 525320 | tf_op jit(solution)/shard_map/ppermute | solution.py:56
  16.7 24.8 %collective-permute-start = (f32[288,128]{1,0:T(8,128)S(1)}, f32[288,128]{1,0:T(8,128)S(1)}, u32[]{:S(2)}, u32[]{:S(2)}) collective-permute-start(f32[288,128]{1,0:T(8,128)S(1)} %get-tuple-element.24), channel_id=1, source_target_pairs={{0,4},{4,0},{8,12},{12,8},{16,20},{20,16},{24,28},{28,24},{1,5},{5... | collective-permute-start | bytes 442376 | tf_op jit(solution)/shard_map/ppermute | solution.py:49
  17.3 24.2 %collective-permute-start.1 = (f32[288,128]{1,0:T(8,128)S(1)}, f32[288,128]{1,0:T(8,128)S(1)}, u32[]{:S(2)}, u32[]{:S(2)}) collective-permute-start(f32[288,128]{1,0:T(8,128)S(1)} %get-tuple-element.25), channel_id=1, source_target_pairs={{4,8},{8,4},{12,16},{16,12},{20,24},{24,20},{5,9},{9,5},{13,17},{1... | collective-permute-start | bytes 442376 | tf_op jit(solution)/shard_map/ppermute | solution.py:56
  20.6 3.3 %collective-permute-start.7 = (f32[48,128]{1,0:T(8,128)S(1)}, f32[48,128]{1,0:T(8,128)S(1)}, u32[]{:S(2)}, u32[]{:S(2)}) collective-permute-start(f32[48,128]{1,0:T(8,128)S(1)} %get-tuple-element.28.refs_11_), channel_id=1, source_target_pairs={{0,3},{1,2},{2,1},{3,0},{4,7},{5,6},{6,5},{7,4},{8,11},{9,10},{10,... | collective-permute-start | bytes 73736 | tf_op jit(solution)/shard_map/ppermute | solution.py:49
  23.9 3.8 %collective-permute-start.6 = (f32[48,128]{1,0:T(8,128)S(1)}, f32[48,128]{1,0:T(8,128)S(1)}, u32[]{:S(2)}, u32[]{:S(2)}) collective-permute-start(f32[48,128]{1,0:T(8,128)S(1)} %get-tuple-element.28.refs_11_), channel_id=1, source_target_pairs={{0,2},{1,3},{2,0},{3,1},{4,6},{5,7},{6,4},{7,5},{8,10},{9,11},{10,... | collective-permute-start | bytes 73736 | tf_op jit(solution)/shard_map/ppermute | solution.py:49
  27.7 3.8 %collective-permute-start.10 = (f32[48,128]{1,0:T(8,128)S(1)}, f32[48,128]{1,0:T(8,128)S(1)}, u32[]{:S(2)}, u32[]{:S(2)}) collective-permute-start(f32[48,128]{1,0:T(8,128)S(1)} %get-tuple-element.32.refs_17_), channel_id=1, source_target_pairs={{0,24},{4,28},{8,16},{12,20},{16,8},{20,12},{24,0},{28,4},{1,25},{... | collective-permute-start | bytes 73736 | tf_op jit(solution)/shard_map/ppermute | solution.py:49
  31.6 4.7 %collective-permute-start.9 = (f32[48,128]{1,0:T(8,128)S(1)}, f32[48,128]{1,0:T(8,128)S(1)}, u32[]{:S(2)}, u32[]{:S(2)}) collective-permute-start(f32[48,128]{1,0:T(8,128)S(1)} %get-tuple-element.32.refs_17_), channel_id=1, source_target_pairs={{0,16},{4,20},{8,24},{12,28},{16,0},{20,4},{24,8},{28,12},{1,17},{... | collective-permute-start | bytes 73736 | tf_op jit(solution)/shard_map/ppermute | solution.py:49
  36.3 5.2 %collective-permute-start.8 = (f32[48,128]{1,0:T(8,128)S(1)}, f32[48,128]{1,0:T(8,128)S(1)}, u32[]{:S(2)}, u32[]{:S(2)}) collective-permute-start(f32[48,128]{1,0:T(8,128)S(1)} %get-tuple-element.32.refs_17_), channel_id=1, source_target_pairs={{0,8},{4,12},{8,0},{12,4},{16,24},{20,28},{24,16},{28,20},{1,9},{5... | collective-permute-start | bytes 73736 | tf_op jit(solution)/shard_map/ppermute | solution.py:49
  41.5 0.7 copy-start.6
  49.9 13.5 %collective-permute-start.11 = (f32[264,128]{1,0:T(8,128)S(1)}, f32[264,128]{1,0:T(8,128)S(1)}, u32[]{:S(2)}, u32[]{:S(2)}) collective-permute-start(f32[264,128]{1,0:T(8,128)S(1)} %get-tuple-element.35), channel_id=1, source_target_pairs={{0,1},{1,0},{2,3},{3,2},{4,5},{5,4},{6,7},{7,6},{8,9},{9,8},{10,11... | collective-permute-start | bytes 405512 | tf_op jit(solution)/shard_map/ppermute | solution.py:49
  50.0 13.4 %collective-permute-start.12 = (f32[216,128]{1,0:T(8,128)S(1)}, f32[216,128]{1,0:T(8,128)S(1)}, u32[]{:S(2)}, u32[]{:S(2)}) collective-permute-start(f32[216,128]{1,0:T(8,128)S(1)} %get-tuple-element.36), channel_id=1, source_target_pairs={{1,2},{2,1},{5,6},{6,5},{9,10},{10,9},{13,14},{14,13},{17,18},{18,... | collective-permute-start | bytes 331784 | tf_op jit(solution)/shard_map/ppermute | solution.py:56
  52.2 15.2 %collective-permute-start.15 = (f32[192,128]{1,0:T(8,128)S(1)}, f32[192,128]{1,0:T(8,128)S(1)}, u32[]{:S(2)}, u32[]{:S(2)}) collective-permute-start(f32[192,128]{1,0:T(8,128)S(1)} %get-tuple-element.40), channel_id=1, source_target_pairs={{0,4},{4,0},{8,12},{12,8},{16,20},{20,16},{24,28},{28,24},{1,5},{5... | collective-permute-start | bytes 294920 | tf_op jit(solution)/shard_map/ppermute | solution.py:49
  52.3 15.1 %collective-permute-start.16 = (f32[192,128]{1,0:T(8,128)S(1)}, f32[192,128]{1,0:T(8,128)S(1)}, u32[]{:S(2)}, u32[]{:S(2)}) collective-permute-start(f32[192,128]{1,0:T(8,128)S(1)} %get-tuple-element.41), channel_id=1, source_target_pairs={{4,8},{8,4},{12,16},{16,12},{20,24},{24,20},{5,9},{9,5},{13,17},{1... | collective-permute-start | bytes 294920 | tf_op jit(solution)/shard_map/ppermute | solution.py:56
  56.2 3.9 %collective-permute-start.13 = (f32[48,128]{1,0:T(8,128)S(1)}, f32[48,128]{1,0:T(8,128)S(1)}, u32[]{:S(2)}, u32[]{:S(2)}) collective-permute-start(f32[48,128]{1,0:T(8,128)S(1)} %get-tuple-element.37), channel_id=1, source_target_pairs={{0,2},{1,3},{2,0},{3,1},{4,6},{5,7},{6,4},{7,5},{8,10},{9,11},{10,... | collective-permute-start | bytes 73736 | tf_op jit(solution)/shard_map/ppermute | solution.py:49
  60.1 3.3 %collective-permute-start.14 = (f32[48,128]{1,0:T(8,128)S(1)}, f32[48,128]{1,0:T(8,128)S(1)}, u32[]{:S(2)}, u32[]{:S(2)}) collective-permute-start(f32[48,128]{1,0:T(8,128)S(1)} %get-tuple-element.38), channel_id=1, source_target_pairs={{0,3},{1,2},{2,1},{3,0},{4,7},{5,6},{6,5},{7,4},{8,11},{9,10},{10,... | collective-permute-start | bytes 73736 | tf_op jit(solution)/shard_map/ppermute | solution.py:49
  63.4 4.0 %collective-permute-start.17 = (f32[40,128]{1,0:T(8,128)S(1)}, f32[40,128]{1,0:T(8,128)S(1)}, u32[]{:S(2)}, u32[]{:S(2)}) collective-permute-start(f32[40,128]{1,0:T(8,128)S(1)} %get-tuple-element.42), channel_id=1, source_target_pairs={{0,4},{4,0},{8,12},{12,8},{16,20},{20,16},{24,28},{28,24},{1,5},{5... | collective-permute-start | bytes 61448 | tf_op jit(solution)/shard_map/ppermute | solution.py:49
  65.0 6.6 %collective-permute-start.18 = (f32[40,128]{1,0:T(8,128)S(1)}, f32[40,128]{1,0:T(8,128)S(1)}, u32[]{:S(2)}, u32[]{:S(2)}) collective-permute-start(f32[40,128]{1,0:T(8,128)S(1)} %get-tuple-element.43), channel_id=1, source_target_pairs={{4,8},{8,4},{12,16},{16,12},{20,24},{24,20},{5,9},{9,5},{13,17},{1... | collective-permute-start | bytes 61448 | tf_op jit(solution)/shard_map/ppermute | solution.py:56

commit v3 on v0

v3 whole, which is shorter than its diff:
```python
import jax
import jax.numpy as jnp
from jax import lax
from jax.experimental import pallas as pl
from jax.experimental.pallas import tpu as pltpu
from jax.sharding import PartitionSpec as P

STEPS = 3
RIM = 3
INNER = RIM - 1
NC = 4
CX = 16
CY = 16
BLOCKS = CX + 8
PITCH = CY + 8
FIRST = 4
FIELD = BLOCKS * PITCH
CORE = CX * PITCH

profile_weight = 0.125
f32 = jnp.float32
bf16 = jnp.bfloat16

VMEM = pl.BlockSpec(memory_space=pltpu.VMEM)
HBM = pl.BlockSpec(memory_space=pltpu.HBM)


def call(body, outs, ins, scratch=(), in_specs=None, flops=1000000, limit=40 * 2**20):
    shapes = [
        out if isinstance(out, jax.ShapeDtypeStruct) else jax.ShapeDtypeStruct(out, f32)
        for out in outs
    ]
    size = sum(4 * value.size for value in ins)
    return pl.pallas_call(
        body,
        out_shape=shapes,
        in_specs=in_specs or [VMEM] * len(ins),
        out_specs=[VMEM] * len(shapes),
        scratch_shapes=list(scratch),
        compiler_params=pltpu.CompilerParams(vmem_limit_bytes=limit),
        cost_estimate=pl.CostEstimate(flops=flops, bytes_accessed=size, transcendentals=0),
    )(*ins)


def swap(block, axis, xor):
    return lax.ppermute(block, axis, [(i, i ^ xor) for i in range(lax.axis_size(axis))])


def pair_b(block, axis):
    count = lax.axis_size(axis)
    pairs = [(0, 0), (count - 1, count - 1)]
    for low in range(1, count - 1, 2):
        pairs += [(low, low + 1), (low + 1, low)]
    return lax.ppermute(block, axis, pairs)


def place_on(axis):
    me = lax.axis_index(axis)
    return lax.rem(me, 2) == 0, me > 0, me < lax.axis_size(axis) - 1


def split(value):
    top = value.astype(bf16)
    return top, (value - top.astype(f32)).astype(bf16)


def two_part_dot(left, value):
    top, low = split(value)
    return jnp.dot(left, top, preferred_element_type=f32) + jnp.dot(
        left, low, preferred_element_type=f32
    )


def layers(reach):
    found, at = [], 0
    for away in range(1, reach + 1):
        found.append((away, at, reach - away))
        at += CY + 2 * (reach - away)
    return found, at


WIDE, WIDE_ROWS = layers(RIM)
SLIM, SLIM_ROWS = layers(INNER)
X_COEF = NC * WIDE_ROWS
X_HALO = X_COEF + 3 * SLIM_ROWS

Y_COEF = NC * RIM * CX
Y_TILE = Y_COEF + 3 * INNER * CX
Y_HALO = Y_TILE + CX


def pack_y(
    delta, eddy, courant, alpha, tile_map, beam_rows, out_a, out_b, out_beams, *scratch
):
    fine, coefs, tiles, beams, profiles, sems = scratch
    even, _, _ = place_on("gy")
    moves = [
        pltpu.make_async_copy(source, target, sems.at[i])
        for i, (source, target) in enumerate(
            [
                (delta, fine),
                (eddy, coefs.at[0]),
                (courant.at[0], coefs.at[1]),
                (courant.at[1], coefs.at[2]),
                (tile_map, tiles),
                (beam_rows, beams),
                (alpha, profiles),
            ]
        )
    ]
    for move in moves:
        move.start()
    for move in moves:
        move.wait()

    def put(at, field, away):
        north = field[pl.ds(CY - away, CX, stride=CY)]
        south = field[pl.ds(away - 1, CX, stride=CY)]
        out_a[at : at + CX] = jnp.where(even, north, south)
        out_b[at : at + CX] = jnp.where(even, south, north)

    for c in range(NC):
        for away in range(1, RIM + 1):
            put((c * RIM + away - 1) * CX, fine.at[c], away)
    for f in range(3):
        for away in range(1, INNER + 1):
            put(Y_COEF + (f * INNER + away - 1) * CX, coefs.at[f], away)
    for out in (out_a, out_b):
        out[Y_TILE : Y_TILE + CX] = jnp.full((CX, 128), -1.0, f32)
        out[Y_TILE : Y_TILE + CX, 0:CY] = tiles[...].astype(f32)
    out_a[Y_HALO:] = profiles[...]
    per = beams.shape[1]
    for i in range(beams.shape[0]):
        out_beams[i * per : (i + 1) * per] = beams[i]


def y_sides(got_a, got_b, rows, fill=0.0):
    even, low, high = place_on("gy")
    first, second = got_a[rows], got_b[rows]
    north, south = jnp.where(even, first, second), jnp.where(even, second, first)
    return jnp.where(high, north, fill), jnp.where(low, south, fill)


def x_sides(got_a, got_b, rows):
    even, low, high = place_on("gx")
    first, second = got_a[rows], got_b[rows]
    west, east = jnp.where(even, second, first), jnp.where(even, first, second)
    return jnp.where(low, west, 0.0), jnp.where(high, east, 0.0)


def gather_known(ny, alpha, got_a, others, known):
    owned = alpha.shape[0]
    known[0:owned] = alpha[...]
    known[owned : 2 * owned] = got_a[Y_HALO:]
    for s, other in enumerate(others):
        known[(2 + s) * owned : (3 + s) * owned] = other[...]


def tile_numbers(ny, tile_map, got_a, got_b, tiles):
    spot = lax.broadcasted_iota(jnp.int32, (CX, 128), 1)
    north, south = y_sides(got_a, got_b, pl.ds(Y_TILE, CX), -1.0)
    near = jnp.where(
        (spot >= CY) & (spot < CY + RIM),
        pltpu.roll(north, CY, 1),
        jnp.where((spot >= PITCH - RIM) & (spot < PITCH), pltpu.roll(south, PITCH - CY, 1), -1.0),
    )
    tiles[...] = jnp.full(tiles.shape, -1.0, f32)
    tiles[0:CX] = near
    tiles[0:CX, 0:CY] = tile_map[...].astype(f32)
    return jnp.transpose(tiles[...])[0:PITCH]


def tile_ids(ny, owned):
    me = lax.axis_index("gy")
    lane = lax.broadcasted_iota(jnp.int32, (1, ny * owned), 1)
    ids = lane
    for s in range(ny):
        here = (lane >= s * owned) & (lane < (s + 1) * owned)
        ids = jnp.where(here, jnp.bitwise_xor(me, s) * owned + lane - s * owned, ids)
    return ids.astype(f32)


def by_variable(ref, count):
    return jnp.concatenate([ref[pl.ds(c, count, stride=NC)] for c in range(NC)], axis=1)


def pack_x(ny, delta, eddy, courant, alpha, tile_map, y_a, y_b, beams, *rest):
    others = rest[: ny - 2]
    out_a, out_b, field, picks, known, tiles = rest[ny - 2 :]
    even, _, _ = place_on("gx")
    owned = alpha.shape[0] // NC
    gather_known(ny, alpha, y_a, others, known)
    turned = tile_numbers(ny, tile_map, y_a, y_b, tiles)
    ids = tile_ids(ny, owned)
    columns = [x for x in range(RIM)] + [CX - RIM + x for x in range(RIM)]
    for i, x in enumerate(columns):
        picks[i * PITCH : (i + 1) * PITCH] = (turned[:, x : x + 1] == ids).astype(f32)
    fine = two_part_dot(picks[...].astype(bf16), by_variable(known, ny * owned))

    def fill(own, y_base, reach, c):
        for i, x in enumerate(columns):
            at = i * PITCH
            field[at + CY : at + PITCH] = jnp.zeros((PITCH - CY, 128), f32)
            field[at : at + CY] = own[x * CY : (x + 1) * CY]
        for away in range(1, reach + 1):
            for first, base in ((0, 0), (CX - RIM, RIM * PITCH)):
                rows = pl.ds(y_base + (away - 1) * CX + first, RIM)
                north, south = y_sides(y_a, y_b, rows)
                field[pl.ds(base + CY - 1 + away, RIM, stride=PITCH)] = north
                field[pl.ds(base + PITCH - away, RIM, stride=PITCH)] = south
        if c is not None:
            field[...] += profile_weight * fine[:, c * 128 : (c + 1) * 128]

    def put(at, found):
        for away, start, extra in found:
            east, west = (2 * RIM - away) * PITCH, (away - 1) * PITCH
            here = at + start
            for source, target, size in (
                (PITCH - extra, 0, extra),
                (0, extra, CY + extra),
            ):
                if size:
                    first = field[east + source : east + source + size]
                    second = field[west + source : west + source + size]
                    rows = slice(here + target, here + target + size)
                    out_a[rows] = jnp.where(even, first, second)
                    out_b[rows] = jnp.where(even, second, first)

    for c in range(NC):
        fill(delta.at[c], c * RIM * CX, RIM, c)
        put(c * WIDE_ROWS, WIDE)
    for f in range(3):
        own = eddy if f == 0 else courant.at[f - 1]
        fill(own, Y_COEF + f * INNER * CX, INNER, None)
        put(X_COEF + f * SLIM_ROWS, SLIM)
    out_a[X_HALO:] = beams[...]


def prepare(
    ny,
    nx,
    delta,
    eddy,
    courant,
    alpha,
    tile_map,
    gate_beam,
    gate_index,
    gate_column,
    gate_live,
    precision,
    weights,
    y_a,
    y_b,
    *rest,
):
    others = rest[: ny - 2]
    core, coef, picks, wide, slot_pick, slot_push, beam_pick, columns = rest[ny - 2 : ny + 6]
    known, tiles, meta = rest[ny + 6 :]
    owned = alpha.shape[0] // NC

    def fill(ref, base, own, y_base, reach):
        for x in range(CX):
            at = base + x * PITCH
            ref[at : at + CY] = own[x * CY : (x + 1) * CY]
            ref[at + CY : at + PITCH] = jnp.zeros((PITCH - CY, 128), f32)
        for away in range(1, reach + 1):
            north, south = y_sides(y_a, y_b, pl.ds(y_base + (away - 1) * CX, CX))
            ref[pl.ds(base + CY - 1 + away, CX, stride=PITCH)] = north
            ref[pl.ds(base + PITCH - away, CX, stride=PITCH)] = south

    for c in range(NC):
        fill(core, c * CORE, delta.at[c], c * RIM * CX, RIM)
    for f in range(3):
        own = eddy if f == 0 else courant.at[f - 1]
        fill(coef, f * CORE, own, Y_COEF + f * INNER * CX, INNER)

    def combine(b, carry):
        at = pl.multiple_of(b * PITCH, 8)
        combined = combine_coefs(*[coef[pl.ds(f * CORE + at, PITCH)] for f in range(3)])
        for f, value in enumerate(combined):
            coef[pl.ds(f * CORE + at, PITCH)] = value
        return carry

    lax.fori_loop(0, CX, combine, 0)

    gather_known(ny, alpha, y_a, others, known)
    turned = tile_numbers(ny, tile_map, y_a, y_b, tiles)
    ids = tile_ids(ny, owned)
    for x in range(CX):
        picks[x * PITCH : (x + 1) * PITCH] = (turned[:, x : x + 1] == ids).astype(f32)
    fine = two_part_dot(picks[...].astype(bf16), by_variable(known, ny * owned))
    for c in range(NC):
        core[c * CORE : (c + 1) * CORE] += profile_weight * fine[:, c * 128 : (c + 1) * 128]

    slots = gate_column.shape[1]
    for c in range(NC):
        wide[:, c * 128 : (c + 1) * 128] = weights[pl.ds(c, slots, stride=NC)]
    beam = gate_beam[...]
    per_beam = beam_pick.shape[1]
    held = per_beam // nx
    relative = jnp.bitwise_xor(beam // held, lax.axis_index("gx"))
    relative = ((relative & 1) * (nx // 2) + (relative >> 1)) * held + lax.rem(beam, held)
    meta[...] = jnp.zeros(meta.shape, f32)
    meta[0:1] = gate_column[...].astype(f32)
    meta[1:2] = relative.astype(f32)
    meta[2:3] = gate_index[...].astype(f32)
    meta[3:4] = gate_live[...].astype(f32) * precision[...]
    turned = jnp.transpose(meta[...])
    columns[...] = turned
    slot_lane = lax.broadcasted_iota(jnp.int32, (slots, CX * CY), 1).astype(f32)
    slot_pick[...] = (slot_lane == turned[:, 0:1]).astype(f32).astype(bf16)
    column_row = lax.broadcasted_iota(jnp.int32, (CX * CY, slots), 0)
    slot_push[...] = (column_row == gate_column[...]).astype(f32).astype(bf16)
    beam_lane = lax.broadcasted_iota(jnp.int32, (slots, per_beam), 1).astype(f32)
    beam_pick[...] = (beam_lane == turned[:, 1:2]).astype(f32).astype(bf16)


def combine_coefs(viscous, along_x, along_y):
    half_x, half_y = 0.5 * along_x, 0.5 * along_y
    return (
        1.0 - 4.0 * viscous,
        viscous - half_x,
        viscous + half_x,
        viscous - half_y,
        viscous + half_y,
    )


def main(core, coef_core, wide, slot_pick, slot_push, beam_pick, columns, beams, x_a, x_b, *rest):
    out_a, out_b, out_core, state_0, state_1, coef, raw, forcing, table = rest
    even, _, _ = place_on("gx")
    slots = columns.shape[0]
    per_beam = beam_pick.shape[1]
    half = beams.shape[0]
    table[0:half] = beams[...]
    table[half:] = x_a[X_HALO:]

    def clear(ref, base, blocks):
        for b in blocks:
            at = base + b * PITCH
            ref[at : at + PITCH] = jnp.zeros((PITCH, 128), f32)

    def fill(ref, base, x_base, found):
        for away, start, extra in found:
            for source, target, size in (
                (0, PITCH - extra, extra),
                (extra, 0, CY + extra),
            ):
                if size:
                    at = x_base + start + source
                    west, east = x_sides(x_a, x_b, pl.ds(at, size))
                    at = base + (FIRST - away) * PITCH + target
                    ref[at : at + size] = west
                    at = base + (FIRST + CX - 1 + away) * PITCH + target
                    ref[at : at + size] = east

    rim = [FIRST - 3, FIRST - 2, FIRST - 1, FIRST + CX, FIRST + CX + 1, FIRST + CX + 2]
    for c in range(NC):
        at = c * FIELD + FIRST * PITCH
        state_0[at : at + CORE] = core[c * CORE : (c + 1) * CORE]
        clear(state_0, c * FIELD, rim)
        fill(state_0, c * FIELD, c * WIDE_ROWS, WIDE)
    for f in range(3):
        clear(raw, f * FIELD, rim[1:5])
        fill(raw, f * FIELD, X_COEF + f * SLIM_ROWS, SLIM)
    for f in range(5):
        at = f * FIELD + FIRST * PITCH
        coef[at : at + CORE] = coef_core[f * CORE : (f + 1) * CORE]
        clear(coef, f * FIELD, [0, 1, BLOCKS - 2, BLOCKS - 1])
    for b in rim[1:5]:
        rows = [slice(f * FIELD + b * PITCH, f * FIELD + (b + 1) * PITCH) for f in range(5)]
        for f, value in enumerate(combine_coefs(*[raw[rows[f]] for f in range(3)])):
            coef[rows[f]] = value

    gate_lane = lax.broadcasted_iota(jnp.int32, (slots, 128), 1).astype(f32)
    gate_here = gate_lane == columns[:, 2:3]
    scaled = columns[:, 3:4]

    def forward(source, target, low, high):
        def body(b, carry):
            at = pl.multiple_of(b * PITCH, 8)
            k = [coef[pl.ds(f * FIELD + at, PITCH)] for f in range(5)]
            for c in range(NC):
                base = c * FIELD + at
                here = source[pl.ds(base, PITCH)]
                target[pl.ds(base, PITCH)] = (
                    k[0] * here
                    + k[1] * source[pl.ds(base + PITCH, PITCH)]
                    + k[2] * source[pl.ds(base - PITCH, PITCH)]
                    + k[3] * pltpu.roll(here, PITCH - 1, 0)
                    + k[4] * pltpu.roll(here, 1, 0)
                )
            return carry

        lax.fori_loop(low, high, body, 0)

    buffers = [state_0, state_1]
    for step in range(STEPS):
        source, target = buffers[step % 2], buffers[(step + 1) % 2]
        forward(source, target, 2 + step, BLOCKS - 2 - step)
        own = jnp.concatenate(
            [
                jnp.concatenate(
                    [
                        target[c * FIELD + b * PITCH : c * FIELD + b * PITCH + CY]
                        for b in range(FIRST, FIRST + CX)
                    ],
                    axis=0,
                )
                for c in range(NC)
            ],
            axis=1,
        )
        picked = two_part_dot(slot_pick[...], own) * wide[...]
        rows = two_part_dot(beam_pick[...], table[pl.ds(step, per_beam, stride=STEPS)])
        tally = -jnp.where(gate_here, rows, 0.0)
        for c in range(NC):
            tally = tally + picked[:, c * 128 : (c + 1) * 128]
        misfit = scaled * jnp.sum(tally, axis=1, keepdims=True)
        forcing[step * CX * CY : (step + 1) * CX * CY] = two_part_dot(
            slot_push[...], misfit * wide[...]
        )

    for c in range(NC):
        clear(state_0, c * FIELD, [0, 1, 2, 3, BLOCKS - 4, BLOCKS - 3, BLOCKS - 2, BLOCKS - 1])
        clear(state_1, c * FIELD, [1, 2, BLOCKS - 3, BLOCKS - 2])

    def add_forcing(ref, step):
        for c in range(NC):
            for x in range(CX):
                at = c * FIELD + (FIRST + x) * PITCH
                first = step * CX * CY + x * CY
                value = forcing[first : first + CY, c * 128 : (c + 1) * 128]
                if step == STEPS - 1:
                    ref[at : at + CY] = value
                    ref[at + CY : at + PITCH] = jnp.zeros((PITCH - CY, 128), f32)
                else:
                    ref[at : at + CY] += value

    def backward(source, target, low, high):
        def body(b, carry):
            at = pl.multiple_of(b * PITCH, 8)
            k = [
                coef[pl.ds(at, PITCH)],
                coef[pl.ds(FIELD + at - PITCH, PITCH)],
                coef[pl.ds(2 * FIELD + at + PITCH, PITCH)],
                coef[pl.ds(3 * FIELD + at, PITCH)],
                coef[pl.ds(4 * FIELD + at, PITCH)],
            ]
            for c in range(NC):
                base = c * FIELD + at
                here = source[pl.ds(base, PITCH)]
                target[pl.ds(base, PITCH)] = (
                    k[0] * here
                    + k[1] * source[pl.ds(base - PITCH, PITCH)]
                    + k[2] * source[pl.ds(base + PITCH, PITCH)]
                    + pltpu.roll(k[3] * here, 1, 0)
                    + pltpu.roll(k[4] * here, PITCH - 1, 0)
                )
            return carry

        lax.fori_loop(low, high, body, 0)

    for step in range(STEPS):
        source, target = buffers[step % 2], buffers[(step + 1) % 2]
        add_forcing(source, STEPS - 1 - step)
        backward(source, target, FIRST - 1 - step, FIRST + CX + 1 + step)
    final = buffers[STEPS % 2]

    for c in range(NC):
        at = c * FIELD + FIRST * PITCH
        out_core[c * CORE : (c + 1) * CORE] = final[at : at + CORE]
        for away, start, extra in WIDE:
            for source, target, size in (
                (PITCH - extra, 0, extra),
                (0, extra, CY + extra),
            ):
                if size:
                    at = c * FIELD + (FIRST - away) * PITCH + source
                    west = final[at : at + size]
                    at = c * FIELD + (FIRST + CX - 1 + away) * PITCH + source
                    east = final[at : at + size]
                    at = c * WIDE_ROWS + start + target
                    out_a[at : at + size] = jnp.where(even, east, west)
                    out_b[at : at + size] = jnp.where(even, west, east)


def add_x(ny, delta, picks, core, x_a, x_b, *rest):
    out_a, out_b, out_near, out_sums = rest[:4]
    out_others = rest[4:-2]
    field, sums = rest[-2:]
    even, _, _ = place_on("gy")
    total = picks.shape[1]
    rows = total * NC // ny
    field[...] = core[...]
    for c in range(NC):
        for away, start, extra in WIDE:
            for source, target, size in (
                (0, PITCH - extra, extra),
                (extra, 0, CY + extra),
            ):
                if size:
                    at = c * WIDE_ROWS + start + source
                    west, east = x_sides(x_a, x_b, pl.ds(at, size))
                    at = c * CORE + (away - 1) * PITCH + target
                    field[at : at + size] += west
                    at = c * CORE + (CX - away) * PITCH + target
                    field[at : at + size] += east
    for c in range(NC):
        for away in range(1, RIM + 1):
            north = field[pl.ds(c * CORE + CY - 1 + away, CX, stride=PITCH)]
            south = field[pl.ds(c * CORE + PITCH - away, CX, stride=PITCH)]
            at = (c * RIM + away - 1) * CX
            out_a[at : at + CX] = jnp.where(even, north, south)
            out_b[at : at + CX] = jnp.where(even, south, north)
        for x in range(CX):
            at = c * CORE + x * PITCH
            here = slice(x * CY, (x + 1) * CY)
            out_near[c, here] = delta[c, here] + field[at : at + CY]
    adjoint = jnp.concatenate([field[c * CORE : (c + 1) * CORE] for c in range(NC)], axis=1)
    tile_sums = two_part_dot(jnp.transpose(picks[...]).astype(bf16), adjoint)
    for c in range(NC):
        sums[pl.ds(c, total, stride=NC)] = tile_sums[:, c * 128 : (c + 1) * 128]
    out_sums[...] = sums[0:rows]
    out_a[Y_COEF:] = sums[rows : 2 * rows]
    for s, other in enumerate(out_others):
        other[...] = sums[(2 + s) * rows : (3 + s) * rows]


def add_y(alpha, near, sums, y_a, y_b, *rest):
    others = rest[:-2]
    out_delta, out_alpha = rest[-2:]
    out_delta[...] = near[...]
    for c in range(NC):
        for away in range(1, RIM + 1):
            north, south = y_sides(y_a, y_b, pl.ds((c * RIM + away - 1) * CX, CX))
            high = pl.ds(CY - away, CX, stride=CY)
            low = pl.ds(away - 1, CX, stride=CY)
            out_delta[c, high] = out_delta[c, high] + north
            out_delta[c, low] = out_delta[c, low] + south
    total = sums[...] + y_a[Y_COEF:]
    for other in others:
        total = total + other[...]
    out_alpha[...] = alpha[...] + profile_weight * total


def on_device(
    delta,
    alpha,
    eddy,
    courant,
    tile_map,
    obs_rows,
    gate_beam,
    gate_index,
    gate_column,
    gate_live,
    obs_weight,
    obs_precision,
):
    nx = lax.axis_size("gx")
    ny = lax.axis_size("gy")
    owned = alpha.shape[1]
    slots = gate_column.shape[2]
    fine = delta.reshape(NC, CX * CY, 128)
    eddy = eddy.reshape(CX * CY, 128)
    courant = courant.reshape(2, CX * CY, 128)
    control = alpha.reshape(owned * NC, 128)
    weights = obs_weight.reshape(slots * NC, 128)
    gates = [
        value.reshape(1, slots)
        for value in (gate_beam, gate_index, gate_column, gate_live, obs_precision)
    ]
    own_beams = obs_rows.shape[0]
    beam_count = nx * own_beams
    rows = owned * NC
    total = ny * owned

    y_a, y_b, beams = call(
        pack_y,
        [(Y_HALO + rows, 128), (Y_HALO, 128), (own_beams * STEPS, 128)],
        [fine, eddy, courant, control, tile_map, obs_rows],
        [
            pltpu.VMEM(fine.shape, f32),
            pltpu.VMEM((3, CX * CY, 128), f32),
            pltpu.VMEM(tile_map.shape, jnp.int32),
            pltpu.VMEM(obs_rows.shape, f32),
            pltpu.VMEM(control.shape, f32),
            pltpu.SemaphoreType.DMA((7,)),
        ],
        in_specs=[HBM] * 6,
    )
    y_a = swap(y_a, "gy", 1)
    y_b = pair_b(y_b, "gy")
    others = [swap(control, "gy", xor) for xor in range(2, ny)]
    xor = 2
    while xor < nx:
        beams = jnp.concatenate([beams, swap(beams, "gx", xor)])
        xor *= 2

    x_a, x_b = call(
        lambda *refs: pack_x(ny, *refs),
        [(X_HALO + beams.shape[0], 128), (X_HALO, 128)],
        [fine, eddy, courant, control, tile_map, y_a, y_b, beams, *others],
        [
            pltpu.VMEM((2 * RIM * PITCH, 128), f32),
            pltpu.VMEM((2 * RIM * PITCH, total), f32),
            pltpu.VMEM((total * NC, 128), f32),
            pltpu.VMEM((128, 128), f32),
        ],
    )
    x_a = swap(x_a, "gx", 1)
    x_b = pair_b(x_b, "gx")

    core, coef, picks, wide, slot_pick, slot_push, beam_pick, columns = call(
        lambda *refs: prepare(ny, nx, *refs),
        [
            (NC * CORE, 128),
            (5 * CORE, 128),
            (CORE, total),
            (slots, NC * 128),
            jax.ShapeDtypeStruct((slots, CX * CY), bf16),
            jax.ShapeDtypeStruct((CX * CY, slots), bf16),
            jax.ShapeDtypeStruct((slots, beam_count), bf16),
            (slots, 8),
        ],
        [fine, eddy, courant, control, tile_map, *gates, weights, y_a, y_b, *others],
        [
            pltpu.VMEM((total * NC, 128), f32),
            pltpu.VMEM((128, 128), f32),
            pltpu.VMEM((8, slots), f32),
        ],
        flops=3000000,
    )

    back_a, back_b, core = call(
        main,
        [(X_COEF, 128), (X_COEF, 128), (NC * CORE, 128)],
        [core, coef, wide, slot_pick, slot_push, beam_pick, columns, beams, x_a, x_b],
        [
            pltpu.VMEM((NC * FIELD, 128), f32),
            pltpu.VMEM((NC * FIELD, 128), f32),
            pltpu.VMEM((5 * FIELD, 128), f32),
            pltpu.VMEM((3 * FIELD, 128), f32),
            pltpu.VMEM((STEPS * CX * CY, NC * 128), f32),
            pltpu.VMEM((beam_count * STEPS, 128), f32),
        ],
        flops=30000000,
    )
    x_a = swap(back_a, "gx", 1)
    x_b = pair_b(back_b, "gx")
    back_a, back_b, near, sums, *back = call(
        lambda *refs: add_x(ny, *refs),
        [(Y_COEF + rows, 128), (Y_COEF, 128), fine.shape, (rows, 128)] + [(rows, 128)] * (ny - 2),
        [fine, picks, core, x_a, x_b],
        [pltpu.VMEM((NC * CORE, 128), f32), pltpu.VMEM((total * NC, 128), f32)],
    )
    y_a = swap(back_a, "gy", 1)
    y_b = pair_b(back_b, "gy")
    others = [swap(value, "gy", xor) for xor, value in zip(range(2, ny), back)]
    grad_delta, grad_alpha = call(
        add_y,
        [fine.shape, control.shape],
        [control, near, sums, y_a, y_b, *others],
    )
    return grad_delta.reshape(delta.shape), grad_alpha.reshape(alpha.shape)


def solution(mesh):
    return jax.shard_map(
        on_device,
        mesh=mesh,
        in_specs=(
            P(None, "gx", "gy", None),
            P("gx", "gy", None, None),
            P("gx", "gy", None),
            P(None, "gx", "gy", None),
            P("gx", "gy"),
            P(("gx", "gy"), None, None),
            P("gx", "gy", None),
            P("gx", "gy", None),
            P("gx", "gy", None),
            P("gx", "gy", None),
            P("gx", "gy", None, None, None),
            P("gx", "gy", None),
        ),
        out_specs=(P(None, "gx", "gy", None), P("gx", "gy", None, None)),
        check_vma=False,
    )
```

time: 259 us -> 51.1 us (0.20)
  the two profiles are of different devices: /device:TPU:0 before, /device:TPU:16 now
where the time goes in v3:
time: 51.1 us; the launch traced here: 50.7 us
  starting transfers between devices  18.2 us (36%)
  waiting for transfers between devices  17.6 us (34%)
  Pallas kernels  9.74 us (19%)
  local copies, waits for them, and re-layouts  4.3 us (8%)
  between operations  0.83 us (2%)
    ppermute x10, starting transfers between devices, swap(): lax.ppermute(block, axis, [(i, i ^ xor) for i in range(lax.axis_size(axis...  13.1 us
    pallas_call x6, Pallas kernels, call(): pl.pallas_call(body, out_shape=shapes, in_specs=in_specs or [VMEM] * len(...  9.74 us
    ppermute x10, waiting for transfers between devices, swap(): lax.ppermute(block, axis, [(i, i ^ xor) for i in range(lax.axis_size(axis...  9.64 us
    ppermute x4, waiting for transfers between devices, pair_b(): return lax.ppermute(block, axis, pairs)  7.98 us
    ppermute x4, starting transfers between devices, pair_b(): return lax.ppermute(block, axis, pairs)  5.14 us
    unnamed x27, local copies, waits for them, and re-layouts  4.3 us
  transfers between devices with their start and end apart: 14, of which 6 were waited for; matrix products, arithmetic and copies ran while one was open for 1% of the time, Pallas kernels for 3%

profile of v3, /device:TPU:16, one launch (start us, length us, event | category | flops | bytes accessed | tf_op | source)
XLA Modules:
  0.0 50.7 jit_solution(13163713942728657048)
XLA Ops:
  0.6 1.0 %collective-permute-start.3 = (f32[16,128]{1,0:T(8,128)}, f32[16,128]{1,0:T(8,128)S(1)}, u32[]{:S(2)}, u32[]{:S(2)}) collective-permute-start(f32[16,128]{1,0:T(8,128)} %bitcast.23), channel_id=1, source_target_pairs={{0,3},{1,2},{2,1},{3,0},{4,7},{5,6},{6,5},{7,4},{8,11},{9,10},{10,... | collective-permute-start | bytes 24584 | tf_op jit(solution)/shard_map/ppermute | solution.py:46
  1.6 0.6 %collective-permute-start.2 = (f32[16,128]{1,0:T(8,128)}, f32[16,128]{1,0:T(8,128)S(1)}, u32[]{:S(2)}, u32[]{:S(2)}) collective-permute-start(f32[16,128]{1,0:T(8,128)} %bitcast.24), channel_id=1, source_target_pairs={{0,2},{1,3},{2,0},{3,1},{4,6},{5,7},{6,4},{7,5},{8,10},{9,11},{10,... | collective-permute-start | bytes 24584 | tf_op jit(solution)/shard_map/ppermute | solution.py:46
  2.3 0.0 copy-start.5
  2.3 0.0 copy-start.6
  2.3 0.7 %copy.14.beam_rows = f32[8,3,128]{2,1,0:T(4,128)S(1)} copy(f32[8,3,128]{2,0,1:T(8,128)} %param.17) | data formatting | bytes 24576 | tf_op args[5]
  3.0 0.0 copy-done.5
  3.0 0.0 copy-done.6
  3.0 0.0 copy-start
  3.0 1.0 %copy-done = f32[4,16,16,128]{3,2,1,0:T(8,128)S(1)} copy-done((f32[4,16,16,128]{3,2,1,0:T(8,128)S(1)}, f32[4,16,16,128]{3,2,1,0:T(8,128)}, u32[]{:S(2)}) %copy-start) | copy-done | bytes 524312
  4.1 0.0 copy-start.2
  4.1 0.9 %copy-done.2 = f32[2,16,16,128]{3,2,1,0:T(8,128)S(1)} copy-done((f32[2,16,16,128]{3,2,1,0:T(8,128)S(1)}, f32[2,16,16,128]{3,2,1,0:T(8,128)}, u32[]{:S(2)}) %copy-start.2) | copy-done | bytes 262168
  5.0 0.0 copy-start.3
  5.0 0.9 %copy-done.3 = f32[16,16,128]{2,1,0:T(8,128)S(1)} copy-done((f32[16,16,128]{2,1,0:T(8,128)S(1)}, f32[16,16,128]{2,1,0:T(8,128)}, u32[]{:S(2)}) %copy-start.3) | copy-done | bytes 131096
  5.9 0.7 %shard_map.131 = (f32[320,128]{1,0:T(8,128)S(1)}, f32[304,128]{1,0:T(8,128)S(1)}, f32[24,128]{1,0:T(8,128)S(1)}) custom-call(f32[4,256,128]{2,1,0:T(8,128)S(1)} %bitcast.12, f32[256,128]{1,0:T(8,128)S(1)} %bitcast.19, f32[2,256,128]{2,1,0:T(8,128)S(1)} %bitcast.16, f32[16,128]{1,0:T(8,128)S(1)} %bitcast.25, s32[16,16]{1,0:T(8,128)S(1)} %copy-done.6, ...), custom_call_target="tpu_custom_call" | custom-call | flops 1000000 | bytes 939008 | tf_op jit(solution)/shard_map/pallas_call | solution.py:34
  6.6 1.6 %collective-permute-start.4 = (f32[24,128]{1,0:T(8,128)S(1)}, f32[24,128]{1,0:T(8,128)S(1)}, u32[]{:S(2)}, u32[]{:S(2)}) collective-permute-start(f32[24,128]{1,0:T(8,128)S(1)} %get-tuple-element.36), channel_id=1, source_target_pairs={{0,8},{4,12},{8,0},{12,4},{16,24},{20,28},{24,16},{28,20},{1,9},{5... | collective-permute-start | bytes 36872 | tf_op jit(solution)/shard_map/ppermute | solution.py:46
  8.3 0.7 %collective-permute-start.1 = (f32[304,128]{1,0:T(8,128)S(1)}, f32[304,128]{1,0:T(8,128)S(1)}, u32[]{:S(2)}, u32[]{:S(2)}) collective-permute-start(f32[304,128]{1,0:T(8,128)S(1)} %get-tuple-element.27), channel_id=1, source_target_pairs={{0,0},{3,3},{1,2},{2,1},{4,4},{7,7},{5,6},{6,5},{8,8},{11,11},{9,1... | collective-permute-start | bytes 466952 | tf_op jit(solution)/shard_map/ppermute | solution.py:54
  9.0 2.8 %collective-permute-start = (f32[320,128]{1,0:T(8,128)S(1)}, f32[320,128]{1,0:T(8,128)S(1)}, u32[]{:S(2)}, u32[]{:S(2)}) collective-permute-start(f32[320,128]{1,0:T(8,128)S(1)} %get-tuple-element.26), channel_id=1, source_target_pairs={{0,1},{1,0},{2,3},{3,2},{4,5},{5,4},{6,7},{7,6},{8,9},{9,8},{10,11... | collective-permute-start | bytes 491528 | tf_op jit(solution)/shard_map/ppermute | solution.py:46
  11.8 0.0 collective-permute-done.4
  11.8 0.4 collective-permute-start.5
  12.2 4.4 %collective-permute-done.5 = f32[48,128]{1,0:T(8,128)S(1)} collective-permute-done((f32[48,128]{1,0:T(8,128)S(1)}, f32[48,128]{1,0:T(8,128)S(1)}, u32[]{:S(2)}, u32[]{:S(2)}) %collective-permute-start.5) | collective-permute-done | bytes 24608 | tf_op jit(solution)/shard_map/ppermute | solution.py:46
  16.6 0.0 copy-start.4
  16.6 0.0 collective-permute-done.3.refs_14_.refs_9_
  16.6 0.0 collective-permute-done.2.refs_13_.refs_8_
  16.6 0.0 collective-permute-done.1.refs_12_.refs_6_
  16.6 0.0 collective-permute-done.refs_11_.refs_5_
  16.6 0.0 copy-start.8
  16.6 0.0 copy-start.9
  16.6 0.0 copy-start.10
  16.6 0.0 copy-start.11
  16.7 0.6 %shard_map.133 = (f32[414,128]{1,0:T(8,128)S(1)}, f32[318,128]{1,0:T(8,128)S(1)}) custom-call(f32[4,256,128]{2,1,0:T(8,128)S(1)} %bitcast.13, f32[256,128]{1,0:T(8,128)S(1)} %bitcast.20, f32[2,256,128]{2,1,0:T(8,128)S(1)} %bitcast.17, f32[16,128]{1,0:T(8,128)S(1)} %bitcast.26, s32[16,16]{1,0:T(8,128)S(1)} %copy-done.6, ...), custom_call_target="tpu_custom_call" | custom-call | flops 1000000 | bytes 1311744 | tf_op jit(solution)/shard_map/pallas_call | solution.py:34
  17.2 1.6 %collective-permute-start.6 = (f32[414,128]{1,0:T(8,128)S(1)}, f32[414,128]{1,0:T(8,128)S(1)}, u32[]{:S(2)}, u32[]{:S(2)}) collective-permute-start(f32[414,128]{1,0:T(8,128)S(1)} %get-tuple-element.37), channel_id=1, source_target_pairs={{0,4},{4,0},{8,12},{12,8},{16,20},{20,16},{24,28},{28,24},{1,5},{5... | collective-permute-start | bytes 635912 | tf_op jit(solution)/shard_map/ppermute | solution.py:46
  18.8 1.9 %collective-permute-start.7 = (f32[318,128]{1,0:T(8,128)S(1)}, f32[318,128]{1,0:T(8,128)S(1)}, u32[]{:S(2)}, u32[]{:S(2)}) collective-permute-start(f32[318,128]{1,0:T(8,128)S(1)} %get-tuple-element.38), channel_id=1, source_target_pairs={{0,0},{28,28},{4,8},{8,4},{12,16},{16,12},{20,24},{24,20},{1,1},{2... | collective-permute-start | bytes 488456 | tf_op jit(solution)/shard_map/ppermute | solution.py:54
  20.7 0.0 copy-start.7
  20.7 0.0 copy-done.4
  20.7 0.0 copy-done.8
  20.7 0.0 copy-done.9
  20.8 0.0 copy-done.10
  20.8 0.0 copy-done.11
  20.8 0.6 %copy-done.7 = s32[1,1,256]{2,1,0:T(1,128)S(1)} copy-done((s32[1,1,256]{2,1,0:T(1,128)S(1)}, s32[1,1,256]{2,1,0:T(1,128)}, u32[]{:S(2)}) %copy-start.7) | copy-done | bytes 1048
  21.4 1.0 %shard_map.132 = (f32[1536,128]{1,0:T(8,128)S(1)}, f32[1920,128]{1,0:T(8,128)S(1)}, f32[384,16]{1,0:T(8,128)S(1)}, f32[256,512]{1,0:T(8,128)S(1)}, bf16[256,256]...) custom-call(f32[4,256,128]{2,1,0:T(8,128)S(1)} %bitcast.14, ...), custom_call_target="tpu_custom_call" | custom-call | flops 3000000 | bytes 1792000 | tf_op jit(solution)/shard_map/pallas_call | solution.py:34
  22.4 4.5 %collective-permute-done.7.x_b = f32[318,128]{1,0:T(8,128)S(1)} collective-permute-done((f32[318,128]{1,0:T(8,128)S(1)}, f32[318,128]{1,0:T(8,128)S(1)}, u32[]{:S(2)}, u32[]{:S(2)}) %collective-permute-start.7) | collective-permute-done | bytes 162848 | tf_op jit(solution)/shard_map/ppermute | solution.py:54
  26.9 0.0 collective-permute-done.6.x_a
  26.9 0.0 copy-start.1
  26.9 6.1 %shard_map.134 = (f32[216,128]{1,0:T(8,128)S(1)}, f32[216,128]{1,0:T(8,128)S(1)}, f32[1536,128]{1,0:T(8,128)S(1)}) custom-call(f32[1536,128]{1,0:T(8,128)S(1)} %get-tuple-element.29.core, f32[1920,128]{1,0:T(8,128)S(1)} %get-tuple-element.30.coef_core, f32[256,512]{1,0:T(8,128)S(1)} %get-tuple-element.31.wide, ...), custom_call_target="tpu_custom_call" | custom-call | flops 30000000 | bytes 3315712 | tf_op jit(solution)/shard_map/pallas_call | solution.py:34
  33.1 1.6 %collective-permute-start.8 = (f32[216,128]{1,0:T(8,128)S(1)}, f32[216,128]{1,0:T(8,128)S(1)}, u32[]{:S(2)}, u32[]{:S(2)}) collective-permute-start(f32[216,128]{1,0:T(8,128)S(1)} %get-tuple-element.40), channel_id=1, source_target_pairs={{0,4},{4,0},{8,12},{12,8},{16,20},{20,16},{24,28},{28,24},{1,5},{5... | collective-permute-start | bytes 331784 | tf_op jit(solution)/shard_map/ppermute | solution.py:46
  34.7 1.9 %collective-permute-start.9 = (f32[216,128]{1,0:T(8,128)S(1)}, f32[216,128]{1,0:T(8,128)S(1)}, u32[]{:S(2)}, u32[]{:S(2)}) collective-permute-start(f32[216,128]{1,0:T(8,128)S(1)} %get-tuple-element.41), channel_id=1, source_target_pairs={{0,0},{28,28},{4,8},{8,4},{12,16},{16,12},{20,24},{24,20},{1,1},{2... | collective-permute-start | bytes 331784 | tf_op jit(solution)/shard_map/ppermute | solution.py:54
  36.6 2.2 %collective-permute-done.8.refs_3_ = f32[216,128]{1,0:T(8,128)S(1)} collective-permute-done((f32[216,128]{1,0:T(8,128)S(1)}, f32[216,128]{1,0:T(8,128)S(1)}, u32[]{:S(2)}, u32[]{:S(2)}) %collective-permute-start.8) | collective-permute-done | bytes 110624 | tf_op jit(solution)/shard_map/ppermute | solution.py:46
  38.7 3.5 %collective-permute-done.9.refs_4_ = f32[216,128]{1,0:T(8,128)S(1)} collective-permute-done((f32[216,128]{1,0:T(8,128)S(1)}, f32[216,128]{1,0:T(8,128)S(1)}, u32[]{:S(2)}, u32[]{:S(2)}) %collective-permute-start.9) | collective-permute-done | bytes 110624 | tf_op jit(solution)/shard_map/ppermute | solution.py:54
  42.2 0.0 copy-done.1
  42.2 0.4 shard_map.135
  42.6 0.0 collective-permute-start.10
  42.6 0.7 %collective-permute-start.11 = (f32[192,128]{1,0:T(8,128)S(1)}, f32[192,128]{1,0:T(8,128)S(1)}, u32[]{:S(2)}, u32[]{:S(2)}) collective-permute-start(f32[192,128]{1,0:T(8,128)S(1)} %get-tuple-element.45), channel_id=1, source_target_pairs={{0,0},{3,3},{1,2},{2,1},{4,4},{7,7},{5,6},{6,5},{8,8},{11,11},{9,1... | collective-permute-start | bytes 294920 | tf_op jit(solution)/shard_map/ppermute | solution.py:54
  43.3 3.4 %collective-permute-start.12 = (f32[16,128]{1,0:T(8,128)S(1)}, f32[16,128]{1,0:T(8,128)S(1)}, u32[]{:S(2)}, u32[]{:S(2)}) collective-permute-start(f32[16,128]{1,0:T(8,128)S(1)} %get-tuple-element.46), channel_id=1, source_target_pairs={{0,2},{1,3},{2,0},{3,1},{4,6},{5,7},{6,4},{7,5},{8,10},{9,11},{10,... | collective-permute-start | bytes 24584 | tf_op jit(solution)/shard_map/ppermute | solution.py:46
  46.7 0.0 collective-permute-start.13
  46.7 2.6 %collective-permute-done.12.rest_0_ = f32[16,128]{1,0:T(8,128)S(1)} collective-permute-done((f32[16,128]{1,0:T(8,128)S(1)}, f32[16,128]{1,0:T(8,128)S(1)}, u32[]{:S(2)}, u32[]{:S(2)}) %collective-permute-start.12) | collective-permute-done | bytes 8224 | tf_op jit(solution)/shard_map/ppermute | solution.py:46
  49.3 0.5 collective-permute-done.13.rest_1_
  49.8 0.0 collective-permute-done.11.y_b
  49.8 0.0 collective-permute-done.10.y_a
  49.8 0.9 %shard_map.136 = (f32[4,256,128]{2,1,0:T(8,128)}, f32[16,128]{1,0:T(8,128)}) custom-call(f32[16,128]{1,0:T(8,128)S(1)} %bitcast.28, f32[4,256,128]{2,1,0:T(8,128)S(1)} %get-tuple-element.42.near, f32[16,128]{1,0:T(8,128)S(1)} %get-tuple-element.43.sums, f32[208,128]{1,0:T(8,128)S(1)} %collective-permute-done.10.y_a, ...), custom_call_target="tpu_custom_call" | custom-call | flops 1000000 | bytes 761856 | tf_op jit(solution)/shard_map/pallas_call | solution.py:34
  (4 shorter events, 0.0 us)
Async XLA Ops:
  0.6 15.9 %collective-permute-start.3 = (f32[16,128]{1,0:T(8,128)}, f32[16,128]{1,0:T(8,128)S(1)}, u32[]{:S(2)}, u32[]{:S(2)}) collective-permute-start(f32[16,128]{1,0:T(8,128)} %bitcast.23), channel_id=1, source_target_pairs={{0,3},{1,2},{2,1},{3,0},{4,7},{5,6},{6,5},{7,4},{8,11},{9,10},{10,... | collective-permute-start | bytes 24584 | tf_op jit(solution)/shard_map/ppermute | solution.py:46
  1.6 15.0 %collective-permute-start.2 = (f32[16,128]{1,0:T(8,128)}, f32[16,128]{1,0:T(8,128)S(1)}, u32[]{:S(2)}, u32[]{:S(2)}) collective-permute-start(f32[16,128]{1,0:T(8,128)} %bitcast.24), channel_id=1, source_target_pairs={{0,2},{1,3},{2,0},{3,1},{4,6},{5,7},{6,4},{7,5},{8,10},{9,11},{10,... | collective-permute-start | bytes 24584 | tf_op jit(solution)/shard_map/ppermute | solution.py:46
  2.3 0.7 %copy-start.5 = (f32[1,4,4,128]{3,2,1,0:T(4,128)S(1)}, f32[1,4,4,128]{3,2,1,0:T(4,128)}, u32[]{:S(2)}) copy-start(f32[1,4,4,128]{3,2,1,0:T(4,128)} %param.13) | copy-start | bytes 24580
  2.3 0.7 %copy-start.6 = (s32[16,16]{1,0:T(8,128)S(1)}, s32[16,16]{1,0:T(8,128)}, u32[]{:S(2)}) copy-start(s32[16,16]{1,0:T(8,128)} %refs_4_.3) | copy-start | bytes 3076
  3.0 1.0 %copy-start = (f32[4,16,16,128]{3,2,1,0:T(8,128)S(1)}, f32[4,16,16,128]{3,2,1,0:T(8,128)}, u32[]{:S(2)}) copy-start(f32[4,16,16,128]{3,2,1,0:T(8,128)} %param.12) | copy-start | bytes 1572868
  4.1 0.9 %copy-start.2 = (f32[2,16,16,128]{3,2,1,0:T(8,128)S(1)}, f32[2,16,16,128]{3,2,1,0:T(8,128)}, u32[]{:S(2)}) copy-start(f32[2,16,16,128]{3,2,1,0:T(8,128)} %param.15) | copy-start | bytes 786436
  5.0 0.9 %copy-start.3 = (f32[16,16,128]{2,1,0:T(8,128)S(1)}, f32[16,16,128]{2,1,0:T(8,128)}, u32[]{:S(2)}) copy-start(f32[16,16,128]{2,1,0:T(8,128)} %param.14) | copy-start | bytes 393220
  6.6 5.1 %collective-permute-start.4 = (f32[24,128]{1,0:T(8,128)S(1)}, f32[24,128]{1,0:T(8,128)S(1)}, u32[]{:S(2)}, u32[]{:S(2)}) collective-permute-start(f32[24,128]{1,0:T(8,128)S(1)} %get-tuple-element.36), channel_id=1, source_target_pairs={{0,8},{4,12},{8,0},{12,4},{16,24},{20,28},{24,16},{28,20},{1,9},{5... | collective-permute-start | bytes 36872 | tf_op jit(solution)/shard_map/ppermute | solution.py:46
  8.3 8.3 %collective-permute-start.1 = (f32[304,128]{1,0:T(8,128)S(1)}, f32[304,128]{1,0:T(8,128)S(1)}, u32[]{:S(2)}, u32[]{:S(2)}) collective-permute-start(f32[304,128]{1,0:T(8,128)S(1)} %get-tuple-element.27), channel_id=1, source_target_pairs={{0,0},{3,3},{1,2},{2,1},{4,4},{7,7},{5,6},{6,5},{8,8},{11,11},{9,1... | collective-permute-start | bytes 466952 | tf_op jit(solution)/shard_map/ppermute | solution.py:54
  9.0 7.6 %collective-permute-start = (f32[320,128]{1,0:T(8,128)S(1)}, f32[320,128]{1,0:T(8,128)S(1)}, u32[]{:S(2)}, u32[]{:S(2)}) collective-permute-start(f32[320,128]{1,0:T(8,128)S(1)} %get-tuple-element.26), channel_id=1, source_target_pairs={{0,1},{1,0},{2,3},{3,2},{4,5},{5,4},{6,7},{7,6},{8,9},{9,8},{10,11... | collective-permute-start | bytes 491528 | tf_op jit(solution)/shard_map/ppermute | solution.py:46
  11.8 4.8 %collective-permute-start.5 = (f32[48,128]{1,0:T(8,128)S(1)}, f32[48,128]{1,0:T(8,128)S(1)}, u32[]{:S(2)}, u32[]{:S(2)}) collective-permute-start(f32[48,128]{1,0:T(8,128)S(1)} %pad_maximum_fusion), channel_id=1, source_target_pairs={{0,16},{4,20},{8,24},{12,28},{16,0},{20,4},{24,8},{28,12},{1,17},{... | collective-permute-start | bytes 73736 | tf_op jit(solution)/shard_map/ppermute | solution.py:46
  16.6 4.2 %copy-start.4 = (f32[1,1,256,4,128]{4,3,2,1,0:T(4,128)S(1)}, f32[1,1,256,4,128]{4,3,2,1,0:T(4,128)}, u32[]{:S(2)}) copy-start(f32[1,1,256,4,128]{4,3,2,1,0:T(4,128)} %param.22) | copy-start | bytes 1572868
  16.6 4.1 %copy-start.8 = (s32[1,1,256]{2,1,0:T(1,128)S(1)}, s32[1,1,256]{2,1,0:T(1,128)}, u32[]{:S(2)}) copy-start(s32[1,1,256]{2,1,0:T(1,128)} %param.19) | copy-start | bytes 3076
  16.6 4.1 %copy-start.9 = (s32[1,1,256]{2,1,0:T(1,128)S(1)}, s32[1,1,256]{2,1,0:T(1,128)}, u32[]{:S(2)}) copy-start(s32[1,1,256]{2,1,0:T(1,128)} %param.20) | copy-start | bytes 3076
  16.6 4.1 %copy-start.10 = (s32[1,1,256]{2,1,0:T(1,128)S(1)}, s32[1,1,256]{2,1,0:T(1,128)}, u32[]{:S(2)}) copy-start(s32[1,1,256]{2,1,0:T(1,128)} %param.21) | copy-start | bytes 3076
  16.6 4.1 %copy-start.11 = (f32[1,1,256]{2,1,0:T(1,128)S(1)}, f32[1,1,256]{2,1,0:T(1,128)}, u32[]{:S(2)}) copy-start(f32[1,1,256]{2,1,0:T(1,128)} %param.23) | copy-start | bytes 3076
  17.2 9.7 %collective-permute-start.6 = (f32[414,128]{1,0:T(8,128)S(1)}, f32[414,128]{1,0:T(8,128)S(1)}, u32[]{:S(2)}, u32[]{:S(2)}) collective-permute-start(f32[414,128]{1,0:T(8,128)S(1)} %get-tuple-element.37), channel_id=1, source_target_pairs={{0,4},{4,0},{8,12},{12,8},{16,20},{20,16},{24,28},{28,24},{1,5},{5... | collective-permute-start | bytes 635912 | tf_op jit(solution)/shard_map/ppermute | solution.py:46
  18.8 8.1 %collective-permute-start.7 = (f32[318,128]{1,0:T(8,128)S(1)}, f32[318,128]{1,0:T(8,128)S(1)}, u32[]{:S(2)}, u32[]{:S(2)}) collective-permute-start(f32[318,128]{1,0:T(8,128)S(1)} %get-tuple-element.38), channel_id=1, source_target_pairs={{0,0},{28,28},{4,8},{8,4},{12,16},{16,12},{20,24},{24,20},{1,1},{2... | collective-permute-start | bytes 488456 | tf_op jit(solution)/shard_map/ppermute | solution.py:54
  20.7 0.7 %copy-start.7 = (s32[1,1,256]{2,1,0:T(1,128)S(1)}, s32[1,1,256]{2,1,0:T(1,128)}, u32[]{:S(2)}) copy-start(s32[1,1,256]{2,1,0:T(1,128)} %param.18) | copy-start | bytes 3076
  26.9 15.2 %copy-start.1 = (f32[4,16,16,128]{3,2,1,0:T(8,128)S(1)}, f32[4,16,16,128]{3,2,1,0:T(8,128)}, u32[]{:S(2)}) copy-start(f32[4,16,16,128]{3,2,1,0:T(8,128)} %param.12) | copy-start | bytes 1572868
  33.1 5.7 %collective-permute-start.8 = (f32[216,128]{1,0:T(8,128)S(1)}, f32[216,128]{1,0:T(8,128)S(1)}, u32[]{:S(2)}, u32[]{:S(2)}) collective-permute-start(f32[216,128]{1,0:T(8,128)S(1)} %get-tuple-element.40), channel_id=1, source_target_pairs={{0,4},{4,0},{8,12},{12,8},{16,20},{20,16},{24,28},{28,24},{1,5},{5... | collective-permute-start | bytes 331784 | tf_op jit(solution)/shard_map/ppermute | solution.py:46
  34.7 7.5 %collective-permute-start.9 = (f32[216,128]{1,0:T(8,128)S(1)}, f32[216,128]{1,0:T(8,128)S(1)}, u32[]{:S(2)}, u32[]{:S(2)}) collective-permute-start(f32[216,128]{1,0:T(8,128)S(1)} %get-tuple-element.41), channel_id=1, source_target_pairs={{0,0},{28,28},{4,8},{8,4},{12,16},{16,12},{20,24},{24,20},{1,1},{2... | collective-permute-start | bytes 331784 | tf_op jit(solution)/shard_map/ppermute | solution.py:54
  42.6 7.2 %collective-permute-start.10 = (f32[208,128]{1,0:T(8,128)S(1)}, f32[208,128]{1,0:T(8,128)S(1)}, u32[]{:S(2)}, u32[]{:S(2)}) collective-permute-start(f32[208,128]{1,0:T(8,128)S(1)} %get-tuple-element.44), channel_id=1, source_target_pairs={{0,1},{1,0},{2,3},{3,2},{4,5},{5,4},{6,7},{7,6},{8,9},{9,8},{10,11... | collective-permute-start | bytes 319496 | tf_op jit(solution)/shard_map/ppermute | solution.py:46
  42.6 7.2 %collective-permute-start.11 = (f32[192,128]{1,0:T(8,128)S(1)}, f32[192,128]{1,0:T(8,128)S(1)}, u32[]{:S(2)}, u32[]{:S(2)}) collective-permute-start(f32[192,128]{1,0:T(8,128)S(1)} %get-tuple-element.45), channel_id=1, source_target_pairs={{0,0},{3,3},{1,2},{2,1},{4,4},{7,7},{5,6},{6,5},{8,8},{11,11},{9,1... | collective-permute-start | bytes 294920 | tf_op jit(solution)/shard_map/ppermute | solution.py:54
  43.3 6.0 %collective-permute-start.12 = (f32[16,128]{1,0:T(8,128)S(1)}, f32[16,128]{1,0:T(8,128)S(1)}, u32[]{:S(2)}, u32[]{:S(2)}) collective-permute-start(f32[16,128]{1,0:T(8,128)S(1)} %get-tuple-element.46), channel_id=1, source_target_pairs={{0,2},{1,3},{2,0},{3,1},{4,6},{5,7},{6,4},{7,5},{8,10},{9,11},{10,... | collective-permute-start | bytes 24584 | tf_op jit(solution)/shard_map/ppermute | solution.py:46
  46.7 3.1 %collective-permute-start.13 = (f32[16,128]{1,0:T(8,128)S(1)}, f32[16,128]{1,0:T(8,128)S(1)}, u32[]{:S(2)}, u32[]{:S(2)}) collective-permute-start(f32[16,128]{1,0:T(8,128)S(1)} %get-tuple-element.47), channel_id=1, source_target_pairs={{0,3},{1,2},{2,1},{3,0},{4,7},{5,6},{6,5},{7,4},{8,11},{9,10},{10,... | collective-permute-start | bytes 24584 | tf_op jit(solution)/shard_map/ppermute | solution.py:46

commit v4 on v3

--- a/solution.py
+++ b/solution.py
@@ -16,6 +16,8 @@
 FIRST = 4
 FIELD = BLOCKS * PITCH
 CORE = CX * PITCH
+OWN_BEAMS = 8
+BEAM_BITS = 3
 
 profile_weight = 0.125
 f32 = jnp.float32
@@ -46,11 +48,25 @@
     return lax.ppermute(block, axis, [(i, i ^ xor) for i in range(lax.axis_size(axis))])
 
 
-def pair_b(block, axis):
+def pair_b(block, axis, other):
+    count, across = lax.axis_size(axis), lax.axis_size(other)
+
+    def place(i, j):
+        return i * across + j if axis == "gx" else j * count + i
+
+    pairs = []
+    for j in range(across):
+        for i in range(count):
+            if i in (0, count - 1):
+                pairs.append((place(i, j), place(i, j ^ 1)))
+            else:
+                pairs.append((place(i, j), place(i + 1 if i % 2 else i - 1, j)))
+    return lax.ppermute(block, ("gx", "gy"), pairs)
+
+
+def ring_b(block, axis):
     count = lax.axis_size(axis)
-    pairs = [(0, 0), (count - 1, count - 1)]
-    for low in range(1, count - 1, 2):
-        pairs += [(low, low + 1), (low + 1, low)]
+    pairs = [(i, (i + 1 if i % 2 else i - 1) % count) for i in range(count)]
     return lax.ppermute(block, axis, pairs)
 
 
@@ -90,9 +106,30 @@
 
 
 def pack_y(
-    delta, eddy, courant, alpha, tile_map, beam_rows, out_a, out_b, out_beams, *scratch
+    delta,
+    eddy,
+    courant,
+    alpha,
+    tile_map,
+    gate_beam,
+    gate_index,
+    gate_column,
+    gate_live,
+    precision,
+    beam_rows,
+    out_a,
+    out_b,
+    fine,
+    coefs,
+    profiles,
+    near_tiles,
+    meta,
+    beams,
+    tiles,
+    gates,
+    values,
+    sems,
 ):
-    fine, coefs, tiles, beams, profiles, sems = scratch
     even, _, _ = place_on("gy")
     moves = [
         pltpu.make_async_copy(source, target, sems.at[i])
@@ -103,8 +140,13 @@
                 (courant.at[0], coefs.at[1]),
                 (courant.at[1], coefs.at[2]),
                 (tile_map, tiles),
+                (alpha, profiles),
+                (gate_beam, gates.at[0]),
+                (gate_index, gates.at[1]),
+                (gate_column, gates.at[2]),
+                (gate_live, gates.at[3]),
+                (precision, values),
                 (beam_rows, beams),
-                (alpha, profiles),
             ]
         )
     ]
@@ -125,13 +167,20 @@
     for f in range(3):
         for away in range(1, INNER + 1):
             put(Y_COEF + (f * INNER + away - 1) * CX, coefs.at[f], away)
+    near_tiles[...] = jnp.full((CX, 128), -1.0, f32)
+    near_tiles[:, 0:CY] = tiles[...].astype(f32)
     for out in (out_a, out_b):
-        out[Y_TILE : Y_TILE + CX] = jnp.full((CX, 128), -1.0, f32)
-        out[Y_TILE : Y_TILE + CX, 0:CY] = tiles[...].astype(f32)
+        out[Y_TILE : Y_TILE + CX] = near_tiles[...]
     out_a[Y_HALO:] = profiles[...]
-    per = beams.shape[1]
-    for i in range(beams.shape[0]):
-        out_beams[i * per : (i + 1) * per] = beams[i]
+    held = BEAM_BITS
+    beam = gates[0]
+    owner = jnp.bitwise_xor(beam >> held, lax.axis_index("gx"))
+    block = (owner & -4) | ((owner & 1) << 1) | ((owner >> 1) & 1)
+    meta[...] = jnp.zeros(meta.shape, f32)
+    meta[0:1] = gates[2].astype(f32)
+    meta[1:2] = ((block << held) | (beam & ((1 << held) - 1))).astype(f32)
+    meta[2:3] = gates[1].astype(f32)
+    meta[3:4] = gates[3].astype(f32) * values[...]
 
 
 def y_sides(got_a, got_b, rows, fill=0.0):
@@ -148,7 +197,7 @@
     return jnp.where(low, west, 0.0), jnp.where(high, east, 0.0)
 
 
-def gather_known(ny, alpha, got_a, others, known):
+def gather_known(alpha, got_a, others, known):
     owned = alpha.shape[0]
     known[0:owned] = alpha[...]
     known[owned : 2 * owned] = got_a[Y_HALO:]
@@ -156,7 +205,7 @@
         known[(2 + s) * owned : (3 + s) * owned] = other[...]
 
 
-def tile_numbers(ny, tile_map, got_a, got_b, tiles):
+def tile_numbers(near_tiles, got_a, got_b, tiles):
     spot = lax.broadcasted_iota(jnp.int32, (CX, 128), 1)
     north, south = y_sides(got_a, got_b, pl.ds(Y_TILE, CX), -1.0)
     near = jnp.where(
@@ -165,8 +214,7 @@
         jnp.where((spot >= PITCH - RIM) & (spot < PITCH), pltpu.roll(south, PITCH - CY, 1), -1.0),
     )
     tiles[...] = jnp.full(tiles.shape, -1.0, f32)
-    tiles[0:CX] = near
-    tiles[0:CX, 0:CY] = tile_map[...].astype(f32)
+    tiles[0:CX] = jnp.where(spot < CY, near_tiles[...], near)
     return jnp.transpose(tiles[...])[0:PITCH]
 
 
@@ -184,13 +232,13 @@
     return jnp.concatenate([ref[pl.ds(c, count, stride=NC)] for c in range(NC)], axis=1)
 
 
-def pack_x(ny, delta, eddy, courant, alpha, tile_map, y_a, y_b, beams, *rest):
+def pack_x(ny, delta, coefs, alpha, near_tiles, y_a, y_b, own_beams, got_beams, *rest):
     others = rest[: ny - 2]
-    out_a, out_b, field, picks, known, tiles = rest[ny - 2 :]
+    out_a, out_b, beams, field, picks, known, tiles = rest[ny - 2 :]
     even, _, _ = place_on("gx")
     owned = alpha.shape[0] // NC
-    gather_known(ny, alpha, y_a, others, known)
-    turned = tile_numbers(ny, tile_map, y_a, y_b, tiles)
+    gather_known(alpha, y_a, others, known)
+    turned = tile_numbers(near_tiles, y_a, y_b, tiles)
     ids = tile_ids(ny, owned)
     columns = [x for x in range(RIM)] + [CX - RIM + x for x in range(RIM)]
     for i, x in enumerate(columns):
@@ -230,33 +278,18 @@
         fill(delta.at[c], c * RIM * CX, RIM, c)
         put(c * WIDE_ROWS, WIDE)
     for f in range(3):
-        own = eddy if f == 0 else courant.at[f - 1]
-        fill(own, Y_COEF + f * INNER * CX, INNER, None)
+        fill(coefs.at[f], Y_COEF + f * INNER * CX, INNER, None)
         put(X_COEF + f * SLIM_ROWS, SLIM)
+    half = own_beams.shape[0]
+    beams[0:half] = own_beams[...]
+    beams[half:] = got_beams[...]
     out_a[X_HALO:] = beams[...]
 
 
-def prepare(
-    ny,
-    nx,
-    delta,
-    eddy,
-    courant,
-    alpha,
-    tile_map,
-    gate_beam,
-    gate_index,
-    gate_column,
-    gate_live,
-    precision,
-    weights,
-    y_a,
-    y_b,
-    *rest,
-):
+def prepare(ny, delta, coefs, alpha, near_tiles, meta, weights, y_a, y_b, *rest):
     others = rest[: ny - 2]
     core, coef, picks, wide, slot_pick, slot_push, beam_pick, columns = rest[ny - 2 : ny + 6]
-    known, tiles, meta = rest[ny + 6 :]
+    known, tiles = rest[ny + 6 :]
     owned = alpha.shape[0] // NC
 
     def fill(ref, base, own, y_base, reach):
@@ -272,8 +305,7 @@
     for c in range(NC):
         fill(core, c * CORE, delta.at[c], c * RIM * CX, RIM)
     for f in range(3):
-        own = eddy if f == 0 else courant.at[f - 1]
-        fill(coef, f * CORE, own, Y_COEF + f * INNER * CX, INNER)
+        fill(coef, f * CORE, coefs.at[f], Y_COEF + f * INNER * CX, INNER)
 
     def combine(b, carry):
         at = pl.multiple_of(b * PITCH, 8)
@@ -284,8 +316,8 @@
 
     lax.fori_loop(0, CX, combine, 0)
 
-    gather_known(ny, alpha, y_a, others, known)
-    turned = tile_numbers(ny, tile_map, y_a, y_b, tiles)
+    gather_known(alpha, y_a, others, known)
+    turned = tile_numbers(near_tiles, y_a, y_b, tiles)
     ids = tile_ids(ny, owned)
     for x in range(CX):
         picks[x * PITCH : (x + 1) * PITCH] = (turned[:, x : x + 1] == ids).astype(f32)
@@ -293,25 +325,16 @@
     for c in range(NC):
         core[c * CORE : (c + 1) * CORE] += profile_weight * fine[:, c * 128 : (c + 1) * 128]
 
-    slots = gate_column.shape[1]
+    slots = meta.shape[1]
     for c in range(NC):
         wide[:, c * 128 : (c + 1) * 128] = weights[pl.ds(c, slots, stride=NC)]
-    beam = gate_beam[...]
     per_beam = beam_pick.shape[1]
-    held = per_beam // nx
-    relative = jnp.bitwise_xor(beam // held, lax.axis_index("gx"))
-    relative = ((relative & 1) * (nx // 2) + (relative >> 1)) * held + lax.rem(beam, held)
-    meta[...] = jnp.zeros(meta.shape, f32)
-    meta[0:1] = gate_column[...].astype(f32)
-    meta[1:2] = relative.astype(f32)
-    meta[2:3] = gate_index[...].astype(f32)
-    meta[3:4] = gate_live[...].astype(f32) * precision[...]
     turned = jnp.transpose(meta[...])
     columns[...] = turned
     slot_lane = lax.broadcasted_iota(jnp.int32, (slots, CX * CY), 1).astype(f32)
     slot_pick[...] = (slot_lane == turned[:, 0:1]).astype(f32).astype(bf16)
-    column_row = lax.broadcasted_iota(jnp.int32, (CX * CY, slots), 0)
-    slot_push[...] = (column_row == gate_column[...]).astype(f32).astype(bf16)
+    column_row = lax.broadcasted_iota(jnp.int32, (CX * CY, slots), 0).astype(f32)
+    slot_push[...] = (column_row == meta[0:1]).astype(f32).astype(bf16)
     beam_lane = lax.broadcasted_iota(jnp.int32, (slots, per_beam), 1).astype(f32)
     beam_pick[...] = (beam_lane == turned[:, 1:2]).astype(f32).astype(bf16)
 
@@ -327,20 +350,13 @@
     )
 
 
-def main(core, coef_core, wide, slot_pick, slot_push, beam_pick, columns, beams, x_a, x_b, *rest):
-    out_a, out_b, out_core, state_0, state_1, coef, raw, forcing, table = rest
-    even, _, _ = place_on("gx")
-    slots = columns.shape[0]
-    per_beam = beam_pick.shape[1]
-    half = beams.shape[0]
-    table[0:half] = beams[...]
-    table[half:] = x_a[X_HALO:]
-
-    def clear(ref, base, blocks):
-        for b in blocks:
-            at = base + b * PITCH
-            ref[at : at + PITCH] = jnp.zeros((PITCH, 128), f32)
-
+def clear(ref, base, blocks):
+    for b in blocks:
+        at = base + b * PITCH
+        ref[at : at + PITCH] = jnp.zeros((PITCH, 128), f32)
+
+
+def forecast(core, coef_core, x_a, x_b, tops, lows, coef, state_0, state_1, raw):
     def fill(ref, base, x_base, found):
         for away, start, extra in found:
             for source, target, size in (
@@ -372,10 +388,6 @@
         rows = [slice(f * FIELD + b * PITCH, f * FIELD + (b + 1) * PITCH) for f in range(5)]
         for f, value in enumerate(combine_coefs(*[raw[rows[f]] for f in range(3)])):
             coef[rows[f]] = value
-
-    gate_lane = lax.broadcasted_iota(jnp.int32, (slots, 128), 1).astype(f32)
-    gate_here = gate_lane == columns[:, 2:3]
-    scaled = columns[:, 3:4]
 
     def forward(source, target, low, high):
         def body(b, carry):
@@ -412,15 +424,46 @@
             ],
             axis=1,
         )
-        picked = two_part_dot(slot_pick[...], own) * wide[...]
-        rows = two_part_dot(beam_pick[...], table[pl.ds(step, per_beam, stride=STEPS)])
-        tally = -jnp.where(gate_here, rows, 0.0)
+        rows = slice(step * CX * CY, (step + 1) * CX * CY)
+        tops[rows], lows[rows] = split(own)
+
+
+def main(
+    coef,
+    tops,
+    lows,
+    wide,
+    slot_pick,
+    slot_push,
+    beam_pick,
+    columns,
+    *rest,
+):
+    beams = rest[:-6]
+    out_a, out_b, out_core, state_0, state_1, forcing = rest[-6:]
+    even, _, _ = place_on("gx")
+    slots = columns.shape[0]
+    gate_lane = lax.broadcasted_iota(jnp.int32, (slots, 128), 1).astype(f32)
+    gate_here = gate_lane == columns[:, 2:3]
+    scaled = columns[:, 3:4]
+    for step in range(STEPS):
+        rows = slice(step * CX * CY, (step + 1) * CX * CY)
+        picked = jnp.dot(slot_pick[...], tops[rows], preferred_element_type=f32)
+        picked = picked + jnp.dot(slot_pick[...], lows[rows], preferred_element_type=f32)
+        picked = picked * wide[...]
+        table = []
+        for part in beams:
+            for at in range(0, part.shape[0], STEPS * OWN_BEAMS):
+                first = at + step * OWN_BEAMS
+                table.append(part[first : first + OWN_BEAMS])
+        table = two_part_dot(beam_pick[...], jnp.concatenate(table, axis=0))
+        tally = -jnp.where(gate_here, table, 0.0)
         for c in range(NC):
             tally = tally + picked[:, c * 128 : (c + 1) * 128]
         misfit = scaled * jnp.sum(tally, axis=1, keepdims=True)
-        forcing[step * CX * CY : (step + 1) * CX * CY] = two_part_dot(
-            slot_push[...], misfit * wide[...]
-        )
+        forcing[rows] = two_part_dot(slot_push[...], misfit * wide[...])
+
+    buffers = [state_0, state_1]
 
     for c in range(NC):
         clear(state_0, c * FIELD, [0, 1, 2, 3, BLOCKS - 4, BLOCKS - 3, BLOCKS - 2, BLOCKS - 1])
@@ -489,6 +532,7 @@
 def add_x(ny, delta, picks, core, x_a, x_b, *rest):
     out_a, out_b, out_near, out_sums = rest[:4]
     out_others = rest[4:-2]
+    merged = ny == 4
     field, sums = rest[-2:]
     even, _, _ = place_on("gy")
     total = picks.shape[1]
@@ -524,6 +568,8 @@
         sums[pl.ds(c, total, stride=NC)] = tile_sums[:, c * 128 : (c + 1) * 128]
     out_sums[...] = sums[0:rows]
     out_a[Y_COEF:] = sums[rows : 2 * rows]
+    if merged:
+        out_b[Y_COEF:] = sums[3 * rows : 4 * rows]
     for s, other in enumerate(out_others):
         other[...] = sums[(2 + s) * rows : (3 + s) * rows]
 
@@ -540,6 +586,8 @@
             out_delta[c, high] = out_delta[c, high] + north
             out_delta[c, low] = out_delta[c, low] + south
     total = sums[...] + y_a[Y_COEF:]
+    if y_b.shape[0] > Y_COEF:
+        total = total + y_b[Y_COEF:]
     for other in others:
         total = total + other[...]
     out_alpha[...] = alpha[...] + profile_weight * total
@@ -572,37 +620,44 @@
         value.reshape(1, slots)
         for value in (gate_beam, gate_index, gate_column, gate_live, obs_precision)
     ]
-    own_beams = obs_rows.shape[0]
-    beam_count = nx * own_beams
+    own_beams = jnp.transpose(obs_rows, (1, 0, 2)).reshape(STEPS * OWN_BEAMS, 128)
+    beam_count = nx * OWN_BEAMS
     rows = owned * NC
     total = ny * owned
 
-    y_a, y_b, beams = call(
+    y_a, y_b, fine, coefs, control_near, near_tiles, meta, near_beams = call(
         pack_y,
-        [(Y_HALO + rows, 128), (Y_HALO, 128), (own_beams * STEPS, 128)],
-        [fine, eddy, courant, control, tile_map, obs_rows],
-        [
-            pltpu.VMEM(fine.shape, f32),
-            pltpu.VMEM((3, CX * CY, 128), f32),
+        [
+            (Y_HALO + rows, 128),
+            (Y_HALO, 128),
+            fine.shape,
+            (3, CX * CY, 128),
+            control.shape,
+            (CX, 128),
+            (8, slots),
+            own_beams.shape,
+        ],
+        [
+            pltpu.with_memory_space_constraint(value, pltpu.HBM)
+            for value in (fine, eddy, courant, control, tile_map, *gates, own_beams)
+        ],
+        [
             pltpu.VMEM(tile_map.shape, jnp.int32),
-            pltpu.VMEM(obs_rows.shape, f32),
-            pltpu.VMEM(control.shape, f32),
-            pltpu.SemaphoreType.DMA((7,)),
-        ],
-        in_specs=[HBM] * 6,
+            pltpu.VMEM((4, 1, slots), jnp.int32),
+            pltpu.VMEM((1, slots), f32),
+            pltpu.SemaphoreType.DMA((12,)),
+        ],
+        in_specs=[HBM] * 11,
     )
     y_a = swap(y_a, "gy", 1)
-    y_b = pair_b(y_b, "gy")
+    y_b = pair_b(y_b, "gy", "gx")
     others = [swap(control, "gy", xor) for xor in range(2, ny)]
-    xor = 2
-    while xor < nx:
-        beams = jnp.concatenate([beams, swap(beams, "gx", xor)])
-        xor *= 2
-
-    x_a, x_b = call(
+    got_beams = swap(own_beams, "gx", 2)
+
+    x_a, x_b, beams = call(
         lambda *refs: pack_x(ny, *refs),
-        [(X_HALO + beams.shape[0], 128), (X_HALO, 128)],
-        [fine, eddy, courant, control, tile_map, y_a, y_b, beams, *others],
+        [(X_HALO + 2 * own_beams.shape[0], 128), (X_HALO, 128), (2 * own_beams.shape[0], 128)],
+        [fine, coefs, control_near, near_tiles, y_a, y_b, near_beams, got_beams, *others],
         [
             pltpu.VMEM((2 * RIM * PITCH, 128), f32),
             pltpu.VMEM((2 * RIM * PITCH, total), f32),
@@ -611,10 +666,10 @@
         ],
     )
     x_a = swap(x_a, "gx", 1)
-    x_b = pair_b(x_b, "gx")
+    x_b = pair_b(x_b, "gx", "gy")
 
     core, coef, picks, wide, slot_pick, slot_push, beam_pick, columns = call(
-        lambda *refs: prepare(ny, nx, *refs),
+        lambda *refs: prepare(ny, *refs),
         [
             (NC * CORE, 128),
             (5 * CORE, 128),
@@ -625,44 +680,68 @@
             jax.ShapeDtypeStruct((slots, beam_count), bf16),
             (slots, 8),
         ],
-        [fine, eddy, courant, control, tile_map, *gates, weights, y_a, y_b, *others],
+        [fine, coefs, control_near, near_tiles, meta, weights, y_a, y_b, *others],
         [
             pltpu.VMEM((total * NC, 128), f32),
             pltpu.VMEM((128, 128), f32),
-            pltpu.VMEM((8, slots), f32),
         ],
         flops=3000000,
     )
 
+    beams = [beams, x_a[X_HALO:]]
+    xor = 4
+    while xor < nx:
+        beams = beams + [swap(jnp.concatenate(beams), "gx", xor)]
+        xor *= 2
+
+    tops, lows, coef = call(
+        forecast,
+        [
+            jax.ShapeDtypeStruct((STEPS * CX * CY, NC * 128), bf16),
+            jax.ShapeDtypeStruct((STEPS * CX * CY, NC * 128), bf16),
+            (5 * FIELD, 128),
+        ],
+        [core, coef, x_a, x_b],
+        [
+            pltpu.VMEM((NC * FIELD, 128), f32),
+            pltpu.VMEM((NC * FIELD, 128), f32),
+            pltpu.VMEM((3 * FIELD, 128), f32),
+        ],
+        flops=10000000,
+    )
     back_a, back_b, core = call(
         main,
         [(X_COEF, 128), (X_COEF, 128), (NC * CORE, 128)],
-        [core, coef, wide, slot_pick, slot_push, beam_pick, columns, beams, x_a, x_b],
+        [coef, tops, lows, wide, slot_pick, slot_push, beam_pick, columns, *beams],
         [
             pltpu.VMEM((NC * FIELD, 128), f32),
             pltpu.VMEM((NC * FIELD, 128), f32),
-            pltpu.VMEM((5 * FIELD, 128), f32),
-            pltpu.VMEM((3 * FIELD, 128), f32),
             pltpu.VMEM((STEPS * CX * CY, NC * 128), f32),
-            pltpu.VMEM((beam_count * STEPS, 128), f32),
-        ],
-        flops=30000000,
+        ],
+        flops=20000000,
     )
     x_a = swap(back_a, "gx", 1)
-    x_b = pair_b(back_b, "gx")
+    x_b = pair_b(back_b, "gx", "gy")
+    loose = [xor for xor in range(2, ny) if ny != 4 or xor != 3]
     back_a, back_b, near, sums, *back = call(
         lambda *refs: add_x(ny, *refs),
-        [(Y_COEF + rows, 128), (Y_COEF, 128), fine.shape, (rows, 128)] + [(rows, 128)] * (ny - 2),
+        [
+            (Y_COEF + rows, 128),
+            (Y_COEF + (rows if ny == 4 else 0), 128),
+            fine.shape,
+            (rows, 128),
+        ]
+        + [(rows, 128)] * len(loose),
         [fine, picks, core, x_a, x_b],
         [pltpu.VMEM((NC * CORE, 128), f32), pltpu.VMEM((total * NC, 128), f32)],
     )
     y_a = swap(back_a, "gy", 1)
-    y_b = pair_b(back_b, "gy")
-    others = [swap(value, "gy", xor) for xor, value in zip(range(2, ny), back)]
+    y_b = ring_b(back_b, "gy")
+    others = [swap(value, "gy", xor) for xor, value in zip(loose, back)]
     grad_delta, grad_alpha = call(
         add_y,
         [fine.shape, control.shape],
-        [control, near, sums, y_a, y_b, *others],
+        [control_near, near, sums, y_a, y_b, *others],
     )
     return grad_delta.reshape(delta.shape), grad_alpha.reshape(alpha.shape)
 

time: 51.1 us -> 43.5 us (0.85)
  the two profiles are of different devices: /device:TPU:16 before, /device:TPU:0 now
where the time goes in v4:
time: 43.5 us; the launch traced here: 43.3 us
  waiting for transfers between devices  17.6 us (40%)
  starting transfers between devices  14.7 us (34%)
  Pallas kernels  10.3 us (24%)
  between operations  0.72 us (2%)
    ppermute x9, waiting for transfers between devices, swap(): lax.ppermute(block, axis, [(i, i ^ xor) for i in range(lax.axis_size(axis...  17.6 us
    ppermute x9, starting transfers between devices, swap(): lax.ppermute(block, axis, [(i, i ^ xor) for i in range(lax.axis_size(axis...  10.5 us
    pallas_call x7, Pallas kernels, call(): pl.pallas_call(body, out_shape=shapes, in_specs=in_specs or [VMEM] * len(...  10.3 us
    ppermute x3, starting transfers between devices, pair_b(): return lax.ppermute(block, ('gx', 'gy'), pairs)  2.6 us
    ppermute x1, starting transfers between devices, ring_b(): return lax.ppermute(block, axis, pairs)  1.63 us
  transfers between devices with their start and end apart: 13, of which 4 were waited for; matrix products, arithmetic and copies ran while one was open for 0% of the time, Pallas kernels for 7%

profile of v4, /device:TPU:0, one launch (start us, length us, event | category | flops | bytes accessed | tf_op | source)
XLA Modules:
  0.0 43.3 jit_solution(16992725849225927874)
XLA Ops:
  0.6 0.0 copy-start
  0.6 1.4 %shard_map.131 = (f32[320,128]{1,0:T(8,128)S(1)}, f32[304,128]{1,0:T(8,128)S(1)}, f32[4,256,128]{2,1,0:T(8,128)S(1)}, f32[3,256,128]{2,1,0:T(8,128)S(1)}, f32[16...) custom-call(f32[4,256,128]{2,1,0:T(8,128)} %bitcast.16, ...), custom_call_target="tpu_custom_call" | custom-call | flops 1000000 | bytes 944128 | tf_op jit(solution)/shard_map/pallas_call | solution.py:36
  2.1 0.5 %collective-permute-start = (f32[320,128]{1,0:T(8,128)S(1)}, f32[320,128]{1,0:T(8,128)S(1)}, u32[]{:S(2)}, u32[]{:S(2)}) collective-permute-start(f32[320,128]{1,0:T(8,128)S(1)} %get-tuple-element.39), channel_id=1, source_target_pairs={{0,1},{1,0},{2,3},{3,2},{4,5},{5,4},{6,7},{7,6},{8,9},{9,8},{10,11... | collective-permute-start | bytes 491528 | tf_op jit(solution)/shard_map/ppermute | solution.py:48
  2.6 2.6 %collective-permute-start.1 = (f32[304,128]{1,0:T(8,128)S(1)}, f32[304,128]{1,0:T(8,128)S(1)}, u32[]{:S(2)}, u32[]{:S(2)}) collective-permute-start(f32[304,128]{1,0:T(8,128)S(1)} %get-tuple-element.40), channel_id=1, source_target_pairs={{0,4},{1,2},{2,1},{3,7},{4,0},{5,6},{6,5},{7,3},{8,12},{9,10},{10,... | collective-permute-start | bytes 466952 | tf_op jit(solution)/shard_map/ppermute | solution.py:64
  5.2 1.6 %collective-permute-start.4 = (f32[24,128]{1,0:T(8,128)}, f32[24,128]{1,0:T(8,128)S(1)}, u32[]{:S(2)}, u32[]{:S(2)}) collective-permute-start(f32[24,128]{1,0:T(8,128)} %bitcast.20), channel_id=1, source_target_pairs={{0,8},{4,12},{8,0},{12,4},{16,24},{20,28},{24,16},{28,20},{1,9},{5... | collective-permute-start | bytes 36872 | tf_op jit(solution)/shard_map/ppermute | solution.py:48
  6.8 0.5 %collective-permute-start.2 = (f32[16,128]{1,0:T(8,128)}, f32[16,128]{1,0:T(8,128)S(1)}, u32[]{:S(2)}, u32[]{:S(2)}) collective-permute-start(f32[16,128]{1,0:T(8,128)} %bitcast.22), channel_id=1, source_target_pairs={{0,2},{1,3},{2,0},{3,1},{4,6},{5,7},{6,4},{7,5},{8,10},{9,11},{10,... | collective-permute-start | bytes 24584 | tf_op jit(solution)/shard_map/ppermute | solution.py:48
  7.3 0.6 %collective-permute-start.3 = (f32[16,128]{1,0:T(8,128)}, f32[16,128]{1,0:T(8,128)S(1)}, u32[]{:S(2)}, u32[]{:S(2)}) collective-permute-start(f32[16,128]{1,0:T(8,128)} %bitcast.23), channel_id=1, source_target_pairs={{0,3},{1,2},{2,1},{3,0},{4,7},{5,6},{6,5},{7,4},{8,11},{9,10},{10,... | collective-permute-start | bytes 24584 | tf_op jit(solution)/shard_map/ppermute | solution.py:48
  7.9 2.8 %collective-permute-done.2.refs_8_ = f32[16,128]{1,0:T(8,128)S(1)} collective-permute-done((f32[16,128]{1,0:T(8,128)}, f32[16,128]{1,0:T(8,128)S(1)}, u32[]{:S(2)}, u32[]{:S(2)}) %collective-permute-start.2) | collective-permute-done | bytes 8224 | tf_op jit(solution)/shard_map/ppermute | solution.py:48
  10.7 0.0 collective-permute-done.3.refs_9_
  10.7 0.0 collective-permute-done.4.refs_7_
  10.7 0.0 collective-permute-done.1.refs_7_.refs_5_
  10.7 0.0 collective-permute-done.refs_6_.refs_4_
  10.7 0.5 %shard_map.133 = (f32[366,128]{1,0:T(8,128)S(1)}, f32[318,128]{1,0:T(8,128)S(1)}, f32[48,128]{1,0:T(8,128)S(1)}) custom-call(f32[4,256,128]{2,1,0:T(8,128)S(1)} %get-tuple-element.35.refs_0_, f32[3,256,128]{2,1,0:T(8,128)S(1)} %get-tuple-element.36.refs_1_, f32[16,128]{1,0:T(8,128)S(1)} %get-tuple-element.34.refs_2_.alpha, ...), custom_call_target="tpu_custom_call" | custom-call | flops 1000000 | bytes 1294336 | tf_op jit(solution)/shard_map/pallas_call | solution.py:36
  11.2 1.5 %collective-permute-start.5 = (f32[366,128]{1,0:T(8,128)S(1)}, f32[366,128]{1,0:T(8,128)S(1)}, u32[]{:S(2)}, u32[]{:S(2)}) collective-permute-start(f32[366,128]{1,0:T(8,128)S(1)} %get-tuple-element.45), channel_id=1, source_target_pairs={{0,4},{4,0},{8,12},{12,8},{16,20},{20,16},{24,28},{28,24},{1,5},{5... | collective-permute-start | bytes 562184 | tf_op jit(solution)/shard_map/ppermute | solution.py:48
  12.7 0.0 collective-permute-start.6
  12.7 7.2 %collective-permute-done.5.x_a = f32[366,128]{1,0:T(8,128)S(1)} collective-permute-done((f32[366,128]{1,0:T(8,128)S(1)}, f32[366,128]{1,0:T(8,128)S(1)}, u32[]{:S(2)}, u32[]{:S(2)}) %collective-permute-start.5) | collective-permute-done | bytes 187424 | tf_op jit(solution)/shard_map/ppermute | solution.py:48
  19.9 4.6 %collective-permute-start.7 = (f32[96,128]{1,0:T(8,128)S(1)}, f32[96,128]{1,0:T(8,128)S(1)}, u32[]{:S(2)}, u32[]{:S(2)}) collective-permute-start(f32[96,128]{1,0:T(8,128)S(1)} %pad_maximum_fusion), channel_id=1, source_target_pairs={{0,16},{4,20},{8,24},{12,28},{16,0},{20,4},{24,8},{28,12},{1,17},{... | collective-permute-start | bytes 147464 | tf_op jit(solution)/shard_map/ppermute | solution.py:48
  24.6 0.0 copy-done
  24.6 1.0 %shard_map.132 = (f32[1536,128]{1,0:T(8,128)S(1)}, f32[1920,128]{1,0:T(8,128)S(1)}, f32[384,16]{1,0:T(8,128)S(1)}, f32[256,512]{1,0:T(8,128)S(1)}, bf16[256,256]...) custom-call(f32[4,256,128]{2,1,0:T(8,128)S(1)} %get-tuple-element.35.refs_0_, ...), custom_call_target="tpu_custom_call" | custom-call | flops 3000000 | bytes 1802240 | tf_op jit(solution)/shard_map/pallas_call | solution.py:36
  25.6 0.0 collective-permute-done.6.x_b
  25.6 2.0 %shard_map.134 = (bf16[768,512]{1,0:T(8,128)(2,1)S(1)}, bf16[768,512]{1,0:T(8,128)(2,1)S(1)}, f32[2880,128]{1,0:T(8,128)S(1)}) custom-call(f32[1536,128]{1,0:T(8,128)S(1)} %get-tuple-element.42.core, f32[1920,128]{1,0:T(8,128)S(1)} %get-tuple-element.43.coef_core, f32[366,128]{1,0:T(8,128)S(1)} %collective-permute-done.5.x_a, ...), custom_call_target="tpu_custom_call" | custom-call | flops 10000000 | bytes 2119680 | tf_op jit(solution)/shard_map/pallas_call | solution.py:36
  27.6 0.0 collective-permute-done.7.rest_2_
  27.6 4.1 %shard_map.135 = (f32[216,128]{1,0:T(8,128)S(1)}, f32[216,128]{1,0:T(8,128)S(1)}, f32[1536,128]{1,0:T(8,128)S(1)}) custom-call(f32[2880,128]{1,0:T(8,128)S(1)} %get-tuple-element.47.coef, bf16[768,512]{1,0:T(8,128)(2,1)S(1)} %get-tuple-element.48.tops, bf16[768,512]{1,0:T(8,128)(2,1)S(1)} %get-tuple-element.49.lows, f32[256,512]{1,0:T(8,128)S(1)} %get-tuple-element.50.wide, ...), custom_call_target="tpu_custom_call" | custom-call | flops 20000000 | bytes 5840896 | tf_op jit(solution)/shard_map/pallas_call | solution.py:36
  31.6 0.6 %collective-permute-start.8 = (f32[216,128]{1,0:T(8,128)S(1)}, f32[216,128]{1,0:T(8,128)S(1)}, u32[]{:S(2)}, u32[]{:S(2)}) collective-permute-start(f32[216,128]{1,0:T(8,128)S(1)} %get-tuple-element.57), channel_id=1, source_target_pairs={{0,4},{4,0},{8,12},{12,8},{16,20},{20,16},{24,28},{28,24},{1,5},{5... | collective-permute-start | bytes 331784 | tf_op jit(solution)/shard_map/ppermute | solution.py:48
  32.2 0.0 collective-permute-start.9
  32.2 4.2 %collective-permute-done.8.refs_3_ = f32[216,128]{1,0:T(8,128)S(1)} collective-permute-done((f32[216,128]{1,0:T(8,128)S(1)}, f32[216,128]{1,0:T(8,128)S(1)}, u32[]{:S(2)}, u32[]{:S(2)}) %collective-permute-start.8) | collective-permute-done | bytes 110624 | tf_op jit(solution)/shard_map/ppermute | solution.py:48
  36.4 0.0 collective-permute-done.9.refs_4_
  36.4 0.4 shard_map.136
  36.8 0.0 collective-permute-start.10
  36.8 1.6 %collective-permute-start.11 = (f32[208,128]{1,0:T(8,128)S(1)}, f32[208,128]{1,0:T(8,128)S(1)}, u32[]{:S(2)}, u32[]{:S(2)}) collective-permute-start(f32[208,128]{1,0:T(8,128)S(1)} %get-tuple-element.62), channel_id=1, source_target_pairs={{0,3},{1,2},{2,1},{3,0},{4,7},{5,6},{6,5},{7,4},{8,11},{9,10},{10,... | collective-permute-start | bytes 319496 | tf_op jit(solution)/shard_map/ppermute | solution.py:70
  38.5 0.5 %collective-permute-start.12 = (f32[16,128]{1,0:T(8,128)S(1)}, f32[16,128]{1,0:T(8,128)S(1)}, u32[]{:S(2)}, u32[]{:S(2)}) collective-permute-start(f32[16,128]{1,0:T(8,128)S(1)} %get-tuple-element.63), channel_id=1, source_target_pairs={{0,2},{1,3},{2,0},{3,1},{4,6},{5,7},{6,4},{7,5},{8,10},{9,11},{10,... | collective-permute-start | bytes 24584 | tf_op jit(solution)/shard_map/ppermute | solution.py:48
  39.0 3.4 %collective-permute-done.12.rest_0_ = f32[16,128]{1,0:T(8,128)S(1)} collective-permute-done((f32[16,128]{1,0:T(8,128)S(1)}, f32[16,128]{1,0:T(8,128)S(1)}, u32[]{:S(2)}, u32[]{:S(2)}) %collective-permute-start.12) | collective-permute-done | bytes 8224 | tf_op jit(solution)/shard_map/ppermute | solution.py:48
  42.4 0.0 collective-permute-done.10.y_a
  42.4 0.0 collective-permute-done.11.y_b
  42.4 0.9 %shard_map.137 = (f32[4,256,128]{2,1,0:T(8,128)}, f32[16,128]{1,0:T(8,128)}) custom-call(f32[16,128]{1,0:T(8,128)S(1)} %get-tuple-element.34.refs_2_.alpha, f32[4,256,128]{2,1,0:T(8,128)S(1)} %get-tuple-element.59.near, f32[16,128]{1,0:T(8,128)S(1)} %get-tuple-element.60.sums, f32[208,128]{1,0:T(8,128)S(1)} %collective-permute-done.10.y_a, ...), custom_call_target="tpu_custom_call" | custom-call | flops 1000000 | bytes 761856 | tf_op jit(solution)/shard_map/pallas_call | solution.py:36
  (2 shorter events, 0.0 us)
Async XLA Ops:
  0.6 23.9 %copy-start = (f32[1,1,256,4,128]{4,3,2,1,0:T(4,128)S(1)}, f32[1,1,256,4,128]{4,3,2,1,0:T(4,128)}, u32[]{:S(2)}) copy-start(f32[1,1,256,4,128]{4,3,2,1,0:T(4,128)} %param.22) | copy-start | bytes 1572868
  2.1 8.6 %collective-permute-start = (f32[320,128]{1,0:T(8,128)S(1)}, f32[320,128]{1,0:T(8,128)S(1)}, u32[]{:S(2)}, u32[]{:S(2)}) collective-permute-start(f32[320,128]{1,0:T(8,128)S(1)} %get-tuple-element.39), channel_id=1, source_target_pairs={{0,1},{1,0},{2,3},{3,2},{4,5},{5,4},{6,7},{7,6},{8,9},{9,8},{10,11... | collective-permute-start | bytes 491528 | tf_op jit(solution)/shard_map/ppermute | solution.py:48
  2.6 8.1 %collective-permute-start.1 = (f32[304,128]{1,0:T(8,128)S(1)}, f32[304,128]{1,0:T(8,128)S(1)}, u32[]{:S(2)}, u32[]{:S(2)}) collective-permute-start(f32[304,128]{1,0:T(8,128)S(1)} %get-tuple-element.40), channel_id=1, source_target_pairs={{0,4},{1,2},{2,1},{3,7},{4,0},{5,6},{6,5},{7,3},{8,12},{9,10},{10,... | collective-permute-start | bytes 466952 | tf_op jit(solution)/shard_map/ppermute | solution.py:64
  5.2 5.5 %collective-permute-start.4 = (f32[24,128]{1,0:T(8,128)}, f32[24,128]{1,0:T(8,128)S(1)}, u32[]{:S(2)}, u32[]{:S(2)}) collective-permute-start(f32[24,128]{1,0:T(8,128)} %bitcast.20), channel_id=1, source_target_pairs={{0,8},{4,12},{8,0},{12,4},{16,24},{20,28},{24,16},{28,20},{1,9},{5... | collective-permute-start | bytes 36872 | tf_op jit(solution)/shard_map/ppermute | solution.py:48
  6.8 3.9 %collective-permute-start.2 = (f32[16,128]{1,0:T(8,128)}, f32[16,128]{1,0:T(8,128)S(1)}, u32[]{:S(2)}, u32[]{:S(2)}) collective-permute-start(f32[16,128]{1,0:T(8,128)} %bitcast.22), channel_id=1, source_target_pairs={{0,2},{1,3},{2,0},{3,1},{4,6},{5,7},{6,4},{7,5},{8,10},{9,11},{10,... | collective-permute-start | bytes 24584 | tf_op jit(solution)/shard_map/ppermute | solution.py:48
  7.3 3.4 %collective-permute-start.3 = (f32[16,128]{1,0:T(8,128)}, f32[16,128]{1,0:T(8,128)S(1)}, u32[]{:S(2)}, u32[]{:S(2)}) collective-permute-start(f32[16,128]{1,0:T(8,128)} %bitcast.23), channel_id=1, source_target_pairs={{0,3},{1,2},{2,1},{3,0},{4,7},{5,6},{6,5},{7,4},{8,11},{9,10},{10,... | collective-permute-start | bytes 24584 | tf_op jit(solution)/shard_map/ppermute | solution.py:48
  11.2 8.7 %collective-permute-start.5 = (f32[366,128]{1,0:T(8,128)S(1)}, f32[366,128]{1,0:T(8,128)S(1)}, u32[]{:S(2)}, u32[]{:S(2)}) collective-permute-start(f32[366,128]{1,0:T(8,128)S(1)} %get-tuple-element.45), channel_id=1, source_target_pairs={{0,4},{4,0},{8,12},{12,8},{16,20},{20,16},{24,28},{28,24},{1,5},{5... | collective-permute-start | bytes 562184 | tf_op jit(solution)/shard_map/ppermute | solution.py:48
  12.7 12.8 %collective-permute-start.6 = (f32[318,128]{1,0:T(8,128)S(1)}, f32[318,128]{1,0:T(8,128)S(1)}, u32[]{:S(2)}, u32[]{:S(2)}) collective-permute-start(f32[318,128]{1,0:T(8,128)S(1)} %get-tuple-element.46), channel_id=1, source_target_pairs={{0,1},{4,8},{8,4},{12,16},{16,12},{20,24},{24,20},{28,29},{1,0},{5... | collective-permute-start | bytes 488456 | tf_op jit(solution)/shard_map/ppermute | solution.py:64
  19.9 7.6 %collective-permute-start.7 = (f32[96,128]{1,0:T(8,128)S(1)}, f32[96,128]{1,0:T(8,128)S(1)}, u32[]{:S(2)}, u32[]{:S(2)}) collective-permute-start(f32[96,128]{1,0:T(8,128)S(1)} %pad_maximum_fusion), channel_id=1, source_target_pairs={{0,16},{4,20},{8,24},{12,28},{16,0},{20,4},{24,8},{28,12},{1,17},{... | collective-permute-start | bytes 147464 | tf_op jit(solution)/shard_map/ppermute | solution.py:48
  31.6 4.8 %collective-permute-start.8 = (f32[216,128]{1,0:T(8,128)S(1)}, f32[216,128]{1,0:T(8,128)S(1)}, u32[]{:S(2)}, u32[]{:S(2)}) collective-permute-start(f32[216,128]{1,0:T(8,128)S(1)} %get-tuple-element.57), channel_id=1, source_target_pairs={{0,4},{4,0},{8,12},{12,8},{16,20},{20,16},{24,28},{28,24},{1,5},{5... | collective-permute-start | bytes 331784 | tf_op jit(solution)/shard_map/ppermute | solution.py:48
  32.2 4.2 %collective-permute-start.9 = (f32[216,128]{1,0:T(8,128)S(1)}, f32[216,128]{1,0:T(8,128)S(1)}, u32[]{:S(2)}, u32[]{:S(2)}) collective-permute-start(f32[216,128]{1,0:T(8,128)S(1)} %get-tuple-element.58), channel_id=1, source_target_pairs={{0,1},{4,8},{8,4},{12,16},{16,12},{20,24},{24,20},{28,29},{1,0},{5... | collective-permute-start | bytes 331784 | tf_op jit(solution)/shard_map/ppermute | solution.py:64
  36.8 5.5 %collective-permute-start.10 = (f32[208,128]{1,0:T(8,128)S(1)}, f32[208,128]{1,0:T(8,128)S(1)}, u32[]{:S(2)}, u32[]{:S(2)}) collective-permute-start(f32[208,128]{1,0:T(8,128)S(1)} %get-tuple-element.61), channel_id=1, source_target_pairs={{0,1},{1,0},{2,3},{3,2},{4,5},{5,4},{6,7},{7,6},{8,9},{9,8},{10,11... | collective-permute-start | bytes 319496 | tf_op jit(solution)/shard_map/ppermute | solution.py:48
  36.8 5.5 %collective-permute-start.11 = (f32[208,128]{1,0:T(8,128)S(1)}, f32[208,128]{1,0:T(8,128)S(1)}, u32[]{:S(2)}, u32[]{:S(2)}) collective-permute-start(f32[208,128]{1,0:T(8,128)S(1)} %get-tuple-element.62), channel_id=1, source_target_pairs={{0,3},{1,2},{2,1},{3,0},{4,7},{5,6},{6,5},{7,4},{8,11},{9,10},{10,... | collective-permute-start | bytes 319496 | tf_op jit(solution)/shard_map/ppermute | solution.py:70
  38.5 3.9 %collective-permute-start.12 = (f32[16,128]{1,0:T(8,128)S(1)}, f32[16,128]{1,0:T(8,128)S(1)}, u32[]{:S(2)}, u32[]{:S(2)}) collective-permute-start(f32[16,128]{1,0:T(8,128)S(1)} %get-tuple-element.63), channel_id=1, source_target_pairs={{0,2},{1,3},{2,0},{3,1},{4,6},{5,7},{6,4},{7,5},{8,10},{9,11},{10,... | collective-permute-start | bytes 24584 | tf_op jit(solution)/shard_map/ppermute | solution.py:48

commit v5 on v4

v5 whole, which is shorter than its diff:
```python
import jax
import jax.numpy as jnp
from jax import lax
from jax.experimental import pallas as pl
from jax.experimental.pallas import tpu as pltpu
from jax.sharding import PartitionSpec as P

STEPS = 3
RIM = 3
INNER = RIM - 1
NC = 4
CX = 16
CY = 16
BLOCKS = CX + 8
PITCH = CY + 8
FIRST = 4
FIELD = BLOCKS * PITCH
OWN_BEAMS = 8
BEAM_BITS = 3
BEAM_ROWS = STEPS * OWN_BEAMS

BULK_COEF = NC * RIM * CY
BULK = BULK_COEF + 3 * INNER * CY

profile_weight = 0.125
f32 = jnp.float32
bf16 = jnp.bfloat16

VMEM = pl.BlockSpec(memory_space=pltpu.VMEM)
HBM = pl.BlockSpec(memory_space=pltpu.HBM)


def call(body, outs, ins, scratch=(), in_specs=None, flops=1000000, limit=40 * 2**20):
    shapes = [
        out if isinstance(out, jax.ShapeDtypeStruct) else jax.ShapeDtypeStruct(out, f32)
        for out in outs
    ]
    size = sum(4 * value.size for value in ins)
    return pl.pallas_call(
        body,
        out_shape=shapes,
        in_specs=in_specs or [VMEM] * len(ins),
        out_specs=[VMEM] * len(shapes),
        scratch_shapes=list(scratch),
        compiler_params=pltpu.CompilerParams(vmem_limit_bytes=limit),
        cost_estimate=pl.CostEstimate(flops=flops, bytes_accessed=size, transcendentals=0),
    )(*ins)


def swap(block, axis, xor):
    return lax.ppermute(block, axis, [(i, i ^ xor) for i in range(lax.axis_size(axis))])


def pair_b(block, axis, other):
    count, across = lax.axis_size(axis), lax.axis_size(other)

    def place(i, j):
        return i * across + j if axis == "gx" else j * count + i

    pairs = []
    for j in range(across):
        for i in range(count):
            if i in (0, count - 1):
                pairs.append((place(i, j), place(i, j ^ 1)))
            else:
                pairs.append((place(i, j), place(i + 1 if i % 2 else i - 1, j)))
    return lax.ppermute(block, ("gx", "gy"), pairs)


def ring_b(block, axis):
    count = lax.axis_size(axis)
    pairs = [(i, (i + 1 if i % 2 else i - 1) % count) for i in range(count)]
    return lax.ppermute(block, axis, pairs)


def place_on(axis):
    me = lax.axis_index(axis)
    return lax.rem(me, 2) == 0, me > 0, me < lax.axis_size(axis) - 1


def split(value):
    top = value.astype(bf16)
    return top, (value - top.astype(f32)).astype(bf16)


def two_part_dot(left, value):
    top, low = split(value)
    return jnp.dot(left, top, preferred_element_type=f32) + jnp.dot(
        left, low, preferred_element_type=f32
    )


def layers(reach):
    found, at = [], 0
    for away in range(1, reach + 1):
        found.append((away, at, reach - away))
        at += CX + 2 * (reach - away)
    return found, at


WIDE, WIDE_ROWS = layers(RIM)
SLIM, SLIM_ROWS = layers(INNER)
Y_COEF = NC * WIDE_ROWS
Y_TILE = Y_COEF + 3 * SLIM_ROWS
Y_HALO = Y_TILE + BLOCKS

CORNER = sum(extra for _, _, extra in WIDE)
COEF_CORNER = sum(extra for _, _, extra in SLIM)


def small_places(profile_rows):
    corner = profile_rows + RIM
    coef_corner = corner + 2 * NC * CORNER
    return profile_rows, corner, coef_corner, coef_corner + 2 * 3 * COEF_CORNER


def y_sides(got_a, got_b, rows, fill=0.0):
    even, low, high = place_on("gy")
    first, second = got_a[rows], got_b[rows]
    north, south = jnp.where(even, first, second), jnp.where(even, second, first)
    return jnp.where(high, north, fill), jnp.where(low, south, fill)


def x_sides(got_a, got_b, rows, fill=0.0):
    even, low, high = place_on("gx")
    first, second = got_a[rows], got_b[rows]
    west, east = jnp.where(even, second, first), jnp.where(even, first, second)
    return jnp.where(low, west, fill), jnp.where(high, east, fill)


def put_pair(out_a, out_b, even, at, above, below):
    rows = slice(at, at + above.shape[0])
    out_a[rows] = jnp.where(even, above, below)
    out_b[rows] = jnp.where(even, below, above)


def pack_x(
    delta,
    eddy,
    courant,
    alpha,
    tile_map,
    gate_beam,
    gate_index,
    gate_column,
    gate_live,
    precision,
    beam_rows,
    small_a,
    small_b,
    bulk_a,
    bulk_b,
    fine,
    coefs,
    profiles,
    near_tiles,
    meta,
    beams,
    tiles,
    gates,
    values,
    sems,
):
    even, _, _ = place_on("gx")
    moves = [
        pltpu.make_async_copy(source, target, sems.at[i])
        for i, (source, target) in enumerate(
            [
                (delta, fine),
                (eddy, coefs.at[0]),
                (courant.at[0], coefs.at[1]),
                (courant.at[1], coefs.at[2]),
                (tile_map, tiles),
                (alpha, profiles),
                (gate_beam, gates.at[0]),
                (gate_index, gates.at[1]),
                (gate_column, gates.at[2]),
                (gate_live, gates.at[3]),
                (precision, values),
                (beam_rows, beams),
            ]
        )
    ]
    for move in moves:
        move.start()
    for move in moves:
        move.wait()

    tile, corner, coef_corner, beam = small_places(profiles.shape[0])
    near_tiles[...] = jnp.full((CX, 128), -1.0, f32)
    near_tiles[:, 0:CY] = tiles[...].astype(f32)
    small_a[0:tile] = profiles[...]
    small_b[0:tile] = profiles[...]
    numbers = near_tiles[...]
    put_pair(small_a, small_b, even, tile, numbers[CX - RIM :], numbers[:RIM])

    def corners(at, field, reach, side):
        for away in range(1, reach):
            y = CY - away if side == 0 else away - 1
            width = reach - away
            for i in range(width):
                east = field[pl.ds((CX - width + i) * CY + y, 1)]
                west = field[pl.ds(i * CY + y, 1)]
                put_pair(small_a, small_b, even, at, east, west)
                at += 1

    for side in range(2):
        for c in range(NC):
            corners(corner + (side * NC + c) * CORNER, fine.at[c], RIM, side)
        for f in range(3):
            corners(coef_corner + (side * 3 + f) * COEF_CORNER, coefs.at[f], INNER, side)
    small_a[beam:] = beams[...]

    wide, slim = RIM * CY, INNER * CY
    for c in range(NC):
        put_pair(bulk_a, bulk_b, even, c * wide, fine[c, CX * CY - wide :], fine[c, :wide])
    for f in range(3):
        east, west = coefs[f, CX * CY - slim :], coefs[f, :slim]
        put_pair(bulk_a, bulk_b, even, BULK_COEF + f * slim, east, west)

    beam = gates[0]
    block = jnp.bitwise_xor(beam >> BEAM_BITS, lax.axis_index("gx"))
    meta[...] = jnp.zeros(meta.shape, f32)
    meta[0:1] = gates[2].astype(f32)
    meta[1:2] = ((block << BEAM_BITS) | (beam & (OWN_BEAMS - 1))).astype(f32)
    meta[2:3] = gates[1].astype(f32)
    meta[3:4] = gates[3].astype(f32) * values[...]


def pack_y(
    fine,
    coefs,
    control,
    tiles,
    beams,
    got_a,
    got_b,
    out_a,
    out_b,
    profiles,
    near_tiles,
    beam_pair,
):
    even, _, _ = place_on("gy")
    count = control.shape[0]
    tile, corner, coef_corner, beam = small_places(count)

    def sides(at, size, fill=0.0):
        return x_sides(got_a, got_b, slice(at, at + size), fill)

    def edge(at, found, own, north_corner, south_corner):
        for away, start, width in found:
            here = at + start
            if width:
                north_w, north_e = sides(north_corner, width)
                south_w, south_e = sides(south_corner, width)
                put_pair(out_a, out_b, even, here, north_w, south_w)
                put_pair(out_a, out_b, even, here + width + CX, north_e, south_e)
                north_corner += width
                south_corner += width
            north = own[pl.ds(CY - away, CX, stride=CY)]
            south = own[pl.ds(away - 1, CX, stride=CY)]
            put_pair(out_a, out_b, even, here + width, north, south)

    west, east = sides(0, count)
    profiles[0:count] = west
    profiles[count : 2 * count] = control[...]
    profiles[2 * count :] = east
    for c in range(NC):
        north, south = corner + c * CORNER, corner + (NC + c) * CORNER
        edge(c * WIDE_ROWS, WIDE, fine.at[c], north, south)
    for f in range(3):
        north, south = coef_corner + f * COEF_CORNER, coef_corner + (3 + f) * COEF_CORNER
        edge(Y_COEF + f * SLIM_ROWS, SLIM, coefs.at[f], north, south)
    west, east = sides(tile, RIM, -1.0)
    near_tiles[...] = jnp.full(near_tiles.shape, -1.0, f32)
    near_tiles[FIRST - RIM : FIRST] = west
    near_tiles[FIRST : FIRST + CX] = tiles[...]
    near_tiles[FIRST + CX : FIRST + CX + RIM] = east
    out_a[Y_TILE:Y_HALO] = near_tiles[...]
    out_b[Y_TILE:Y_HALO] = near_tiles[...]
    out_a[Y_HALO:] = profiles[...]
    beam_pair[0:BEAM_ROWS] = beams[...]
    beam_pair[BEAM_ROWS:] = got_a[beam:]


def slot_xor(ny, slot):
    half = ny // 2
    return 2 * slot if slot < half else 2 * (slot - half) + 1


def tile_ids(ny, owned):
    me = lax.axis_index("gy")
    group = 3 * owned
    lane = lax.broadcasted_iota(jnp.int32, (1, ny * group), 1)
    found = []
    for strip in range(3):
        ids = jnp.full((1, ny * group), -2, jnp.int32)
        for s in range(ny):
            base = s * group + strip * owned
            here = (lane >= base) & (lane < base + owned)
            ids = jnp.where(
                here, jnp.bitwise_xor(me, slot_xor(ny, s)) * owned + lane - base, ids
            )
        found.append(ids.astype(f32))
    return found


def by_variable(ref, count):
    return jnp.concatenate([ref[pl.ds(c, count, stride=NC)] for c in range(NC)], axis=1)


def combine_coefs(viscous, along_x, along_y):
    half_x, half_y = 0.5 * along_x, 0.5 * along_y
    return (
        1.0 - 4.0 * viscous,
        viscous - half_x,
        viscous + half_x,
        viscous - half_y,
        viscous + half_y,
    )


def prepare(
    ny, parts, fine, coefs, near_tiles, meta, weights, y_a, y_b, profiles, *rest
):
    others = rest[:parts]
    field, coef, picks, wide, slot_pick, slot_push, beam_pick, columns, known, tiles = rest[parts:]
    per_slot = profiles.shape[0]
    total = picks.shape[1]
    owned = total // (3 * ny)
    inner = [FIRST - 2, FIRST - 1, FIRST + CX, FIRST + CX + 1]

    def fill(ref, base, own, y_base, reach, found):
        for b in range(FIRST - reach, FIRST + CX + reach):
            at = base + b * PITCH
            if FIRST <= b < FIRST + CX:
                ref[at : at + CY] = own[(b - FIRST) * CY : (b - FIRST + 1) * CY]
                ref[at + CY : at + PITCH] = jnp.zeros((PITCH - CY, 128), f32)
            else:
                ref[at : at + PITCH] = jnp.zeros((PITCH, 128), f32)
        for away, start, width in found:
            size = CX + 2 * width
            north, south = y_sides(y_a, y_b, pl.ds(y_base + start, size))
            at = base + (FIRST - width) * PITCH
            ref[pl.ds(at + CY - 1 + away, size, stride=PITCH)] = north
            ref[pl.ds(at + PITCH - away, size, stride=PITCH)] = south

    for f in range(3):
        fill(coef, f * FIELD, coefs.at[f], Y_COEF + f * SLIM_ROWS, INNER, SLIM)

    def combine(b, carry):
        at = pl.multiple_of(b * PITCH, 8)
        combined = combine_coefs(*[coef[pl.ds(f * FIELD + at, PITCH)] for f in range(3)])
        for f, value in enumerate(combined):
            coef[pl.ds(f * FIELD + at, PITCH)] = value
        return carry

    lax.fori_loop(FIRST, FIRST + CX, combine, 0)
    for f in range(5):
        for b in [0, 1, BLOCKS - 2, BLOCKS - 1] + (inner if f > 2 else []):
            at = f * FIELD + b * PITCH
            coef[at : at + PITCH] = jnp.zeros((PITCH, 128), f32)

    known[0:per_slot] = profiles[...]
    half = ny // 2 * per_slot
    at = per_slot
    for other in others:
        if at == half:
            known[at : at + per_slot] = y_a[Y_HALO:]
            at += per_slot
        known[at : at + other.shape[0]] = other[...]
        at += other.shape[0]

    spot = lax.broadcasted_iota(jnp.int32, (BLOCKS, 128), 1)
    north, south = y_sides(y_a, y_b, pl.ds(Y_TILE, BLOCKS), -1.0)
    near = jnp.where(
        (spot >= CY) & (spot < CY + RIM),
        pltpu.roll(north, CY, 1),
        jnp.where((spot >= PITCH - RIM) & (spot < PITCH), pltpu.roll(south, PITCH - CY, 1), -1.0),
    )
    tiles[...] = jnp.full(tiles.shape, -1.0, f32)
    tiles[0:BLOCKS] = jnp.where(spot < CY, near_tiles[...], near)
    turned = jnp.transpose(tiles[...])[0:PITCH]
    ids = tile_ids(ny, owned)
    for b in range(BLOCKS):
        strip = 0 if b < FIRST else 1 if b < FIRST + CX else 2
        picks[b * PITCH : (b + 1) * PITCH] = (turned[:, b : b + 1] == ids[strip]).astype(f32)
    control = two_part_dot(picks[...].astype(bf16), by_variable(known, total))
    for c in range(NC):
        fill(field, c * FIELD, fine.at[c], c * WIDE_ROWS, RIM, WIDE)
        rows = slice(c * FIELD + PITCH, (c + 1) * FIELD - PITCH)
        field[rows] += profile_weight * control[PITCH:-PITCH, c * 128 : (c + 1) * 128]

    slots = meta.shape[1]
    for c in range(NC):
        wide[:, c * 128 : (c + 1) * 128] = weights[pl.ds(c, slots, stride=NC)]
    per_beam = beam_pick.shape[1]
    turned = jnp.transpose(meta[...])
    columns[...] = turned
    slot_lane = lax.broadcasted_iota(jnp.int32, (slots, CX * CY), 1).astype(f32)
    slot_pick[...] = (slot_lane == turned[:, 0:1]).astype(f32).astype(bf16)
    column_row = lax.broadcasted_iota(jnp.int32, (CX * CY, slots), 0).astype(f32)
    slot_push[...] = (column_row == meta[0:1]).astype(f32).astype(bf16)
    beam_lane = lax.broadcasted_iota(jnp.int32, (slots, per_beam), 1).astype(f32)
    beam_pick[...] = (beam_lane == turned[:, 1:2]).astype(f32).astype(bf16)


def clear(ref, base, blocks):
    for b in blocks:
        at = base + b * PITCH
        ref[at : at + PITCH] = jnp.zeros((PITCH, 128), f32)


def forecast(field, near_coef, bulk_a, bulk_b, tops, lows, coef, state_0, state_1):
    for c in range(NC):
        rows = slice(c * FIELD + PITCH, (c + 1) * FIELD - PITCH)
        state_0[rows] = field[rows]
        for h in range(RIM):
            west, east = x_sides(bulk_a, bulk_b, pl.ds((c * RIM + h) * CY, CY))
            at = c * FIELD + (FIRST - RIM + h) * PITCH
            state_0[at : at + CY] += west
            at = c * FIELD + (FIRST + CX + h) * PITCH
            state_0[at : at + CY] += east
    coef[...] = near_coef[...]
    for h in range(INNER):
        sides = []
        for f in range(3):
            sides.append(x_sides(bulk_a, bulk_b, pl.ds(BULK_COEF + (f * INNER + h) * CY, CY)))
        for side, b in enumerate((FIRST - INNER + h, FIRST + CX + h)):
            raw = []
            for f in range(3):
                at = f * FIELD + b * PITCH
                coef[at : at + CY] += sides[f][side]
                raw.append(coef[at : at + PITCH])
            for f, value in enumerate(combine_coefs(*raw)):
                at = f * FIELD + b * PITCH
                coef[at : at + PITCH] = value

    def forward(source, target, low, high):
        def body(b, carry):
            at = pl.multiple_of(b * PITCH, 8)
            k = [coef[pl.ds(f * FIELD + at, PITCH)] for f in range(5)]
            for c in range(NC):
                base = c * FIELD + at
                here = source[pl.ds(base, PITCH)]
                target[pl.ds(base, PITCH)] = (
                    k[0] * here
                    + k[1] * source[pl.ds(base + PITCH, PITCH)]
                    + k[2] * source[pl.ds(base - PITCH, PITCH)]
                    + k[3] * pltpu.roll(here, PITCH - 1, 0)
                    + k[4] * pltpu.roll(here, 1, 0)
                )
            return carry

        lax.fori_loop(low, high, body, 0)

    buffers = [state_0, state_1]
    for step in range(STEPS):
        source, target = buffers[step % 2], buffers[(step + 1) % 2]
        forward(source, target, 2 + step, BLOCKS - 2 - step)
        own = jnp.concatenate(
            [
                jnp.concatenate(
                    [
                        target[c * FIELD + b * PITCH : c * FIELD + b * PITCH + CY]
                        for b in range(FIRST, FIRST + CX)
                    ],
                    axis=0,
                )
                for c in range(NC)
            ],
            axis=1,
        )
        rows = slice(step * CX * CY, (step + 1) * CX * CY)
        tops[rows], lows[rows] = split(own)


def main(
    ny,
    parts,
    coef,
    tops,
    lows,
    wide,
    slot_pick,
    slot_push,
    beam_pick,
    columns,
    *rest,
):
    picks, fine, *beams = rest[: 2 + parts]
    out_a, out_b, bulk_a, bulk_b, out_near, out_sums, *out_others = rest[2 + parts : -4]
    state_0, state_1, forcing, sums = rest[-4:]
    even, _, _ = place_on("gy")
    even_x, _, _ = place_on("gx")
    total = picks.shape[1]
    per_slot = total * NC // ny
    slots = columns.shape[0]
    gate_lane = lax.broadcasted_iota(jnp.int32, (slots, 128), 1).astype(f32)
    gate_here = gate_lane == columns[:, 2:3]
    scaled = columns[:, 3:4]
    for step in range(STEPS):
        rows = slice(step * CX * CY, (step + 1) * CX * CY)
        picked = jnp.dot(slot_pick[...], tops[rows], preferred_element_type=f32)
        picked = picked + jnp.dot(slot_pick[...], lows[rows], preferred_element_type=f32)
        picked = picked * wide[...]
        table = []
        for part in beams:
            for at in range(0, part.shape[0], STEPS * OWN_BEAMS):
                first = at + step * OWN_BEAMS
                table.append(part[first : first + OWN_BEAMS])
        table = two_part_dot(beam_pick[...], jnp.concatenate(table, axis=0))
        tally = -jnp.where(gate_here, table, 0.0)
        for c in range(NC):
            tally = tally + picked[:, c * 128 : (c + 1) * 128]
        misfit = scaled * jnp.sum(tally, axis=1, keepdims=True)
        forcing[rows] = two_part_dot(slot_push[...], misfit * wide[...])

    buffers = [state_0, state_1]

    for c in range(NC):
        clear(state_0, c * FIELD, [0, 1, 2, 3, BLOCKS - 4, BLOCKS - 3, BLOCKS - 2, BLOCKS - 1])
        clear(state_1, c * FIELD, [1, 2, BLOCKS - 3, BLOCKS - 2])

    def add_forcing(ref, step):
        for c in range(NC):
            for x in range(CX):
                at = c * FIELD + (FIRST + x) * PITCH
                first = step * CX * CY + x * CY
                value = forcing[first : first + CY, c * 128 : (c + 1) * 128]
                if step == STEPS - 1:
                    ref[at : at + CY] = value
                    ref[at + CY : at + PITCH] = jnp.zeros((PITCH - CY, 128), f32)
                else:
                    ref[at : at + CY] += value

    def backward(source, target, low, high):
        def body(b, carry):
            at = pl.multiple_of(b * PITCH, 8)
            k = [
                coef[pl.ds(at, PITCH)],
                coef[pl.ds(FIELD + at - PITCH, PITCH)],
                coef[pl.ds(2 * FIELD + at + PITCH, PITCH)],
                coef[pl.ds(3 * FIELD + at, PITCH)],
                coef[pl.ds(4 * FIELD + at, PITCH)],
            ]
            for c in range(NC):
                base = c * FIELD + at
                here = source[pl.ds(base, PITCH)]
                target[pl.ds(base, PITCH)] = (
                    k[0] * here
                    + k[1] * source[pl.ds(base - PITCH, PITCH)]
                    + k[2] * source[pl.ds(base + PITCH, PITCH)]
                    + pltpu.roll(k[3] * here, 1, 0)
                    + pltpu.roll(k[4] * here, PITCH - 1, 0)
                )
            return carry

        lax.fori_loop(low, high, body, 0)

    for step in range(STEPS):
        source, target = buffers[step % 2], buffers[(step + 1) % 2]
        add_forcing(source, STEPS - 1 - step)
        backward(source, target, FIRST - 1 - step, FIRST + CX + 1 + step)
    final = buffers[STEPS % 2]

    for c in range(NC):
        for h in range(RIM):
            at = c * FIELD + (FIRST - RIM + h) * PITCH
            west = final[at : at + CY]
            at = c * FIELD + (FIRST + CX + h) * PITCH
            put_pair(bulk_a, bulk_b, even_x, (c * RIM + h) * CY, final[at : at + CY], west)
        for away, start, width in WIDE:
            at = c * FIELD + (FIRST - width) * PITCH
            size = CX + 2 * width
            north = final[pl.ds(at + CY - 1 + away, size, stride=PITCH)]
            south = final[pl.ds(at + PITCH - away, size, stride=PITCH)]
            put_pair(out_a, out_b, even, c * WIDE_ROWS + start, north, south)
        for x in range(CX):
            at = c * FIELD + (FIRST + x) * PITCH
            rows = slice(x * CY, (x + 1) * CY)
            out_near[c, rows] = fine[c, rows] + final[at : at + CY]

    for c in range(NC):
        clear(final, c * FIELD, [0, BLOCKS - 1])
    adjoint = jnp.concatenate([final[c * FIELD : (c + 1) * FIELD] for c in range(NC)], axis=1)
    tile_sums = two_part_dot(jnp.transpose(picks[...]).astype(bf16), adjoint)
    for c in range(NC):
        sums[pl.ds(c, total, stride=NC)] = tile_sums[:, c * 128 : (c + 1) * 128]
    out_sums[...] = sums[0:per_slot]
    outs = dict(zip(loose_slots(ny), out_others))
    for s in range(1, ny):
        rows = slice(s * per_slot, (s + 1) * per_slot)
        if s in outs:
            outs[s][...] = sums[rows]
        elif slot_xor(ny, s) == 1:
            out_a[Y_COEF:] = sums[rows]
        else:
            out_b[Y_COEF:] = sums[rows]


def loose_slots(ny):
    ridden = (0, 1, 3) if ny == 4 else (0, 1)
    return [s for s in range(ny) if slot_xor(ny, s) not in ridden]


def pack_home(sums, got_a, got_b, *rest):
    others = rest[:-3]
    out_a, out_b, out_sum = rest[-3:]
    owned = sums.shape[0] // 3
    even, _, _ = place_on("gx")
    total = sums[...] + got_a[Y_COEF:]
    if got_b.shape[0] > Y_COEF:
        total = total + got_b[Y_COEF:]
    for other in others:
        total = total + other[...]
    put_pair(out_a, out_b, even, 0, total[2 * owned :], total[0:owned])
    out_sum[...] = total[owned : 2 * owned]
    at = owned
    for c in range(NC):
        for away, start, width in WIDE:
            if width:
                first = c * WIDE_ROWS + start
                west = y_sides(got_a, got_b, pl.ds(first, width))
                east = y_sides(got_a, got_b, pl.ds(first + width + CX, width))
                for side in range(2):
                    put_pair(out_a, out_b, even, at, east[side], west[side])
                    at += width


def finish(alpha, near, own_sum, y_a, y_b, bulk_a, bulk_b, small_a, small_b, out_delta, out_alpha):
    owned = own_sum.shape[0]
    wide = RIM * CY
    out_delta[...] = near[...]
    at = owned
    for c in range(NC):
        west, east = x_sides(bulk_a, bulk_b, pl.ds(c * wide, wide))
        out_delta[c, 0:wide] += west
        out_delta[c, CX * CY - wide :] += east
        for away, start, width in WIDE:
            north, south = y_sides(y_a, y_b, pl.ds(c * WIDE_ROWS + start + width, CX))
            high = pl.ds(CY - away, CX, stride=CY)
            low = pl.ds(away - 1, CX, stride=CY)
            out_delta[c, high] = out_delta[c, high] + north
            out_delta[c, low] = out_delta[c, low] + south
            for y in (CY - away, away - 1):
                for i in range(width):
                    west, east = x_sides(small_a, small_b, slice(at + i, at + i + 1))
                    out_delta[c, pl.ds(i * CY + y, 1)] += west
                    out_delta[c, pl.ds((CX - width + i) * CY + y, 1)] += east
                at += width
    west, east = x_sides(small_a, small_b, slice(0, owned))
    out_alpha[...] = alpha[...] + profile_weight * (own_sum[...] + west + east)


def on_device(
    delta,
    alpha,
    eddy,
    courant,
    tile_map,
    obs_rows,
    gate_beam,
    gate_index,
    gate_column,
    gate_live,
    obs_weight,
    obs_precision,
):
    nx = lax.axis_size("gx")
    ny = lax.axis_size("gy")
    owned = alpha.shape[1]
    slots = gate_column.shape[2]
    gates = [
        value.reshape(1, slots)
        for value in (gate_beam, gate_index, gate_column, gate_live, obs_precision)
    ]
    control = alpha.reshape(owned * NC, 128)
    weights = obs_weight.reshape(slots * NC, 128)
    rows = owned * NC
    per_slot = 3 * rows
    total = 3 * ny * owned
    beam_at = small_places(rows)[-1]
    tile = (NC, CX * CY, 128)

    small_a, small_b, bulk_a, bulk_b, fine, coefs, control, tiles, meta, beams = call(
        pack_x,
        [
            (beam_at + BEAM_ROWS, 128),
            (beam_at, 128),
            (BULK, 128),
            (BULK, 128),
            tile,
            (3, CX * CY, 128),
            (rows, 128),
            (CX, 128),
            (8, slots),
            (BEAM_ROWS, 128),
        ],
        [
            pltpu.with_memory_space_constraint(value, pltpu.HBM)
            for value in (
                delta.reshape(tile),
                eddy.reshape(CX * CY, 128),
                courant.reshape(2, CX * CY, 128),
                control,
                tile_map,
                *gates,
                jnp.transpose(obs_rows, (1, 0, 2)).reshape(BEAM_ROWS, 128),
            )
        ],
        [
            pltpu.VMEM(tile_map.shape, jnp.int32),
            pltpu.VMEM((4, 1, slots), jnp.int32),
            pltpu.VMEM((1, slots), f32),
            pltpu.SemaphoreType.DMA((12,)),
        ],
        in_specs=[HBM] * 11,
    )
    small_a = swap(small_a, "gx", 1)
    small_b = pair_b(small_b, "gx", "gy")
    bulk_a = swap(bulk_a, "gx", 1)
    bulk_b = pair_b(bulk_b, "gx", "gy")

    y_a, y_b, profiles, near_tiles, beams = call(
        pack_y,
        [
            (Y_HALO + per_slot, 128),
            (Y_HALO, 128),
            (per_slot, 128),
            (BLOCKS, 128),
            (2 * BEAM_ROWS, 128),
        ],
        [fine, coefs, control, tiles, beams, small_a, small_b],
    )
    others, xor = [], 2
    while xor < ny:
        held = jnp.concatenate([profiles] + others) if others else profiles
        others.append(swap(held, "gy", xor))
        xor *= 2
    y_a = swap(y_a, "gy", 1)
    y_b = pair_b(y_b, "gy", "gx")
    others.append(swap(jnp.concatenate(others) if len(others) > 1 else others[0], "gy", 1))
    beams = [beams]
    xor = 2
    while xor < nx:
        held = jnp.concatenate(beams) if len(beams) > 1 else beams[0]
        beams.append(swap(held, "gx", xor))
        xor *= 2

    field, coef, picks, wide, slot_pick, slot_push, beam_pick, columns = call(
        lambda *refs: prepare(ny, len(others), *refs),
        [
            (NC * FIELD, 128),
            (5 * FIELD, 128),
            (FIELD, total),
            (slots, NC * 128),
            jax.ShapeDtypeStruct((slots, CX * CY), bf16),
            jax.ShapeDtypeStruct((CX * CY, slots), bf16),
            jax.ShapeDtypeStruct((slots, nx * OWN_BEAMS), bf16),
            (slots, 8),
        ],
        [fine, coefs, near_tiles, meta, weights, y_a, y_b, profiles, *others],
        [pltpu.VMEM((total * NC, 128), f32), pltpu.VMEM((128, 128), f32)],
        flops=3000000,
    )
    tops, lows, coef = call(
        forecast,
        [
            jax.ShapeDtypeStruct((STEPS * CX * CY, NC * 128), bf16),
            jax.ShapeDtypeStruct((STEPS * CX * CY, NC * 128), bf16),
            (5 * FIELD, 128),
        ],
        [field, coef, bulk_a, bulk_b],
        [pltpu.VMEM((NC * FIELD, 128), f32), pltpu.VMEM((NC * FIELD, 128), f32)],
        flops=10000000,
    )
    loose = loose_slots(ny)
    back_a, back_b, bulk_a, bulk_b, near, sums, *back = call(
        lambda *refs: main(ny, len(beams), *refs),
        [
            (Y_COEF + per_slot, 128),
            (Y_COEF + (per_slot if ny == 4 else 0), 128),
            (BULK_COEF, 128),
            (BULK_COEF, 128),
            tile,
            (per_slot, 128),
        ]
        + [(per_slot, 128)] * len(loose),
        [
            coef,
            tops,
            lows,
            wide,
            slot_pick,
            slot_push,
            beam_pick,
            columns,
            picks,
            fine,
            *beams,
        ],
        [
            pltpu.VMEM((NC * FIELD, 128), f32),
            pltpu.VMEM((NC * FIELD, 128), f32),
            pltpu.VMEM((STEPS * CX * CY, NC * 128), f32),
            pltpu.VMEM((total * NC, 128), f32),
        ],
        flops=20000000,
    )
    y_a = swap(back_a, "gy", 1)
    y_b = ring_b(back_b, "gy")
    others = [swap(value, "gy", slot_xor(ny, s)) for s, value in zip(loose, back)]
    bulk_a = swap(bulk_a, "gx", 1)
    bulk_b = pair_b(bulk_b, "gx", "gy")
    home_rows = rows + 2 * NC * CORNER
    small_a, small_b, own_sum = call(
        pack_home,
        [(home_rows, 128), (home_rows, 128), (rows, 128)],
        [sums, y_a, y_b, *others],
    )
    small_a = swap(small_a, "gx", 1)
    small_b = pair_b(small_b, "gx", "gy")
    grad_delta, grad_alpha = call(
        finish,
        [tile, (rows, 128)],
        [control, near, own_sum, y_a, y_b, bulk_a, bulk_b, small_a, small_b],
    )
    return grad_delta.reshape(delta.shape), grad_alpha.reshape(alpha.shape)


def solution(mesh):
    return jax.shard_map(
        on_device,
        mesh=mesh,
        in_specs=(
            P(None, "gx", "gy", None),
            P("gx", "gy", None, None),
            P("gx", "gy", None),
            P(None, "gx", "gy", None),
            P("gx", "gy"),
            P(("gx", "gy"), None, None),
            P("gx", "gy", None),
            P("gx", "gy", None),
            P("gx", "gy", None),
            P("gx", "gy", None),
            P("gx", "gy", None, None, None),
            P("gx", "gy", None),
        ),
        out_specs=(P(None, "gx", "gy", None), P("gx", "gy", None, None)),
        check_vma=False,
    )
```

time: 43.5 us -> 43.5 us (level)
  the two profiles are of different devices: /device:TPU:0 before, /device:TPU:10 now
where the time goes in v5:
time: 43.5 us; the launch traced here: 43.4 us
  waiting for transfers between devices  17.3 us (40%)
  starting transfers between devices  15.3 us (35%)
  Pallas kernels  10 us (23%)
  between operations  0.73 us (2%)
    pallas_call x7, Pallas kernels, call(): pl.pallas_call(body, out_shape=shapes, in_specs=in_specs or [VMEM] * len(...  10 us
    ppermute x11, waiting for transfers between devices, swap(): lax.ppermute(block, axis, [(i, i ^ xor) for i in range(lax.axis_size(axis...  9.98 us
    ppermute x11, starting transfers between devices, swap(): lax.ppermute(block, axis, [(i, i ^ xor) for i in range(lax.axis_size(axis...  9.25 us
    ppermute x5, waiting for transfers between devices, pair_b(): return lax.ppermute(block, ('gx', 'gy'), pairs)  7.3 us
    ppermute x5, starting transfers between devices, pair_b(): return lax.ppermute(block, ('gx', 'gy'), pairs)  3.99 us
    ppermute x1, starting transfers between devices, ring_b(): return lax.ppermute(block, axis, pairs)  2.09 us
  transfers between devices with their start and end apart: 17, of which 7 were waited for; matrix products, arithmetic and copies ran while one was open for 0% of the time, Pallas kernels for 7%

profile of v5, /device:TPU:10, one launch (start us, length us, event | category | flops | bytes accessed | tf_op | source)
XLA Modules:
  0.0 43.4 jit_solution(645076827295961918)
XLA Ops:
  0.6 0.0 copy-start
  0.6 1.4 %shard_map.131 = (f32[73,128]{1,0:T(8,128)S(1)}, f32[49,128]{1,0:T(8,128)S(1)}, f32[288,128]{1,0:T(8,128)S(1)}, f32[288,128]{1,0:T(8,128)S(1)}, f32[4,256,128]{2...) custom-call(f32[4,256,128]{2,1,0:T(8,128)} %bitcast.16, ...), custom_call_target="tpu_custom_call" | custom-call | flops 1000000 | bytes 944128 | tf_op jit(solution)/shard_map/pallas_call | solution.py:39
  2.0 1.6 %collective-permute-start = (f32[73,128]{1,0:T(8,128)S(1)}, f32[73,128]{1,0:T(8,128)S(1)}, u32[]{:S(2)}, u32[]{:S(2)}) collective-permute-start(f32[73,128]{1,0:T(8,128)S(1)} %get-tuple-element.45), channel_id=1, source_target_pairs={{0,4},{4,0},{8,12},{12,8},{16,20},{20,16},{24,28},{28,24},{1,5},{5... | collective-permute-start | bytes 112136 | tf_op jit(solution)/shard_map/ppermute | solution.py:51
  3.6 0.4 collective-permute-start.1
  4.0 4.4 %collective-permute-done.1.got_b = f32[49,128]{1,0:T(8,128)S(1)} collective-permute-done((f32[49,128]{1,0:T(8,128)S(1)}, f32[49,128]{1,0:T(8,128)S(1)}, u32[]{:S(2)}, u32[]{:S(2)}) %collective-permute-start.1) | collective-permute-done | bytes 25120 | tf_op jit(solution)/shard_map/ppermute | solution.py:67
  8.4 0.0 collective-permute-done.got_a
  8.4 0.1 shard_map.132
  8.5 0.1 collective-permute-start.2
  8.6 0.6 %collective-permute-start.4 = (f32[48,128]{1,0:T(8,128)S(1)}, f32[48,128]{1,0:T(8,128)S(1)}, u32[]{:S(2)}, u32[]{:S(2)}) collective-permute-start(f32[48,128]{1,0:T(8,128)S(1)} %get-tuple-element.51.refs_7_), channel_id=1, source_target_pairs={{0,2},{1,3},{2,0},{3,1},{4,6},{5,7},{6,4},{7,5},{8,10},{9,11},{10,... | collective-permute-start | bytes 73736 | tf_op jit(solution)/shard_map/ppermute | solution.py:51
  9.2 0.0 collective-permute-start.8
  9.2 1.3 %collective-permute-start.3 = (f32[342,128]{1,0:T(8,128)S(1)}, f32[342,128]{1,0:T(8,128)S(1)}, u32[]{:S(2)}, u32[]{:S(2)}) collective-permute-start(f32[342,128]{1,0:T(8,128)S(1)} %get-tuple-element.50), channel_id=1, source_target_pairs={{0,4},{1,2},{2,1},{3,7},{4,0},{5,6},{6,5},{7,3},{8,12},{9,10},{10,... | collective-permute-start | bytes 525320 | tf_op jit(solution)/shard_map/ppermute | solution.py:67
  10.5 0.7 %collective-permute-start.6 = (f32[288,128]{1,0:T(8,128)S(1)}, f32[288,128]{1,0:T(8,128)S(1)}, u32[]{:S(2)}, u32[]{:S(2)}) collective-permute-start(f32[288,128]{1,0:T(8,128)S(1)} %get-tuple-element.54), channel_id=1, source_target_pairs={{0,4},{4,0},{8,12},{12,8},{16,20},{20,16},{24,28},{28,24},{1,5},{5... | collective-permute-start | bytes 442376 | tf_op jit(solution)/shard_map/ppermute | solution.py:51
  11.1 1.6 %collective-permute-done.4.refs_8_ = f32[48,128]{1,0:T(8,128)S(1)} collective-permute-done((f32[48,128]{1,0:T(8,128)S(1)}, f32[48,128]{1,0:T(8,128)S(1)}, u32[]{:S(2)}, u32[]{:S(2)}) %collective-permute-start.4) | collective-permute-done | bytes 24608 | tf_op jit(solution)/shard_map/ppermute | solution.py:51
  12.7 0.9 %collective-permute-start.7 = (f32[288,128]{1,0:T(8,128)S(1)}, f32[288,128]{1,0:T(8,128)S(1)}, u32[]{:S(2)}, u32[]{:S(2)}) collective-permute-start(f32[288,128]{1,0:T(8,128)S(1)} %get-tuple-element.55), channel_id=1, source_target_pairs={{0,1},{4,8},{8,4},{12,16},{16,12},{20,24},{24,20},{28,29},{1,0},{5... | collective-permute-start | bytes 442376 | tf_op jit(solution)/shard_map/ppermute | solution.py:67
  13.7 0.0 collective-permute-done.8.refs_11_
  13.7 0.0 collective-permute-start.5
  13.7 1.2 %collective-permute-done.5.refs_9_ = f32[48,128]{1,0:T(8,128)S(1)} collective-permute-done((f32[48,128]{1,0:T(8,128)S(1)}, f32[48,128]{1,0:T(8,128)S(1)}, u32[]{:S(2)}, u32[]{:S(2)}) %collective-permute-start.5) | collective-permute-done | bytes 24608 | tf_op jit(solution)/shard_map/ppermute | solution.py:51
  14.9 2.6 %collective-permute-start.9 = (f32[96,128]{1,0:T(8,128)S(1)}, f32[96,128]{1,0:T(8,128)S(1)}, u32[]{:S(2)}, u32[]{:S(2)}) collective-permute-start(f32[96,128]{1,0:T(8,128)S(1)} %pad_maximum_fusion), channel_id=1, source_target_pairs={{0,16},{4,20},{8,24},{12,28},{16,0},{20,4},{24,8},{28,12},{1,17},{... | collective-permute-start | bytes 147464 | tf_op jit(solution)/shard_map/ppermute | solution.py:51
  17.5 0.0 collective-permute-done.3.refs_6_
  17.5 0.0 collective-permute-done.2.refs_5_
  17.5 0.0 copy-done
  17.5 1.0 %shard_map.133 = (f32[2304,128]{1,0:T(8,128)S(1)}, f32[2880,128]{1,0:T(8,128)S(1)}, f32[576,48]{1,0:T(8,128)S(1)}, f32[256,512]{1,0:T(8,128)S(1)}, bf16[256,256]...) custom-call(f32[4,256,128]{2,1,0:T(8,128)S(1)} %get-tuple-element.41.fine.re, ...), custom_call_target="tpu_custom_call" | custom-call | flops 3000000 | bytes 1910784 | tf_op jit(solution)/shard_map/pallas_call | solution.py:39
  18.5 1.7 %collective-permute-done.6.bulk_a = f32[288,128]{1,0:T(8,128)S(1)} collective-permute-done((f32[288,128]{1,0:T(8,128)S(1)}, f32[288,128]{1,0:T(8,128)S(1)}, u32[]{:S(2)}, u32[]{:S(2)}) %collective-permute-start.6) | collective-permute-done | bytes 147488 | tf_op jit(solution)/shard_map/ppermute | solution.py:51
  20.2 0.0 collective-permute-done.7.bulk_b
  20.2 1.9 %shard_map.134 = (bf16[768,512]{1,0:T(8,128)(2,1)S(1)}, bf16[768,512]{1,0:T(8,128)(2,1)S(1)}, f32[2880,128]{1,0:T(8,128)S(1)}) custom-call(f32[2304,128]{1,0:T(8,128)S(1)} %get-tuple-element.52.field, f32[2880,128]{1,0:T(8,128)S(1)} %get-tuple-element.53.near_coef, f32[288,128]{1,0:T(8,128)S(1)} %collective-permute-done.6.bulk_a, ...), custom_call_target="tpu_custom_call" | custom-call | flops 10000000 | bytes 2949120 | tf_op jit(solution)/shard_map/pallas_call | solution.py:39
  22.1 0.0 collective-permute-done.9.refs_12_
  22.1 4.5 %shard_map.135 = (f32[264,128]{1,0:T(8,128)S(1)}, f32[264,128]{1,0:T(8,128)S(1)}, f32[192,128]{1,0:T(8,128)S(1)}, f32[192,128]{1,0:T(8,128)S(1)}, f32[4,256,128]...) custom-call(f32[2880,128]{1,0:T(8,128)S(1)} %get-tuple-element.56.refs_0_, ...), custom_call_target="tpu_custom_call" | custom-call | flops 20000000 | bytes 6475776 | tf_op jit(solution)/shard_map/pallas_call | solution.py:39
  26.7 0.1 collective-permute-start.10
  26.7 2.1 %collective-permute-start.11 = (f32[264,128]{1,0:T(8,128)S(1)}, f32[264,128]{1,0:T(8,128)S(1)}, u32[]{:S(2)}, u32[]{:S(2)}) collective-permute-start(f32[264,128]{1,0:T(8,128)S(1)} %get-tuple-element.69), channel_id=1, source_target_pairs={{0,3},{1,2},{2,1},{3,0},{4,7},{5,6},{6,5},{7,4},{8,11},{9,10},{10,... | collective-permute-start | bytes 405512 | tf_op jit(solution)/shard_map/ppermute | solution.py:73
  28.8 0.6 %collective-permute-start.13 = (f32[192,128]{1,0:T(8,128)S(1)}, f32[192,128]{1,0:T(8,128)S(1)}, u32[]{:S(2)}, u32[]{:S(2)}) collective-permute-start(f32[192,128]{1,0:T(8,128)S(1)} %get-tuple-element.72), channel_id=1, source_target_pairs={{0,4},{4,0},{8,12},{12,8},{16,20},{20,16},{24,28},{28,24},{1,5},{5... | collective-permute-start | bytes 294920 | tf_op jit(solution)/shard_map/ppermute | solution.py:51
  29.4 1.4 %collective-permute-start.14 = (f32[192,128]{1,0:T(8,128)S(1)}, f32[192,128]{1,0:T(8,128)S(1)}, u32[]{:S(2)}, u32[]{:S(2)}) collective-permute-start(f32[192,128]{1,0:T(8,128)S(1)} %get-tuple-element.73), channel_id=1, source_target_pairs={{0,1},{4,8},{8,4},{12,16},{16,12},{20,24},{24,20},{28,29},{1,0},{5... | collective-permute-start | bytes 294920 | tf_op jit(solution)/shard_map/ppermute | solution.py:67
  30.8 0.1 collective-permute-start.12
  30.9 3.7 %collective-permute-done.12.rest_0_ = f32[48,128]{1,0:T(8,128)S(1)} collective-permute-done((f32[48,128]{1,0:T(8,128)S(1)}, f32[48,128]{1,0:T(8,128)S(1)}, u32[]{:S(2)}, u32[]{:S(2)}) %collective-permute-start.12) | collective-permute-done | bytes 24608 | tf_op jit(solution)/shard_map/ppermute | solution.py:51
  34.6 0.0 collective-permute-done.10.got_a.y_a
  34.6 0.0 collective-permute-done.11.got_b.y_b
  34.7 3.0 %collective-permute-start.15 = (f32[40,128]{1,0:T(8,128)S(1)}, f32[40,128]{1,0:T(8,128)S(1)}, u32[]{:S(2)}, u32[]{:S(2)}) collective-permute-start(f32[40,128]{1,0:T(8,128)S(1)} %get-tuple-element.74), channel_id=1, source_target_pairs={{0,4},{4,0},{8,12},{12,8},{16,20},{20,16},{24,28},{28,24},{1,5},{5... | collective-permute-start | bytes 61448 | tf_op jit(solution)/shard_map/ppermute | solution.py:51
  37.7 0.0 collective-permute-start.16
  37.7 0.0 collective-permute-done.13.bulk_a
  37.7 0.0 collective-permute-done.14.bulk_b
  37.7 1.8 %collective-permute-done.15.small_a = f32[40,128]{1,0:T(8,128)S(1)} collective-permute-done((f32[40,128]{1,0:T(8,128)S(1)}, f32[40,128]{1,0:T(8,128)S(1)}, u32[]{:S(2)}, u32[]{:S(2)}) %collective-permute-start.15) | collective-permute-done | bytes 20512 | tf_op jit(solution)/shard_map/ppermute | solution.py:51
  39.4 2.9 %collective-permute-done.16.small_b = f32[40,128]{1,0:T(8,128)S(1)} collective-permute-done((f32[40,128]{1,0:T(8,128)S(1)}, f32[40,128]{1,0:T(8,128)S(1)}, u32[]{:S(2)}, u32[]{:S(2)}) %collective-permute-start.16) | collective-permute-done | bytes 20512 | tf_op jit(solution)/shard_map/ppermute | solution.py:67
  42.3 1.0 %shard_map.137 = (f32[4,256,128]{2,1,0:T(8,128)}, f32[16,128]{1,0:T(8,128)}) custom-call(f32[16,128]{1,0:T(8,128)S(1)} %get-tuple-element.40.control.alpha, f32[4,256,128]{2,1,0:T(8,128)S(1)} %get-tuple-element.66.near, f32[16,128]{1,0:T(8,128)S(1)} %get-tuple-element.71.own_sum, f32[264,128]{1,0:T(8,128)S(1)} %collective-permute-done.10.got_a.y_a, ...), custom_call_target="tpu_custom_call" | custom-call | flops 1000000 | bytes 1048576 | tf_op jit(solution)/shard_map/pallas_call | solution.py:39
  (2 shorter events, 0.0 us)
Async XLA Ops:
  0.6 16.8 %copy-start = (f32[1,1,256,4,128]{4,3,2,1,0:T(4,128)S(1)}, f32[1,1,256,4,128]{4,3,2,1,0:T(4,128)}, u32[]{:S(2)}) copy-start(f32[1,1,256,4,128]{4,3,2,1,0:T(4,128)} %param.22) | copy-start | bytes 1572868
  2.0 6.4 %collective-permute-start = (f32[73,128]{1,0:T(8,128)S(1)}, f32[73,128]{1,0:T(8,128)S(1)}, u32[]{:S(2)}, u32[]{:S(2)}) collective-permute-start(f32[73,128]{1,0:T(8,128)S(1)} %get-tuple-element.45), channel_id=1, source_target_pairs={{0,4},{4,0},{8,12},{12,8},{16,20},{20,16},{24,28},{28,24},{1,5},{5... | collective-permute-start | bytes 112136 | tf_op jit(solution)/shard_map/ppermute | solution.py:51
  3.6 4.8 %collective-permute-start.1 = (f32[49,128]{1,0:T(8,128)S(1)}, f32[49,128]{1,0:T(8,128)S(1)}, u32[]{:S(2)}, u32[]{:S(2)}) collective-permute-start(f32[49,128]{1,0:T(8,128)S(1)} %get-tuple-element.46), channel_id=1, source_target_pairs={{0,1},{4,8},{8,4},{12,16},{16,12},{20,24},{24,20},{28,29},{1,0},{5... | collective-permute-start | bytes 75272 | tf_op jit(solution)/shard_map/ppermute | solution.py:67
  8.5 8.9 %collective-permute-start.2 = (f32[390,128]{1,0:T(8,128)S(1)}, f32[390,128]{1,0:T(8,128)S(1)}, u32[]{:S(2)}, u32[]{:S(2)}) collective-permute-start(f32[390,128]{1,0:T(8,128)S(1)} %get-tuple-element.49), channel_id=1, source_target_pairs={{0,1},{1,0},{2,3},{3,2},{4,5},{5,4},{6,7},{7,6},{8,9},{9,8},{10,11... | collective-permute-start | bytes 599048 | tf_op jit(solution)/shard_map/ppermute | solution.py:51
  8.6 4.2 %collective-permute-start.4 = (f32[48,128]{1,0:T(8,128)S(1)}, f32[48,128]{1,0:T(8,128)S(1)}, u32[]{:S(2)}, u32[]{:S(2)}) collective-permute-start(f32[48,128]{1,0:T(8,128)S(1)} %get-tuple-element.51.refs_7_), channel_id=1, source_target_pairs={{0,2},{1,3},{2,0},{3,1},{4,6},{5,7},{6,4},{7,5},{8,10},{9,11},{10,... | collective-permute-start | bytes 73736 | tf_op jit(solution)/shard_map/ppermute | solution.py:51
  9.2 4.5 %collective-permute-start.8 = (f32[48,128]{1,0:T(8,128)S(1)}, f32[48,128]{1,0:T(8,128)S(1)}, u32[]{:S(2)}, u32[]{:S(2)}) collective-permute-start(f32[48,128]{1,0:T(8,128)S(1)} %get-tuple-element.65.refs_10_), channel_id=1, source_target_pairs={{0,8},{4,12},{8,0},{12,4},{16,24},{20,28},{24,16},{28,20},{1,9},{5... | collective-permute-start | bytes 73736 | tf_op jit(solution)/shard_map/ppermute | solution.py:51
  9.2 8.3 %collective-permute-start.3 = (f32[342,128]{1,0:T(8,128)S(1)}, f32[342,128]{1,0:T(8,128)S(1)}, u32[]{:S(2)}, u32[]{:S(2)}) collective-permute-start(f32[342,128]{1,0:T(8,128)S(1)} %get-tuple-element.50), channel_id=1, source_target_pairs={{0,4},{1,2},{2,1},{3,7},{4,0},{5,6},{6,5},{7,3},{8,12},{9,10},{10,... | collective-permute-start | bytes 525320 | tf_op jit(solution)/shard_map/ppermute | solution.py:67
  10.5 9.7 %collective-permute-start.6 = (f32[288,128]{1,0:T(8,128)S(1)}, f32[288,128]{1,0:T(8,128)S(1)}, u32[]{:S(2)}, u32[]{:S(2)}) collective-permute-start(f32[288,128]{1,0:T(8,128)S(1)} %get-tuple-element.54), channel_id=1, source_target_pairs={{0,4},{4,0},{8,12},{12,8},{16,20},{20,16},{24,28},{28,24},{1,5},{5... | collective-permute-start | bytes 442376 | tf_op jit(solution)/shard_map/ppermute | solution.py:51
  12.7 7.4 %collective-permute-start.7 = (f32[288,128]{1,0:T(8,128)S(1)}, f32[288,128]{1,0:T(8,128)S(1)}, u32[]{:S(2)}, u32[]{:S(2)}) collective-permute-start(f32[288,128]{1,0:T(8,128)S(1)} %get-tuple-element.55), channel_id=1, source_target_pairs={{0,1},{4,8},{8,4},{12,16},{16,12},{20,24},{24,20},{28,29},{1,0},{5... | collective-permute-start | bytes 442376 | tf_op jit(solution)/shard_map/ppermute | solution.py:67
  13.7 1.2 %collective-permute-start.5 = (f32[48,128]{1,0:T(8,128)S(1)}, f32[48,128]{1,0:T(8,128)S(1)}, u32[]{:S(2)}, u32[]{:S(2)}) collective-permute-start(f32[48,128]{1,0:T(8,128)S(1)} %collective-permute-done.4.refs_8_), channel_id=1, source_target_pairs={{0,1},{1,0},{2,3},{3,2},{4,5},{5,4},{6,7},{7,6},{8,9},{9,8},{10,11... | collective-permute-start | bytes 73736 | tf_op jit(solution)/shard_map/ppermute | solution.py:51
  14.9 7.3 %collective-permute-start.9 = (f32[96,128]{1,0:T(8,128)S(1)}, f32[96,128]{1,0:T(8,128)S(1)}, u32[]{:S(2)}, u32[]{:S(2)}) collective-permute-start(f32[96,128]{1,0:T(8,128)S(1)} %pad_maximum_fusion), channel_id=1, source_target_pairs={{0,16},{4,20},{8,24},{12,28},{16,0},{20,4},{24,8},{28,12},{1,17},{... | collective-permute-start | bytes 147464 | tf_op jit(solution)/shard_map/ppermute | solution.py:51
  26.7 8.0 %collective-permute-start.10 = (f32[264,128]{1,0:T(8,128)S(1)}, f32[264,128]{1,0:T(8,128)S(1)}, u32[]{:S(2)}, u32[]{:S(2)}) collective-permute-start(f32[264,128]{1,0:T(8,128)S(1)} %get-tuple-element.68), channel_id=1, source_target_pairs={{0,1},{1,0},{2,3},{3,2},{4,5},{5,4},{6,7},{7,6},{8,9},{9,8},{10,11... | collective-permute-start | bytes 405512 | tf_op jit(solution)/shard_map/ppermute | solution.py:51
  26.7 7.9 %collective-permute-start.11 = (f32[264,128]{1,0:T(8,128)S(1)}, f32[264,128]{1,0:T(8,128)S(1)}, u32[]{:S(2)}, u32[]{:S(2)}) collective-permute-start(f32[264,128]{1,0:T(8,128)S(1)} %get-tuple-element.69), channel_id=1, source_target_pairs={{0,3},{1,2},{2,1},{3,0},{4,7},{5,6},{6,5},{7,4},{8,11},{9,10},{10,... | collective-permute-start | bytes 405512 | tf_op jit(solution)/shard_map/ppermute | solution.py:73
  28.8 8.8 %collective-permute-start.13 = (f32[192,128]{1,0:T(8,128)S(1)}, f32[192,128]{1,0:T(8,128)S(1)}, u32[]{:S(2)}, u32[]{:S(2)}) collective-permute-start(f32[192,128]{1,0:T(8,128)S(1)} %get-tuple-element.72), channel_id=1, source_target_pairs={{0,4},{4,0},{8,12},{12,8},{16,20},{20,16},{24,28},{28,24},{1,5},{5... | collective-permute-start | bytes 294920 | tf_op jit(solution)/shard_map/ppermute | solution.py:51
  29.4 8.3 %collective-permute-start.14 = (f32[192,128]{1,0:T(8,128)S(1)}, f32[192,128]{1,0:T(8,128)S(1)}, u32[]{:S(2)}, u32[]{:S(2)}) collective-permute-start(f32[192,128]{1,0:T(8,128)S(1)} %get-tuple-element.73), channel_id=1, source_target_pairs={{0,1},{4,8},{8,4},{12,16},{16,12},{20,24},{24,20},{28,29},{1,0},{5... | collective-permute-start | bytes 294920 | tf_op jit(solution)/shard_map/ppermute | solution.py:67
  30.8 3.8 %collective-permute-start.12 = (f32[48,128]{1,0:T(8,128)S(1)}, f32[48,128]{1,0:T(8,128)S(1)}, u32[]{:S(2)}, u32[]{:S(2)}) collective-permute-start(f32[48,128]{1,0:T(8,128)S(1)} %get-tuple-element.70), channel_id=1, source_target_pairs={{0,2},{1,3},{2,0},{3,1},{4,6},{5,7},{6,4},{7,5},{8,10},{9,11},{10,... | collective-permute-start | bytes 73736 | tf_op jit(solution)/shard_map/ppermute | solution.py:51
  34.7 4.8 %collective-permute-start.15 = (f32[40,128]{1,0:T(8,128)S(1)}, f32[40,128]{1,0:T(8,128)S(1)}, u32[]{:S(2)}, u32[]{:S(2)}) collective-permute-start(f32[40,128]{1,0:T(8,128)S(1)} %get-tuple-element.74), channel_id=1, source_target_pairs={{0,4},{4,0},{8,12},{12,8},{16,20},{20,16},{24,28},{28,24},{1,5},{5... | collective-permute-start | bytes 61448 | tf_op jit(solution)/shard_map/ppermute | solution.py:51
  37.7 4.7 %collective-permute-start.16 = (f32[40,128]{1,0:T(8,128)S(1)}, f32[40,128]{1,0:T(8,128)S(1)}, u32[]{:S(2)}, u32[]{:S(2)}) collective-permute-start(f32[40,128]{1,0:T(8,128)S(1)} %get-tuple-element.75), channel_id=1, source_target_pairs={{0,1},{4,8},{8,4},{12,16},{16,12},{20,24},{24,20},{28,29},{1,0},{5... | collective-permute-start | bytes 61448 | tf_op jit(solution)/shard_map/ppermute | solution.py:67

commit v6 on v5

--- a/solution.py
+++ b/solution.py
@@ -99,19 +99,27 @@
 
 
 WIDE, WIDE_ROWS = layers(RIM)
-SLIM, SLIM_ROWS = layers(INNER)
-Y_COEF = NC * WIDE_ROWS
-Y_TILE = Y_COEF + 3 * SLIM_ROWS
-Y_HALO = Y_TILE + BLOCKS
-
+BACK = NC * WIDE_ROWS
 CORNER = sum(extra for _, _, extra in WIDE)
-COEF_CORNER = sum(extra for _, _, extra in SLIM)
+
+Y_COEF = NC * RIM * CX
+Y_TILE = Y_COEF + 3 * INNER * CX
+Y_HALO = Y_TILE + CX
+
+
+def corners(reach):
+    return [
+        (dx, side, dy)
+        for dx in range(1, reach)
+        for side in range(2)
+        for dy in range(1, reach - dx + 1)
+    ]
 
 
 def small_places(profile_rows):
     corner = profile_rows + RIM
-    coef_corner = corner + 2 * NC * CORNER
-    return profile_rows, corner, coef_corner, coef_corner + 2 * 3 * COEF_CORNER
+    coef_corner = corner + NC * len(corners(RIM))
+    return profile_rows, corner, coef_corner, coef_corner + 3 * len(corners(INNER))
 
 
 def y_sides(got_a, got_b, rows, fill=0.0):
@@ -134,7 +142,7 @@
     out_b[rows] = jnp.where(even, below, above)
 
 
-def pack_x(
+def pack_first(
     delta,
     eddy,
     courant,
@@ -146,8 +154,8 @@
     gate_live,
     precision,
     beam_rows,
-    small_a,
-    small_b,
+    y_a,
+    y_b,
     bulk_a,
     bulk_b,
     fine,
@@ -161,7 +169,8 @@
     values,
     sems,
 ):
-    even, _, _ = place_on("gx")
+    even_x, _, _ = place_on("gx")
+    even, _, _ = place_on("gy")
     moves = [
         pltpu.make_async_copy(source, target, sems.at[i])
         for i, (source, target) in enumerate(
@@ -186,40 +195,34 @@
     for move in moves:
         move.wait()
 
-    tile, corner, coef_corner, beam = small_places(profiles.shape[0])
     near_tiles[...] = jnp.full((CX, 128), -1.0, f32)
     near_tiles[:, 0:CY] = tiles[...].astype(f32)
-    small_a[0:tile] = profiles[...]
-    small_b[0:tile] = profiles[...]
-    numbers = near_tiles[...]
-    put_pair(small_a, small_b, even, tile, numbers[CX - RIM :], numbers[:RIM])
-
-    def corners(at, field, reach, side):
-        for away in range(1, reach):
-            y = CY - away if side == 0 else away - 1
-            width = reach - away
-            for i in range(width):
-                east = field[pl.ds((CX - width + i) * CY + y, 1)]
-                west = field[pl.ds(i * CY + y, 1)]
-                put_pair(small_a, small_b, even, at, east, west)
-                at += 1
-
-    for side in range(2):
-        for c in range(NC):
-            corners(corner + (side * NC + c) * CORNER, fine.at[c], RIM, side)
-        for f in range(3):
-            corners(coef_corner + (side * 3 + f) * COEF_CORNER, coefs.at[f], INNER, side)
-    small_a[beam:] = beams[...]
+
+    def edges(at, field, reach):
+        for away in range(1, reach + 1):
+            north = field[pl.ds(CY - away, CX, stride=CY)]
+            south = field[pl.ds(away - 1, CX, stride=CY)]
+            put_pair(y_a, y_b, even, at + (away - 1) * CX, north, south)
+
+    for c in range(NC):
+        edges(c * RIM * CX, fine.at[c], RIM)
+    for f in range(3):
+        edges(Y_COEF + f * INNER * CX, coefs.at[f], INNER)
+    y_a[Y_TILE:Y_HALO] = near_tiles[...]
+    y_b[Y_TILE:Y_HALO] = near_tiles[...]
+    y_a[Y_HALO:] = profiles[...]
 
     wide, slim = RIM * CY, INNER * CY
     for c in range(NC):
-        put_pair(bulk_a, bulk_b, even, c * wide, fine[c, CX * CY - wide :], fine[c, :wide])
+        put_pair(bulk_a, bulk_b, even_x, c * wide, fine[c, CX * CY - wide :], fine[c, :wide])
     for f in range(3):
         east, west = coefs[f, CX * CY - slim :], coefs[f, :slim]
-        put_pair(bulk_a, bulk_b, even, BULK_COEF + f * slim, east, west)
+        put_pair(bulk_a, bulk_b, even_x, BULK_COEF + f * slim, east, west)
 
     beam = gates[0]
-    block = jnp.bitwise_xor(beam >> BEAM_BITS, lax.axis_index("gx"))
+    owner = jnp.bitwise_xor(beam >> BEAM_BITS, lax.axis_index("gx"))
+    half = lax.axis_size("gx") // 2
+    block = (owner >> 1) + (owner & 1) * half
     meta[...] = jnp.zeros(meta.shape, f32)
     meta[0:1] = gates[2].astype(f32)
     meta[1:2] = ((block << BEAM_BITS) | (beam & (OWN_BEAMS - 1))).astype(f32)
@@ -227,61 +230,50 @@
     meta[3:4] = gates[3].astype(f32) * values[...]
 
 
-def pack_y(
-    fine,
-    coefs,
-    control,
-    tiles,
-    beams,
-    got_a,
-    got_b,
-    out_a,
-    out_b,
-    profiles,
-    near_tiles,
-    beam_pair,
-):
-    even, _, _ = place_on("gy")
-    count = control.shape[0]
-    tile, corner, coef_corner, beam = small_places(count)
-
-    def sides(at, size, fill=0.0):
-        return x_sides(got_a, got_b, slice(at, at + size), fill)
-
-    def edge(at, found, own, north_corner, south_corner):
-        for away, start, width in found:
-            here = at + start
-            if width:
-                north_w, north_e = sides(north_corner, width)
-                south_w, south_e = sides(south_corner, width)
-                put_pair(out_a, out_b, even, here, north_w, south_w)
-                put_pair(out_a, out_b, even, here + width + CX, north_e, south_e)
-                north_corner += width
-                south_corner += width
-            north = own[pl.ds(CY - away, CX, stride=CY)]
-            south = own[pl.ds(away - 1, CX, stride=CY)]
-            put_pair(out_a, out_b, even, here + width, north, south)
-
-    west, east = sides(0, count)
-    profiles[0:count] = west
-    profiles[count : 2 * count] = control[...]
-    profiles[2 * count :] = east
-    for c in range(NC):
-        north, south = corner + c * CORNER, corner + (NC + c) * CORNER
-        edge(c * WIDE_ROWS, WIDE, fine.at[c], north, south)
+def tile_numbers(near_tiles, y_a, y_b):
+    spot = lax.broadcasted_iota(jnp.int32, (CX, 128), 1)
+    north, south = y_sides(y_a, y_b, pl.ds(Y_TILE, CX), -1.0)
+    near = jnp.where(
+        (spot >= CY) & (spot < CY + RIM),
+        pltpu.roll(north, CY, 1),
+        jnp.where((spot >= PITCH - RIM) & (spot < PITCH), pltpu.roll(south, PITCH - CY, 1), -1.0),
+    )
+    return jnp.where(spot < CY, near_tiles[...], near)
+
+
+def strip_profiles(ny, control, y_a, others):
+    return [control[...]] + [o[...] for o in others[:-1]] + [y_a[Y_HALO:], others[-1][...]]
+
+
+def pack_small(ny, control, near_tiles, y_a, y_b, beams, *rest):
+    others = rest[:-3]
+    out_a, out_b, numbers = rest[-3:]
+    even, _, _ = place_on("gx")
+    rows = ny * control.shape[0]
+    tile, corner, coef_corner, beam = small_places(rows)
+    at = 0
+    for piece in strip_profiles(ny, control, y_a, others):
+        out_a[at : at + piece.shape[0]] = piece
+        out_b[at : at + piece.shape[0]] = piece
+        at += piece.shape[0]
+    numbers[...] = tile_numbers(near_tiles, y_a, y_b)
+    put_pair(out_a, out_b, even, tile, numbers[CX - RIM :], numbers[:RIM])
+
+    def put_corners(at, base, reach):
+        for dx, side, dy in corners(reach):
+            first = base + (dy - 1) * CX
+            east = y_sides(y_a, y_b, pl.ds(first + CX - dx, 1))[side]
+            west = y_sides(y_a, y_b, pl.ds(first + dx - 1, 1))[side]
+            put_pair(out_a, out_b, even, at, east, west)
+            at += 1
+        return at
+
+    at = corner
+    for c in range(NC):
+        at = put_corners(at, c * RIM * CX, RIM)
     for f in range(3):
-        north, south = coef_corner + f * COEF_CORNER, coef_corner + (3 + f) * COEF_CORNER
-        edge(Y_COEF + f * SLIM_ROWS, SLIM, coefs.at[f], north, south)
-    west, east = sides(tile, RIM, -1.0)
-    near_tiles[...] = jnp.full(near_tiles.shape, -1.0, f32)
-    near_tiles[FIRST - RIM : FIRST] = west
-    near_tiles[FIRST : FIRST + CX] = tiles[...]
-    near_tiles[FIRST + CX : FIRST + CX + RIM] = east
-    out_a[Y_TILE:Y_HALO] = near_tiles[...]
-    out_b[Y_TILE:Y_HALO] = near_tiles[...]
-    out_a[Y_HALO:] = profiles[...]
-    beam_pair[0:BEAM_ROWS] = beams[...]
-    beam_pair[BEAM_ROWS:] = got_a[beam:]
+        at = put_corners(at, Y_COEF + f * INNER * CX, INNER)
+    out_a[beam:] = beams[...]
 
 
 def slot_xor(ny, slot):
@@ -321,33 +313,70 @@
     )
 
 
+def clear(ref, base, blocks):
+    for b in blocks:
+        at = base + b * PITCH
+        ref[at : at + PITCH] = jnp.zeros((PITCH, 128), f32)
+
+
+def add_profiles(known, picks, pieces_by_strip, place):
+    known[...] = jnp.zeros(known.shape, f32)
+    for strip, pieces, rows in pieces_by_strip:
+        slot = 0
+        for piece in pieces:
+            for first in range(0, piece.shape[0], rows):
+                at = (slot * 3 + strip) * rows
+                known[at : at + rows] = piece[first : first + rows]
+                slot += 1
+    control = two_part_dot(picks[...].astype(bf16), by_variable(known, picks.shape[1]))
+    for c in range(NC):
+        place(c, profile_weight * control[:, c * 128 : (c + 1) * 128])
+
+
 def prepare(
-    ny, parts, fine, coefs, near_tiles, meta, weights, y_a, y_b, profiles, *rest
+    ny,
+    parts,
+    fine,
+    coefs,
+    near_tiles,
+    meta,
+    weights,
+    y_a,
+    y_b,
+    bulk_a,
+    bulk_b,
+    control,
+    *rest,
 ):
     others = rest[:parts]
     field, coef, picks, wide, slot_pick, slot_push, beam_pick, columns, known, tiles = rest[parts:]
-    per_slot = profiles.shape[0]
     total = picks.shape[1]
-    owned = total // (3 * ny)
-    inner = [FIRST - 2, FIRST - 1, FIRST + CX, FIRST + CX + 1]
-
-    def fill(ref, base, own, y_base, reach, found):
-        for b in range(FIRST - reach, FIRST + CX + reach):
-            at = base + b * PITCH
-            if FIRST <= b < FIRST + CX:
-                ref[at : at + CY] = own[(b - FIRST) * CY : (b - FIRST + 1) * CY]
-                ref[at + CY : at + PITCH] = jnp.zeros((PITCH - CY, 128), f32)
-            else:
-                ref[at : at + PITCH] = jnp.zeros((PITCH, 128), f32)
-        for away, start, width in found:
-            size = CX + 2 * width
-            north, south = y_sides(y_a, y_b, pl.ds(y_base + start, size))
-            at = base + (FIRST - width) * PITCH
-            ref[pl.ds(at + CY - 1 + away, size, stride=PITCH)] = north
-            ref[pl.ds(at + PITCH - away, size, stride=PITCH)] = south
+    rows = control.shape[0]
+    owned = rows // NC
+
+    def fill(ref, base, own, y_base, reach, bulk_base):
+        for x in range(CX):
+            at = base + (FIRST + x) * PITCH
+            ref[at : at + CY] = own[x * CY : (x + 1) * CY]
+            ref[at + CY : at + PITCH] = jnp.zeros((PITCH - CY, 128), f32)
+        for away in range(1, reach + 1):
+            north, south = y_sides(y_a, y_b, pl.ds(y_base + (away - 1) * CX, CX))
+            at = base + FIRST * PITCH
+            ref[pl.ds(at + CY - 1 + away, CX, stride=PITCH)] = north
+            ref[pl.ds(at + PITCH - away, CX, stride=PITCH)] = south
+        clear(ref, base, [*range(FIRST), *range(FIRST + CX, BLOCKS)])
+        for h in range(reach):
+            west, east = x_sides(bulk_a, bulk_b, pl.ds(bulk_base + h * CY, CY))
+            at = base + (FIRST - reach + h) * PITCH
+            ref[at : at + CY] = west
+            at = base + (FIRST + CX + h) * PITCH
+            ref[at : at + CY] = east
 
     for f in range(3):
-        fill(coef, f * FIELD, coefs.at[f], Y_COEF + f * SLIM_ROWS, INNER, SLIM)
+        bulk_base = BULK_COEF + f * INNER * CY
+        fill(coef, f * FIELD, coefs.at[f], Y_COEF + f * INNER * CX, INNER, bulk_base)
+    for f in range(3, 5):
+        clear(coef, f * FIELD, [*range(FIRST), *range(FIRST + CX, BLOCKS)])
 
     def combine(b, carry):
         at = pl.multiple_of(b * PITCH, 8)
@@ -357,40 +386,21 @@
         return carry
 
     lax.fori_loop(FIRST, FIRST + CX, combine, 0)
-    for f in range(5):
-        for b in [0, 1, BLOCKS - 2, BLOCKS - 1] + (inner if f > 2 else []):
-            at = f * FIELD + b * PITCH
-            coef[at : at + PITCH] = jnp.zeros((PITCH, 128), f32)
-
-    known[0:per_slot] = profiles[...]
-    half = ny // 2 * per_slot
-    at = per_slot
-    for other in others:
-        if at == half:
-            known[at : at + per_slot] = y_a[Y_HALO:]
-            at += per_slot
-        known[at : at + other.shape[0]] = other[...]
-        at += other.shape[0]
-
-    spot = lax.broadcasted_iota(jnp.int32, (BLOCKS, 128), 1)
-    north, south = y_sides(y_a, y_b, pl.ds(Y_TILE, BLOCKS), -1.0)
-    near = jnp.where(
-        (spot >= CY) & (spot < CY + RIM),
-        pltpu.roll(north, CY, 1),
-        jnp.where((spot >= PITCH - RIM) & (spot < PITCH), pltpu.roll(south, PITCH - CY, 1), -1.0),
-    )
+
     tiles[...] = jnp.full(tiles.shape, -1.0, f32)
-    tiles[0:BLOCKS] = jnp.where(spot < CY, near_tiles[...], near)
+    tiles[0:CX] = tile_numbers(near_tiles, y_a, y_b)
     turned = jnp.transpose(tiles[...])[0:PITCH]
     ids = tile_ids(ny, owned)
-    for b in range(BLOCKS):
-        strip = 0 if b < FIRST else 1 if b < FIRST + CX else 2
-        picks[b * PITCH : (b + 1) * PITCH] = (turned[:, b : b + 1] == ids[strip]).astype(f32)
-    control = two_part_dot(picks[...].astype(bf16), by_variable(known, total))
-    for c in range(NC):
-        fill(field, c * FIELD, fine.at[c], c * WIDE_ROWS, RIM, WIDE)
-        rows = slice(c * FIELD + PITCH, (c + 1) * FIELD - PITCH)
-        field[rows] += profile_weight * control[PITCH:-PITCH, c * 128 : (c + 1) * 128]
+    for x in range(CX):
+        picks[x * PITCH : (x + 1) * PITCH] = (turned[:, x : x + 1] == ids[1]).astype(f32)
+    for c in range(NC):
+        fill(field, c * FIELD, fine.at[c], c * RIM * CX, RIM, c * RIM * CY)
+
+    def place(c, value):
+        at = c * FIELD + FIRST * PITCH
+        field[at : at + CX * PITCH] += value
+
+    add_profiles(known, picks, [(1, strip_profiles(ny, control, y_a, others), rows)], place)
 
     slots = meta.shape[1]
     for c in range(NC):
@@ -406,36 +416,66 @@
     beam_pick[...] = (beam_lane == turned[:, 1:2]).astype(f32).astype(bf16)
 
 
-def clear(ref, base, blocks):
-    for b in blocks:
-        at = base + b * PITCH
-        ref[at : at + PITCH] = jnp.zeros((PITCH, 128), f32)
-
-
-def forecast(field, near_coef, bulk_a, bulk_b, tops, lows, coef, state_0, state_1):
-    for c in range(NC):
-        rows = slice(c * FIELD + PITCH, (c + 1) * FIELD - PITCH)
-        state_0[rows] = field[rows]
-        for h in range(RIM):
-            west, east = x_sides(bulk_a, bulk_b, pl.ds((c * RIM + h) * CY, CY))
-            at = c * FIELD + (FIRST - RIM + h) * PITCH
-            state_0[at : at + CY] += west
-            at = c * FIELD + (FIRST + CX + h) * PITCH
-            state_0[at : at + CY] += east
+def forecast(
+    ny,
+    rows,
+    field,
+    near_coef,
+    small_a,
+    small_b,
+    tops,
+    lows,
+    coef,
+    picks,
+    state_0,
+    state_1,
+    known,
+    tiles,
+):
+    strip_rows = ny * rows
+    tile, corner, coef_corner, _ = small_places(strip_rows)
+
+    def put_corners(ref, base, reach, small_base):
+        for i, (dx, side, dy) in enumerate(corners(reach)):
+            west, east = x_sides(small_a, small_b, pl.ds(small_base + i, 1))
+            row = CY - 1 + dy if side == 0 else PITCH - dy
+            at = base + (FIRST - dx) * PITCH + row
+            ref[at : at + 1] = west
+            at = base + (FIRST + CX - 1 + dx) * PITCH + row
+            ref[at : at + 1] = east
+
+    for c in range(NC):
+        part = slice(c * FIELD + PITCH, (c + 1) * FIELD - PITCH)
+        state_0[part] = field[part]
+        base = c * len(corners(RIM))
+        put_corners(state_0, c * FIELD, RIM, corner + base)
     coef[...] = near_coef[...]
-    for h in range(INNER):
-        sides = []
-        for f in range(3):
-            sides.append(x_sides(bulk_a, bulk_b, pl.ds(BULK_COEF + (f * INNER + h) * CY, CY)))
-        for side, b in enumerate((FIRST - INNER + h, FIRST + CX + h)):
-            raw = []
-            for f in range(3):
-                at = f * FIELD + b * PITCH
-                coef[at : at + CY] += sides[f][side]
-                raw.append(coef[at : at + PITCH])
-            for f, value in enumerate(combine_coefs(*raw)):
-                at = f * FIELD + b * PITCH
-                coef[at : at + PITCH] = value
+    for f in range(3):
+        base = f * len(corners(INNER))
+        put_corners(coef, f * FIELD, INNER, coef_corner + base)
+    for b in (FIRST - 2, FIRST - 1, FIRST + CX, FIRST + CX + 1):
+        at = [slice(f * FIELD + b * PITCH, f * FIELD + (b + 1) * PITCH) for f in range(5)]
+        for f, value in enumerate(combine_coefs(*[coef[at[f]] for f in range(3)])):
+            coef[at[f]] = value
+
+    west, east = x_sides(small_a, small_b, slice(tile, tile + RIM), -1.0)
+    tiles[...] = jnp.full(tiles.shape, -1.0, f32)
+    tiles[0:RIM] = west
+    tiles[RIM : 2 * RIM] = east
+    turned = jnp.transpose(tiles[...])[0:PITCH]
+    ids = tile_ids(ny, rows // NC)
+    for i in range(2 * RIM):
+        here = turned[:, i : i + 1] == ids[0 if i < RIM else 2]
+        picks[i * PITCH : (i + 1) * PITCH] = here.astype(f32)
+
+    def place(c, value):
+        at = c * FIELD + (FIRST - RIM) * PITCH
+        state_0[at : at + RIM * PITCH] += value[: RIM * PITCH]
+        at = c * FIELD + (FIRST + CX) * PITCH
+        state_0[at : at + RIM * PITCH] += value[RIM * PITCH :]
+
+    west, east = x_sides(small_a, small_b, slice(0, strip_rows))
+    add_profiles(known, picks, [(0, [west], rows), (2, [east], rows)], place)
 
     def forward(source, target, low, high):
         def body(b, carry):
@@ -489,11 +529,11 @@
     columns,
     *rest,
 ):
-    picks, fine, *beams = rest[: 2 + parts]
-    out_a, out_b, bulk_a, bulk_b, out_near, out_sums, *out_others = rest[2 + parts : -4]
-    state_0, state_1, forcing, sums = rest[-4:]
+    picks, rim_picks, *beams = rest[: 2 + parts]
+    out_a, out_b, final, out_sums, *out_others = rest[2 + parts : -3]
+    state_0, forcing, sums = rest[-3:]
+    state_1 = final
     even, _, _ = place_on("gy")
-    even_x, _, _ = place_on("gx")
     total = picks.shape[1]
     per_slot = total * NC // ny
     slots = columns.shape[0]
@@ -563,29 +603,27 @@
         source, target = buffers[step % 2], buffers[(step + 1) % 2]
         add_forcing(source, STEPS - 1 - step)
         backward(source, target, FIRST - 1 - step, FIRST + CX + 1 + step)
-    final = buffers[STEPS % 2]
-
-    for c in range(NC):
-        for h in range(RIM):
-            at = c * FIELD + (FIRST - RIM + h) * PITCH
-            west = final[at : at + CY]
-            at = c * FIELD + (FIRST + CX + h) * PITCH
-            put_pair(bulk_a, bulk_b, even_x, (c * RIM + h) * CY, final[at : at + CY], west)
+    for c in range(NC):
         for away, start, width in WIDE:
             at = c * FIELD + (FIRST - width) * PITCH
             size = CX + 2 * width
             north = final[pl.ds(at + CY - 1 + away, size, stride=PITCH)]
             south = final[pl.ds(at + PITCH - away, size, stride=PITCH)]
             put_pair(out_a, out_b, even, c * WIDE_ROWS + start, north, south)
-        for x in range(CX):
-            at = c * FIELD + (FIRST + x) * PITCH
-            rows = slice(x * CY, (x + 1) * CY)
-            out_near[c, rows] = fine[c, rows] + final[at : at + CY]
-
-    for c in range(NC):
-        clear(final, c * FIELD, [0, BLOCKS - 1])
-    adjoint = jnp.concatenate([final[c * FIELD : (c + 1) * FIELD] for c in range(NC)], axis=1)
-    tile_sums = two_part_dot(jnp.transpose(picks[...]).astype(bf16), adjoint)
+
+    def blocks(low, high):
+        return jnp.concatenate(
+            [final[c * FIELD + low * PITCH : c * FIELD + high * PITCH] for c in range(NC)], axis=1
+        )
+
+    def across(one_hot):
+        return jnp.transpose(one_hot[...]).astype(bf16)
+
+    rim = jnp.concatenate(
+        [blocks(FIRST - RIM, FIRST), blocks(FIRST + CX, FIRST + CX + RIM)], axis=0
+    )
+    tile_sums = two_part_dot(across(picks), blocks(FIRST, FIRST + CX))
+    tile_sums = tile_sums + two_part_dot(across(rim_picks), rim)
     for c in range(NC):
         sums[pl.ds(c, total, stride=NC)] = tile_sums[:, c * 128 : (c + 1) * 128]
     out_sums[...] = sums[0:per_slot]
@@ -595,14 +633,28 @@
         if s in outs:
             outs[s][...] = sums[rows]
         elif slot_xor(ny, s) == 1:
-            out_a[Y_COEF:] = sums[rows]
+            out_a[BACK:] = sums[rows]
         else:
-            out_b[Y_COEF:] = sums[rows]
+            out_b[BACK:] = sums[rows]
 
 
 def loose_slots(ny):
     ridden = (0, 1, 3) if ny == 4 else (0, 1)
     return [s for s in range(ny) if slot_xor(ny, s) not in ridden]
+
+
+def pack_bulk(fine, final, bulk_a, bulk_b, near):
+    even, _, _ = place_on("gx")
+    for c in range(NC):
+        for h in range(RIM):
+            at = c * FIELD + (FIRST - RIM + h) * PITCH
+            west = final[at : at + CY]
+            at = c * FIELD + (FIRST + CX + h) * PITCH
+            put_pair(bulk_a, bulk_b, even, (c * RIM + h) * CY, final[at : at + CY], west)
+        for x in range(CX):
+            at = c * FIELD + (FIRST + x) * PITCH
+            rows = slice(x * CY, (x + 1) * CY)
+            near[c, rows] = fine[c, rows] + final[at : at + CY]
 
 
 def pack_home(sums, got_a, got_b, *rest):
@@ -610,9 +662,9 @@
     out_a, out_b, out_sum = rest[-3:]
     owned = sums.shape[0] // 3
     even, _, _ = place_on("gx")
-    total = sums[...] + got_a[Y_COEF:]
-    if got_b.shape[0] > Y_COEF:
-        total = total + got_b[Y_COEF:]
+    total = sums[...] + got_a[BACK:]
+    if got_b.shape[0] > BACK:
+        total = total + got_b[BACK:]
     for other in others:
         total = total + other[...]
     put_pair(out_a, out_b, even, 0, total[2 * owned :], total[0:owned])
@@ -681,14 +733,15 @@
     rows = owned * NC
     per_slot = 3 * rows
     total = 3 * ny * owned
-    beam_at = small_places(rows)[-1]
+    beam_at = small_places(ny * rows)[-1]
     tile = (NC, CX * CY, 128)
-
-    small_a, small_b, bulk_a, bulk_b, fine, coefs, control, tiles, meta, beams = call(
-        pack_x,
+    own_beams = jnp.transpose(obs_rows, (1, 0, 2)).reshape(BEAM_ROWS, 128)
+
+    y_a, y_b, bulk_a, bulk_b, fine, coefs, near_control, near_tiles, meta, near_beams = call(
+        pack_first,
         [
-            (beam_at + BEAM_ROWS, 128),
-            (beam_at, 128),
+            (Y_HALO + rows, 128),
+            (Y_HALO, 128),
             (BULK, 128),
             (BULK, 128),
             tile,
@@ -707,7 +760,7 @@
                 control,
                 tile_map,
                 *gates,
-                jnp.transpose(obs_rows, (1, 0, 2)).reshape(BEAM_ROWS, 128),
+                own_beams,
             )
         ],
         [
@@ -718,73 +771,71 @@
         ],
         in_specs=[HBM] * 11,
     )
+    y_a = swap(y_a, "gy", 1)
+    y_b = pair_b(y_b, "gy", "gx")
+    bulk_a = swap(bulk_a, "gx", 1)
+    bulk_b = pair_b(bulk_b, "gx", "gy")
+    got_beams, xor = own_beams, 2
+    while xor < nx:
+        got_beams = jnp.concatenate([got_beams, swap(got_beams, "gx", xor)])
+        xor *= 2
+    others, xor = [], 2
+    while xor < ny:
+        held = jnp.concatenate([control] + others) if others else control
+        others.append(swap(held, "gy", xor))
+        xor *= 2
+    others.append(swap(jnp.concatenate(others) if len(others) > 1 else others[0], "gy", 1))
+
+    small_a, small_b = call(
+        lambda *refs: pack_small(ny, *refs),
+        [(beam_at + got_beams.shape[0], 128), (beam_at, 128)],
+        [near_control, near_tiles, y_a, y_b, got_beams, *others],
+        [pltpu.VMEM((CX, 128), f32)],
+    )
     small_a = swap(small_a, "gx", 1)
     small_b = pair_b(small_b, "gx", "gy")
-    bulk_a = swap(bulk_a, "gx", 1)
-    bulk_b = pair_b(bulk_b, "gx", "gy")
-
-    y_a, y_b, profiles, near_tiles, beams = call(
-        pack_y,
-        [
-            (Y_HALO + per_slot, 128),
-            (Y_HALO, 128),
-            (per_slot, 128),
-            (BLOCKS, 128),
-            (2 * BEAM_ROWS, 128),
-        ],
-        [fine, coefs, control, tiles, beams, small_a, small_b],
-    )
-    others, xor = [], 2
-    while xor < ny:
-        held = jnp.concatenate([profiles] + others) if others else profiles
-        others.append(swap(held, "gy", xor))
-        xor *= 2
-    y_a = swap(y_a, "gy", 1)
-    y_b = pair_b(y_b, "gy", "gx")
-    others.append(swap(jnp.concatenate(others) if len(others) > 1 else others[0], "gy", 1))
-    beams = [beams]
-    xor = 2
-    while xor < nx:
-        held = jnp.concatenate(beams) if len(beams) > 1 else beams[0]
-        beams.append(swap(held, "gx", xor))
-        xor *= 2
 
     field, coef, picks, wide, slot_pick, slot_push, beam_pick, columns = call(
         lambda *refs: prepare(ny, len(others), *refs),
         [
             (NC * FIELD, 128),
             (5 * FIELD, 128),
-            (FIELD, total),
+            (CX * PITCH, total),
             (slots, NC * 128),
             jax.ShapeDtypeStruct((slots, CX * CY), bf16),
             jax.ShapeDtypeStruct((CX * CY, slots), bf16),
             jax.ShapeDtypeStruct((slots, nx * OWN_BEAMS), bf16),
             (slots, 8),
         ],
-        [fine, coefs, near_tiles, meta, weights, y_a, y_b, profiles, *others],
+        [fine, coefs, near_tiles, meta, weights, y_a, y_b, bulk_a, bulk_b, near_control, *others],
         [pltpu.VMEM((total * NC, 128), f32), pltpu.VMEM((128, 128), f32)],
         flops=3000000,
     )
-    tops, lows, coef = call(
-        forecast,
+    beams = [got_beams, small_a[beam_at:]]
+    tops, lows, coef, rim_picks = call(
+        lambda *refs: forecast(ny, rows, *refs),
         [
             jax.ShapeDtypeStruct((STEPS * CX * CY, NC * 128), bf16),
             jax.ShapeDtypeStruct((STEPS * CX * CY, NC * 128), bf16),
             (5 * FIELD, 128),
+            (2 * RIM * PITCH, total),
         ],
-        [field, coef, bulk_a, bulk_b],
-        [pltpu.VMEM((NC * FIELD, 128), f32), pltpu.VMEM((NC * FIELD, 128), f32)],
+        [field, coef, small_a, small_b],
+        [
+            pltpu.VMEM((NC * FIELD, 128), f32),
+            pltpu.VMEM((NC * FIELD, 128), f32),
+            pltpu.VMEM((total * NC, 128), f32),
+            pltpu.VMEM((128, 128), f32),
+        ],
         flops=10000000,
     )
     loose = loose_slots(ny)
-    back_a, back_b, bulk_a, bulk_b, near, sums, *back = call(
+    back_a, back_b, final, sums, *back = call(
         lambda *refs: main(ny, len(beams), *refs),
         [
-            (Y_COEF + per_slot, 128),
-            (Y_COEF + (per_slot if ny == 4 else 0), 128),
-            (BULK_COEF, 128),
-            (BULK_COEF, 128),
-            tile,
+            (BACK + per_slot, 128),
+            (BACK + (per_slot if ny == 4 else 0), 128),
+            (NC * FIELD, 128),
             (per_slot, 128),
         ]
         + [(per_slot, 128)] * len(loose),
@@ -798,11 +849,10 @@
             beam_pick,
             columns,
             picks,
-            fine,
+            rim_picks,
             *beams,
         ],
         [
-            pltpu.VMEM((NC * FIELD, 128), f32),
             pltpu.VMEM((NC * FIELD, 128), f32),
             pltpu.VMEM((STEPS * CX * CY, NC * 128), f32),
             pltpu.VMEM((total * NC, 128), f32),
@@ -812,6 +862,9 @@
     y_a = swap(back_a, "gy", 1)
     y_b = ring_b(back_b, "gy")
     others = [swap(value, "gy", slot_xor(ny, s)) for s, value in zip(loose, back)]
+    bulk_a, bulk_b, near = call(
+        pack_bulk, [(BULK_COEF, 128), (BULK_COEF, 128), tile], [fine, final]
+    )
     bulk_a = swap(bulk_a, "gx", 1)
     bulk_b = pair_b(bulk_b, "gx", "gy")
     home_rows = rows + 2 * NC * CORNER
@@ -825,7 +878,7 @@
     grad_delta, grad_alpha = call(
         finish,
         [tile, (rows, 128)],
-        [control, near, own_sum, y_a, y_b, bulk_a, bulk_b, small_a, small_b],
+        [near_control, near, own_sum, y_a, y_b, bulk_a, bulk_b, small_a, small_b],
     )
     return grad_delta.reshape(delta.shape), grad_alpha.reshape(alpha.shape)
 

time: 43.5 us -> 43.2 us (level)
  the two profiles are of different devices: /device:TPU:10 before, /device:TPU:0 now
where the time goes in v6:
time: 43.2 us; the launch traced here: 42.5 us
  starting transfers between devices  19.1 us (44%)
  Pallas kernels  10.9 us (25%)
  waiting for transfers between devices  10.3 us (24%)
  other arithmetic  1.42 us (3%)
  between operations  0.73 us (2%)
    ppermute x11, starting transfers between devices, swap(): lax.ppermute(block, axis, [(i, i ^ xor) for i in range(lax.axis_size(axis...  16.1 us
    pallas_call x8, Pallas kernels, call(): pl.pallas_call(body, out_shape=shapes, in_specs=in_specs or [VMEM] * len(...  10.9 us
    ppermute x11, waiting for transfers between devices, swap(): lax.ppermute(block, axis, [(i, i ^ xor) for i in range(lax.axis_size(axis...  10.3 us
    ppermute x5, starting transfers between devices, pair_b(): return lax.ppermute(block, ('gx', 'gy'), pairs)  1.6 us
    concatenate x2, other arithmetic, on_device(): got_beams = jnp.concatenate([got_beams, swap(got_beams, 'gx', xor)])  1.42 us
    ppermute x1, starting transfers between devices, ring_b(): return lax.ppermute(block, axis, pairs)  1.39 us
  transfers between devices with their start and end apart: 17, of which 5 were waited for; matrix products, arithmetic and copies ran while one was open for 3% of the time, Pallas kernels for 7%

profile of v6, /device:TPU:0, one launch (start us, length us, event | category | flops | bytes accessed | tf_op | source)
XLA Modules:
  0.0 42.5 jit_solution(7297933391426458772)
XLA Ops:
  0.6 0.0 copy-start
  0.6 3.1 %collective-permute-start.6 = (f32[24,128]{1,0:T(8,128)}, f32[24,128]{1,0:T(8,128)S(1)}, u32[]{:S(2)}, u32[]{:S(2)}) collective-permute-start(f32[24,128]{1,0:T(8,128)} %bitcast.19), channel_id=1, source_target_pairs={{0,8},{4,12},{8,0},{12,4},{16,24},{20,28},{24,16},{28,20},{1,9},{5... | collective-permute-start | bytes 36872 | tf_op jit(solution)/shard_map/ppermute | solution.py:51
  3.7 2.0 %shard_map.131 = (f32[320,128]{1,0:T(8,128)S(1)}, f32[304,128]{1,0:T(8,128)S(1)}, f32[288,128]{1,0:T(8,128)S(1)}, f32[288,128]{1,0:T(8,128)S(1)}, f32[4,256,128]...) custom-call(f32[4,256,128]{2,1,0:T(8,128)} %bitcast.16, ...), custom_call_target="tpu_custom_call" | custom-call | flops 1000000 | bytes 944128 | tf_op jit(solution)/shard_map/pallas_call | solution.py:39
  5.7 0.1 collective-permute-start
  5.8 1.6 %collective-permute-start.1 = (f32[304,128]{1,0:T(8,128)S(1)}, f32[304,128]{1,0:T(8,128)S(1)}, u32[]{:S(2)}, u32[]{:S(2)}) collective-permute-start(f32[304,128]{1,0:T(8,128)S(1)} %get-tuple-element.44), channel_id=1, source_target_pairs={{0,4},{1,2},{2,1},{3,7},{4,0},{5,6},{6,5},{7,3},{8,12},{9,10},{10,... | collective-permute-start | bytes 466952 | tf_op jit(solution)/shard_map/ppermute | solution.py:67
  7.4 0.0 collective-permute-done.6
  7.4 0.7 %pad_maximum_fusion.1 = f32[48,128]{1,0:T(8,128)S(1)} fusion(f32[24,128]{1,0:T(8,128)S(1)} %collective-permute-done.6, f32[24,128]{1,0:T(8,128)} %bitcast.21), kind=kLoop, calls=%fused_computation.1 | loop fusion | flops 6144 | bytes 49152 | tf_op jit(solution)/shard_map/concatenate | solution.py:780
  8.1 2.6 %collective-permute-start.7 = (f32[48,128]{1,0:T(8,128)S(1)}, f32[48,128]{1,0:T(8,128)S(1)}, u32[]{:S(2)}, u32[]{:S(2)}) collective-permute-start(f32[48,128]{1,0:T(8,128)S(1)} %pad_maximum_fusion.1), channel_id=1, source_target_pairs={{0,16},{4,20},{8,24},{12,28},{16,0},{20,4},{24,8},{28,12},{1,17},{... | collective-permute-start | bytes 73736 | tf_op jit(solution)/shard_map/ppermute | solution.py:51
  10.7 0.5 %collective-permute-start.4 = (f32[16,128]{1,0:T(8,128)}, f32[16,128]{1,0:T(8,128)S(1)}, u32[]{:S(2)}, u32[]{:S(2)}) collective-permute-start(f32[16,128]{1,0:T(8,128)} %bitcast.24), channel_id=1, source_target_pairs={{0,2},{1,3},{2,0},{3,1},{4,6},{5,7},{6,4},{7,5},{8,10},{9,11},{10,... | collective-permute-start | bytes 24584 | tf_op jit(solution)/shard_map/ppermute | solution.py:51
  11.2 1.5 %collective-permute-start.2 = (f32[288,128]{1,0:T(8,128)S(1)}, f32[288,128]{1,0:T(8,128)S(1)}, u32[]{:S(2)}, u32[]{:S(2)}) collective-permute-start(f32[288,128]{1,0:T(8,128)S(1)} %get-tuple-element.45), channel_id=1, source_target_pairs={{0,4},{4,0},{8,12},{12,8},{16,20},{20,16},{24,28},{28,24},{1,5},{5... | collective-permute-start | bytes 442376 | tf_op jit(solution)/shard_map/ppermute | solution.py:51
  12.7 1.8 %collective-permute-done.4.refs_10_.refs_5_ = f32[16,128]{1,0:T(8,128)S(1)} collective-permute-done((f32[16,128]{1,0:T(8,128)}, f32[16,128]{1,0:T(8,128)S(1)}, u32[]{:S(2)}, u32[]{:S(2)}) %collective-permute-start.4) | collective-permute-done | bytes 8224 | tf_op jit(solution)/shard_map/ppermute | solution.py:51
  14.5 0.0 collective-permute-start.3
  14.5 0.0 collective-permute-done.7
  14.5 0.5 %collective-permute-start.5 = (f32[16,128]{1,0:T(8,128)S(1)}, f32[16,128]{1,0:T(8,128)S(1)}, u32[]{:S(2)}, u32[]{:S(2)}) collective-permute-start(f32[16,128]{1,0:T(8,128)S(1)} %collective-permute-done.4.refs_10_.refs_5_), channel_id=1, source_target_pairs={{0,1},{1,0},{2,3},{3,2},{4,5},{5,4},{6,7},{7,6},{8,9},{9,8},{10,11... | collective-permute-start | bytes 24584 | tf_op jit(solution)/shard_map/ppermute | solution.py:51
  15.0 0.7 %pad_maximum_fusion.refs_4_.refs_10_ = f32[96,128]{1,0:T(8,128)S(1)} fusion(f32[48,128]{1,0:T(8,128)S(1)} %collective-permute-done.7, f32[24,128]{1,0:T(8,128)S(1)} %collective-permute-done.6, f32[24,128]{1,0:T(8,128)} %bitcast.22), kind=kLoop, calls=%fused_computation | loop fusion | flops 24576 | bytes 98304 | tf_op jit(solution)/shard_map/concatenate | solution.py:780
  15.8 0.2 collective-permute-done.5.refs_11_.refs_6_
  15.9 0.0 collective-permute-done.1.refs_6_.refs_3_
  15.9 0.0 collective-permute-done.refs_5_.refs_2_
  15.9 0.1 shard_map.133
  16.0 1.7 %collective-permute-start.8 = (f32[193,128]{1,0:T(8,128)S(1)}, f32[193,128]{1,0:T(8,128)S(1)}, u32[]{:S(2)}, u32[]{:S(2)}) collective-permute-start(f32[193,128]{1,0:T(8,128)S(1)} %get-tuple-element.49), channel_id=1, source_target_pairs={{0,4},{4,0},{8,12},{12,8},{16,20},{20,16},{24,28},{28,24},{1,5},{5... | collective-permute-start | bytes 296456 | tf_op jit(solution)/shard_map/ppermute | solution.py:51
  17.8 0.0 collective-permute-start.9
  17.8 0.0 collective-permute-done.2.refs_7_
  17.8 0.0 collective-permute-done.3.refs_8_
  17.8 0.0 copy-done
  17.8 1.0 %shard_map.132 = (f32[2304,128]{1,0:T(8,128)S(1)}, f32[2880,128]{1,0:T(8,128)S(1)}, f32[384,48]{1,0:T(8,128)S(1)}, f32[256,512]{1,0:T(8,128)S(1)}, bf16[256,256]...) custom-call(f32[4,256,128]{2,1,0:T(8,128)S(1)} %get-tuple-element.39.refs_0_, ...), custom_call_target="tpu_custom_call" | custom-call | flops 3000000 | bytes 2097152 | tf_op jit(solution)/shard_map/pallas_call | solution.py:39
  18.8 3.5 %collective-permute-done.8.refs_2_ = f32[193,128]{1,0:T(8,128)S(1)} collective-permute-done((f32[193,128]{1,0:T(8,128)S(1)}, f32[193,128]{1,0:T(8,128)S(1)}, u32[]{:S(2)}, u32[]{:S(2)}) %collective-permute-start.8) | collective-permute-done | bytes 98848 | tf_op jit(solution)/shard_map/ppermute | solution.py:51
  22.2 0.0 collective-permute-done.9.refs_3_
  22.2 2.2 %shard_map.134 = (bf16[768,512]{1,0:T(8,128)(2,1)S(1)}, bf16[768,512]{1,0:T(8,128)(2,1)S(1)}, f32[2880,128]{1,0:T(8,128)S(1)}, f32[144,48]{1,0:T(8,128)S(1)}) custom-call(f32[2304,128]{1,0:T(8,128)S(1)} %get-tuple-element.47.refs_0_, f32[2880,128]{1,0:T(8,128)S(1)} %get-tuple-element.48.refs_1_, f32[193,128]{1,0:T(8,128)S(1)} %collective-permute-done.8.refs_2_, ...), custom_call_target="tpu_custom_call" | custom-call | flops 10000000 | bytes 2802688 | tf_op jit(solution)/shard_map/pallas_call | solution.py:39
  24.4 4.6 %shard_map.135 = (f32[264,128]{1,0:T(8,128)S(1)}, f32[264,128]{1,0:T(8,128)S(1)}, f32[2304,128]{1,0:T(8,128)S(1)}, f32[48,128]{1,0:T(8,128)S(1)}, f32[48,128]{1,0:T(8,128)S(1)}) custom-call(f32[2880,128]{1,0:T(8,128)S(1)} %get-tuple-element.51.refs_0_, bf16[768,512]{1,0:T(8,128)(2,1)S(1)} %get-tuple-element.52.refs_1_, ...), custom_call_target="tpu_custom_call" | custom-call | flops 20000000 | bytes 5942272 | tf_op jit(solution)/shard_map/pallas_call | solution.py:39
  29.0 0.1 collective-permute-start.10
  29.1 1.4 %collective-permute-start.11 = (f32[264,128]{1,0:T(8,128)S(1)}, f32[264,128]{1,0:T(8,128)S(1)}, u32[]{:S(2)}, u32[]{:S(2)}) collective-permute-start(f32[264,128]{1,0:T(8,128)S(1)} %get-tuple-element.65), channel_id=1, source_target_pairs={{0,3},{1,2},{2,1},{3,0},{4,7},{5,6},{6,5},{7,4},{8,11},{9,10},{10,... | collective-permute-start | bytes 405512 | tf_op jit(solution)/shard_map/ppermute | solution.py:73
  30.5 0.1 shard_map.136
  30.6 2.5 %collective-permute-start.13 = (f32[192,128]{1,0:T(8,128)S(1)}, f32[192,128]{1,0:T(8,128)S(1)}, u32[]{:S(2)}, u32[]{:S(2)}) collective-permute-start(f32[192,128]{1,0:T(8,128)S(1)} %get-tuple-element.68), channel_id=1, source_target_pairs={{0,4},{4,0},{8,12},{12,8},{16,20},{20,16},{24,28},{28,24},{1,5},{5... | collective-permute-start | bytes 294920 | tf_op jit(solution)/shard_map/ppermute | solution.py:51
  33.1 0.0 collective-permute-start.14
  33.1 0.7 %collective-permute-start.12 = (f32[48,128]{1,0:T(8,128)S(1)}, f32[48,128]{1,0:T(8,128)S(1)}, u32[]{:S(2)}, u32[]{:S(2)}) collective-permute-start(f32[48,128]{1,0:T(8,128)S(1)} %get-tuple-element.66), channel_id=1, source_target_pairs={{0,2},{1,3},{2,0},{3,1},{4,6},{5,7},{6,4},{7,5},{8,10},{9,11},{10,... | collective-permute-start | bytes 73736 | tf_op jit(solution)/shard_map/ppermute | solution.py:51
  33.8 3.1 %collective-permute-done.12.rest_0_ = f32[48,128]{1,0:T(8,128)S(1)} collective-permute-done((f32[48,128]{1,0:T(8,128)S(1)}, f32[48,128]{1,0:T(8,128)S(1)}, u32[]{:S(2)}, u32[]{:S(2)}) %collective-permute-start.12) | collective-permute-done | bytes 24608 | tf_op jit(solution)/shard_map/ppermute | solution.py:51
  36.9 0.0 collective-permute-done.10.got_a.y_a
  36.9 0.0 collective-permute-done.11.got_b.y_b
  37.0 2.7 %collective-permute-start.15 = (f32[40,128]{1,0:T(8,128)S(1)}, f32[40,128]{1,0:T(8,128)S(1)}, u32[]{:S(2)}, u32[]{:S(2)}) collective-permute-start(f32[40,128]{1,0:T(8,128)S(1)} %get-tuple-element.70), channel_id=1, source_target_pairs={{0,4},{4,0},{8,12},{12,8},{16,20},{20,16},{24,28},{28,24},{1,5},{5... | collective-permute-start | bytes 61448 | tf_op jit(solution)/shard_map/ppermute | solution.py:51
  39.7 0.0 collective-permute-start.16
  39.7 0.0 collective-permute-done.13.bulk_a
  39.7 0.0 collective-permute-done.14.bulk_b
  39.7 1.8 %collective-permute-done.15.small_a = f32[40,128]{1,0:T(8,128)S(1)} collective-permute-done((f32[40,128]{1,0:T(8,128)S(1)}, f32[40,128]{1,0:T(8,128)S(1)}, u32[]{:S(2)}, u32[]{:S(2)}) %collective-permute-start.15) | collective-permute-done | bytes 20512 | tf_op jit(solution)/shard_map/ppermute | solution.py:51
  41.5 0.0 collective-permute-done.16.small_b
  41.5 1.0 %shard_map.138 = (f32[4,256,128]{2,1,0:T(8,128)}, f32[16,128]{1,0:T(8,128)}) custom-call(f32[16,128]{1,0:T(8,128)S(1)} %get-tuple-element.38.refs_9_.refs_0_.alpha, f32[4,256,128]{2,1,0:T(8,128)S(1)} %get-tuple-element.62.near, f32[16,128]{1,0:T(8,128)S(1)} %get-tuple-element.67.own_sum, f32[264,128]{1,0:T(8,128)S(1)} %collective-permute-done.10.got_a.y_a, ...), custom_call_target="tpu_custom_call" | custom-call | flops 1000000 | bytes 1048576 | tf_op jit(solution)/shard_map/pallas_call | solution.py:39
  (2 shorter events, 0.0 us)
Async XLA Ops:
  0.6 17.1 %copy-start = (f32[1,1,256,4,128]{4,3,2,1,0:T(4,128)S(1)}, f32[1,1,256,4,128]{4,3,2,1,0:T(4,128)}, u32[]{:S(2)}) copy-start(f32[1,1,256,4,128]{4,3,2,1,0:T(4,128)} %param.22) | copy-start | bytes 1572868
  0.6 6.7 %collective-permute-start.6 = (f32[24,128]{1,0:T(8,128)}, f32[24,128]{1,0:T(8,128)S(1)}, u32[]{:S(2)}, u32[]{:S(2)}) collective-permute-start(f32[24,128]{1,0:T(8,128)} %bitcast.19), channel_id=1, source_target_pairs={{0,8},{4,12},{8,0},{12,4},{16,24},{20,28},{24,16},{28,20},{1,9},{5... | collective-permute-start | bytes 36872 | tf_op jit(solution)/shard_map/ppermute | solution.py:51
  5.7 10.2 %collective-permute-start = (f32[320,128]{1,0:T(8,128)S(1)}, f32[320,128]{1,0:T(8,128)S(1)}, u32[]{:S(2)}, u32[]{:S(2)}) collective-permute-start(f32[320,128]{1,0:T(8,128)S(1)} %get-tuple-element.43), channel_id=1, source_target_pairs={{0,1},{1,0},{2,3},{3,2},{4,5},{5,4},{6,7},{7,6},{8,9},{9,8},{10,11... | collective-permute-start | bytes 491528 | tf_op jit(solution)/shard_map/ppermute | solution.py:51
  5.8 10.1 %collective-permute-start.1 = (f32[304,128]{1,0:T(8,128)S(1)}, f32[304,128]{1,0:T(8,128)S(1)}, u32[]{:S(2)}, u32[]{:S(2)}) collective-permute-start(f32[304,128]{1,0:T(8,128)S(1)} %get-tuple-element.44), channel_id=1, source_target_pairs={{0,4},{1,2},{2,1},{3,7},{4,0},{5,6},{6,5},{7,3},{8,12},{9,10},{10,... | collective-permute-start | bytes 466952 | tf_op jit(solution)/shard_map/ppermute | solution.py:67
  8.1 6.5 %collective-permute-start.7 = (f32[48,128]{1,0:T(8,128)S(1)}, f32[48,128]{1,0:T(8,128)S(1)}, u32[]{:S(2)}, u32[]{:S(2)}) collective-permute-start(f32[48,128]{1,0:T(8,128)S(1)} %pad_maximum_fusion.1), channel_id=1, source_target_pairs={{0,16},{4,20},{8,24},{12,28},{16,0},{20,4},{24,8},{28,12},{1,17},{... | collective-permute-start | bytes 73736 | tf_op jit(solution)/shard_map/ppermute | solution.py:51
  10.7 3.9 %collective-permute-start.4 = (f32[16,128]{1,0:T(8,128)}, f32[16,128]{1,0:T(8,128)S(1)}, u32[]{:S(2)}, u32[]{:S(2)}) collective-permute-start(f32[16,128]{1,0:T(8,128)} %bitcast.24), channel_id=1, source_target_pairs={{0,2},{1,3},{2,0},{3,1},{4,6},{5,7},{6,4},{7,5},{8,10},{9,11},{10,... | collective-permute-start | bytes 24584 | tf_op jit(solution)/shard_map/ppermute | solution.py:51
  11.2 6.6 %collective-permute-start.2 = (f32[288,128]{1,0:T(8,128)S(1)}, f32[288,128]{1,0:T(8,128)S(1)}, u32[]{:S(2)}, u32[]{:S(2)}) collective-permute-start(f32[288,128]{1,0:T(8,128)S(1)} %get-tuple-element.45), channel_id=1, source_target_pairs={{0,4},{4,0},{8,12},{12,8},{16,20},{20,16},{24,28},{28,24},{1,5},{5... | collective-permute-start | bytes 442376 | tf_op jit(solution)/shard_map/ppermute | solution.py:51
  14.5 3.2 %collective-permute-start.3 = (f32[288,128]{1,0:T(8,128)S(1)}, f32[288,128]{1,0:T(8,128)S(1)}, u32[]{:S(2)}, u32[]{:S(2)}) collective-permute-start(f32[288,128]{1,0:T(8,128)S(1)} %get-tuple-element.46), channel_id=1, source_target_pairs={{0,1},{4,8},{8,4},{12,16},{16,12},{20,24},{24,20},{28,29},{1,0},{5... | collective-permute-start | bytes 442376 | tf_op jit(solution)/shard_map/ppermute | solution.py:67
  14.5 1.4 %collective-permute-start.5 = (f32[16,128]{1,0:T(8,128)S(1)}, f32[16,128]{1,0:T(8,128)S(1)}, u32[]{:S(2)}, u32[]{:S(2)}) collective-permute-start(f32[16,128]{1,0:T(8,128)S(1)} %collective-permute-done.4.refs_10_.refs_5_), channel_id=1, source_target_pairs={{0,1},{1,0},{2,3},{3,2},{4,5},{5,4},{6,7},{7,6},{8,9},{9,8},{10,11... | collective-permute-start | bytes 24584 | tf_op jit(solution)/shard_map/ppermute | solution.py:51
  16.0 6.2 %collective-permute-start.8 = (f32[193,128]{1,0:T(8,128)S(1)}, f32[193,128]{1,0:T(8,128)S(1)}, u32[]{:S(2)}, u32[]{:S(2)}) collective-permute-start(f32[193,128]{1,0:T(8,128)S(1)} %get-tuple-element.49), channel_id=1, source_target_pairs={{0,4},{4,0},{8,12},{12,8},{16,20},{20,16},{24,28},{28,24},{1,5},{5... | collective-permute-start | bytes 296456 | tf_op jit(solution)/shard_map/ppermute | solution.py:51
  17.8 4.5 %collective-permute-start.9 = (f32[97,128]{1,0:T(8,128)S(1)}, f32[97,128]{1,0:T(8,128)S(1)}, u32[]{:S(2)}, u32[]{:S(2)}) collective-permute-start(f32[97,128]{1,0:T(8,128)S(1)} %get-tuple-element.50), channel_id=1, source_target_pairs={{0,1},{4,8},{8,4},{12,16},{16,12},{20,24},{24,20},{28,29},{1,0},{5... | collective-permute-start | bytes 149000 | tf_op jit(solution)/shard_map/ppermute | solution.py:67
  29.0 7.9 %collective-permute-start.10 = (f32[264,128]{1,0:T(8,128)S(1)}, f32[264,128]{1,0:T(8,128)S(1)}, u32[]{:S(2)}, u32[]{:S(2)}) collective-permute-start(f32[264,128]{1,0:T(8,128)S(1)} %get-tuple-element.64), channel_id=1, source_target_pairs={{0,1},{1,0},{2,3},{3,2},{4,5},{5,4},{6,7},{7,6},{8,9},{9,8},{10,11... | collective-permute-start | bytes 405512 | tf_op jit(solution)/shard_map/ppermute | solution.py:51
  29.1 7.8 %collective-permute-start.11 = (f32[264,128]{1,0:T(8,128)S(1)}, f32[264,128]{1,0:T(8,128)S(1)}, u32[]{:S(2)}, u32[]{:S(2)}) collective-permute-start(f32[264,128]{1,0:T(8,128)S(1)} %get-tuple-element.65), channel_id=1, source_target_pairs={{0,3},{1,2},{2,1},{3,0},{4,7},{5,6},{6,5},{7,4},{8,11},{9,10},{10,... | collective-permute-start | bytes 405512 | tf_op jit(solution)/shard_map/ppermute | solution.py:73
  30.6 9.1 %collective-permute-start.13 = (f32[192,128]{1,0:T(8,128)S(1)}, f32[192,128]{1,0:T(8,128)S(1)}, u32[]{:S(2)}, u32[]{:S(2)}) collective-permute-start(f32[192,128]{1,0:T(8,128)S(1)} %get-tuple-element.68), channel_id=1, source_target_pairs={{0,4},{4,0},{8,12},{12,8},{16,20},{20,16},{24,28},{28,24},{1,5},{5... | collective-permute-start | bytes 294920 | tf_op jit(solution)/shard_map/ppermute | solution.py:51
  33.1 6.6 %collective-permute-start.14 = (f32[192,128]{1,0:T(8,128)S(1)}, f32[192,128]{1,0:T(8,128)S(1)}, u32[]{:S(2)}, u32[]{:S(2)}) collective-permute-start(f32[192,128]{1,0:T(8,128)S(1)} %get-tuple-element.69), channel_id=1, source_target_pairs={{0,1},{4,8},{8,4},{12,16},{16,12},{20,24},{24,20},{28,29},{1,0},{5... | collective-permute-start | bytes 294920 | tf_op jit(solution)/shard_map/ppermute | solution.py:67
  33.1 3.8 %collective-permute-start.12 = (f32[48,128]{1,0:T(8,128)S(1)}, f32[48,128]{1,0:T(8,128)S(1)}, u32[]{:S(2)}, u32[]{:S(2)}) collective-permute-start(f32[48,128]{1,0:T(8,128)S(1)} %get-tuple-element.66), channel_id=1, source_target_pairs={{0,2},{1,3},{2,0},{3,1},{4,6},{5,7},{6,4},{7,5},{8,10},{9,11},{10,... | collective-permute-start | bytes 73736 | tf_op jit(solution)/shard_map/ppermute | solution.py:51
  37.0 4.5 %collective-permute-start.15 = (f32[40,128]{1,0:T(8,128)S(1)}, f32[40,128]{1,0:T(8,128)S(1)}, u32[]{:S(2)}, u32[]{:S(2)}) collective-permute-start(f32[40,128]{1,0:T(8,128)S(1)} %get-tuple-element.70), channel_id=1, source_target_pairs={{0,4},{4,0},{8,12},{12,8},{16,20},{20,16},{24,28},{28,24},{1,5},{5... | collective-permute-start | bytes 61448 | tf_op jit(solution)/shard_map/ppermute | solution.py:51
  39.7 1.8 %collective-permute-start.16 = (f32[40,128]{1,0:T(8,128)S(1)}, f32[40,128]{1,0:T(8,128)S(1)}, u32[]{:S(2)}, u32[]{:S(2)}) collective-permute-start(f32[40,128]{1,0:T(8,128)S(1)} %get-tuple-element.71), channel_id=1, source_target_pairs={{0,1},{4,8},{8,4},{12,16},{16,12},{20,24},{24,20},{28,29},{1,0},{5... | collective-permute-start | bytes 61448 | tf_op jit(solution)/shard_map/ppermute | solution.py:67

commit v7 on v4

--- a/solution.py
+++ b/solution.py
@@ -17,7 +17,6 @@
 FIELD = BLOCKS * PITCH
 CORE = CX * PITCH
 OWN_BEAMS = 8
-BEAM_BITS = 3
 
 profile_weight = 0.125
 f32 = jnp.float32
@@ -172,13 +171,9 @@
     for out in (out_a, out_b):
         out[Y_TILE : Y_TILE + CX] = near_tiles[...]
     out_a[Y_HALO:] = profiles[...]
-    held = BEAM_BITS
-    beam = gates[0]
-    owner = jnp.bitwise_xor(beam >> held, lax.axis_index("gx"))
-    block = (owner & -4) | ((owner & 1) << 1) | ((owner >> 1) & 1)
     meta[...] = jnp.zeros(meta.shape, f32)
     meta[0:1] = gates[2].astype(f32)
-    meta[1:2] = ((block << held) | (beam & ((1 << held) - 1))).astype(f32)
+    meta[1:2] = gates[0].astype(f32)
     meta[2:3] = gates[1].astype(f32)
     meta[3:4] = gates[3].astype(f32) * values[...]
 
@@ -232,7 +227,7 @@
     return jnp.concatenate([ref[pl.ds(c, count, stride=NC)] for c in range(NC)], axis=1)
 
 
-def pack_x(ny, delta, coefs, alpha, near_tiles, y_a, y_b, own_beams, got_beams, *rest):
+def pack_x(ny, delta, coefs, alpha, near_tiles, y_a, y_b, own_beams, *rest):
     others = rest[: ny - 2]
     out_a, out_b, beams, field, picks, known, tiles = rest[ny - 2 :]
     even, _, _ = place_on("gx")
@@ -280,10 +275,9 @@
     for f in range(3):
         fill(coefs.at[f], Y_COEF + f * INNER * CX, INNER, None)
         put(X_COEF + f * SLIM_ROWS, SLIM)
-    half = own_beams.shape[0]
-    beams[0:half] = own_beams[...]
-    beams[half:] = got_beams[...]
-    out_a[X_HALO:] = beams[...]
+    rows = own_beams.shape[0]
+    for at in range(0, beams.shape[0], rows):
+        beams[at : at + rows] = own_beams[...]
 
 
 def prepare(ny, delta, coefs, alpha, near_tiles, meta, weights, y_a, y_b, *rest):
@@ -652,12 +646,11 @@
     y_a = swap(y_a, "gy", 1)
     y_b = pair_b(y_b, "gy", "gx")
     others = [swap(control, "gy", xor) for xor in range(2, ny)]
-    got_beams = swap(own_beams, "gx", 2)
 
     x_a, x_b, beams = call(
         lambda *refs: pack_x(ny, *refs),
-        [(X_HALO + 2 * own_beams.shape[0], 128), (X_HALO, 128), (2 * own_beams.shape[0], 128)],
-        [fine, coefs, control_near, near_tiles, y_a, y_b, near_beams, got_beams, *others],
+        [(X_HALO, 128), (X_HALO, 128), (nx * own_beams.shape[0], 128)],
+        [fine, coefs, control_near, near_tiles, y_a, y_b, near_beams, *others],
         [
             pltpu.VMEM((2 * RIM * PITCH, 128), f32),
             pltpu.VMEM((2 * RIM * PITCH, total), f32),
@@ -688,12 +681,7 @@
         flops=3000000,
     )
 
-    beams = [beams, x_a[X_HALO:]]
-    xor = 4
-    while xor < nx:
-        beams = beams + [swap(jnp.concatenate(beams), "gx", xor)]
-        xor *= 2
-
+    beams = [lax.all_to_all(beams, "gx", 0, 0, tiled=True)]
     tops, lows, coef = call(
         forecast,
         [

time: 43.5 us -> 49.9 us (1.15)
  local copies, waits for them, and re-layouts: 0.01 us -> 7.28 us
  waiting for transfers between devices: 17.6 us -> 14.2 us
  starting transfers between devices: 14.7 us -> 16.4 us
  Pallas kernels: 10.3 us -> 10.8 us
    unnamed x2 -> x22, local copies, waits for them, and re-layouts: 0.01 us -> 7.28 us
    all_to_all x0 -> x1, starting transfers between devices: none -> 4.88 us  [on_device(): beams = [lax.all_to_all(beams, 'gx', 0, 0, tiled=True)]]
    ppermute x9 -> x7, waiting for transfers between devices: 17.6 us -> 14.2 us  [swap(): lax.ppermute(block, axis, [(i, i ^ xor) for i in range(lax.axis_size(axis...]
    ppermute x9 -> x7, starting transfers between devices: 10.5 us -> 7.77 us  [swap(): lax.ppermute(block, axis, [(i, i ^ xor) for i in range(lax.axis_size(axis...]
  transfers between devices with their start and end apart: 13 -> 12, of which waited for: 4 -> 5; matrix products, arithmetic and copies ran while one was open for 0% -> 0% of each run, Pallas kernels for 7% -> 6%
where the time goes in v7:
time: 49.9 us; the launch traced here: 49.5 us
  starting transfers between devices  16.4 us (33%)
  waiting for transfers between devices  14.2 us (28%)
  Pallas kernels  10.8 us (22%)
  local copies, waits for them, and re-layouts  7.28 us (15%)
  between operations  0.72 us (1%)
    ppermute x7, waiting for transfers between devices, swap(): lax.ppermute(block, axis, [(i, i ^ xor) for i in range(lax.axis_size(axis...  14.2 us
    pallas_call x7, Pallas kernels, call(): pl.pallas_call(body, out_shape=shapes, in_specs=in_specs or [VMEM] * len(...  10.8 us
    ppermute x7, starting transfers between devices, swap(): lax.ppermute(block, axis, [(i, i ^ xor) for i in range(lax.axis_size(axis...  7.77 us
    unnamed x22, local copies, waits for them, and re-layouts  7.28 us
    all_to_all x1, starting transfers between devices, on_device(): beams = [lax.all_to_all(beams, 'gx', 0, 0, tiled=True)]  4.88 us
    ppermute x3, starting transfers between devices, pair_b(): return lax.ppermute(block, ('gx', 'gy'), pairs)  2.6 us
    ppermute x1, starting transfers between devices, ring_b(): return lax.ppermute(block, axis, pairs)  1.17 us
  transfers between devices with their start and end apart: 12, of which 5 were waited for; matrix products, arithmetic and copies ran while one was open for 0% of the time, Pallas kernels for 6%

profile of v7, /device:TPU:0, one launch (start us, length us, event | category | flops | bytes accessed | tf_op | source)
XLA Modules:
  0.0 49.5 jit_solution(5085848649781604493)
XLA Ops:
  0.6 0.0 copy-start.2
  0.6 1.4 %shard_map.131 = (f32[320,128]{1,0:T(8,128)S(1)}, f32[304,128]{1,0:T(8,128)S(1)}, f32[4,256,128]{2,1,0:T(8,128)S(1)}, f32[3,256,128]{2,1,0:T(8,128)S(1)}, f32[16...) custom-call(f32[4,256,128]{2,1,0:T(8,128)} %bitcast.19, ...), custom_call_target="tpu_custom_call" | custom-call | flops 1000000 | bytes 944128 | tf_op jit(solution)/shard_map/pallas_call | solution.py:35
  2.1 0.5 %collective-permute-start = (f32[320,128]{1,0:T(8,128)S(1)}, f32[320,128]{1,0:T(8,128)S(1)}, u32[]{:S(2)}, u32[]{:S(2)}) collective-permute-start(f32[320,128]{1,0:T(8,128)S(1)} %get-tuple-element.39), channel_id=1, source_target_pairs={{0,1},{1,0},{2,3},{3,2},{4,5},{5,4},{6,7},{7,6},{8,9},{9,8},{10,11... | collective-permute-start | bytes 491528 | tf_op jit(solution)/shard_map/ppermute | solution.py:47
  2.6 2.6 %collective-permute-start.1 = (f32[304,128]{1,0:T(8,128)S(1)}, f32[304,128]{1,0:T(8,128)S(1)}, u32[]{:S(2)}, u32[]{:S(2)}) collective-permute-start(f32[304,128]{1,0:T(8,128)S(1)} %get-tuple-element.40), channel_id=1, source_target_pairs={{0,4},{1,2},{2,1},{3,7},{4,0},{5,6},{6,5},{7,3},{8,12},{9,10},{10,... | collective-permute-start | bytes 466952 | tf_op jit(solution)/shard_map/ppermute | solution.py:63
  5.2 1.2 %collective-permute-start.3 = (f32[16,128]{1,0:T(8,128)}, f32[16,128]{1,0:T(8,128)S(1)}, u32[]{:S(2)}, u32[]{:S(2)}) collective-permute-start(f32[16,128]{1,0:T(8,128)} %bitcast.24), channel_id=1, source_target_pairs={{0,3},{1,2},{2,1},{3,0},{4,7},{5,6},{6,5},{7,4},{8,11},{9,10},{10,... | collective-permute-start | bytes 24584 | tf_op jit(solution)/shard_map/ppermute | solution.py:47
  6.4 0.5 collective-permute-start.2
  6.9 1.6 %collective-permute-done.3.refs_9_.refs_8_ = f32[16,128]{1,0:T(8,128)S(1)} collective-permute-done((f32[16,128]{1,0:T(8,128)}, f32[16,128]{1,0:T(8,128)S(1)}, u32[]{:S(2)}, u32[]{:S(2)}) %collective-permute-start.3) | collective-permute-done | bytes 8224 | tf_op jit(solution)/shard_map/ppermute | solution.py:47
  8.5 1.8 %collective-permute-done.2.refs_8_.refs_7_ = f32[16,128]{1,0:T(8,128)S(1)} collective-permute-done((f32[16,128]{1,0:T(8,128)}, f32[16,128]{1,0:T(8,128)S(1)}, u32[]{:S(2)}, u32[]{:S(2)}) %collective-permute-start.2) | collective-permute-done | bytes 8224 | tf_op jit(solution)/shard_map/ppermute | solution.py:47
  10.3 0.0 collective-permute-done.1.refs_7_.refs_5_
  10.3 0.0 collective-permute-done.refs_6_.refs_4_
  10.3 1.1 %shard_map.133 = (f32[318,128]{1,0:T(8,128)S(1)}, f32[318,128]{1,0:T(8,128)S(1)}, f32[192,128]{1,0:T(8,128)}) custom-call(f32[4,256,128]{2,1,0:T(8,128)S(1)} %get-tuple-element.35.refs_0_, f32[3,256,128]{2,1,0:T(8,128)S(1)} %get-tuple-element.36.refs_1_, f32[16,128]{1,0:T(8,128)S(1)} %get-tuple-element.34.refs_2_.alpha, ...), custom_call_target="tpu_custom_call" | custom-call | flops 1000000 | bytes 1282048 | tf_op jit(solution)/shard_map/pallas_call | solution.py:35
  11.4 4.9 %all-to-all-start = ((f32[8,24,128]{2,1,0:T(8,128)}), f32[8,24,128]{2,1,0:T(8,128)S(1)}, u32[]{:S(2)}, u32[]{:S(2)}) async-start(f32[8,24,128]{2,1,0:T(8,128)} %bitcast.12), calls=%async_computation | async-start | bytes 196608 | tf_op jit(solution)/shard_map/all_to_all | solution.py:684
  16.3 2.0 %collective-permute-start.4 = (f32[318,128]{1,0:T(8,128)S(1)}, f32[318,128]{1,0:T(8,128)S(1)}, u32[]{:S(2)}, u32[]{:S(2)}) collective-permute-start(f32[318,128]{1,0:T(8,128)S(1)} %get-tuple-element.45), channel_id=1, source_target_pairs={{0,4},{4,0},{8,12},{12,8},{16,20},{20,16},{24,28},{28,24},{1,5},{5... | collective-permute-start | bytes 488456 | tf_op jit(solution)/shard_map/ppermute | solution.py:47
  18.3 0.0 collective-permute-start.5
  18.3 0.0 copy-done.2
  18.3 1.0 %shard_map.132 = (f32[1536,128]{1,0:T(8,128)S(1)}, f32[1920,128]{1,0:T(8,128)S(1)}, f32[384,16]{1,0:T(8,128)S(1)}, f32[256,512]{1,0:T(8,128)S(1)}, bf16[256,256]...) custom-call(f32[4,256,128]{2,1,0:T(8,128)S(1)} %get-tuple-element.35.refs_0_, ...), custom_call_target="tpu_custom_call" | custom-call | flops 3000000 | bytes 1802240 | tf_op jit(solution)/shard_map/pallas_call | solution.py:35
  19.3 0.0 copy-start.3
  19.3 0.7 %copy-done.3 = f32[384,16]{1,0:T(8,128)} copy-done((f32[384,16]{1,0:T(8,128)}, f32[384,16]{1,0:T(8,128)S(1)}, u32[]{:S(2)}) %copy-start.3) | copy-done | bytes 24600
  20.0 0.0 copy-start.5
  20.0 0.6 %copy-done.5 = bf16[256,256]{1,0:T(8,128)(2,1)} copy-done((bf16[256,256]{1,0:T(8,128)(2,1)}, bf16[256,256]{1,0:T(8,128)(2,1)S(1)}, u32[]{:S(2)}) %copy-start.5) | copy-done | bytes 131096
  20.6 0.0 copy-start.7
  20.6 0.7 %copy-done.7 = f32[256,8]{1,0:T(8,128)} copy-done((f32[256,8]{1,0:T(8,128)}, f32[256,8]{1,0:T(8,128)S(1)}, u32[]{:S(2)}) %copy-start.7) | copy-done | bytes 8216
  21.3 0.0 copy-start.9
  21.3 0.6 %copy-done.9 = bf16[256,64]{1,0:T(8,128)(2,1)} copy-done((bf16[256,64]{1,0:T(8,128)(2,1)}, bf16[256,64]{1,0:T(8,128)(2,1)S(1)}, u32[]{:S(2)}) %copy-start.9) | copy-done | bytes 32792
  21.9 3.5 %collective-permute-done.4.x_a = f32[318,128]{1,0:T(8,128)S(1)} collective-permute-done((f32[318,128]{1,0:T(8,128)S(1)}, f32[318,128]{1,0:T(8,128)S(1)}, u32[]{:S(2)}, u32[]{:S(2)}) %collective-permute-start.4) | collective-permute-done | bytes 162848 | tf_op jit(solution)/shard_map/ppermute | solution.py:47
  25.4 0.0 collective-permute-done.5.x_b
  25.4 1.9 %shard_map.134 = (bf16[768,512]{1,0:T(8,128)(2,1)S(1)}, bf16[768,512]{1,0:T(8,128)(2,1)S(1)}, f32[2880,128]{1,0:T(8,128)S(1)}) custom-call(f32[1536,128]{1,0:T(8,128)S(1)} %get-tuple-element.42.core, f32[1920,128]{1,0:T(8,128)S(1)} %get-tuple-element.43.coef_core, f32[318,128]{1,0:T(8,128)S(1)} %collective-permute-done.4.x_a, ...), custom_call_target="tpu_custom_call" | custom-call | flops 10000000 | bytes 2095104 | tf_op jit(solution)/shard_map/pallas_call | solution.py:35
  27.3 0.0 copy-start
  27.3 0.9 %copy-done = bf16[768,512]{1,0:T(8,128)(2,1)} copy-done((bf16[768,512]{1,0:T(8,128)(2,1)}, bf16[768,512]{1,0:T(8,128)(2,1)S(1)}, u32[]{:S(2)}) %copy-start) | copy-done | bytes 786456
  28.2 0.0 all-to-all-done
  28.2 0.0 copy-start.1
  28.2 1.1 %copy-done.1 = bf16[768,512]{1,0:T(8,128)(2,1)S(1)} copy-done((bf16[768,512]{1,0:T(8,128)(2,1)S(1)}, bf16[768,512]{1,0:T(8,128)(2,1)}, u32[]{:S(2)}) %copy-start.1) | copy-done | bytes 786456
  29.4 0.0 copy-start.6
  29.4 0.9 %copy-done.6 = bf16[256,256]{1,0:T(8,128)(2,1)S(1)} copy-done((bf16[256,256]{1,0:T(8,128)(2,1)S(1)}, bf16[256,256]{1,0:T(8,128)(2,1)}, u32[]{:S(2)}) %copy-start.6) | copy-done | bytes 131096
  30.3 0.0 copy-start.8
  30.3 0.9 %copy-done.8 = f32[256,8]{1,0:T(8,128)S(1)} copy-done((f32[256,8]{1,0:T(8,128)S(1)}, f32[256,8]{1,0:T(8,128)}, u32[]{:S(2)}) %copy-start.8) | copy-done | bytes 8216
  31.2 0.0 copy-start.10
  31.2 0.8 %copy-done.10 = bf16[256,64]{1,0:T(8,128)(2,1)S(1)} copy-done((bf16[256,64]{1,0:T(8,128)(2,1)S(1)}, bf16[256,64]{1,0:T(8,128)(2,1)}, u32[]{:S(2)}) %copy-start.10) | copy-done | bytes 32792
  32.0 0.0 copy-start.4
  32.0 4.0 %shard_map.135 = (f32[216,128]{1,0:T(8,128)S(1)}, f32[216,128]{1,0:T(8,128)S(1)}, f32[1536,128]{1,0:T(8,128)S(1)}) custom-call(f32[2880,128]{1,0:T(8,128)S(1)} %get-tuple-element.47.coef, bf16[768,512]{1,0:T(8,128)(2,1)S(1)} %get-tuple-element.48.tops, bf16[768,512]{1,0:T(8,128)(2,1)S(1)} %copy-done.1, f32[256,512]{1,0:T(8,128)S(1)} %get-tuple-element.50.wide, ...), custom_call_target="tpu_custom_call" | custom-call | flops 20000000 | bytes 5840896 | tf_op jit(solution)/shard_map/pallas_call | solution.py:35
  36.1 2.5 %collective-permute-start.6 = (f32[216,128]{1,0:T(8,128)S(1)}, f32[216,128]{1,0:T(8,128)S(1)}, u32[]{:S(2)}, u32[]{:S(2)}) collective-permute-start(f32[216,128]{1,0:T(8,128)S(1)} %get-tuple-element.57), channel_id=1, source_target_pairs={{0,4},{4,0},{8,12},{12,8},{16,20},{20,16},{24,28},{28,24},{1,5},{5... | collective-permute-start | bytes 331784 | tf_op jit(solution)/shard_map/ppermute | solution.py:47
  38.6 0.0 collective-permute-start.7
  38.6 4.0 %collective-permute-done.6.refs_3_ = f32[216,128]{1,0:T(8,128)S(1)} collective-permute-done((f32[216,128]{1,0:T(8,128)S(1)}, f32[216,128]{1,0:T(8,128)S(1)}, u32[]{:S(2)}, u32[]{:S(2)}) %collective-permute-start.6) | collective-permute-done | bytes 110624 | tf_op jit(solution)/shard_map/ppermute | solution.py:47
  42.6 0.0 collective-permute-done.7.refs_4_
  42.6 0.0 copy-done.4
  42.6 0.4 shard_map.136
  43.0 0.0 collective-permute-start.8
  43.0 1.2 %collective-permute-start.9 = (f32[208,128]{1,0:T(8,128)S(1)}, f32[208,128]{1,0:T(8,128)S(1)}, u32[]{:S(2)}, u32[]{:S(2)}) collective-permute-start(f32[208,128]{1,0:T(8,128)S(1)} %get-tuple-element.62), channel_id=1, source_target_pairs={{0,3},{1,2},{2,1},{3,0},{4,7},{5,6},{6,5},{7,4},{8,11},{9,10},{10,... | collective-permute-start | bytes 319496 | tf_op jit(solution)/shard_map/ppermute | solution.py:69
  44.2 1.0 %collective-permute-start.10 = (f32[16,128]{1,0:T(8,128)S(1)}, f32[16,128]{1,0:T(8,128)S(1)}, u32[]{:S(2)}, u32[]{:S(2)}) collective-permute-start(f32[16,128]{1,0:T(8,128)S(1)} %get-tuple-element.63), channel_id=1, source_target_pairs={{0,2},{1,3},{2,0},{3,1},{4,6},{5,7},{6,4},{7,5},{8,10},{9,11},{10,... | collective-permute-start | bytes 24584 | tf_op jit(solution)/shard_map/ppermute | solution.py:47
  45.1 3.4 %collective-permute-done.10.rest_0_ = f32[16,128]{1,0:T(8,128)S(1)} collective-permute-done((f32[16,128]{1,0:T(8,128)S(1)}, f32[16,128]{1,0:T(8,128)S(1)}, u32[]{:S(2)}, u32[]{:S(2)}) %collective-permute-start.10) | collective-permute-done | bytes 8224 | tf_op jit(solution)/shard_map/ppermute | solution.py:47
  48.5 0.0 collective-permute-done.8.y_a
  48.5 0.0 collective-permute-done.9.y_b
  48.5 0.9 %shard_map.137 = (f32[4,256,128]{2,1,0:T(8,128)}, f32[16,128]{1,0:T(8,128)}) custom-call(f32[16,128]{1,0:T(8,128)S(1)} %get-tuple-element.34.refs_2_.alpha, f32[4,256,128]{2,1,0:T(8,128)S(1)} %get-tuple-element.59.near, f32[16,128]{1,0:T(8,128)S(1)} %get-tuple-element.60.sums, f32[208,128]{1,0:T(8,128)S(1)} %collective-permute-done.8.y_a, ...), custom_call_target="tpu_custom_call" | custom-call | flops 1000000 | bytes 761856 | tf_op jit(solution)/shard_map/pallas_call | solution.py:35
Async XLA Ops:
  0.6 17.6 %copy-start.2 = (f32[1,1,256,4,128]{4,3,2,1,0:T(4,128)S(1)}, f32[1,1,256,4,128]{4,3,2,1,0:T(4,128)}, u32[]{:S(2)}) copy-start(f32[1,1,256,4,128]{4,3,2,1,0:T(4,128)} %param.22) | copy-start | bytes 1572868
  2.1 8.2 %collective-permute-start = (f32[320,128]{1,0:T(8,128)S(1)}, f32[320,128]{1,0:T(8,128)S(1)}, u32[]{:S(2)}, u32[]{:S(2)}) collective-permute-start(f32[320,128]{1,0:T(8,128)S(1)} %get-tuple-element.39), channel_id=1, source_target_pairs={{0,1},{1,0},{2,3},{3,2},{4,5},{5,4},{6,7},{7,6},{8,9},{9,8},{10,11... | collective-permute-start | bytes 491528 | tf_op jit(solution)/shard_map/ppermute | solution.py:47
  2.6 7.7 %collective-permute-start.1 = (f32[304,128]{1,0:T(8,128)S(1)}, f32[304,128]{1,0:T(8,128)S(1)}, u32[]{:S(2)}, u32[]{:S(2)}) collective-permute-start(f32[304,128]{1,0:T(8,128)S(1)} %get-tuple-element.40), channel_id=1, source_target_pairs={{0,4},{1,2},{2,1},{3,7},{4,0},{5,6},{6,5},{7,3},{8,12},{9,10},{10,... | collective-permute-start | bytes 466952 | tf_op jit(solution)/shard_map/ppermute | solution.py:63
  5.2 3.3 %collective-permute-start.3 = (f32[16,128]{1,0:T(8,128)}, f32[16,128]{1,0:T(8,128)S(1)}, u32[]{:S(2)}, u32[]{:S(2)}) collective-permute-start(f32[16,128]{1,0:T(8,128)} %bitcast.24), channel_id=1, source_target_pairs={{0,3},{1,2},{2,1},{3,0},{4,7},{5,6},{6,5},{7,4},{8,11},{9,10},{10,... | collective-permute-start | bytes 24584 | tf_op jit(solution)/shard_map/ppermute | solution.py:47
  6.4 3.9 %collective-permute-start.2 = (f32[16,128]{1,0:T(8,128)}, f32[16,128]{1,0:T(8,128)S(1)}, u32[]{:S(2)}, u32[]{:S(2)}) collective-permute-start(f32[16,128]{1,0:T(8,128)} %bitcast.25), channel_id=1, source_target_pairs={{0,2},{1,3},{2,0},{3,1},{4,6},{5,7},{6,4},{7,5},{8,10},{9,11},{10,... | collective-permute-start | bytes 24584 | tf_op jit(solution)/shard_map/ppermute | solution.py:47
  11.4 16.9 %all-to-all-start = ((f32[8,24,128]{2,1,0:T(8,128)}), f32[8,24,128]{2,1,0:T(8,128)S(1)}, u32[]{:S(2)}, u32[]{:S(2)}) async-start(f32[8,24,128]{2,1,0:T(8,128)} %bitcast.12), calls=%async_computation | async-start | bytes 196608 | tf_op jit(solution)/shard_map/all_to_all | solution.py:684
  16.3 9.1 %collective-permute-start.4 = (f32[318,128]{1,0:T(8,128)S(1)}, f32[318,128]{1,0:T(8,128)S(1)}, u32[]{:S(2)}, u32[]{:S(2)}) collective-permute-start(f32[318,128]{1,0:T(8,128)S(1)} %get-tuple-element.45), channel_id=1, source_target_pairs={{0,4},{4,0},{8,12},{12,8},{16,20},{20,16},{24,28},{28,24},{1,5},{5... | collective-permute-start | bytes 488456 | tf_op jit(solution)/shard_map/ppermute | solution.py:47
  18.3 7.1 %collective-permute-start.5 = (f32[318,128]{1,0:T(8,128)S(1)}, f32[318,128]{1,0:T(8,128)S(1)}, u32[]{:S(2)}, u32[]{:S(2)}) collective-permute-start(f32[318,128]{1,0:T(8,128)S(1)} %get-tuple-element.46), channel_id=1, source_target_pairs={{0,1},{4,8},{8,4},{12,16},{16,12},{20,24},{24,20},{28,29},{1,0},{5... | collective-permute-start | bytes 488456 | tf_op jit(solution)/shard_map/ppermute | solution.py:63
  19.3 0.7 %copy-start.3 = (f32[384,16]{1,0:T(8,128)}, f32[384,16]{1,0:T(8,128)S(1)}, u32[]{:S(2)}) copy-start(f32[384,16]{1,0:T(8,128)S(1)} %get-tuple-element.41.refs_1_) | copy-start | bytes 73732
  20.0 0.7 %copy-start.5 = (bf16[256,256]{1,0:T(8,128)(2,1)}, bf16[256,256]{1,0:T(8,128)(2,1)S(1)}, u32[]{:S(2)}) copy-start(bf16[256,256]{1,0:T(8,128)(2,1)S(1)} %get-tuple-element.52.slot_push) | copy-start | bytes 393220
  20.6 0.7 %copy-start.7 = (f32[256,8]{1,0:T(8,128)}, f32[256,8]{1,0:T(8,128)S(1)}, u32[]{:S(2)}) copy-start(f32[256,8]{1,0:T(8,128)S(1)} %get-tuple-element.54.columns) | copy-start | bytes 24580
  21.3 0.6 %copy-start.9 = (bf16[256,64]{1,0:T(8,128)(2,1)}, bf16[256,64]{1,0:T(8,128)(2,1)S(1)}, u32[]{:S(2)}) copy-start(bf16[256,64]{1,0:T(8,128)(2,1)S(1)} %get-tuple-element.53.beam_pick) | copy-start | bytes 98308
  27.3 0.9 %copy-start = (bf16[768,512]{1,0:T(8,128)(2,1)}, bf16[768,512]{1,0:T(8,128)(2,1)S(1)}, u32[]{:S(2)}) copy-start(bf16[768,512]{1,0:T(8,128)(2,1)S(1)} %get-tuple-element.49.lows) | copy-start | bytes 2359300
  28.2 1.1 %copy-start.1 = (bf16[768,512]{1,0:T(8,128)(2,1)S(1)}, bf16[768,512]{1,0:T(8,128)(2,1)}, u32[]{:S(2)}) copy-start(bf16[768,512]{1,0:T(8,128)(2,1)} %copy-done) | copy-start | bytes 2359300
  29.4 0.9 %copy-start.6 = (bf16[256,256]{1,0:T(8,128)(2,1)S(1)}, bf16[256,256]{1,0:T(8,128)(2,1)}, u32[]{:S(2)}) copy-start(bf16[256,256]{1,0:T(8,128)(2,1)} %copy-done.5) | copy-start | bytes 393220
  30.3 0.9 %copy-start.8 = (f32[256,8]{1,0:T(8,128)S(1)}, f32[256,8]{1,0:T(8,128)}, u32[]{:S(2)}) copy-start(f32[256,8]{1,0:T(8,128)} %copy-done.7) | copy-start | bytes 24580
  31.2 0.8 %copy-start.10 = (bf16[256,64]{1,0:T(8,128)(2,1)S(1)}, bf16[256,64]{1,0:T(8,128)(2,1)}, u32[]{:S(2)}) copy-start(bf16[256,64]{1,0:T(8,128)(2,1)} %copy-done.9) | copy-start | bytes 98308
  32.0 10.6 %copy-start.4 = (f32[384,16]{1,0:T(8,128)S(1)}, f32[384,16]{1,0:T(8,128)}, u32[]{:S(2)}) copy-start(f32[384,16]{1,0:T(8,128)} %copy-done.3) | copy-start | bytes 73732
  36.1 6.5 %collective-permute-start.6 = (f32[216,128]{1,0:T(8,128)S(1)}, f32[216,128]{1,0:T(8,128)S(1)}, u32[]{:S(2)}, u32[]{:S(2)}) collective-permute-start(f32[216,128]{1,0:T(8,128)S(1)} %get-tuple-element.57), channel_id=1, source_target_pairs={{0,4},{4,0},{8,12},{12,8},{16,20},{20,16},{24,28},{28,24},{1,5},{5... | collective-permute-start | bytes 331784 | tf_op jit(solution)/shard_map/ppermute | solution.py:47
  38.6 4.0 %collective-permute-start.7 = (f32[216,128]{1,0:T(8,128)S(1)}, f32[216,128]{1,0:T(8,128)S(1)}, u32[]{:S(2)}, u32[]{:S(2)}) collective-permute-start(f32[216,128]{1,0:T(8,128)S(1)} %get-tuple-element.58), channel_id=1, source_target_pairs={{0,1},{4,8},{8,4},{12,16},{16,12},{20,24},{24,20},{28,29},{1,0},{5... | collective-permute-start | bytes 331784 | tf_op jit(solution)/shard_map/ppermute | solution.py:63
  43.0 5.5 %collective-permute-start.8 = (f32[208,128]{1,0:T(8,128)S(1)}, f32[208,128]{1,0:T(8,128)S(1)}, u32[]{:S(2)}, u32[]{:S(2)}) collective-permute-start(f32[208,128]{1,0:T(8,128)S(1)} %get-tuple-element.61), channel_id=1, source_target_pairs={{0,1},{1,0},{2,3},{3,2},{4,5},{5,4},{6,7},{7,6},{8,9},{9,8},{10,11... | collective-permute-start | bytes 319496 | tf_op jit(solution)/shard_map/ppermute | solution.py:47
  43.0 5.5 %collective-permute-start.9 = (f32[208,128]{1,0:T(8,128)S(1)}, f32[208,128]{1,0:T(8,128)S(1)}, u32[]{:S(2)}, u32[]{:S(2)}) collective-permute-start(f32[208,128]{1,0:T(8,128)S(1)} %get-tuple-element.62), channel_id=1, source_target_pairs={{0,3},{1,2},{2,1},{3,0},{4,7},{5,6},{6,5},{7,4},{8,11},{9,10},{10,... | collective-permute-start | bytes 319496 | tf_op jit(solution)/shard_map/ppermute | solution.py:69
  44.2 4.3 %collective-permute-start.10 = (f32[16,128]{1,0:T(8,128)S(1)}, f32[16,128]{1,0:T(8,128)S(1)}, u32[]{:S(2)}, u32[]{:S(2)}) collective-permute-start(f32[16,128]{1,0:T(8,128)S(1)} %get-tuple-element.63), channel_id=1, source_target_pairs={{0,2},{1,3},{2,0},{3,1},{4,6},{5,7},{6,4},{7,5},{8,10},{9,11},{10,... | collective-permute-start | bytes 24584 | tf_op jit(solution)/shard_map/ppermute | solution.py:47

commit v8 on v4

--- a/solution.py
+++ b/solution.py
@@ -175,7 +175,7 @@
     held = BEAM_BITS
     beam = gates[0]
     owner = jnp.bitwise_xor(beam >> held, lax.axis_index("gx"))
-    block = (owner & -4) | ((owner & 1) << 1) | ((owner >> 1) & 1)
+    block = (owner >> 1) + (owner & 1) * (lax.axis_size("gx") // 2)
     meta[...] = jnp.zeros(meta.shape, f32)
     meta[0:1] = gates[2].astype(f32)
     meta[1:2] = ((block << held) | (beam & ((1 << held) - 1))).astype(f32)
@@ -232,9 +232,9 @@
     return jnp.concatenate([ref[pl.ds(c, count, stride=NC)] for c in range(NC)], axis=1)
 
 
-def pack_x(ny, delta, coefs, alpha, near_tiles, y_a, y_b, own_beams, got_beams, *rest):
+def pack_x(ny, delta, coefs, alpha, near_tiles, y_a, y_b, beams, *rest):
     others = rest[: ny - 2]
-    out_a, out_b, beams, field, picks, known, tiles = rest[ny - 2 :]
+    out_a, out_b, field, picks, known, tiles = rest[ny - 2 :]
     even, _, _ = place_on("gx")
     owned = alpha.shape[0] // NC
     gather_known(alpha, y_a, others, known)
@@ -280,9 +280,6 @@
     for f in range(3):
         fill(coefs.at[f], Y_COEF + f * INNER * CX, INNER, None)
         put(X_COEF + f * SLIM_ROWS, SLIM)
-    half = own_beams.shape[0]
-    beams[0:half] = own_beams[...]
-    beams[half:] = got_beams[...]
     out_a[X_HALO:] = beams[...]
 
 
@@ -439,7 +436,7 @@
     columns,
     *rest,
 ):
-    beams = rest[:-6]
+    beams, x_a = rest[:-6]
     out_a, out_b, out_core, state_0, state_1, forcing = rest[-6:]
     even, _, _ = place_on("gx")
     slots = columns.shape[0]
@@ -452,8 +449,8 @@
         picked = picked + jnp.dot(slot_pick[...], lows[rows], preferred_element_type=f32)
         picked = picked * wide[...]
         table = []
-        for part in beams:
-            for at in range(0, part.shape[0], STEPS * OWN_BEAMS):
+        for part, low in ((beams, 0), (x_a, X_HALO)):
+            for at in range(low, part.shape[0], STEPS * OWN_BEAMS):
                 first = at + step * OWN_BEAMS
                 table.append(part[first : first + OWN_BEAMS])
         table = two_part_dot(beam_pick[...], jnp.concatenate(table, axis=0))
@@ -652,12 +649,15 @@
     y_a = swap(y_a, "gy", 1)
     y_b = pair_b(y_b, "gy", "gx")
     others = [swap(control, "gy", xor) for xor in range(2, ny)]
-    got_beams = swap(own_beams, "gx", 2)
-
-    x_a, x_b, beams = call(
+    beams, xor = near_beams, 2
+    while xor < nx:
+        beams = jnp.concatenate([beams, swap(beams, "gx", xor)])
+        xor *= 2
+
+    x_a, x_b = call(
         lambda *refs: pack_x(ny, *refs),
-        [(X_HALO + 2 * own_beams.shape[0], 128), (X_HALO, 128), (2 * own_beams.shape[0], 128)],
-        [fine, coefs, control_near, near_tiles, y_a, y_b, near_beams, got_beams, *others],
+        [(X_HALO + beams.shape[0], 128), (X_HALO, 128)],
+        [fine, coefs, control_near, near_tiles, y_a, y_b, beams, *others],
         [
             pltpu.VMEM((2 * RIM * PITCH, 128), f32),
             pltpu.VMEM((2 * RIM * PITCH, total), f32),
@@ -688,11 +688,6 @@
         flops=3000000,
     )
 
-    beams = [beams, x_a[X_HALO:]]
-    xor = 4
-    while xor < nx:
-        beams = beams + [swap(jnp.concatenate(beams), "gx", xor)]
-        xor *= 2
 
     tops, lows, coef = call(
         forecast,
@@ -712,7 +707,7 @@
     back_a, back_b, core = call(
         main,
         [(X_COEF, 128), (X_COEF, 128), (NC * CORE, 128)],
-        [coef, tops, lows, wide, slot_pick, slot_push, beam_pick, columns, *beams],
+        [coef, tops, lows, wide, slot_pick, slot_push, beam_pick, columns, beams, x_a],
         [
             pltpu.VMEM((NC * FIELD, 128), f32),
             pltpu.VMEM((NC * FIELD, 128), f32),

time: 43.5 us -> 42.1 us (0.968)
  the two profiles are of different devices: /device:TPU:0 before, /device:TPU:16 now
where the time goes in v8:
time: 42.1 us; the launch traced here: 41.9 us
  waiting for transfers between devices  20.5 us (49%)
  starting transfers between devices  10.5 us (25%)
  Pallas kernels  10.2 us (24%)
  between operations  0.71 us (2%)
    ppermute x9, waiting for transfers between devices, swap(): lax.ppermute(block, axis, [(i, i ^ xor) for i in range(lax.axis_size(axis...  13.9 us
    pallas_call x7, Pallas kernels, call(): pl.pallas_call(body, out_shape=shapes, in_specs=in_specs or [VMEM] * len(...  10.2 us
    ppermute x9, starting transfers between devices, swap(): lax.ppermute(block, axis, [(i, i ^ xor) for i in range(lax.axis_size(axis...  7.19 us
    ppermute x3, waiting for transfers between devices, pair_b(): return lax.ppermute(block, ('gx', 'gy'), pairs)  6.64 us
    ppermute x3, starting transfers between devices, pair_b(): return lax.ppermute(block, ('gx', 'gy'), pairs)  2.01 us
    ppermute x1, starting transfers between devices, ring_b(): return lax.ppermute(block, axis, pairs)  1.27 us
  transfers between devices with their start and end apart: 13, of which 7 were waited for; matrix products, arithmetic and copies ran while one was open for 0% of the time, Pallas kernels for 6%

profile of v8, /device:TPU:16, one launch (start us, length us, event | category | flops | bytes accessed | tf_op | source)
XLA Modules:
  0.0 41.9 jit_solution(16574822518532916428)
XLA Ops:
  0.6 0.0 copy-start
  0.6 1.0 %collective-permute-start.3 = (f32[16,128]{1,0:T(8,128)}, f32[16,128]{1,0:T(8,128)S(1)}, u32[]{:S(2)}, u32[]{:S(2)}) collective-permute-start(f32[16,128]{1,0:T(8,128)} %bitcast.20), channel_id=1, source_target_pairs={{0,3},{1,2},{2,1},{3,0},{4,7},{5,6},{6,5},{7,4},{8,11},{9,10},{10,... | collective-permute-start | bytes 24584 | tf_op jit(solution)/shard_map/ppermute | solution.py:48
  1.6 0.6 %collective-permute-start.2 = (f32[16,128]{1,0:T(8,128)}, f32[16,128]{1,0:T(8,128)S(1)}, u32[]{:S(2)}, u32[]{:S(2)}) collective-permute-start(f32[16,128]{1,0:T(8,128)} %bitcast.21), channel_id=1, source_target_pairs={{0,2},{1,3},{2,0},{3,1},{4,6},{5,7},{6,4},{7,5},{8,10},{9,11},{10,... | collective-permute-start | bytes 24584 | tf_op jit(solution)/shard_map/ppermute | solution.py:48
  2.3 1.4 %shard_map.131 = (f32[320,128]{1,0:T(8,128)S(1)}, f32[304,128]{1,0:T(8,128)S(1)}, f32[4,256,128]{2,1,0:T(8,128)S(1)}, f32[3,256,128]{2,1,0:T(8,128)S(1)}, f32[16...) custom-call(f32[4,256,128]{2,1,0:T(8,128)} %bitcast.16, ...), custom_call_target="tpu_custom_call" | custom-call | flops 1000000 | bytes 944128 | tf_op jit(solution)/shard_map/pallas_call | solution.py:36
  3.6 1.6 %collective-permute-start.4 = (f32[24,128]{1,0:T(8,128)S(1)}, f32[24,128]{1,0:T(8,128)S(1)}, u32[]{:S(2)}, u32[]{:S(2)}) collective-permute-start(f32[24,128]{1,0:T(8,128)S(1)} %get-tuple-element.43), channel_id=1, source_target_pairs={{0,8},{4,12},{8,0},{12,4},{16,24},{20,28},{24,16},{28,20},{1,9},{5... | collective-permute-start | bytes 36872 | tf_op jit(solution)/shard_map/ppermute | solution.py:48
  5.3 1.5 %collective-permute-start.1 = (f32[304,128]{1,0:T(8,128)S(1)}, f32[304,128]{1,0:T(8,128)S(1)}, u32[]{:S(2)}, u32[]{:S(2)}) collective-permute-start(f32[304,128]{1,0:T(8,128)S(1)} %get-tuple-element.39), channel_id=1, source_target_pairs={{0,4},{1,2},{2,1},{3,7},{4,0},{5,6},{6,5},{7,3},{8,12},{9,10},{10,... | collective-permute-start | bytes 466952 | tf_op jit(solution)/shard_map/ppermute | solution.py:64
  6.8 0.0 collective-permute-start
  6.8 0.6 %collective-permute-done.4 = f32[24,128]{1,0:T(8,128)S(1)} collective-permute-done((f32[24,128]{1,0:T(8,128)S(1)}, f32[24,128]{1,0:T(8,128)S(1)}, u32[]{:S(2)}, u32[]{:S(2)}) %collective-permute-start.4) | collective-permute-done | bytes 12320 | tf_op jit(solution)/shard_map/ppermute | solution.py:48
  7.4 0.3 collective-permute-start.5
  7.7 4.4 %collective-permute-done.5 = f32[48,128]{1,0:T(8,128)S(1)} collective-permute-done((f32[48,128]{1,0:T(8,128)S(1)}, f32[48,128]{1,0:T(8,128)S(1)}, u32[]{:S(2)}, u32[]{:S(2)}) %collective-permute-start.5) | collective-permute-done | bytes 24608 | tf_op jit(solution)/shard_map/ppermute | solution.py:48
  12.1 0.0 collective-permute-done.3.refs_9_.refs_8_
  12.2 0.0 collective-permute-done.2.refs_8_.refs_7_
  12.2 0.0 collective-permute-done.1.refs_7_.refs_5_
  12.2 0.0 collective-permute-done.refs_6_.refs_4_
  12.2 0.5 %shard_map.133 = (f32[414,128]{1,0:T(8,128)S(1)}, f32[318,128]{1,0:T(8,128)S(1)}) custom-call(f32[4,256,128]{2,1,0:T(8,128)S(1)} %get-tuple-element.34.refs_0_, f32[3,256,128]{2,1,0:T(8,128)S(1)} %get-tuple-element.35.refs_1_, f32[16,128]{1,0:T(8,128)S(1)} %get-tuple-element.33.refs_2_.alpha, f32[16,128]{1,0:T(8,128)S(1)} %get-tuple-element.36.refs_3_, ...), custom_call_target="tpu_custom_call" | custom-call | flops 1000000 | bytes 1318912 | tf_op jit(solution)/shard_map/pallas_call | solution.py:36
  12.7 1.6 %collective-permute-start.6 = (f32[414,128]{1,0:T(8,128)S(1)}, f32[414,128]{1,0:T(8,128)S(1)}, u32[]{:S(2)}, u32[]{:S(2)}) collective-permute-start(f32[414,128]{1,0:T(8,128)S(1)} %get-tuple-element.44), channel_id=1, source_target_pairs={{0,4},{4,0},{8,12},{12,8},{16,20},{20,16},{24,28},{28,24},{1,5},{5... | collective-permute-start | bytes 635912 | tf_op jit(solution)/shard_map/ppermute | solution.py:48
  14.3 0.4 collective-permute-start.7
  14.7 0.0 copy-done
  14.7 1.0 %shard_map.132 = (f32[1536,128]{1,0:T(8,128)S(1)}, f32[1920,128]{1,0:T(8,128)S(1)}, f32[384,16]{1,0:T(8,128)S(1)}, f32[256,512]{1,0:T(8,128)S(1)}, bf16[256,256]...) custom-call(f32[4,256,128]{2,1,0:T(8,128)S(1)} %get-tuple-element.34.refs_0_, ...), custom_call_target="tpu_custom_call" | custom-call | flops 3000000 | bytes 1802240 | tf_op jit(solution)/shard_map/pallas_call | solution.py:36
  15.7 4.9 %collective-permute-done.7.x_b = f32[318,128]{1,0:T(8,128)S(1)} collective-permute-done((f32[318,128]{1,0:T(8,128)S(1)}, f32[318,128]{1,0:T(8,128)S(1)}, u32[]{:S(2)}, u32[]{:S(2)}) %collective-permute-start.7) | collective-permute-done | bytes 162848 | tf_op jit(solution)/shard_map/ppermute | solution.py:64
  20.6 1.7 %collective-permute-done.6.x_a.rest_1_ = f32[414,128]{1,0:T(8,128)S(1)} collective-permute-done((f32[414,128]{1,0:T(8,128)S(1)}, f32[414,128]{1,0:T(8,128)S(1)}, u32[]{:S(2)}, u32[]{:S(2)}) %collective-permute-start.6) | collective-permute-done | bytes 212000 | tf_op jit(solution)/shard_map/ppermute | solution.py:48
  22.3 2.0 %shard_map.134 = (bf16[768,512]{1,0:T(8,128)(2,1)S(1)}, bf16[768,512]{1,0:T(8,128)(2,1)S(1)}, f32[2880,128]{1,0:T(8,128)S(1)}) custom-call(f32[1536,128]{1,0:T(8,128)S(1)} %get-tuple-element.41.core, f32[1920,128]{1,0:T(8,128)S(1)} %get-tuple-element.42.coef_core, f32[414,128]{1,0:T(8,128)S(1)} %collective-permute-done.6.x_a.rest_1_, ...), custom_call_target="tpu_custom_call" | custom-call | flops 10000000 | bytes 2144256 | tf_op jit(solution)/shard_map/pallas_call | solution.py:36
  24.3 4.0 %shard_map.135 = (f32[216,128]{1,0:T(8,128)S(1)}, f32[216,128]{1,0:T(8,128)S(1)}, f32[1536,128]{1,0:T(8,128)S(1)}) custom-call(f32[2880,128]{1,0:T(8,128)S(1)} %get-tuple-element.46.coef, bf16[768,512]{1,0:T(8,128)(2,1)S(1)} %get-tuple-element.47.tops, bf16[768,512]{1,0:T(8,128)(2,1)S(1)} %get-tuple-element.48.lows, f32[256,512]{1,0:T(8,128)S(1)} %get-tuple-element.49.wide, ...), custom_call_target="tpu_custom_call" | custom-call | flops 20000000 | bytes 6003712 | tf_op jit(solution)/shard_map/pallas_call | solution.py:36
  28.3 1.1 %collective-permute-start.8 = (f32[216,128]{1,0:T(8,128)S(1)}, f32[216,128]{1,0:T(8,128)S(1)}, u32[]{:S(2)}, u32[]{:S(2)}) collective-permute-start(f32[216,128]{1,0:T(8,128)S(1)} %get-tuple-element.55), channel_id=1, source_target_pairs={{0,4},{4,0},{8,12},{12,8},{16,20},{20,16},{24,28},{28,24},{1,5},{5... | collective-permute-start | bytes 331784 | tf_op jit(solution)/shard_map/ppermute | solution.py:48
  29.4 0.1 collective-permute-start.9
  29.5 3.8 %collective-permute-done.8.refs_3_ = f32[216,128]{1,0:T(8,128)S(1)} collective-permute-done((f32[216,128]{1,0:T(8,128)S(1)}, f32[216,128]{1,0:T(8,128)S(1)}, u32[]{:S(2)}, u32[]{:S(2)}) %collective-permute-start.8) | collective-permute-done | bytes 110624 | tf_op jit(solution)/shard_map/ppermute | solution.py:48
  33.4 1.7 %collective-permute-done.9.refs_4_ = f32[216,128]{1,0:T(8,128)S(1)} collective-permute-done((f32[216,128]{1,0:T(8,128)S(1)}, f32[216,128]{1,0:T(8,128)S(1)}, u32[]{:S(2)}, u32[]{:S(2)}) %collective-permute-start.9) | collective-permute-done | bytes 110624 | tf_op jit(solution)/shard_map/ppermute | solution.py:64
  35.1 0.4 shard_map.136
  35.5 0.0 collective-permute-start.10
  35.5 1.3 %collective-permute-start.11 = (f32[208,128]{1,0:T(8,128)S(1)}, f32[208,128]{1,0:T(8,128)S(1)}, u32[]{:S(2)}, u32[]{:S(2)}) collective-permute-start(f32[208,128]{1,0:T(8,128)S(1)} %get-tuple-element.60), channel_id=1, source_target_pairs={{0,3},{1,2},{2,1},{3,0},{4,7},{5,6},{6,5},{7,4},{8,11},{9,10},{10,... | collective-permute-start | bytes 319496 | tf_op jit(solution)/shard_map/ppermute | solution.py:70
  36.7 0.9 %collective-permute-start.12 = (f32[16,128]{1,0:T(8,128)S(1)}, f32[16,128]{1,0:T(8,128)S(1)}, u32[]{:S(2)}, u32[]{:S(2)}) collective-permute-start(f32[16,128]{1,0:T(8,128)S(1)} %get-tuple-element.61), channel_id=1, source_target_pairs={{0,2},{1,3},{2,0},{3,1},{4,6},{5,7},{6,4},{7,5},{8,10},{9,11},{10,... | collective-permute-start | bytes 24584 | tf_op jit(solution)/shard_map/ppermute | solution.py:48
  37.6 3.4 %collective-permute-done.12.rest_0_ = f32[16,128]{1,0:T(8,128)S(1)} collective-permute-done((f32[16,128]{1,0:T(8,128)S(1)}, f32[16,128]{1,0:T(8,128)S(1)}, u32[]{:S(2)}, u32[]{:S(2)}) %collective-permute-start.12) | collective-permute-done | bytes 8224 | tf_op jit(solution)/shard_map/ppermute | solution.py:48
  41.0 0.0 collective-permute-done.10.y_a
  41.0 0.0 collective-permute-done.11.y_b
  41.0 0.9 %shard_map.137 = (f32[4,256,128]{2,1,0:T(8,128)}, f32[16,128]{1,0:T(8,128)}) custom-call(f32[16,128]{1,0:T(8,128)S(1)} %get-tuple-element.33.refs_2_.alpha, f32[4,256,128]{2,1,0:T(8,128)S(1)} %get-tuple-element.57.near, f32[16,128]{1,0:T(8,128)S(1)} %get-tuple-element.58.sums, f32[208,128]{1,0:T(8,128)S(1)} %collective-permute-done.10.y_a, ...), custom_call_target="tpu_custom_call" | custom-call | flops 1000000 | bytes 761856 | tf_op jit(solution)/shard_map/pallas_call | solution.py:36
  (4 shorter events, 0.0 us)
Async XLA Ops:
  0.6 14.1 %copy-start = (f32[1,1,256,4,128]{4,3,2,1,0:T(4,128)S(1)}, f32[1,1,256,4,128]{4,3,2,1,0:T(4,128)}, u32[]{:S(2)}) copy-start(f32[1,1,256,4,128]{4,3,2,1,0:T(4,128)} %param.22) | copy-start | bytes 1572868
  0.6 11.5 %collective-permute-start.3 = (f32[16,128]{1,0:T(8,128)}, f32[16,128]{1,0:T(8,128)S(1)}, u32[]{:S(2)}, u32[]{:S(2)}) collective-permute-start(f32[16,128]{1,0:T(8,128)} %bitcast.20), channel_id=1, source_target_pairs={{0,3},{1,2},{2,1},{3,0},{4,7},{5,6},{6,5},{7,4},{8,11},{9,10},{10,... | collective-permute-start | bytes 24584 | tf_op jit(solution)/shard_map/ppermute | solution.py:48
  1.6 10.5 %collective-permute-start.2 = (f32[16,128]{1,0:T(8,128)}, f32[16,128]{1,0:T(8,128)S(1)}, u32[]{:S(2)}, u32[]{:S(2)}) collective-permute-start(f32[16,128]{1,0:T(8,128)} %bitcast.21), channel_id=1, source_target_pairs={{0,2},{1,3},{2,0},{3,1},{4,6},{5,7},{6,4},{7,5},{8,10},{9,11},{10,... | collective-permute-start | bytes 24584 | tf_op jit(solution)/shard_map/ppermute | solution.py:48
  3.6 3.8 %collective-permute-start.4 = (f32[24,128]{1,0:T(8,128)S(1)}, f32[24,128]{1,0:T(8,128)S(1)}, u32[]{:S(2)}, u32[]{:S(2)}) collective-permute-start(f32[24,128]{1,0:T(8,128)S(1)} %get-tuple-element.43), channel_id=1, source_target_pairs={{0,8},{4,12},{8,0},{12,4},{16,24},{20,28},{24,16},{28,20},{1,9},{5... | collective-permute-start | bytes 36872 | tf_op jit(solution)/shard_map/ppermute | solution.py:48
  5.3 6.9 %collective-permute-start.1 = (f32[304,128]{1,0:T(8,128)S(1)}, f32[304,128]{1,0:T(8,128)S(1)}, u32[]{:S(2)}, u32[]{:S(2)}) collective-permute-start(f32[304,128]{1,0:T(8,128)S(1)} %get-tuple-element.39), channel_id=1, source_target_pairs={{0,4},{1,2},{2,1},{3,7},{4,0},{5,6},{6,5},{7,3},{8,12},{9,10},{10,... | collective-permute-start | bytes 466952 | tf_op jit(solution)/shard_map/ppermute | solution.py:64
  6.8 5.4 %collective-permute-start = (f32[320,128]{1,0:T(8,128)S(1)}, f32[320,128]{1,0:T(8,128)S(1)}, u32[]{:S(2)}, u32[]{:S(2)}) collective-permute-start(f32[320,128]{1,0:T(8,128)S(1)} %get-tuple-element.38), channel_id=1, source_target_pairs={{0,1},{1,0},{2,3},{3,2},{4,5},{5,4},{6,7},{7,6},{8,9},{9,8},{10,11... | collective-permute-start | bytes 491528 | tf_op jit(solution)/shard_map/ppermute | solution.py:48
  7.4 4.7 %collective-permute-start.5 = (f32[48,128]{1,0:T(8,128)S(1)}, f32[48,128]{1,0:T(8,128)S(1)}, u32[]{:S(2)}, u32[]{:S(2)}) collective-permute-start(f32[48,128]{1,0:T(8,128)S(1)} %pad_maximum_fusion), channel_id=1, source_target_pairs={{0,16},{4,20},{8,24},{12,28},{16,0},{20,4},{24,8},{28,12},{1,17},{... | collective-permute-start | bytes 73736 | tf_op jit(solution)/shard_map/ppermute | solution.py:48
  12.7 9.6 %collective-permute-start.6 = (f32[414,128]{1,0:T(8,128)S(1)}, f32[414,128]{1,0:T(8,128)S(1)}, u32[]{:S(2)}, u32[]{:S(2)}) collective-permute-start(f32[414,128]{1,0:T(8,128)S(1)} %get-tuple-element.44), channel_id=1, source_target_pairs={{0,4},{4,0},{8,12},{12,8},{16,20},{20,16},{24,28},{28,24},{1,5},{5... | collective-permute-start | bytes 635912 | tf_op jit(solution)/shard_map/ppermute | solution.py:48
  14.3 6.3 %collective-permute-start.7 = (f32[318,128]{1,0:T(8,128)S(1)}, f32[318,128]{1,0:T(8,128)S(1)}, u32[]{:S(2)}, u32[]{:S(2)}) collective-permute-start(f32[318,128]{1,0:T(8,128)S(1)} %get-tuple-element.45), channel_id=1, source_target_pairs={{0,1},{4,8},{8,4},{12,16},{16,12},{20,24},{24,20},{28,29},{1,0},{5... | collective-permute-start | bytes 488456 | tf_op jit(solution)/shard_map/ppermute | solution.py:64
  28.3 5.1 %collective-permute-start.8 = (f32[216,128]{1,0:T(8,128)S(1)}, f32[216,128]{1,0:T(8,128)S(1)}, u32[]{:S(2)}, u32[]{:S(2)}) collective-permute-start(f32[216,128]{1,0:T(8,128)S(1)} %get-tuple-element.55), channel_id=1, source_target_pairs={{0,4},{4,0},{8,12},{12,8},{16,20},{20,16},{24,28},{28,24},{1,5},{5... | collective-permute-start | bytes 331784 | tf_op jit(solution)/shard_map/ppermute | solution.py:48
  29.4 5.6 %collective-permute-start.9 = (f32[216,128]{1,0:T(8,128)S(1)}, f32[216,128]{1,0:T(8,128)S(1)}, u32[]{:S(2)}, u32[]{:S(2)}) collective-permute-start(f32[216,128]{1,0:T(8,128)S(1)} %get-tuple-element.56), channel_id=1, source_target_pairs={{0,1},{4,8},{8,4},{12,16},{16,12},{20,24},{24,20},{28,29},{1,0},{5... | collective-permute-start | bytes 331784 | tf_op jit(solution)/shard_map/ppermute | solution.py:64
  35.5 5.5 %collective-permute-start.10 = (f32[208,128]{1,0:T(8,128)S(1)}, f32[208,128]{1,0:T(8,128)S(1)}, u32[]{:S(2)}, u32[]{:S(2)}) collective-permute-start(f32[208,128]{1,0:T(8,128)S(1)} %get-tuple-element.59), channel_id=1, source_target_pairs={{0,1},{1,0},{2,3},{3,2},{4,5},{5,4},{6,7},{7,6},{8,9},{9,8},{10,11... | collective-permute-start | bytes 319496 | tf_op jit(solution)/shard_map/ppermute | solution.py:48
  35.5 5.5 %collective-permute-start.11 = (f32[208,128]{1,0:T(8,128)S(1)}, f32[208,128]{1,0:T(8,128)S(1)}, u32[]{:S(2)}, u32[]{:S(2)}) collective-permute-start(f32[208,128]{1,0:T(8,128)S(1)} %get-tuple-element.60), channel_id=1, source_target_pairs={{0,3},{1,2},{2,1},{3,0},{4,7},{5,6},{6,5},{7,4},{8,11},{9,10},{10,... | collective-permute-start | bytes 319496 | tf_op jit(solution)/shard_map/ppermute | solution.py:70
  36.7 4.2 %collective-permute-start.12 = (f32[16,128]{1,0:T(8,128)S(1)}, f32[16,128]{1,0:T(8,128)S(1)}, u32[]{:S(2)}, u32[]{:S(2)}) collective-permute-start(f32[16,128]{1,0:T(8,128)S(1)} %get-tuple-element.61), channel_id=1, source_target_pairs={{0,2},{1,3},{2,0},{3,1},{4,6},{5,7},{6,4},{7,5},{8,10},{9,11},{10,... | collective-permute-start | bytes 24584 | tf_op jit(solution)/shard_map/ppermute | solution.py:48

commit v9 on v4

--- a/solution.py
+++ b/solution.py
@@ -232,9 +232,9 @@
     return jnp.concatenate([ref[pl.ds(c, count, stride=NC)] for c in range(NC)], axis=1)
 
 
-def pack_x(ny, delta, coefs, alpha, near_tiles, y_a, y_b, own_beams, got_beams, *rest):
+def pack_x(ny, delta, coefs, alpha, near_tiles, y_a, y_b, *rest):
     others = rest[: ny - 2]
-    out_a, out_b, beams, field, picks, known, tiles = rest[ny - 2 :]
+    out_a, out_b, field, picks, known, tiles = rest[ny - 2 :]
     even, _, _ = place_on("gx")
     owned = alpha.shape[0] // NC
     gather_known(alpha, y_a, others, known)
@@ -280,10 +280,6 @@
     for f in range(3):
         fill(coefs.at[f], Y_COEF + f * INNER * CX, INNER, None)
         put(X_COEF + f * SLIM_ROWS, SLIM)
-    half = own_beams.shape[0]
-    beams[0:half] = own_beams[...]
-    beams[half:] = got_beams[...]
-    out_a[X_HALO:] = beams[...]
 
 
 def prepare(ny, delta, coefs, alpha, near_tiles, meta, weights, y_a, y_b, *rest):
@@ -652,12 +648,13 @@
     y_a = swap(y_a, "gy", 1)
     y_b = pair_b(y_b, "gy", "gx")
     others = [swap(control, "gy", xor) for xor in range(2, ny)]
-    got_beams = swap(own_beams, "gx", 2)
-
-    x_a, x_b, beams = call(
+    beams = jnp.concatenate([near_beams, swap(own_beams, "gx", 2)])
+    beams = [beams] + [swap(beams, "gx", xor) for xor in range(1, nx) if xor % 4 < 2]
+
+    x_a, x_b = call(
         lambda *refs: pack_x(ny, *refs),
-        [(X_HALO + 2 * own_beams.shape[0], 128), (X_HALO, 128), (2 * own_beams.shape[0], 128)],
-        [fine, coefs, control_near, near_tiles, y_a, y_b, near_beams, got_beams, *others],
+        [(X_HALO, 128), (X_HALO, 128)],
+        [fine, coefs, control_near, near_tiles, y_a, y_b, *others],
         [
             pltpu.VMEM((2 * RIM * PITCH, 128), f32),
             pltpu.VMEM((2 * RIM * PITCH, total), f32),
@@ -688,11 +685,6 @@
         flops=3000000,
     )
 
-    beams = [beams, x_a[X_HALO:]]
-    xor = 4
-    while xor < nx:
-        beams = beams + [swap(jnp.concatenate(beams), "gx", xor)]
-        xor *= 2
 
     tops, lows, coef = call(
         forecast,

time: 43.5 us -> 39.2 us (0.901); the launches traced: 43.3 us -> 38.4 us
  waiting for transfers between devices: 17.6 us -> 10.7 us
  starting transfers between devices: 14.7 us -> 16.7 us
    ppermute x9 -> x11, waiting for transfers between devices: 17.6 us -> 10.7 us  [swap(): lax.ppermute(block, axis, [(i, i ^ xor) for i in range(lax.axis_size(axis...]
    ppermute x9 -> x11, starting transfers between devices: 10.5 us -> 13.1 us  [swap(): lax.ppermute(block, axis, [(i, i ^ xor) for i in range(lax.axis_size(axis...]
    ppermute x1, starting transfers between devices: 1.63 us -> 0.98 us  [ring_b(): return lax.ppermute(block, axis, pairs)]
  transfers between devices with their start and end apart: 13 -> 15, of which waited for: 4 -> 5; matrix products, arithmetic and copies ran while one was open for 0% -> 0% of each run, Pallas kernels for 7% -> 9%
where the time goes in v9:
time: 39.2 us; the launch traced here: 38.4 us
  starting transfers between devices  16.7 us (43%)
  waiting for transfers between devices  10.7 us (27%)
  Pallas kernels  10.3 us (26%)
  between operations  0.73 us (2%)
    ppermute x11, starting transfers between devices, swap(): lax.ppermute(block, axis, [(i, i ^ xor) for i in range(lax.axis_size(axis...  13.1 us
    ppermute x11, waiting for transfers between devices, swap(): lax.ppermute(block, axis, [(i, i ^ xor) for i in range(lax.axis_size(axis...  10.7 us
    pallas_call x7, Pallas kernels, call(): pl.pallas_call(body, out_shape=shapes, in_specs=in_specs or [VMEM] * len(...  10.3 us
    ppermute x3, starting transfers between devices, pair_b(): return lax.ppermute(block, ('gx', 'gy'), pairs)  2.6 us
    ppermute x1, starting transfers between devices, ring_b(): return lax.ppermute(block, axis, pairs)  0.98 us
  transfers between devices with their start and end apart: 15, of which 5 were waited for; matrix products, arithmetic and copies ran while one was open for 0% of the time, Pallas kernels for 9%

profile of v9, /device:TPU:0, one launch (start us, length us, event | category | flops | bytes accessed | tf_op | source)
XLA Modules:
  0.0 38.4 jit_solution(3142607622330405749)
XLA Ops:
  0.6 0.0 copy-start
  0.6 1.4 %shard_map.131 = (f32[320,128]{1,0:T(8,128)S(1)}, f32[304,128]{1,0:T(8,128)S(1)}, f32[4,256,128]{2,1,0:T(8,128)S(1)}, f32[3,256,128]{2,1,0:T(8,128)S(1)}, f32[16...) custom-call(f32[4,256,128]{2,1,0:T(8,128)} %bitcast.16, ...), custom_call_target="tpu_custom_call" | custom-call | flops 1000000 | bytes 944128 | tf_op jit(solution)/shard_map/pallas_call | solution.py:36
  2.1 0.5 %collective-permute-start = (f32[320,128]{1,0:T(8,128)S(1)}, f32[320,128]{1,0:T(8,128)S(1)}, u32[]{:S(2)}, u32[]{:S(2)}) collective-permute-start(f32[320,128]{1,0:T(8,128)S(1)} %get-tuple-element.38), channel_id=1, source_target_pairs={{0,1},{1,0},{2,3},{3,2},{4,5},{5,4},{6,7},{7,6},{8,9},{9,8},{10,11... | collective-permute-start | bytes 491528 | tf_op jit(solution)/shard_map/ppermute | solution.py:48
  2.6 2.6 %collective-permute-start.1 = (f32[304,128]{1,0:T(8,128)S(1)}, f32[304,128]{1,0:T(8,128)S(1)}, u32[]{:S(2)}, u32[]{:S(2)}) collective-permute-start(f32[304,128]{1,0:T(8,128)S(1)} %get-tuple-element.39), channel_id=1, source_target_pairs={{0,4},{1,2},{2,1},{3,7},{4,0},{5,6},{6,5},{7,3},{8,12},{9,10},{10,... | collective-permute-start | bytes 466952 | tf_op jit(solution)/shard_map/ppermute | solution.py:64
  5.2 0.1 collective-permute-start.2
  5.2 1.4 %collective-permute-start.3 = (f32[16,128]{1,0:T(8,128)}, f32[16,128]{1,0:T(8,128)S(1)}, u32[]{:S(2)}, u32[]{:S(2)}) collective-permute-start(f32[16,128]{1,0:T(8,128)} %bitcast.23), channel_id=1, source_target_pairs={{0,3},{1,2},{2,1},{3,0},{4,7},{5,6},{6,5},{7,4},{8,11},{9,10},{10,... | collective-permute-start | bytes 24584 | tf_op jit(solution)/shard_map/ppermute | solution.py:48
  6.6 1.6 %collective-permute-start.6 = (f32[24,128]{1,0:T(8,128)}, f32[24,128]{1,0:T(8,128)S(1)}, u32[]{:S(2)}, u32[]{:S(2)}) collective-permute-start(f32[24,128]{1,0:T(8,128)} %bitcast.20), channel_id=1, source_target_pairs={{0,8},{4,12},{8,0},{12,4},{16,24},{20,28},{24,16},{28,20},{1,9},{5... | collective-permute-start | bytes 36872 | tf_op jit(solution)/shard_map/ppermute | solution.py:48
  8.2 0.8 %collective-permute-done.2.refs_8_.refs_6_ = f32[16,128]{1,0:T(8,128)S(1)} collective-permute-done((f32[16,128]{1,0:T(8,128)}, f32[16,128]{1,0:T(8,128)S(1)}, u32[]{:S(2)}, u32[]{:S(2)}) %collective-permute-start.2) | collective-permute-done | bytes 8224 | tf_op jit(solution)/shard_map/ppermute | solution.py:48
  9.0 0.0 collective-permute-done.3.refs_9_.refs_7_
  9.0 0.0 collective-permute-done.1.refs_7_.refs_5_
  9.1 0.0 collective-permute-done.refs_6_.refs_4_
  9.1 0.5 %shard_map.133 = (f32[318,128]{1,0:T(8,128)S(1)}, f32[318,128]{1,0:T(8,128)S(1)}) custom-call(f32[4,256,128]{2,1,0:T(8,128)S(1)} %get-tuple-element.34.refs_0_, f32[3,256,128]{2,1,0:T(8,128)S(1)} %get-tuple-element.35.refs_1_, f32[16,128]{1,0:T(8,128)S(1)} %get-tuple-element.33.refs_2_.alpha, f32[16,128]{1,0:T(8,128)S(1)} %get-tuple-element.36.refs_3_, ...), custom_call_target="tpu_custom_call" | custom-call | flops 1000000 | bytes 1269760 | tf_op jit(solution)/shard_map/pallas_call | solution.py:36
  9.6 1.7 %collective-permute-start.4 = (f32[318,128]{1,0:T(8,128)S(1)}, f32[318,128]{1,0:T(8,128)S(1)}, u32[]{:S(2)}, u32[]{:S(2)}) collective-permute-start(f32[318,128]{1,0:T(8,128)S(1)} %get-tuple-element.43), channel_id=1, source_target_pairs={{0,4},{4,0},{8,12},{12,8},{16,20},{20,16},{24,28},{28,24},{1,5},{5... | collective-permute-start | bytes 488456 | tf_op jit(solution)/shard_map/ppermute | solution.py:48
  11.3 0.0 collective-permute-start.5
  11.3 0.0 collective-permute-done.6
  11.4 3.1 %collective-permute-start.7 = (f32[48,128]{1,0:T(8,128)S(1)}, f32[48,128]{1,0:T(8,128)S(1)}, u32[]{:S(2)}, u32[]{:S(2)}) collective-permute-start(f32[48,128]{1,0:T(8,128)S(1)} %constant_dynamic-update-slice_fusion.rest_0_), channel_id=1, source_target_pairs={{0,4},{4,0},{8,12},{12,8},{16,20},{20,16},{24,28},{28,24},{1,5},{5... | collective-permute-start | bytes 73736 | tf_op jit(solution)/shard_map/ppermute | solution.py:48
  14.5 2.6 %collective-permute-start.8 = (f32[48,128]{1,0:T(8,128)S(1)}, f32[48,128]{1,0:T(8,128)S(1)}, u32[]{:S(2)}, u32[]{:S(2)}) collective-permute-start(f32[48,128]{1,0:T(8,128)S(1)} %constant_dynamic-update-slice_fusion.rest_0_), channel_id=1, source_target_pairs={{0,16},{4,20},{8,24},{12,28},{16,0},{20,4},{24,8},{28,12},{1,17},{... | collective-permute-start | bytes 73736 | tf_op jit(solution)/shard_map/ppermute | solution.py:48
  17.0 0.0 collective-permute-start.9
  17.1 0.0 copy-done
  17.1 1.0 %shard_map.132 = (f32[1536,128]{1,0:T(8,128)S(1)}, f32[1920,128]{1,0:T(8,128)S(1)}, f32[384,16]{1,0:T(8,128)S(1)}, f32[256,512]{1,0:T(8,128)S(1)}, bf16[256,256]...) custom-call(f32[4,256,128]{2,1,0:T(8,128)S(1)} %get-tuple-element.34.refs_0_, ...), custom_call_target="tpu_custom_call" | custom-call | flops 3000000 | bytes 1802240 | tf_op jit(solution)/shard_map/pallas_call | solution.py:36
  18.1 1.0 %collective-permute-done.4.x_a = f32[318,128]{1,0:T(8,128)S(1)} collective-permute-done((f32[318,128]{1,0:T(8,128)S(1)}, f32[318,128]{1,0:T(8,128)S(1)}, u32[]{:S(2)}, u32[]{:S(2)}) %collective-permute-start.4) | collective-permute-done | bytes 162848 | tf_op jit(solution)/shard_map/ppermute | solution.py:48
  19.1 0.0 collective-permute-done.5.x_b
  19.1 1.9 %shard_map.134 = (bf16[768,512]{1,0:T(8,128)(2,1)S(1)}, bf16[768,512]{1,0:T(8,128)(2,1)S(1)}, f32[2880,128]{1,0:T(8,128)S(1)}) custom-call(f32[1536,128]{1,0:T(8,128)S(1)} %get-tuple-element.41.core, f32[1920,128]{1,0:T(8,128)S(1)} %get-tuple-element.42.coef_core, f32[318,128]{1,0:T(8,128)S(1)} %collective-permute-done.4.x_a, ...), custom_call_target="tpu_custom_call" | custom-call | flops 10000000 | bytes 2095104 | tf_op jit(solution)/shard_map/pallas_call | solution.py:36
  21.0 0.0 collective-permute-done.7.rest_1_
  21.0 0.0 collective-permute-done.8.rest_2_
  21.0 1.6 %collective-permute-done.9.rest_3_ = f32[48,128]{1,0:T(8,128)S(1)} collective-permute-done((f32[48,128]{1,0:T(8,128)S(1)}, f32[48,128]{1,0:T(8,128)S(1)}, u32[]{:S(2)}, u32[]{:S(2)}) %collective-permute-start.9) | collective-permute-done | bytes 24608 | tf_op jit(solution)/shard_map/ppermute | solution.py:48
  22.7 4.0 %shard_map.135 = (f32[216,128]{1,0:T(8,128)S(1)}, f32[216,128]{1,0:T(8,128)S(1)}, f32[1536,128]{1,0:T(8,128)S(1)}) custom-call(f32[2880,128]{1,0:T(8,128)S(1)} %get-tuple-element.45.coef, bf16[768,512]{1,0:T(8,128)(2,1)S(1)} %get-tuple-element.46.tops, bf16[768,512]{1,0:T(8,128)(2,1)S(1)} %get-tuple-element.47.lows, f32[256,512]{1,0:T(8,128)S(1)} %get-tuple-element.48.wide, ...), custom_call_target="tpu_custom_call" | custom-call | flops 20000000 | bytes 5840896 | tf_op jit(solution)/shard_map/pallas_call | solution.py:36
  26.7 1.0 %collective-permute-start.10 = (f32[216,128]{1,0:T(8,128)S(1)}, f32[216,128]{1,0:T(8,128)S(1)}, u32[]{:S(2)}, u32[]{:S(2)}) collective-permute-start(f32[216,128]{1,0:T(8,128)S(1)} %get-tuple-element.55), channel_id=1, source_target_pairs={{0,4},{4,0},{8,12},{12,8},{16,20},{20,16},{24,28},{28,24},{1,5},{5... | collective-permute-start | bytes 331784 | tf_op jit(solution)/shard_map/ppermute | solution.py:48
  27.7 0.0 collective-permute-start.11
  27.7 3.8 %collective-permute-done.10.refs_3_ = f32[216,128]{1,0:T(8,128)S(1)} collective-permute-done((f32[216,128]{1,0:T(8,128)S(1)}, f32[216,128]{1,0:T(8,128)S(1)}, u32[]{:S(2)}, u32[]{:S(2)}) %collective-permute-start.10) | collective-permute-done | bytes 110624 | tf_op jit(solution)/shard_map/ppermute | solution.py:48
  31.5 0.0 collective-permute-done.11.refs_4_
  31.5 0.4 %shard_map.136 = (f32[208,128]{1,0:T(8,128)S(1)}, f32[208,128]{1,0:T(8,128)S(1)}, f32[4,256,128]{2,1,0:T(8,128)S(1)}, f32[16,128]{1,0:T(8,128)S(1)}, f32[16,128]{1,0:T(8,128)S(1)}) custom-call(f32[4,256,128]{2,1,0:T(8,128)S(1)} %get-tuple-element.34.refs_0_, f32[384,16]{1,0:T(8,128)S(1)} %get-tuple-element.40.refs_1_, ...), custom_call_target="tpu_custom_call" | custom-call | flops 1000000 | bytes 1556480 | tf_op jit(solution)/shard_map/pallas_call | solution.py:36
  31.9 0.0 collective-permute-start.12
  31.9 1.0 %collective-permute-start.13 = (f32[208,128]{1,0:T(8,128)S(1)}, f32[208,128]{1,0:T(8,128)S(1)}, u32[]{:S(2)}, u32[]{:S(2)}) collective-permute-start(f32[208,128]{1,0:T(8,128)S(1)} %get-tuple-element.60), channel_id=1, source_target_pairs={{0,3},{1,2},{2,1},{3,0},{4,7},{5,6},{6,5},{7,4},{8,11},{9,10},{10,... | collective-permute-start | bytes 319496 | tf_op jit(solution)/shard_map/ppermute | solution.py:70
  32.9 1.2 %collective-permute-start.14 = (f32[16,128]{1,0:T(8,128)S(1)}, f32[16,128]{1,0:T(8,128)S(1)}, u32[]{:S(2)}, u32[]{:S(2)}) collective-permute-start(f32[16,128]{1,0:T(8,128)S(1)} %get-tuple-element.61), channel_id=1, source_target_pairs={{0,2},{1,3},{2,0},{3,1},{4,6},{5,7},{6,4},{7,5},{8,10},{9,11},{10,... | collective-permute-start | bytes 24584 | tf_op jit(solution)/shard_map/ppermute | solution.py:48
  34.1 3.4 %collective-permute-done.14.rest_0_ = f32[16,128]{1,0:T(8,128)S(1)} collective-permute-done((f32[16,128]{1,0:T(8,128)S(1)}, f32[16,128]{1,0:T(8,128)S(1)}, u32[]{:S(2)}, u32[]{:S(2)}) %collective-permute-start.14) | collective-permute-done | bytes 8224 | tf_op jit(solution)/shard_map/ppermute | solution.py:48
  37.4 0.0 collective-permute-done.12.y_a
  37.4 0.0 collective-permute-done.13.y_b
  37.5 0.9 %shard_map.137 = (f32[4,256,128]{2,1,0:T(8,128)}, f32[16,128]{1,0:T(8,128)}) custom-call(f32[16,128]{1,0:T(8,128)S(1)} %get-tuple-element.33.refs_2_.alpha, f32[4,256,128]{2,1,0:T(8,128)S(1)} %get-tuple-element.57.near, f32[16,128]{1,0:T(8,128)S(1)} %get-tuple-element.58.sums, f32[208,128]{1,0:T(8,128)S(1)} %collective-permute-done.12.y_a, ...), custom_call_target="tpu_custom_call" | custom-call | flops 1000000 | bytes 761856 | tf_op jit(solution)/shard_map/pallas_call | solution.py:36
  (2 shorter events, 0.0 us)
Async XLA Ops:
  0.6 16.4 %copy-start = (f32[1,1,256,4,128]{4,3,2,1,0:T(4,128)S(1)}, f32[1,1,256,4,128]{4,3,2,1,0:T(4,128)}, u32[]{:S(2)}) copy-start(f32[1,1,256,4,128]{4,3,2,1,0:T(4,128)} %param.22) | copy-start | bytes 1572868
  2.1 7.0 %collective-permute-start = (f32[320,128]{1,0:T(8,128)S(1)}, f32[320,128]{1,0:T(8,128)S(1)}, u32[]{:S(2)}, u32[]{:S(2)}) collective-permute-start(f32[320,128]{1,0:T(8,128)S(1)} %get-tuple-element.38), channel_id=1, source_target_pairs={{0,1},{1,0},{2,3},{3,2},{4,5},{5,4},{6,7},{7,6},{8,9},{9,8},{10,11... | collective-permute-start | bytes 491528 | tf_op jit(solution)/shard_map/ppermute | solution.py:48
  2.6 6.5 %collective-permute-start.1 = (f32[304,128]{1,0:T(8,128)S(1)}, f32[304,128]{1,0:T(8,128)S(1)}, u32[]{:S(2)}, u32[]{:S(2)}) collective-permute-start(f32[304,128]{1,0:T(8,128)S(1)} %get-tuple-element.39), channel_id=1, source_target_pairs={{0,4},{1,2},{2,1},{3,7},{4,0},{5,6},{6,5},{7,3},{8,12},{9,10},{10,... | collective-permute-start | bytes 466952 | tf_op jit(solution)/shard_map/ppermute | solution.py:64
  5.2 3.9 %collective-permute-start.2 = (f32[16,128]{1,0:T(8,128)}, f32[16,128]{1,0:T(8,128)S(1)}, u32[]{:S(2)}, u32[]{:S(2)}) collective-permute-start(f32[16,128]{1,0:T(8,128)} %bitcast.22), channel_id=1, source_target_pairs={{0,2},{1,3},{2,0},{3,1},{4,6},{5,7},{6,4},{7,5},{8,10},{9,11},{10,... | collective-permute-start | bytes 24584 | tf_op jit(solution)/shard_map/ppermute | solution.py:48
  5.2 3.8 %collective-permute-start.3 = (f32[16,128]{1,0:T(8,128)}, f32[16,128]{1,0:T(8,128)S(1)}, u32[]{:S(2)}, u32[]{:S(2)}) collective-permute-start(f32[16,128]{1,0:T(8,128)} %bitcast.23), channel_id=1, source_target_pairs={{0,3},{1,2},{2,1},{3,0},{4,7},{5,6},{6,5},{7,4},{8,11},{9,10},{10,... | collective-permute-start | bytes 24584 | tf_op jit(solution)/shard_map/ppermute | solution.py:48
  6.6 4.7 %collective-permute-start.6 = (f32[24,128]{1,0:T(8,128)}, f32[24,128]{1,0:T(8,128)S(1)}, u32[]{:S(2)}, u32[]{:S(2)}) collective-permute-start(f32[24,128]{1,0:T(8,128)} %bitcast.20), channel_id=1, source_target_pairs={{0,8},{4,12},{8,0},{12,4},{16,24},{20,28},{24,16},{28,20},{1,9},{5... | collective-permute-start | bytes 36872 | tf_op jit(solution)/shard_map/ppermute | solution.py:48
  9.6 9.5 %collective-permute-start.4 = (f32[318,128]{1,0:T(8,128)S(1)}, f32[318,128]{1,0:T(8,128)S(1)}, u32[]{:S(2)}, u32[]{:S(2)}) collective-permute-start(f32[318,128]{1,0:T(8,128)S(1)} %get-tuple-element.43), channel_id=1, source_target_pairs={{0,4},{4,0},{8,12},{12,8},{16,20},{20,16},{24,28},{28,24},{1,5},{5... | collective-permute-start | bytes 488456 | tf_op jit(solution)/shard_map/ppermute | solution.py:48
  11.3 7.7 %collective-permute-start.5 = (f32[318,128]{1,0:T(8,128)S(1)}, f32[318,128]{1,0:T(8,128)S(1)}, u32[]{:S(2)}, u32[]{:S(2)}) collective-permute-start(f32[318,128]{1,0:T(8,128)S(1)} %get-tuple-element.44), channel_id=1, source_target_pairs={{0,1},{4,8},{8,4},{12,16},{16,12},{20,24},{24,20},{28,29},{1,0},{5... | collective-permute-start | bytes 488456 | tf_op jit(solution)/shard_map/ppermute | solution.py:64
  11.4 9.7 %collective-permute-start.7 = (f32[48,128]{1,0:T(8,128)S(1)}, f32[48,128]{1,0:T(8,128)S(1)}, u32[]{:S(2)}, u32[]{:S(2)}) collective-permute-start(f32[48,128]{1,0:T(8,128)S(1)} %constant_dynamic-update-slice_fusion.rest_0_), channel_id=1, source_target_pairs={{0,4},{4,0},{8,12},{12,8},{16,20},{20,16},{24,28},{28,24},{1,5},{5... | collective-permute-start | bytes 73736 | tf_op jit(solution)/shard_map/ppermute | solution.py:48
  14.5 6.6 %collective-permute-start.8 = (f32[48,128]{1,0:T(8,128)S(1)}, f32[48,128]{1,0:T(8,128)S(1)}, u32[]{:S(2)}, u32[]{:S(2)}) collective-permute-start(f32[48,128]{1,0:T(8,128)S(1)} %constant_dynamic-update-slice_fusion.rest_0_), channel_id=1, source_target_pairs={{0,16},{4,20},{8,24},{12,28},{16,0},{20,4},{24,8},{28,12},{1,17},{... | collective-permute-start | bytes 73736 | tf_op jit(solution)/shard_map/ppermute | solution.py:48
  17.0 5.6 %collective-permute-start.9 = (f32[48,128]{1,0:T(8,128)S(1)}, f32[48,128]{1,0:T(8,128)S(1)}, u32[]{:S(2)}, u32[]{:S(2)}) collective-permute-start(f32[48,128]{1,0:T(8,128)S(1)} %constant_dynamic-update-slice_fusion.rest_0_), channel_id=1, source_target_pairs={{0,20},{4,16},{8,28},{12,24},{16,4},{20,0},{24,12},{28,8},{1,21},{... | collective-permute-start | bytes 73736 | tf_op jit(solution)/shard_map/ppermute | solution.py:48
  26.7 4.8 %collective-permute-start.10 = (f32[216,128]{1,0:T(8,128)S(1)}, f32[216,128]{1,0:T(8,128)S(1)}, u32[]{:S(2)}, u32[]{:S(2)}) collective-permute-start(f32[216,128]{1,0:T(8,128)S(1)} %get-tuple-element.55), channel_id=1, source_target_pairs={{0,4},{4,0},{8,12},{12,8},{16,20},{20,16},{24,28},{28,24},{1,5},{5... | collective-permute-start | bytes 331784 | tf_op jit(solution)/shard_map/ppermute | solution.py:48
  27.7 3.8 %collective-permute-start.11 = (f32[216,128]{1,0:T(8,128)S(1)}, f32[216,128]{1,0:T(8,128)S(1)}, u32[]{:S(2)}, u32[]{:S(2)}) collective-permute-start(f32[216,128]{1,0:T(8,128)S(1)} %get-tuple-element.56), channel_id=1, source_target_pairs={{0,1},{4,8},{8,4},{12,16},{16,12},{20,24},{24,20},{28,29},{1,0},{5... | collective-permute-start | bytes 331784 | tf_op jit(solution)/shard_map/ppermute | solution.py:64
  31.9 5.5 %collective-permute-start.12 = (f32[208,128]{1,0:T(8,128)S(1)}, f32[208,128]{1,0:T(8,128)S(1)}, u32[]{:S(2)}, u32[]{:S(2)}) collective-permute-start(f32[208,128]{1,0:T(8,128)S(1)} %get-tuple-element.59), channel_id=1, source_target_pairs={{0,1},{1,0},{2,3},{3,2},{4,5},{5,4},{6,7},{7,6},{8,9},{9,8},{10,11... | collective-permute-start | bytes 319496 | tf_op jit(solution)/shard_map/ppermute | solution.py:48
  31.9 5.5 %collective-permute-start.13 = (f32[208,128]{1,0:T(8,128)S(1)}, f32[208,128]{1,0:T(8,128)S(1)}, u32[]{:S(2)}, u32[]{:S(2)}) collective-permute-start(f32[208,128]{1,0:T(8,128)S(1)} %get-tuple-element.60), channel_id=1, source_target_pairs={{0,3},{1,2},{2,1},{3,0},{4,7},{5,6},{6,5},{7,4},{8,11},{9,10},{10,... | collective-permute-start | bytes 319496 | tf_op jit(solution)/shard_map/ppermute | solution.py:70
  32.9 4.5 %collective-permute-start.14 = (f32[16,128]{1,0:T(8,128)S(1)}, f32[16,128]{1,0:T(8,128)S(1)}, u32[]{:S(2)}, u32[]{:S(2)}) collective-permute-start(f32[16,128]{1,0:T(8,128)S(1)} %get-tuple-element.61), channel_id=1, source_target_pairs={{0,2},{1,3},{2,0},{3,1},{4,6},{5,7},{6,4},{7,5},{8,10},{9,11},{10,... | collective-permute-start | bytes 24584 | tf_op jit(solution)/shard_map/ppermute | solution.py:48

commit v10 on v9

--- a/solution.py
+++ b/solution.py
@@ -64,12 +64,6 @@
     return lax.ppermute(block, ("gx", "gy"), pairs)
 
 
-def ring_b(block, axis):
-    count = lax.axis_size(axis)
-    pairs = [(i, (i + 1 if i % 2 else i - 1) % count) for i in range(count)]
-    return lax.ppermute(block, axis, pairs)
-
-
 def place_on(axis):
     me = lax.axis_index(axis)
     return lax.rem(me, 2) == 0, me > 0, me < lax.axis_size(axis) - 1
@@ -98,7 +92,12 @@
 WIDE, WIDE_ROWS = layers(RIM)
 SLIM, SLIM_ROWS = layers(INNER)
 X_COEF = NC * WIDE_ROWS
+X_CORNERS = 2 * INNER - 2
+X_EXTRA = X_COEF + 3 * X_CORNERS
 X_HALO = X_COEF + 3 * SLIM_ROWS
+
+EARLY_BEAMS = 3 * INNER * CY
+EARLY = EARLY_BEAMS + STEPS * OWN_BEAMS
 
 Y_COEF = NC * RIM * CX
 Y_TILE = Y_COEF + 3 * INNER * CX
@@ -119,12 +118,12 @@
     beam_rows,
     out_a,
     out_b,
+    early,
     fine,
     coefs,
     profiles,
     near_tiles,
     meta,
-    beams,
     tiles,
     gates,
     values,
@@ -146,7 +145,7 @@
                 (gate_column, gates.at[2]),
                 (gate_live, gates.at[3]),
                 (precision, values),
-                (beam_rows, beams),
+                (beam_rows, early.at[pl.ds(EARLY_BEAMS, STEPS * OWN_BEAMS)]),
             ]
         )
     ]
@@ -171,14 +170,18 @@
     near_tiles[:, 0:CY] = tiles[...].astype(f32)
     for out in (out_a, out_b):
         out[Y_TILE : Y_TILE + CX] = near_tiles[...]
+    even_x, _, _ = place_on("gx")
+    slim = INNER * CY
+    for f in range(3):
+        east, west = coefs[f, CX * CY - slim :], coefs[f, :slim]
+        early[f * slim : (f + 1) * slim] = jnp.where(even_x, east, west)
     out_a[Y_HALO:] = profiles[...]
     held = BEAM_BITS
     beam = gates[0]
     owner = jnp.bitwise_xor(beam >> held, lax.axis_index("gx"))
-    block = (owner & -4) | ((owner & 1) << 1) | ((owner >> 1) & 1)
     meta[...] = jnp.zeros(meta.shape, f32)
     meta[0:1] = gates[2].astype(f32)
-    meta[1:2] = ((block << held) | (beam & ((1 << held) - 1))).astype(f32)
+    meta[1:2] = ((owner << held) | (beam & ((1 << held) - 1))).astype(f32)
     meta[2:3] = gates[1].astype(f32)
     meta[3:4] = gates[3].astype(f32) * values[...]
 
@@ -259,7 +262,7 @@
         if c is not None:
             field[...] += profile_weight * fine[:, c * 128 : (c + 1) * 128]
 
-    def put(at, found):
+    def put(at, found, at_a=None):
         for away, start, extra in found:
             east, west = (2 * RIM - away) * PITCH, (away - 1) * PITCH
             here = at + start
@@ -271,15 +274,22 @@
                     first = field[east + source : east + source + size]
                     second = field[west + source : west + source + size]
                     rows = slice(here + target, here + target + size)
-                    out_a[rows] = jnp.where(even, first, second)
                     out_b[rows] = jnp.where(even, second, first)
+                    if at_a is None:
+                        out_a[rows] = jnp.where(even, first, second)
+            if at_a is not None and extra:
+                for row in (PITCH - extra, CY):
+                    first = field[east + row : east + row + extra]
+                    second = field[west + row : west + row + extra]
+                    out_a[at_a : at_a + extra] = jnp.where(even, first, second)
+                    at_a += extra
 
     for c in range(NC):
         fill(delta.at[c], c * RIM * CX, RIM, c)
         put(c * WIDE_ROWS, WIDE)
     for f in range(3):
         fill(coefs.at[f], Y_COEF + f * INNER * CX, INNER, None)
-        put(X_COEF + f * SLIM_ROWS, SLIM)
+        put(X_COEF + f * SLIM_ROWS, SLIM, X_COEF + f * X_CORNERS)
 
 
 def prepare(ny, delta, coefs, alpha, near_tiles, meta, weights, y_a, y_b, *rest):
@@ -352,7 +362,7 @@
         ref[at : at + PITCH] = jnp.zeros((PITCH, 128), f32)
 
 
-def forecast(core, coef_core, x_a, x_b, tops, lows, coef, state_0, state_1, raw):
+def forecast(core, coef_core, early, x_a, x_b, tops, lows, coef, state_0, state_1, raw):
     def fill(ref, base, x_base, found):
         for away, start, extra in found:
             for source, target, size in (
@@ -367,6 +377,7 @@
                     at = base + (FIRST + CX - 1 + away) * PITCH + target
                     ref[at : at + size] = east
 
+    even, has_west, has_east = place_on("gx")
     rim = [FIRST - 3, FIRST - 2, FIRST - 1, FIRST + CX, FIRST + CX + 1, FIRST + CX + 2]
     for c in range(NC):
         at = c * FIELD + FIRST * PITCH
@@ -375,7 +386,25 @@
         fill(state_0, c * FIELD, c * WIDE_ROWS, WIDE)
     for f in range(3):
         clear(raw, f * FIELD, rim[1:5])
-        fill(raw, f * FIELD, X_COEF + f * SLIM_ROWS, SLIM)
+        at_a = X_COEF + f * X_CORNERS
+        for away, start, extra in SLIM:
+            inner = f * INNER * CY
+            west_a = early[pl.ds(inner + (INNER - away) * CY, CY)]
+            east_a = early[pl.ds(inner + (away - 1) * CY, CY)]
+            pieces = [(0, extra, CY, west_a, east_a)]
+            if extra:
+                for row, source in ((PITCH - extra, 0), (CY, extra + CY)):
+                    value = x_a[at_a : at_a + extra]
+                    pieces.append((row, source, extra, value, value))
+                    at_a += extra
+            for row, source, size, west_a, east_a in pieces:
+                at = X_COEF + f * SLIM_ROWS + start + source
+                value = x_b[at : at + size]
+                west, east = jnp.where(even, value, west_a), jnp.where(even, east_a, value)
+                at = f * FIELD + (FIRST - away) * PITCH + row
+                raw[at : at + size] = jnp.where(has_west, west, 0.0)
+                at = f * FIELD + (FIRST + CX - 1 + away) * PITCH + row
+                raw[at : at + size] = jnp.where(has_east, east, 0.0)
     for f in range(5):
         at = f * FIELD + FIRST * PITCH
         coef[at : at + CORE] = coef_core[f * CORE : (f + 1) * CORE]
@@ -528,7 +557,6 @@
 def add_x(ny, delta, picks, core, x_a, x_b, *rest):
     out_a, out_b, out_near, out_sums = rest[:4]
     out_others = rest[4:-2]
-    merged = ny == 4
     field, sums = rest[-2:]
     even, _, _ = place_on("gy")
     total = picks.shape[1]
@@ -564,8 +592,6 @@
         sums[pl.ds(c, total, stride=NC)] = tile_sums[:, c * 128 : (c + 1) * 128]
     out_sums[...] = sums[0:rows]
     out_a[Y_COEF:] = sums[rows : 2 * rows]
-    if merged:
-        out_b[Y_COEF:] = sums[3 * rows : 4 * rows]
     for s, other in enumerate(out_others):
         other[...] = sums[(2 + s) * rows : (3 + s) * rows]
 
@@ -582,8 +608,6 @@
             out_delta[c, high] = out_delta[c, high] + north
             out_delta[c, low] = out_delta[c, low] + south
     total = sums[...] + y_a[Y_COEF:]
-    if y_b.shape[0] > Y_COEF:
-        total = total + y_b[Y_COEF:]
     for other in others:
         total = total + other[...]
     out_alpha[...] = alpha[...] + profile_weight * total
@@ -621,17 +645,17 @@
     rows = owned * NC
     total = ny * owned
 
-    y_a, y_b, fine, coefs, control_near, near_tiles, meta, near_beams = call(
+    y_a, y_b, early, fine, coefs, control_near, near_tiles, meta = call(
         pack_y,
         [
             (Y_HALO + rows, 128),
             (Y_HALO, 128),
+            (EARLY, 128),
             fine.shape,
             (3, CX * CY, 128),
             control.shape,
             (CX, 128),
             (8, slots),
-            own_beams.shape,
         ],
         [
             pltpu.with_memory_space_constraint(value, pltpu.HBM)
@@ -648,12 +672,13 @@
     y_a = swap(y_a, "gy", 1)
     y_b = pair_b(y_b, "gy", "gx")
     others = [swap(control, "gy", xor) for xor in range(2, ny)]
-    beams = jnp.concatenate([near_beams, swap(own_beams, "gx", 2)])
-    beams = [beams] + [swap(beams, "gx", xor) for xor in range(1, nx) if xor % 4 < 2]
+    got_early = swap(early, "gx", 1)
+    beams = jnp.concatenate([early[EARLY_BEAMS:], got_early[EARLY_BEAMS:]])
+    beams = [beams] + [swap(beams, "gx", xor) for xor in range(2, nx, 2)]
 
     x_a, x_b = call(
         lambda *refs: pack_x(ny, *refs),
-        [(X_HALO, 128), (X_HALO, 128)],
+        [(X_EXTRA, 128), (X_HALO, 128)],
         [fine, coefs, control_near, near_tiles, y_a, y_b, *others],
         [
             pltpu.VMEM((2 * RIM * PITCH, 128), f32),
@@ -693,7 +718,7 @@
             jax.ShapeDtypeStruct((STEPS * CX * CY, NC * 128), bf16),
             (5 * FIELD, 128),
         ],
-        [core, coef, x_a, x_b],
+        [core, coef, got_early, x_a, x_b],
         [
             pltpu.VMEM((NC * FIELD, 128), f32),
             pltpu.VMEM((NC * FIELD, 128), f32),
@@ -714,22 +739,21 @@
     )
     x_a = swap(back_a, "gx", 1)
     x_b = pair_b(back_b, "gx", "gy")
-    loose = [xor for xor in range(2, ny) if ny != 4 or xor != 3]
     back_a, back_b, near, sums, *back = call(
         lambda *refs: add_x(ny, *refs),
         [
             (Y_COEF + rows, 128),
-            (Y_COEF + (rows if ny == 4 else 0), 128),
+            (Y_COEF, 128),
             fine.shape,
             (rows, 128),
         ]
-        + [(rows, 128)] * len(loose),
+        + [(rows, 128)] * (ny - 2),
         [fine, picks, core, x_a, x_b],
         [pltpu.VMEM((NC * CORE, 128), f32), pltpu.VMEM((total * NC, 128), f32)],
     )
     y_a = swap(back_a, "gy", 1)
-    y_b = ring_b(back_b, "gy")
-    others = [swap(value, "gy", xor) for xor, value in zip(loose, back)]
+    y_b = pair_b(back_b, "gy", "gx")
+    others = [swap(value, "gy", xor) for xor, value in zip(range(2, ny), back)]
     grad_delta, grad_alpha = call(
         add_y,
         [fine.shape, control.shape],

time: 39.2 us -> 40.7 us (1.038); the launches traced: 38.4 us -> 40.5 us
  waiting for transfers between devices: 10.7 us -> 11.8 us
  starting transfers between devices: 16.7 us -> 17.6 us
    ppermute x3 -> x4, starting transfers between devices: 2.6 us -> 5.21 us  [pair_b(): return lax.ppermute(block, ('gx', 'gy'), pairs)]
    ppermute x11 -> x12, waiting for transfers between devices: 10.7 us -> 11.8 us  [swap(): lax.ppermute(block, axis, [(i, i ^ xor) for i in range(lax.axis_size(axis...]
    ppermute x1 -> x0, starting transfers between devices: 0.98 us -> none  [ring_b(): return lax.ppermute(block, axis, pairs)]
    ppermute x11 -> x12, starting transfers between devices: 13.1 us -> 12.4 us  [swap(): lax.ppermute(block, axis, [(i, i ^ xor) for i in range(lax.axis_size(axis...]
  transfers between devices with their start and end apart: 15 -> 16, of which waited for: 5 -> 5; matrix products, arithmetic and copies ran while one was open for 0% -> 0% of each run, Pallas kernels for 9% -> 9%
where the time goes in v10:
time: 40.7 us; the launch traced here: 40.5 us
  starting transfers between devices  17.6 us (43%)
  waiting for transfers between devices  11.8 us (29%)
  Pallas kernels  10.4 us (26%)
  between operations  0.76 us (2%)
    ppermute x12, starting transfers between devices, swap(): lax.ppermute(block, axis, [(i, i ^ xor) for i in range(lax.axis_size(axis...  12.4 us
    ppermute x12, waiting for transfers between devices, swap(): lax.ppermute(block, axis, [(i, i ^ xor) for i in range(lax.axis_size(axis...  11.8 us
    pallas_call x7, Pallas kernels, call(): pl.pallas_call(body, out_shape=shapes, in_specs=in_specs or [VMEM] * len(...  10.4 us
    ppermute x4, starting transfers between devices, pair_b(): return lax.ppermute(block, ('gx', 'gy'), pairs)  5.21 us
  transfers between devices with their start and end apart: 16, of which 5 were waited for; matrix products, arithmetic and copies ran while one was open for 0% of the time, Pallas kernels for 9%

profile of v10, /device:TPU:0, one launch (start us, length us, event | category | flops | bytes accessed | tf_op | source)
XLA Modules:
  0.0 40.5 jit_solution(10345890568548937116)
XLA Ops:
  0.6 0.0 copy-start
  0.6 1.4 %shard_map.131 = (f32[320,128]{1,0:T(8,128)S(1)}, f32[304,128]{1,0:T(8,128)S(1)}, f32[120,128]{1,0:T(8,128)S(1)}, f32[4,256,128]{2,1,0:T(8,128)S(1)}, f32[3,256,...) custom-call(f32[4,256,128]{2,1,0:T(8,128)} %bitcast.16, ...), custom_call_target="tpu_custom_call" | custom-call | flops 1000000 | bytes 944128 | tf_op jit(solution)/shard_map/pallas_call | solution.py:36
  2.1 0.5 %collective-permute-start = (f32[320,128]{1,0:T(8,128)S(1)}, f32[320,128]{1,0:T(8,128)S(1)}, u32[]{:S(2)}, u32[]{:S(2)}) collective-permute-start(f32[320,128]{1,0:T(8,128)S(1)} %get-tuple-element.39), channel_id=1, source_target_pairs={{0,1},{1,0},{2,3},{3,2},{4,5},{5,4},{6,7},{7,6},{8,9},{9,8},{10,11... | collective-permute-start | bytes 491528 | tf_op jit(solution)/shard_map/ppermute | solution.py:48
  2.6 2.6 %collective-permute-start.1 = (f32[304,128]{1,0:T(8,128)S(1)}, f32[304,128]{1,0:T(8,128)S(1)}, u32[]{:S(2)}, u32[]{:S(2)}) collective-permute-start(f32[304,128]{1,0:T(8,128)S(1)} %get-tuple-element.40), channel_id=1, source_target_pairs={{0,4},{1,2},{2,1},{3,7},{4,0},{5,6},{6,5},{7,3},{8,12},{9,10},{10,... | collective-permute-start | bytes 466952 | tf_op jit(solution)/shard_map/ppermute | solution.py:64
  5.2 0.1 collective-permute-start.4
  5.3 2.0 %collective-permute-start.2 = (f32[16,128]{1,0:T(8,128)}, f32[16,128]{1,0:T(8,128)S(1)}, u32[]{:S(2)}, u32[]{:S(2)}) collective-permute-start(f32[16,128]{1,0:T(8,128)} %bitcast.21), channel_id=1, source_target_pairs={{0,2},{1,3},{2,0},{3,1},{4,6},{5,7},{6,4},{7,5},{8,10},{9,11},{10,... | collective-permute-start | bytes 24584 | tf_op jit(solution)/shard_map/ppermute | solution.py:48
  7.2 0.6 %collective-permute-start.3 = (f32[16,128]{1,0:T(8,128)}, f32[16,128]{1,0:T(8,128)S(1)}, u32[]{:S(2)}, u32[]{:S(2)}) collective-permute-start(f32[16,128]{1,0:T(8,128)} %bitcast.22), channel_id=1, source_target_pairs={{0,3},{1,2},{2,1},{3,0},{4,7},{5,6},{6,5},{7,4},{8,11},{9,10},{10,... | collective-permute-start | bytes 24584 | tf_op jit(solution)/shard_map/ppermute | solution.py:48
  7.9 1.3 %collective-permute-done.2.refs_8_.refs_6_ = f32[16,128]{1,0:T(8,128)S(1)} collective-permute-done((f32[16,128]{1,0:T(8,128)}, f32[16,128]{1,0:T(8,128)S(1)}, u32[]{:S(2)}, u32[]{:S(2)}) %collective-permute-start.2) | collective-permute-done | bytes 8224 | tf_op jit(solution)/shard_map/ppermute | solution.py:48
  9.1 1.4 %collective-permute-done.3.refs_9_.refs_7_ = f32[16,128]{1,0:T(8,128)S(1)} collective-permute-done((f32[16,128]{1,0:T(8,128)}, f32[16,128]{1,0:T(8,128)S(1)}, u32[]{:S(2)}, u32[]{:S(2)}) %collective-permute-start.3) | collective-permute-done | bytes 8224 | tf_op jit(solution)/shard_map/ppermute | solution.py:48
  10.5 0.0 collective-permute-done.1.refs_7_.refs_5_
  10.5 0.0 collective-permute-done.refs_6_.refs_4_
  10.5 0.5 %shard_map.133 = (f32[222,128]{1,0:T(8,128)S(1)}, f32[318,128]{1,0:T(8,128)S(1)}) custom-call(f32[4,256,128]{2,1,0:T(8,128)S(1)} %get-tuple-element.35.refs_0_, f32[3,256,128]{2,1,0:T(8,128)S(1)} %get-tuple-element.36.refs_1_, f32[16,128]{1,0:T(8,128)S(1)} %get-tuple-element.34.refs_2_.alpha, f32[16,128]{1,0:T(8,128)S(1)} %get-tuple-element.37.refs_3_, ...), custom_call_target="tpu_custom_call" | custom-call | flops 1000000 | bytes 1269760 | tf_op jit(solution)/shard_map/pallas_call | solution.py:36
  11.1 0.1 collective-permute-start.6
  11.2 0.0 collective-permute-done.4.early
  11.2 3.1 %collective-permute-start.5 = (f32[222,128]{1,0:T(8,128)S(1)}, f32[222,128]{1,0:T(8,128)S(1)}, u32[]{:S(2)}, u32[]{:S(2)}) collective-permute-start(f32[222,128]{1,0:T(8,128)S(1)} %get-tuple-element.45), channel_id=1, source_target_pairs={{0,4},{4,0},{8,12},{12,8},{16,20},{20,16},{24,28},{28,24},{1,5},{5... | collective-permute-start | bytes 341000 | tf_op jit(solution)/shard_map/ppermute | solution.py:48
  14.3 1.6 %collective-permute-start.7 = (f32[48,128]{1,0:T(8,128)S(1)}, f32[48,128]{1,0:T(8,128)S(1)}, u32[]{:S(2)}, u32[]{:S(2)}) collective-permute-start(f32[48,128]{1,0:T(8,128)S(1)} %pad_maximum_fusion.rest_0_), channel_id=1, source_target_pairs={{0,8},{4,12},{8,0},{12,4},{16,24},{20,28},{24,16},{28,20},{1,9},{5... | collective-permute-start | bytes 73736 | tf_op jit(solution)/shard_map/ppermute | solution.py:48
  15.8 1.0 %collective-permute-start.8 = (f32[48,128]{1,0:T(8,128)S(1)}, f32[48,128]{1,0:T(8,128)S(1)}, u32[]{:S(2)}, u32[]{:S(2)}) collective-permute-start(f32[48,128]{1,0:T(8,128)S(1)} %pad_maximum_fusion.rest_0_), channel_id=1, source_target_pairs={{0,16},{4,20},{8,24},{12,28},{16,0},{20,4},{24,8},{28,12},{1,17},{... | collective-permute-start | bytes 73736 | tf_op jit(solution)/shard_map/ppermute | solution.py:48
  16.9 1.8 %collective-permute-start.9 = (f32[48,128]{1,0:T(8,128)S(1)}, f32[48,128]{1,0:T(8,128)S(1)}, u32[]{:S(2)}, u32[]{:S(2)}) collective-permute-start(f32[48,128]{1,0:T(8,128)S(1)} %pad_maximum_fusion.rest_0_), channel_id=1, source_target_pairs={{0,24},{4,28},{8,16},{12,20},{16,8},{20,12},{24,0},{28,4},{1,25},{... | collective-permute-start | bytes 73736 | tf_op jit(solution)/shard_map/ppermute | solution.py:48
  18.7 0.0 copy-done
  18.7 1.0 %shard_map.132 = (f32[1536,128]{1,0:T(8,128)S(1)}, f32[1920,128]{1,0:T(8,128)S(1)}, f32[384,16]{1,0:T(8,128)S(1)}, f32[256,512]{1,0:T(8,128)S(1)}, bf16[256,256]...) custom-call(f32[4,256,128]{2,1,0:T(8,128)S(1)} %get-tuple-element.35.refs_0_, ...), custom_call_target="tpu_custom_call" | custom-call | flops 3000000 | bytes 1802240 | tf_op jit(solution)/shard_map/pallas_call | solution.py:36
  19.7 0.0 collective-permute-done.5.x_a
  19.7 0.0 collective-permute-done.6.x_b
  19.7 2.0 %shard_map.134 = (bf16[768,512]{1,0:T(8,128)(2,1)S(1)}, bf16[768,512]{1,0:T(8,128)(2,1)S(1)}, f32[2880,128]{1,0:T(8,128)S(1)}) custom-call(f32[1536,128]{1,0:T(8,128)S(1)} %get-tuple-element.42.core, f32[1920,128]{1,0:T(8,128)S(1)} %get-tuple-element.43.coef_core, f32[120,128]{1,0:T(8,128)S(1)} %collective-permute-done.4.early, ...), custom_call_target="tpu_custom_call" | custom-call | flops 10000000 | bytes 2107392 | tf_op jit(solution)/shard_map/pallas_call | solution.py:36
  21.7 0.0 collective-permute-done.7.rest_1_
  21.7 0.0 collective-permute-done.8.rest_2_
  21.7 0.8 %collective-permute-done.9.rest_3_ = f32[48,128]{1,0:T(8,128)S(1)} collective-permute-done((f32[48,128]{1,0:T(8,128)S(1)}, f32[48,128]{1,0:T(8,128)S(1)}, u32[]{:S(2)}, u32[]{:S(2)}) %collective-permute-start.9) | collective-permute-done | bytes 24608 | tf_op jit(solution)/shard_map/ppermute | solution.py:48
  22.5 4.1 %shard_map.135 = (f32[216,128]{1,0:T(8,128)S(1)}, f32[216,128]{1,0:T(8,128)S(1)}, f32[1536,128]{1,0:T(8,128)S(1)}) custom-call(f32[2880,128]{1,0:T(8,128)S(1)} %get-tuple-element.47.coef, bf16[768,512]{1,0:T(8,128)(2,1)S(1)} %get-tuple-element.48.tops, bf16[768,512]{1,0:T(8,128)(2,1)S(1)} %get-tuple-element.49.lows, f32[256,512]{1,0:T(8,128)S(1)} %get-tuple-element.50.wide, ...), custom_call_target="tpu_custom_call" | custom-call | flops 20000000 | bytes 5840896 | tf_op jit(solution)/shard_map/pallas_call | solution.py:36
  26.6 1.5 %collective-permute-start.10 = (f32[216,128]{1,0:T(8,128)S(1)}, f32[216,128]{1,0:T(8,128)S(1)}, u32[]{:S(2)}, u32[]{:S(2)}) collective-permute-start(f32[216,128]{1,0:T(8,128)S(1)} %get-tuple-element.56), channel_id=1, source_target_pairs={{0,4},{4,0},{8,12},{12,8},{16,20},{20,16},{24,28},{28,24},{1,5},{5... | collective-permute-start | bytes 331784 | tf_op jit(solution)/shard_map/ppermute | solution.py:48
  28.1 0.0 collective-permute-start.11
  28.1 4.9 %collective-permute-done.10.refs_3_ = f32[216,128]{1,0:T(8,128)S(1)} collective-permute-done((f32[216,128]{1,0:T(8,128)S(1)}, f32[216,128]{1,0:T(8,128)S(1)}, u32[]{:S(2)}, u32[]{:S(2)}) %collective-permute-start.10) | collective-permute-done | bytes 110624 | tf_op jit(solution)/shard_map/ppermute | solution.py:48
  33.0 0.0 collective-permute-done.11.refs_4_
  33.0 0.4 shard_map.136
  33.4 0.0 collective-permute-start.12
  33.4 2.5 %collective-permute-start.13 = (f32[192,128]{1,0:T(8,128)S(1)}, f32[192,128]{1,0:T(8,128)S(1)}, u32[]{:S(2)}, u32[]{:S(2)}) collective-permute-start(f32[192,128]{1,0:T(8,128)S(1)} %get-tuple-element.61), channel_id=1, source_target_pairs={{0,4},{1,2},{2,1},{3,7},{4,0},{5,6},{6,5},{7,3},{8,12},{9,10},{10,... | collective-permute-start | bytes 294920 | tf_op jit(solution)/shard_map/ppermute | solution.py:64
  35.9 0.0 collective-permute-start.14
  35.9 0.2 collective-permute-start.15
  36.2 3.4 %collective-permute-done.14.rest_0_ = f32[16,128]{1,0:T(8,128)S(1)} collective-permute-done((f32[16,128]{1,0:T(8,128)S(1)}, f32[16,128]{1,0:T(8,128)S(1)}, u32[]{:S(2)}, u32[]{:S(2)}) %collective-permute-start.14) | collective-permute-done | bytes 8224 | tf_op jit(solution)/shard_map/ppermute | solution.py:48
  39.6 0.0 collective-permute-done.15.rest_1_
  39.6 0.0 collective-permute-done.13.y_b
  39.6 0.0 collective-permute-done.12.y_a
  39.6 0.9 %shard_map.137 = (f32[4,256,128]{2,1,0:T(8,128)}, f32[16,128]{1,0:T(8,128)}) custom-call(f32[16,128]{1,0:T(8,128)S(1)} %get-tuple-element.34.refs_2_.alpha, f32[4,256,128]{2,1,0:T(8,128)S(1)} %get-tuple-element.58.near, f32[16,128]{1,0:T(8,128)S(1)} %get-tuple-element.59.sums, f32[208,128]{1,0:T(8,128)S(1)} %collective-permute-done.12.y_a, ...), custom_call_target="tpu_custom_call" | custom-call | flops 1000000 | bytes 761856 | tf_op jit(solution)/shard_map/pallas_call | solution.py:36
  (3 shorter events, 0.0 us)
Async XLA Ops:
  0.6 18.0 %copy-start = (f32[1,1,256,4,128]{4,3,2,1,0:T(4,128)S(1)}, f32[1,1,256,4,128]{4,3,2,1,0:T(4,128)}, u32[]{:S(2)}) copy-start(f32[1,1,256,4,128]{4,3,2,1,0:T(4,128)} %param.22) | copy-start | bytes 1572868
  2.1 8.5 %collective-permute-start = (f32[320,128]{1,0:T(8,128)S(1)}, f32[320,128]{1,0:T(8,128)S(1)}, u32[]{:S(2)}, u32[]{:S(2)}) collective-permute-start(f32[320,128]{1,0:T(8,128)S(1)} %get-tuple-element.39), channel_id=1, source_target_pairs={{0,1},{1,0},{2,3},{3,2},{4,5},{5,4},{6,7},{7,6},{8,9},{9,8},{10,11... | collective-permute-start | bytes 491528 | tf_op jit(solution)/shard_map/ppermute | solution.py:48
  2.6 7.9 %collective-permute-start.1 = (f32[304,128]{1,0:T(8,128)S(1)}, f32[304,128]{1,0:T(8,128)S(1)}, u32[]{:S(2)}, u32[]{:S(2)}) collective-permute-start(f32[304,128]{1,0:T(8,128)S(1)} %get-tuple-element.40), channel_id=1, source_target_pairs={{0,4},{1,2},{2,1},{3,7},{4,0},{5,6},{6,5},{7,3},{8,12},{9,10},{10,... | collective-permute-start | bytes 466952 | tf_op jit(solution)/shard_map/ppermute | solution.py:64
  5.2 6.0 %collective-permute-start.4 = (f32[120,128]{1,0:T(8,128)S(1)}, f32[120,128]{1,0:T(8,128)S(1)}, u32[]{:S(2)}, u32[]{:S(2)}) collective-permute-start(f32[120,128]{1,0:T(8,128)S(1)} %get-tuple-element.44), channel_id=1, source_target_pairs={{0,4},{4,0},{8,12},{12,8},{16,20},{20,16},{24,28},{28,24},{1,5},{5... | collective-permute-start | bytes 184328 | tf_op jit(solution)/shard_map/ppermute | solution.py:48
  5.3 3.9 %collective-permute-start.2 = (f32[16,128]{1,0:T(8,128)}, f32[16,128]{1,0:T(8,128)S(1)}, u32[]{:S(2)}, u32[]{:S(2)}) collective-permute-start(f32[16,128]{1,0:T(8,128)} %bitcast.21), channel_id=1, source_target_pairs={{0,2},{1,3},{2,0},{3,1},{4,6},{5,7},{6,4},{7,5},{8,10},{9,11},{10,... | collective-permute-start | bytes 24584 | tf_op jit(solution)/shard_map/ppermute | solution.py:48
  7.2 3.3 %collective-permute-start.3 = (f32[16,128]{1,0:T(8,128)}, f32[16,128]{1,0:T(8,128)S(1)}, u32[]{:S(2)}, u32[]{:S(2)}) collective-permute-start(f32[16,128]{1,0:T(8,128)} %bitcast.22), channel_id=1, source_target_pairs={{0,3},{1,2},{2,1},{3,0},{4,7},{5,6},{6,5},{7,4},{8,11},{9,10},{10,... | collective-permute-start | bytes 24584 | tf_op jit(solution)/shard_map/ppermute | solution.py:48
  11.1 8.6 %collective-permute-start.6 = (f32[318,128]{1,0:T(8,128)S(1)}, f32[318,128]{1,0:T(8,128)S(1)}, u32[]{:S(2)}, u32[]{:S(2)}) collective-permute-start(f32[318,128]{1,0:T(8,128)S(1)} %get-tuple-element.46), channel_id=1, source_target_pairs={{0,1},{4,8},{8,4},{12,16},{16,12},{20,24},{24,20},{28,29},{1,0},{5... | collective-permute-start | bytes 488456 | tf_op jit(solution)/shard_map/ppermute | solution.py:64
  11.2 8.5 %collective-permute-start.5 = (f32[222,128]{1,0:T(8,128)S(1)}, f32[222,128]{1,0:T(8,128)S(1)}, u32[]{:S(2)}, u32[]{:S(2)}) collective-permute-start(f32[222,128]{1,0:T(8,128)S(1)} %get-tuple-element.45), channel_id=1, source_target_pairs={{0,4},{4,0},{8,12},{12,8},{16,20},{20,16},{24,28},{28,24},{1,5},{5... | collective-permute-start | bytes 341000 | tf_op jit(solution)/shard_map/ppermute | solution.py:48
  14.3 7.4 %collective-permute-start.7 = (f32[48,128]{1,0:T(8,128)S(1)}, f32[48,128]{1,0:T(8,128)S(1)}, u32[]{:S(2)}, u32[]{:S(2)}) collective-permute-start(f32[48,128]{1,0:T(8,128)S(1)} %pad_maximum_fusion.rest_0_), channel_id=1, source_target_pairs={{0,8},{4,12},{8,0},{12,4},{16,24},{20,28},{24,16},{28,20},{1,9},{5... | collective-permute-start | bytes 73736 | tf_op jit(solution)/shard_map/ppermute | solution.py:48
  15.8 5.8 %collective-permute-start.8 = (f32[48,128]{1,0:T(8,128)S(1)}, f32[48,128]{1,0:T(8,128)S(1)}, u32[]{:S(2)}, u32[]{:S(2)}) collective-permute-start(f32[48,128]{1,0:T(8,128)S(1)} %pad_maximum_fusion.rest_0_), channel_id=1, source_target_pairs={{0,16},{4,20},{8,24},{12,28},{16,0},{20,4},{24,8},{28,12},{1,17},{... | collective-permute-start | bytes 73736 | tf_op jit(solution)/shard_map/ppermute | solution.py:48
  16.9 5.6 %collective-permute-start.9 = (f32[48,128]{1,0:T(8,128)S(1)}, f32[48,128]{1,0:T(8,128)S(1)}, u32[]{:S(2)}, u32[]{:S(2)}) collective-permute-start(f32[48,128]{1,0:T(8,128)S(1)} %pad_maximum_fusion.rest_0_), channel_id=1, source_target_pairs={{0,24},{4,28},{8,16},{12,20},{16,8},{20,12},{24,0},{28,4},{1,25},{... | collective-permute-start | bytes 73736 | tf_op jit(solution)/shard_map/ppermute | solution.py:48
  26.6 6.4 %collective-permute-start.10 = (f32[216,128]{1,0:T(8,128)S(1)}, f32[216,128]{1,0:T(8,128)S(1)}, u32[]{:S(2)}, u32[]{:S(2)}) collective-permute-start(f32[216,128]{1,0:T(8,128)S(1)} %get-tuple-element.56), channel_id=1, source_target_pairs={{0,4},{4,0},{8,12},{12,8},{16,20},{20,16},{24,28},{28,24},{1,5},{5... | collective-permute-start | bytes 331784 | tf_op jit(solution)/shard_map/ppermute | solution.py:48
  28.1 4.9 %collective-permute-start.11 = (f32[216,128]{1,0:T(8,128)S(1)}, f32[216,128]{1,0:T(8,128)S(1)}, u32[]{:S(2)}, u32[]{:S(2)}) collective-permute-start(f32[216,128]{1,0:T(8,128)S(1)} %get-tuple-element.57), channel_id=1, source_target_pairs={{0,1},{4,8},{8,4},{12,16},{16,12},{20,24},{24,20},{28,29},{1,0},{5... | collective-permute-start | bytes 331784 | tf_op jit(solution)/shard_map/ppermute | solution.py:64
  33.4 6.2 %collective-permute-start.12 = (f32[208,128]{1,0:T(8,128)S(1)}, f32[208,128]{1,0:T(8,128)S(1)}, u32[]{:S(2)}, u32[]{:S(2)}) collective-permute-start(f32[208,128]{1,0:T(8,128)S(1)} %get-tuple-element.60), channel_id=1, source_target_pairs={{0,1},{1,0},{2,3},{3,2},{4,5},{5,4},{6,7},{7,6},{8,9},{9,8},{10,11... | collective-permute-start | bytes 319496 | tf_op jit(solution)/shard_map/ppermute | solution.py:48
  33.4 6.2 %collective-permute-start.13 = (f32[192,128]{1,0:T(8,128)S(1)}, f32[192,128]{1,0:T(8,128)S(1)}, u32[]{:S(2)}, u32[]{:S(2)}) collective-permute-start(f32[192,128]{1,0:T(8,128)S(1)} %get-tuple-element.61), channel_id=1, source_target_pairs={{0,4},{1,2},{2,1},{3,7},{4,0},{5,6},{6,5},{7,3},{8,12},{9,10},{10,... | collective-permute-start | bytes 294920 | tf_op jit(solution)/shard_map/ppermute | solution.py:64
  35.9 3.7 %collective-permute-start.14 = (f32[16,128]{1,0:T(8,128)S(1)}, f32[16,128]{1,0:T(8,128)S(1)}, u32[]{:S(2)}, u32[]{:S(2)}) collective-permute-start(f32[16,128]{1,0:T(8,128)S(1)} %get-tuple-element.62), channel_id=1, source_target_pairs={{0,2},{1,3},{2,0},{3,1},{4,6},{5,7},{6,4},{7,5},{8,10},{9,11},{10,... | collective-permute-start | bytes 24584 | tf_op jit(solution)/shard_map/ppermute | solution.py:48
  35.9 3.7 %collective-permute-start.15 = (f32[16,128]{1,0:T(8,128)S(1)}, f32[16,128]{1,0:T(8,128)S(1)}, u32[]{:S(2)}, u32[]{:S(2)}) collective-permute-start(f32[16,128]{1,0:T(8,128)S(1)} %get-tuple-element.63), channel_id=1, source_target_pairs={{0,3},{1,2},{2,1},{3,0},{4,7},{5,6},{6,5},{7,4},{8,11},{9,10},{10,... | collective-permute-start | bytes 24584 | tf_op jit(solution)/shard_map/ppermute | solution.py:48

commit v11 on v10

--- a/solution.py
+++ b/solution.py
@@ -62,6 +62,12 @@
             else:
                 pairs.append((place(i, j), place(i + 1 if i % 2 else i - 1, j)))
     return lax.ppermute(block, ("gx", "gy"), pairs)
+
+
+def ring_b(block, axis):
+    count = lax.axis_size(axis)
+    pairs = [(i, (i + 1 if i % 2 else i - 1) % count) for i in range(count)]
+    return lax.ppermute(block, axis, pairs)
 
 
 def place_on(axis):
@@ -204,8 +210,7 @@
     owned = alpha.shape[0]
     known[0:owned] = alpha[...]
     known[owned : 2 * owned] = got_a[Y_HALO:]
-    for s, other in enumerate(others):
-        known[(2 + s) * owned : (3 + s) * owned] = other[...]
+    known[2 * owned :] = others[0][...]
 
 
 def tile_numbers(near_tiles, got_a, got_b, tiles):
@@ -236,8 +241,8 @@
 
 
 def pack_x(ny, delta, coefs, alpha, near_tiles, y_a, y_b, *rest):
-    others = rest[: ny - 2]
-    out_a, out_b, field, picks, known, tiles = rest[ny - 2 :]
+    others = rest[:1]
+    out_a, out_b, field, picks, known, tiles = rest[1:]
     even, _, _ = place_on("gx")
     owned = alpha.shape[0] // NC
     gather_known(alpha, y_a, others, known)
@@ -293,9 +298,9 @@
 
 
 def prepare(ny, delta, coefs, alpha, near_tiles, meta, weights, y_a, y_b, *rest):
-    others = rest[: ny - 2]
-    core, coef, picks, wide, slot_pick, slot_push, beam_pick, columns = rest[ny - 2 : ny + 6]
-    known, tiles = rest[ny + 6 :]
+    others = rest[:1]
+    core, coef, picks, wide, slot_pick, slot_push, beam_pick, columns = rest[1:9]
+    known, tiles = rest[9:]
     owned = alpha.shape[0] // NC
 
     def fill(ref, base, own, y_base, reach):
@@ -592,6 +597,8 @@
         sums[pl.ds(c, total, stride=NC)] = tile_sums[:, c * 128 : (c + 1) * 128]
     out_sums[...] = sums[0:rows]
     out_a[Y_COEF:] = sums[rows : 2 * rows]
+    if ny == 4:
+        out_b[Y_COEF:] = sums[3 * rows : 4 * rows]
     for s, other in enumerate(out_others):
         other[...] = sums[(2 + s) * rows : (3 + s) * rows]
 
@@ -608,6 +615,8 @@
             out_delta[c, high] = out_delta[c, high] + north
             out_delta[c, low] = out_delta[c, low] + south
     total = sums[...] + y_a[Y_COEF:]
+    if y_b.shape[0] > Y_COEF:
+        total = total + y_b[Y_COEF:]
     for other in others:
         total = total + other[...]
     out_alpha[...] = alpha[...] + profile_weight * total
@@ -671,7 +680,7 @@
     )
     y_a = swap(y_a, "gy", 1)
     y_b = pair_b(y_b, "gy", "gx")
-    others = [swap(control, "gy", xor) for xor in range(2, ny)]
+    others = [jnp.concatenate([swap(control, "gy", xor) for xor in range(2, ny)])]
     got_early = swap(early, "gx", 1)
     beams = jnp.concatenate([early[EARLY_BEAMS:], got_early[EARLY_BEAMS:]])
     beams = [beams] + [swap(beams, "gx", xor) for xor in range(2, nx, 2)]
@@ -739,21 +748,22 @@
     )
     x_a = swap(back_a, "gx", 1)
     x_b = pair_b(back_b, "gx", "gy")
+    loose = [xor for xor in range(2, ny) if ny != 4 or xor != 3]
     back_a, back_b, near, sums, *back = call(
         lambda *refs: add_x(ny, *refs),
         [
             (Y_COEF + rows, 128),
-            (Y_COEF, 128),
+            (Y_COEF + (rows if ny == 4 else 0), 128),
             fine.shape,
             (rows, 128),
         ]
-        + [(rows, 128)] * (ny - 2),
+        + [(rows, 128)] * len(loose),
         [fine, picks, core, x_a, x_b],
         [pltpu.VMEM((NC * CORE, 128), f32), pltpu.VMEM((total * NC, 128), f32)],
     )
     y_a = swap(back_a, "gy", 1)
-    y_b = pair_b(back_b, "gy", "gx")
-    others = [swap(value, "gy", xor) for xor, value in zip(range(2, ny), back)]
+    y_b = ring_b(back_b, "gy")
+    others = [swap(value, "gy", xor) for xor, value in zip(loose, back)]
     grad_delta, grad_alpha = call(
         add_y,
         [fine.shape, control.shape],

time: 40.7 us -> 40.2 us (0.988)
  waiting for transfers between devices: 11.8 us -> 11.3 us
    ppermute x12 -> x11, waiting for transfers between devices: 11.8 us -> 7.56 us  [swap(): lax.ppermute(block, axis, [(i, i ^ xor) for i in range(lax.axis_size(axis...]
    ppermute x4 -> x3, waiting for transfers between devices: 0.01 us -> 3.75 us  [pair_b(): return lax.ppermute(block, ('gx', 'gy'), pairs)]
    ppermute x4 -> x3, starting transfers between devices: 5.21 us -> 2.05 us  [pair_b(): return lax.ppermute(block, ('gx', 'gy'), pairs)]
    ppermute x0 -> x1, starting transfers between devices: none -> 2.4 us  [ring_b(): return lax.ppermute(block, axis, pairs)]
    ppermute x12 -> x11, starting transfers between devices: 12.4 us -> 13.2 us  [swap(): lax.ppermute(block, axis, [(i, i ^ xor) for i in range(lax.axis_size(axis...]
  transfers between devices with their start and end apart: 16 -> 15, of which waited for: 5 -> 5; matrix products, arithmetic and copies ran while one was open for 0% -> 0% of each run, Pallas kernels for 9% -> 12%
where the time goes in v11:
time: 40.2 us; the launch traced here: 40.1 us
  starting transfers between devices  17.7 us (44%)
  waiting for transfers between devices  11.3 us (28%)
  Pallas kernels  10.3 us (26%)
  between operations  0.75 us (2%)
    ppermute x11, starting transfers between devices, swap(): lax.ppermute(block, axis, [(i, i ^ xor) for i in range(lax.axis_size(axis...  13.2 us
    pallas_call x7, Pallas kernels, call(): pl.pallas_call(body, out_shape=shapes, in_specs=in_specs or [VMEM] * len(...  10.3 us
    ppermute x11, waiting for transfers between devices, swap(): lax.ppermute(block, axis, [(i, i ^ xor) for i in range(lax.axis_size(axis...  7.56 us
    ppermute x3, waiting for transfers between devices, pair_b(): return lax.ppermute(block, ('gx', 'gy'), pairs)  3.75 us
    ppermute x1, starting transfers between devices, ring_b(): return lax.ppermute(block, axis, pairs)  2.4 us
    ppermute x3, starting transfers between devices, pair_b(): return lax.ppermute(block, ('gx', 'gy'), pairs)  2.05 us
  transfers between devices with their start and end apart: 15, of which 5 were waited for; matrix products, arithmetic and copies ran while one was open for 0% of the time, Pallas kernels for 12%

profile of v11, /device:TPU:0, one launch (start us, length us, event | category | flops | bytes accessed | tf_op | source)
XLA Modules:
  0.0 40.1 jit_solution(15978240226827127583)
XLA Ops:
  0.6 0.0 copy-start
  0.6 3.0 %collective-permute-start.2 = (f32[16,128]{1,0:T(8,128)}, f32[16,128]{1,0:T(8,128)S(1)}, u32[]{:S(2)}, u32[]{:S(2)}) collective-permute-start(f32[16,128]{1,0:T(8,128)} %bitcast.20), channel_id=1, source_target_pairs={{0,2},{1,3},{2,0},{3,1},{4,6},{5,7},{6,4},{7,5},{8,10},{9,11},{10,... | collective-permute-start | bytes 24584 | tf_op jit(solution)/shard_map/ppermute | solution.py:48
  3.6 0.0 collective-permute-start.3
  3.7 1.4 %shard_map.131 = (f32[320,128]{1,0:T(8,128)S(1)}, f32[304,128]{1,0:T(8,128)S(1)}, f32[120,128]{1,0:T(8,128)S(1)}, f32[4,256,128]{2,1,0:T(8,128)S(1)}, f32[3,256,...) custom-call(f32[4,256,128]{2,1,0:T(8,128)} %bitcast.16, ...), custom_call_target="tpu_custom_call" | custom-call | flops 1000000 | bytes 944128 | tf_op jit(solution)/shard_map/pallas_call | solution.py:36
  5.0 0.3 collective-permute-start
  5.3 2.0 %collective-permute-start.1 = (f32[304,128]{1,0:T(8,128)S(1)}, f32[304,128]{1,0:T(8,128)S(1)}, u32[]{:S(2)}, u32[]{:S(2)}) collective-permute-start(f32[304,128]{1,0:T(8,128)S(1)} %get-tuple-element.39), channel_id=1, source_target_pairs={{0,4},{1,2},{2,1},{3,7},{4,0},{5,6},{6,5},{7,3},{8,12},{9,10},{10,... | collective-permute-start | bytes 466952 | tf_op jit(solution)/shard_map/ppermute | solution.py:64
  7.2 0.0 collective-permute-start.4
  7.3 0.0 collective-permute-done.2
  7.3 0.0 collective-permute-done.3
  7.3 3.7 %collective-permute-done.1.refs_7_.refs_5_ = f32[304,128]{1,0:T(8,128)S(1)} collective-permute-done((f32[304,128]{1,0:T(8,128)S(1)}, f32[304,128]{1,0:T(8,128)S(1)}, u32[]{:S(2)}, u32[]{:S(2)}) %collective-permute-start.1) | collective-permute-done | bytes 155680 | tf_op jit(solution)/shard_map/ppermute | solution.py:64
  11.1 0.0 collective-permute-done.refs_6_.refs_4_
  11.1 0.5 %shard_map.133 = (f32[222,128]{1,0:T(8,128)S(1)}, f32[318,128]{1,0:T(8,128)S(1)}) custom-call(f32[4,256,128]{2,1,0:T(8,128)S(1)} %get-tuple-element.34.refs_0_, f32[3,256,128]{2,1,0:T(8,128)S(1)} %get-tuple-element.35.refs_1_, f32[16,128]{1,0:T(8,128)S(1)} %get-tuple-element.33.refs_2_.alpha, f32[16,128]{1,0:T(8,128)S(1)} %get-tuple-element.36.refs_3_, ...), custom_call_target="tpu_custom_call" | custom-call | flops 1000000 | bytes 1269760 | tf_op jit(solution)/shard_map/pallas_call | solution.py:36
  11.6 0.1 collective-permute-start.6
  11.7 0.1 collective-permute-done.4.early
  11.8 3.5 %collective-permute-start.5 = (f32[222,128]{1,0:T(8,128)S(1)}, f32[222,128]{1,0:T(8,128)S(1)}, u32[]{:S(2)}, u32[]{:S(2)}) collective-permute-start(f32[222,128]{1,0:T(8,128)S(1)} %get-tuple-element.44), channel_id=1, source_target_pairs={{0,4},{4,0},{8,12},{12,8},{16,20},{20,16},{24,28},{28,24},{1,5},{5... | collective-permute-start | bytes 341000 | tf_op jit(solution)/shard_map/ppermute | solution.py:48
  15.4 1.6 %collective-permute-start.7 = (f32[48,128]{1,0:T(8,128)S(1)}, f32[48,128]{1,0:T(8,128)S(1)}, u32[]{:S(2)}, u32[]{:S(2)}) collective-permute-start(f32[48,128]{1,0:T(8,128)S(1)} %pad_maximum_fusion.rest_0_), channel_id=1, source_target_pairs={{0,8},{4,12},{8,0},{12,4},{16,24},{20,28},{24,16},{28,20},{1,9},{5... | collective-permute-start | bytes 73736 | tf_op jit(solution)/shard_map/ppermute | solution.py:48
  16.9 1.1 %collective-permute-start.8 = (f32[48,128]{1,0:T(8,128)S(1)}, f32[48,128]{1,0:T(8,128)S(1)}, u32[]{:S(2)}, u32[]{:S(2)}) collective-permute-start(f32[48,128]{1,0:T(8,128)S(1)} %pad_maximum_fusion.rest_0_), channel_id=1, source_target_pairs={{0,16},{4,20},{8,24},{12,28},{16,0},{20,4},{24,8},{28,12},{1,17},{... | collective-permute-start | bytes 73736 | tf_op jit(solution)/shard_map/ppermute | solution.py:48
  18.0 1.7 %collective-permute-start.9 = (f32[48,128]{1,0:T(8,128)S(1)}, f32[48,128]{1,0:T(8,128)S(1)}, u32[]{:S(2)}, u32[]{:S(2)}) collective-permute-start(f32[48,128]{1,0:T(8,128)S(1)} %pad_maximum_fusion.rest_0_), channel_id=1, source_target_pairs={{0,24},{4,28},{8,16},{12,20},{16,8},{20,12},{24,0},{28,4},{1,25},{... | collective-permute-start | bytes 73736 | tf_op jit(solution)/shard_map/ppermute | solution.py:48
  19.7 0.0 copy-done
  19.7 1.0 %shard_map.132 = (f32[1536,128]{1,0:T(8,128)S(1)}, f32[1920,128]{1,0:T(8,128)S(1)}, f32[384,16]{1,0:T(8,128)S(1)}, f32[256,512]{1,0:T(8,128)S(1)}, bf16[256,256]...) custom-call(f32[4,256,128]{2,1,0:T(8,128)S(1)} %get-tuple-element.34.refs_0_, ...), custom_call_target="tpu_custom_call" | custom-call | flops 3000000 | bytes 1802240 | tf_op jit(solution)/shard_map/pallas_call | solution.py:36
  20.7 0.0 collective-permute-done.5.x_a
  20.8 0.0 collective-permute-done.6.x_b
  20.8 2.0 %shard_map.134 = (bf16[768,512]{1,0:T(8,128)(2,1)S(1)}, bf16[768,512]{1,0:T(8,128)(2,1)S(1)}, f32[2880,128]{1,0:T(8,128)S(1)}) custom-call(f32[1536,128]{1,0:T(8,128)S(1)} %get-tuple-element.41.core, f32[1920,128]{1,0:T(8,128)S(1)} %get-tuple-element.42.coef_core, f32[120,128]{1,0:T(8,128)S(1)} %collective-permute-done.4.early, ...), custom_call_target="tpu_custom_call" | custom-call | flops 10000000 | bytes 2107392 | tf_op jit(solution)/shard_map/pallas_call | solution.py:36
  22.7 0.0 collective-permute-done.7.rest_1_
  22.7 0.0 collective-permute-done.8.rest_2_
  22.8 0.9 %collective-permute-done.9.rest_3_ = f32[48,128]{1,0:T(8,128)S(1)} collective-permute-done((f32[48,128]{1,0:T(8,128)S(1)}, f32[48,128]{1,0:T(8,128)S(1)}, u32[]{:S(2)}, u32[]{:S(2)}) %collective-permute-start.9) | collective-permute-done | bytes 24608 | tf_op jit(solution)/shard_map/ppermute | solution.py:48
  23.7 4.1 %shard_map.135 = (f32[216,128]{1,0:T(8,128)S(1)}, f32[216,128]{1,0:T(8,128)S(1)}, f32[1536,128]{1,0:T(8,128)S(1)}) custom-call(f32[2880,128]{1,0:T(8,128)S(1)} %get-tuple-element.46.coef, bf16[768,512]{1,0:T(8,128)(2,1)S(1)} %get-tuple-element.47.tops, bf16[768,512]{1,0:T(8,128)(2,1)S(1)} %get-tuple-element.48.lows, f32[256,512]{1,0:T(8,128)S(1)} %get-tuple-element.49.wide, ...), custom_call_target="tpu_custom_call" | custom-call | flops 20000000 | bytes 5840896 | tf_op jit(solution)/shard_map/pallas_call | solution.py:36
  27.8 1.9 %collective-permute-start.10 = (f32[216,128]{1,0:T(8,128)S(1)}, f32[216,128]{1,0:T(8,128)S(1)}, u32[]{:S(2)}, u32[]{:S(2)}) collective-permute-start(f32[216,128]{1,0:T(8,128)S(1)} %get-tuple-element.55), channel_id=1, source_target_pairs={{0,4},{4,0},{8,12},{12,8},{16,20},{20,16},{24,28},{28,24},{1,5},{5... | collective-permute-start | bytes 331784 | tf_op jit(solution)/shard_map/ppermute | solution.py:48
  29.7 0.0 collective-permute-start.11
  29.7 2.9 %collective-permute-done.10.refs_3_ = f32[216,128]{1,0:T(8,128)S(1)} collective-permute-done((f32[216,128]{1,0:T(8,128)S(1)}, f32[216,128]{1,0:T(8,128)S(1)}, u32[]{:S(2)}, u32[]{:S(2)}) %collective-permute-start.10) | collective-permute-done | bytes 110624 | tf_op jit(solution)/shard_map/ppermute | solution.py:48
  32.6 0.0 collective-permute-done.11.refs_4_
  32.6 0.4 %shard_map.136 = (f32[208,128]{1,0:T(8,128)S(1)}, f32[208,128]{1,0:T(8,128)S(1)}, f32[4,256,128]{2,1,0:T(8,128)S(1)}, f32[16,128]{1,0:T(8,128)S(1)}, f32[16,128]{1,0:T(8,128)S(1)}) custom-call(f32[4,256,128]{2,1,0:T(8,128)S(1)} %get-tuple-element.34.refs_0_, f32[384,16]{1,0:T(8,128)S(1)} %get-tuple-element.40.refs_1_, ...), custom_call_target="tpu_custom_call" | custom-call | flops 1000000 | bytes 1556480 | tf_op jit(solution)/shard_map/pallas_call | solution.py:36
  33.0 0.0 collective-permute-start.12
  33.0 2.4 %collective-permute-start.13 = (f32[208,128]{1,0:T(8,128)S(1)}, f32[208,128]{1,0:T(8,128)S(1)}, u32[]{:S(2)}, u32[]{:S(2)}) collective-permute-start(f32[208,128]{1,0:T(8,128)S(1)} %get-tuple-element.60), channel_id=1, source_target_pairs={{0,3},{1,2},{2,1},{3,0},{4,7},{5,6},{6,5},{7,4},{8,11},{9,10},{10,... | collective-permute-start | bytes 319496 | tf_op jit(solution)/shard_map/ppermute | solution.py:70
  35.4 0.1 collective-permute-start.14
  35.4 3.6 %collective-permute-done.14.rest_0_ = f32[16,128]{1,0:T(8,128)S(1)} collective-permute-done((f32[16,128]{1,0:T(8,128)S(1)}, f32[16,128]{1,0:T(8,128)S(1)}, u32[]{:S(2)}, u32[]{:S(2)}) %collective-permute-start.14) | collective-permute-done | bytes 8224 | tf_op jit(solution)/shard_map/ppermute | solution.py:48
  39.1 0.0 collective-permute-done.12.y_a
  39.1 0.0 collective-permute-done.13.y_b
  39.1 0.9 %shard_map.137 = (f32[4,256,128]{2,1,0:T(8,128)}, f32[16,128]{1,0:T(8,128)}) custom-call(f32[16,128]{1,0:T(8,128)S(1)} %get-tuple-element.33.refs_2_.alpha, f32[4,256,128]{2,1,0:T(8,128)S(1)} %get-tuple-element.57.near, f32[16,128]{1,0:T(8,128)S(1)} %get-tuple-element.58.sums, f32[208,128]{1,0:T(8,128)S(1)} %collective-permute-done.12.y_a, ...), custom_call_target="tpu_custom_call" | custom-call | flops 1000000 | bytes 761856 | tf_op jit(solution)/shard_map/pallas_call | solution.py:36
  (5 shorter events, 0.0 us)
Async XLA Ops:
  0.6 19.1 %copy-start = (f32[1,1,256,4,128]{4,3,2,1,0:T(4,128)S(1)}, f32[1,1,256,4,128]{4,3,2,1,0:T(4,128)}, u32[]{:S(2)}) copy-start(f32[1,1,256,4,128]{4,3,2,1,0:T(4,128)} %param.22) | copy-start | bytes 1572868
  0.6 6.7 %collective-permute-start.2 = (f32[16,128]{1,0:T(8,128)}, f32[16,128]{1,0:T(8,128)S(1)}, u32[]{:S(2)}, u32[]{:S(2)}) collective-permute-start(f32[16,128]{1,0:T(8,128)} %bitcast.20), channel_id=1, source_target_pairs={{0,2},{1,3},{2,0},{3,1},{4,6},{5,7},{6,4},{7,5},{8,10},{9,11},{10,... | collective-permute-start | bytes 24584 | tf_op jit(solution)/shard_map/ppermute | solution.py:48
  3.6 3.7 %collective-permute-start.3 = (f32[16,128]{1,0:T(8,128)}, f32[16,128]{1,0:T(8,128)S(1)}, u32[]{:S(2)}, u32[]{:S(2)}) collective-permute-start(f32[16,128]{1,0:T(8,128)} %bitcast.21), channel_id=1, source_target_pairs={{0,3},{1,2},{2,1},{3,0},{4,7},{5,6},{6,5},{7,4},{8,11},{9,10},{10,... | collective-permute-start | bytes 24584 | tf_op jit(solution)/shard_map/ppermute | solution.py:48
  5.0 6.0 %collective-permute-start = (f32[320,128]{1,0:T(8,128)S(1)}, f32[320,128]{1,0:T(8,128)S(1)}, u32[]{:S(2)}, u32[]{:S(2)}) collective-permute-start(f32[320,128]{1,0:T(8,128)S(1)} %get-tuple-element.38), channel_id=1, source_target_pairs={{0,1},{1,0},{2,3},{3,2},{4,5},{5,4},{6,7},{7,6},{8,9},{9,8},{10,11... | collective-permute-start | bytes 491528 | tf_op jit(solution)/shard_map/ppermute | solution.py:48
  5.3 5.8 %collective-permute-start.1 = (f32[304,128]{1,0:T(8,128)S(1)}, f32[304,128]{1,0:T(8,128)S(1)}, u32[]{:S(2)}, u32[]{:S(2)}) collective-permute-start(f32[304,128]{1,0:T(8,128)S(1)} %get-tuple-element.39), channel_id=1, source_target_pairs={{0,4},{1,2},{2,1},{3,7},{4,0},{5,6},{6,5},{7,3},{8,12},{9,10},{10,... | collective-permute-start | bytes 466952 | tf_op jit(solution)/shard_map/ppermute | solution.py:64
  7.2 4.6 %collective-permute-start.4 = (f32[120,128]{1,0:T(8,128)S(1)}, f32[120,128]{1,0:T(8,128)S(1)}, u32[]{:S(2)}, u32[]{:S(2)}) collective-permute-start(f32[120,128]{1,0:T(8,128)S(1)} %get-tuple-element.43), channel_id=1, source_target_pairs={{0,4},{4,0},{8,12},{12,8},{16,20},{20,16},{24,28},{28,24},{1,5},{5... | collective-permute-start | bytes 184328 | tf_op jit(solution)/shard_map/ppermute | solution.py:48
  11.6 9.1 %collective-permute-start.6 = (f32[318,128]{1,0:T(8,128)S(1)}, f32[318,128]{1,0:T(8,128)S(1)}, u32[]{:S(2)}, u32[]{:S(2)}) collective-permute-start(f32[318,128]{1,0:T(8,128)S(1)} %get-tuple-element.45), channel_id=1, source_target_pairs={{0,1},{4,8},{8,4},{12,16},{16,12},{20,24},{24,20},{28,29},{1,0},{5... | collective-permute-start | bytes 488456 | tf_op jit(solution)/shard_map/ppermute | solution.py:64
  11.8 8.9 %collective-permute-start.5 = (f32[222,128]{1,0:T(8,128)S(1)}, f32[222,128]{1,0:T(8,128)S(1)}, u32[]{:S(2)}, u32[]{:S(2)}) collective-permute-start(f32[222,128]{1,0:T(8,128)S(1)} %get-tuple-element.44), channel_id=1, source_target_pairs={{0,4},{4,0},{8,12},{12,8},{16,20},{20,16},{24,28},{28,24},{1,5},{5... | collective-permute-start | bytes 341000 | tf_op jit(solution)/shard_map/ppermute | solution.py:48
  15.4 7.4 %collective-permute-start.7 = (f32[48,128]{1,0:T(8,128)S(1)}, f32[48,128]{1,0:T(8,128)S(1)}, u32[]{:S(2)}, u32[]{:S(2)}) collective-permute-start(f32[48,128]{1,0:T(8,128)S(1)} %pad_maximum_fusion.rest_0_), channel_id=1, source_target_pairs={{0,8},{4,12},{8,0},{12,4},{16,24},{20,28},{24,16},{28,20},{1,9},{5... | collective-permute-start | bytes 73736 | tf_op jit(solution)/shard_map/ppermute | solution.py:48
  16.9 5.8 %collective-permute-start.8 = (f32[48,128]{1,0:T(8,128)S(1)}, f32[48,128]{1,0:T(8,128)S(1)}, u32[]{:S(2)}, u32[]{:S(2)}) collective-permute-start(f32[48,128]{1,0:T(8,128)S(1)} %pad_maximum_fusion.rest_0_), channel_id=1, source_target_pairs={{0,16},{4,20},{8,24},{12,28},{16,0},{20,4},{24,8},{28,12},{1,17},{... | collective-permute-start | bytes 73736 | tf_op jit(solution)/shard_map/ppermute | solution.py:48
  18.0 5.6 %collective-permute-start.9 = (f32[48,128]{1,0:T(8,128)S(1)}, f32[48,128]{1,0:T(8,128)S(1)}, u32[]{:S(2)}, u32[]{:S(2)}) collective-permute-start(f32[48,128]{1,0:T(8,128)S(1)} %pad_maximum_fusion.rest_0_), channel_id=1, source_target_pairs={{0,24},{4,28},{8,16},{12,20},{16,8},{20,12},{24,0},{28,4},{1,25},{... | collective-permute-start | bytes 73736 | tf_op jit(solution)/shard_map/ppermute | solution.py:48
  27.8 4.8 %collective-permute-start.10 = (f32[216,128]{1,0:T(8,128)S(1)}, f32[216,128]{1,0:T(8,128)S(1)}, u32[]{:S(2)}, u32[]{:S(2)}) collective-permute-start(f32[216,128]{1,0:T(8,128)S(1)} %get-tuple-element.55), channel_id=1, source_target_pairs={{0,4},{4,0},{8,12},{12,8},{16,20},{20,16},{24,28},{28,24},{1,5},{5... | collective-permute-start | bytes 331784 | tf_op jit(solution)/shard_map/ppermute | solution.py:48
  29.7 2.9 %collective-permute-start.11 = (f32[216,128]{1,0:T(8,128)S(1)}, f32[216,128]{1,0:T(8,128)S(1)}, u32[]{:S(2)}, u32[]{:S(2)}) collective-permute-start(f32[216,128]{1,0:T(8,128)S(1)} %get-tuple-element.56), channel_id=1, source_target_pairs={{0,1},{4,8},{8,4},{12,16},{16,12},{20,24},{24,20},{28,29},{1,0},{5... | collective-permute-start | bytes 331784 | tf_op jit(solution)/shard_map/ppermute | solution.py:64
  33.0 6.1 %collective-permute-start.12 = (f32[208,128]{1,0:T(8,128)S(1)}, f32[208,128]{1,0:T(8,128)S(1)}, u32[]{:S(2)}, u32[]{:S(2)}) collective-permute-start(f32[208,128]{1,0:T(8,128)S(1)} %get-tuple-element.59), channel_id=1, source_target_pairs={{0,1},{1,0},{2,3},{3,2},{4,5},{5,4},{6,7},{7,6},{8,9},{9,8},{10,11... | collective-permute-start | bytes 319496 | tf_op jit(solution)/shard_map/ppermute | solution.py:48
  33.0 6.1 %collective-permute-start.13 = (f32[208,128]{1,0:T(8,128)S(1)}, f32[208,128]{1,0:T(8,128)S(1)}, u32[]{:S(2)}, u32[]{:S(2)}) collective-permute-start(f32[208,128]{1,0:T(8,128)S(1)} %get-tuple-element.60), channel_id=1, source_target_pairs={{0,3},{1,2},{2,1},{3,0},{4,7},{5,6},{6,5},{7,4},{8,11},{9,10},{10,... | collective-permute-start | bytes 319496 | tf_op jit(solution)/shard_map/ppermute | solution.py:70
  35.4 3.7 %collective-permute-start.14 = (f32[16,128]{1,0:T(8,128)S(1)}, f32[16,128]{1,0:T(8,128)S(1)}, u32[]{:S(2)}, u32[]{:S(2)}) collective-permute-start(f32[16,128]{1,0:T(8,128)S(1)} %get-tuple-element.61), channel_id=1, source_target_pairs={{0,2},{1,3},{2,0},{3,1},{4,6},{5,7},{6,4},{7,5},{8,10},{9,11},{10,... | collective-permute-start | bytes 24584 | tf_op jit(solution)/shard_map/ppermute | solution.py:48

commit v12 on v9

--- a/solution.py
+++ b/solution.py
@@ -284,8 +284,9 @@
 
 def prepare(ny, delta, coefs, alpha, near_tiles, meta, weights, y_a, y_b, *rest):
     others = rest[: ny - 2]
-    core, coef, picks, wide, slot_pick, slot_push, beam_pick, columns = rest[ny - 2 : ny + 6]
-    known, tiles = rest[ny + 6 :]
+    core, coef, picks, wide, slot_push, beam_pick, columns = rest[ny - 2 : ny + 5]
+    state_1, state_2, tally, edge_pick = rest[ny + 5 : ny + 9]
+    state_3, known, tiles = rest[ny + 9 :]
     owned = alpha.shape[0] // NC
 
     def fill(ref, base, own, y_base, reach):
@@ -328,11 +329,66 @@
     turned = jnp.transpose(meta[...])
     columns[...] = turned
     slot_lane = lax.broadcasted_iota(jnp.int32, (slots, CX * CY), 1).astype(f32)
-    slot_pick[...] = (slot_lane == turned[:, 0:1]).astype(f32).astype(bf16)
+    slot_pick = (slot_lane == turned[:, 0:1]).astype(f32).astype(bf16)
+    edge_lane = lax.broadcasted_iota(jnp.int32, (slots, 128), 1)
+    half = RIM * CY
+    place = jnp.where(edge_lane < half, edge_lane, edge_lane + CX * CY - 2 * half)
+    place = jnp.where(edge_lane < 2 * half, place, -1).astype(f32)
+    near_edge = (place == turned[:, 0:1]).astype(f32).astype(bf16)
+    edge_pick[:, 0:128] = near_edge
+    edge_pick[:, 128:256] = near_edge
     column_row = lax.broadcasted_iota(jnp.int32, (CX * CY, slots), 0).astype(f32)
     slot_push[...] = (column_row == meta[0:1]).astype(f32).astype(bf16)
     beam_lane = lax.broadcasted_iota(jnp.int32, (slots, per_beam), 1).astype(f32)
     beam_pick[...] = (beam_lane == turned[:, 1:2]).astype(f32).astype(bf16)
+
+    states = [core, state_1, state_2, state_3]
+    for step in range(STEPS):
+        source, target = states[step], states[step + 1]
+
+        def body(x, carry, source=source, target=target):
+            at = pl.multiple_of(x * PITCH, 8)
+            k = [coef[pl.ds(f * CORE + at, PITCH)] for f in range(5)]
+            for c in range(NC):
+                base = c * CORE + at
+                target[pl.ds(base, PITCH)] = forward_column(source, base, k)
+            return carry
+
+        lax.fori_loop(step + 1, CX - 1 - step, body, 0)
+        own = []
+        for c in range(NC):
+            pieces = [jnp.zeros(((step + 1) * CY, 128), f32)]
+            for x in range(step + 1, CX - 1 - step):
+                at = c * CORE + x * PITCH
+                pieces.append(target[at : at + CY])
+            own.append(jnp.concatenate(pieces + pieces[:1], axis=0))
+        seen = two_part_dot(slot_pick, jnp.concatenate(own, axis=1)) * wide[...]
+        total = seen[:, 0:128]
+        for c in range(1, NC):
+            total = total + seen[:, c * 128 : (c + 1) * 128]
+        tally[step * slots : (step + 1) * slots] = total
+
+
+def forward_column(source, base, k):
+    here = source[pl.ds(base, PITCH)]
+    return (
+        k[0] * here
+        + k[1] * source[pl.ds(base + PITCH, PITCH)]
+        + k[2] * source[pl.ds(base - PITCH, PITCH)]
+        + k[3] * pltpu.roll(here, PITCH - 1, 0)
+        + k[4] * pltpu.roll(here, 1, 0)
+    )
+
+
+def backward_column(source, base, coef, at):
+    here = source[pl.ds(base, PITCH)]
+    return (
+        coef[pl.ds(at, PITCH)] * here
+        + coef[pl.ds(FIELD + at - PITCH, PITCH)] * source[pl.ds(base - PITCH, PITCH)]
+        + coef[pl.ds(2 * FIELD + at + PITCH, PITCH)] * source[pl.ds(base + PITCH, PITCH)]
+        + pltpu.roll(coef[pl.ds(3 * FIELD + at, PITCH)] * here, 1, 0)
+        + pltpu.roll(coef[pl.ds(4 * FIELD + at, PITCH)] * here, PITCH - 1, 0)
+    )
 
 
 def combine_coefs(viscous, along_x, along_y):
@@ -352,7 +408,27 @@
         ref[at : at + PITCH] = jnp.zeros((PITCH, 128), f32)
 
 
-def forecast(core, coef_core, x_a, x_b, tops, lows, coef, state_0, state_1, raw):
+def edges(
+    core,
+    core_coef,
+    near_1,
+    near_2,
+    tally,
+    wide,
+    edge_pick,
+    slot_push,
+    beam_pick,
+    columns,
+    x_a,
+    x_b,
+    *rest,
+):
+    beams = rest[:-13]
+    out_a, out_b, back_2, back_1, coef, tops, lows = rest[-13:-6]
+    state_0, state_1, state_2, state_3, raw, forcing = rest[-6:]
+    even, _, _ = place_on("gx")
+    slots = columns.shape[0]
+
     def fill(ref, base, x_base, found):
         for away, start, extra in found:
             for source, target, size in (
@@ -367,107 +443,139 @@
                     at = base + (FIRST + CX - 1 + away) * PITCH + target
                     ref[at : at + size] = east
 
+    def copy(source, target, x, count):
+        for c in range(NC):
+            first = c * CORE + x * PITCH
+            at = c * FIELD + (FIRST + x) * PITCH
+            target[at : at + count * PITCH] = source[first : first + count * PITCH]
+
     rim = [FIRST - 3, FIRST - 2, FIRST - 1, FIRST + CX, FIRST + CX + 1, FIRST + CX + 2]
-    for c in range(NC):
-        at = c * FIELD + FIRST * PITCH
-        state_0[at : at + CORE] = core[c * CORE : (c + 1) * CORE]
+    for x, (source, target) in enumerate(((core, state_0), (near_1, state_1), (near_2, state_2))):
+        copy(source, target, x, 2)
+        copy(source, target, CX - 2 - x, 2)
+    for c in range(NC):
         clear(state_0, c * FIELD, rim)
         fill(state_0, c * FIELD, c * WIDE_ROWS, WIDE)
     for f in range(3):
         clear(raw, f * FIELD, rim[1:5])
         fill(raw, f * FIELD, X_COEF + f * SLIM_ROWS, SLIM)
     for f in range(5):
-        at = f * FIELD + FIRST * PITCH
-        coef[at : at + CORE] = coef_core[f * CORE : (f + 1) * CORE]
+        for x in (0, CX - RIM):
+            first, at = f * CORE + x * PITCH, f * FIELD + (FIRST + x) * PITCH
+            coef[at : at + RIM * PITCH] = core_coef[first : first + RIM * PITCH]
         clear(coef, f * FIELD, [0, 1, BLOCKS - 2, BLOCKS - 1])
     for b in rim[1:5]:
         rows = [slice(f * FIELD + b * PITCH, f * FIELD + (b + 1) * PITCH) for f in range(5)]
         for f, value in enumerate(combine_coefs(*[raw[rows[f]] for f in range(3)])):
             coef[rows[f]] = value
 
-    def forward(source, target, low, high):
-        def body(b, carry):
-            at = pl.multiple_of(b * PITCH, 8)
-            k = [coef[pl.ds(f * FIELD + at, PITCH)] for f in range(5)]
-            for c in range(NC):
-                base = c * FIELD + at
-                here = source[pl.ds(base, PITCH)]
-                target[pl.ds(base, PITCH)] = (
-                    k[0] * here
-                    + k[1] * source[pl.ds(base + PITCH, PITCH)]
-                    + k[2] * source[pl.ds(base - PITCH, PITCH)]
-                    + k[3] * pltpu.roll(here, PITCH - 1, 0)
-                    + k[4] * pltpu.roll(here, 1, 0)
-                )
-            return carry
-
-        lax.fori_loop(low, high, body, 0)
-
-    buffers = [state_0, state_1]
-    for step in range(STEPS):
-        source, target = buffers[step % 2], buffers[(step + 1) % 2]
-        forward(source, target, 2 + step, BLOCKS - 2 - step)
-        own = jnp.concatenate(
-            [
-                jnp.concatenate(
-                    [
-                        target[c * FIELD + b * PITCH : c * FIELD + b * PITCH + CY]
-                        for b in range(FIRST, FIRST + CX)
-                    ],
-                    axis=0,
-                )
-                for c in range(NC)
-            ],
-            axis=1,
-        )
-        rows = slice(step * CX * CY, (step + 1) * CX * CY)
-        tops[rows], lows[rows] = split(own)
-
-
-def main(
-    coef,
-    tops,
-    lows,
-    wide,
-    slot_pick,
-    slot_push,
-    beam_pick,
-    columns,
-    *rest,
-):
-    beams = rest[:-6]
-    out_a, out_b, out_core, state_0, state_1, forcing = rest[-6:]
-    even, _, _ = place_on("gx")
-    slots = columns.shape[0]
     gate_lane = lax.broadcasted_iota(jnp.int32, (slots, 128), 1).astype(f32)
     gate_here = gate_lane == columns[:, 2:3]
     scaled = columns[:, 3:4]
+    outer = [*range(RIM), *range(CX - RIM, CX)]
+    half = RIM * CY
+    push = jnp.concatenate([slot_push[0:half], slot_push[CX * CY - half :]], axis=0)
+    states = [state_0, state_1, state_2, state_3]
     for step in range(STEPS):
-        rows = slice(step * CX * CY, (step + 1) * CX * CY)
-        picked = jnp.dot(slot_pick[...], tops[rows], preferred_element_type=f32)
-        picked = picked + jnp.dot(slot_pick[...], lows[rows], preferred_element_type=f32)
-        picked = picked * wide[...]
+        source, target = states[step], states[step + 1]
+        for x in range(step - 2, step + 1):
+            for b in (FIRST + x, FIRST + CX - 1 - x):
+                at = b * PITCH
+                k = [coef[f * FIELD + at : f * FIELD + at + PITCH] for f in range(5)]
+                for c in range(NC):
+                    base = c * FIELD + at
+                    target[base : base + PITCH] = forward_column(source, base, k)
+        zero = jnp.zeros((CY, 128), f32)
+        parts = []
+        for c in range(NC):
+            pieces = []
+            for x in outer:
+                at = c * FIELD + (FIRST + x) * PITCH
+                known = x <= step or x >= CX - 1 - step
+                pieces.append(target[at : at + CY] if known else zero)
+            value = jnp.concatenate(pieces + [jnp.zeros((128 - 2 * half, 128), f32)], axis=0)
+            parts.append(jnp.concatenate(split(value), axis=0))
+        seen = jnp.dot(
+            edge_pick[...], jnp.concatenate(parts, axis=1), preferred_element_type=f32
+        )
+        seen = seen * wide[...]
         table = []
         for part in beams:
             for at in range(0, part.shape[0], STEPS * OWN_BEAMS):
                 first = at + step * OWN_BEAMS
                 table.append(part[first : first + OWN_BEAMS])
         table = two_part_dot(beam_pick[...], jnp.concatenate(table, axis=0))
-        tally = -jnp.where(gate_here, table, 0.0)
+        rows = slice(step * slots, (step + 1) * slots)
+        total = tally[rows] - jnp.where(gate_here, table, 0.0)
         for c in range(NC):
-            tally = tally + picked[:, c * 128 : (c + 1) * 128]
-        misfit = scaled * jnp.sum(tally, axis=1, keepdims=True)
-        forcing[rows] = two_part_dot(slot_push[...], misfit * wide[...])
-
-    buffers = [state_0, state_1]
-
-    for c in range(NC):
-        clear(state_0, c * FIELD, [0, 1, 2, 3, BLOCKS - 4, BLOCKS - 3, BLOCKS - 2, BLOCKS - 1])
-        clear(state_1, c * FIELD, [1, 2, BLOCKS - 3, BLOCKS - 2])
-
-    def add_forcing(ref, step):
+            total = total + seen[:, c * 128 : (c + 1) * 128]
+        misfit = scaled * jnp.sum(total, axis=1, keepdims=True)
+        top, low = split(misfit * wide[...])
+        tops[rows] = top
+        lows[rows] = low
+        forcing[step * 2 * half : (step + 1) * 2 * half] = jnp.dot(
+            push, top, preferred_element_type=f32
+        ) + jnp.dot(push, low, preferred_element_type=f32)
+
+    def forced(step, i, c):
+        at = step * 2 * half + i * CY
+        return forcing[at : at + CY, c * 128 : (c + 1) * 128]
+
+    for c in range(NC):
+        clear(state_0, c * FIELD, [2, 3, BLOCKS - 4, BLOCKS - 3])
+        clear(back_2, c * FIELD, [1, 2, BLOCKS - 3, BLOCKS - 2])
+        clear(back_1, c * FIELD, [0, 1, BLOCKS - 2, BLOCKS - 1])
+        for i, x in enumerate(outer):
+            at = c * FIELD + (FIRST + x) * PITCH
+            state_0[at : at + CY] = forced(STEPS - 1, i, c)
+            state_0[at + CY : at + PITCH] = jnp.zeros((PITCH - CY, 128), f32)
+    fields = [state_0, back_2, back_1, state_3]
+    for step in range(STEPS):
+        source, target = fields[step], fields[step + 1]
+        for x in range(-1 - step, 2 - step):
+            for b in (FIRST + x, FIRST + CX - 1 - x):
+                for c in range(NC):
+                    base = c * FIELD + b * PITCH
+                    target[base : base + PITCH] = backward_column(source, base, coef, b * PITCH)
+        if step < STEPS - 1:
+            for i, x in enumerate(outer):
+                if x < 2 - step or x > CX - 3 + step:
+                    for c in range(NC):
+                        at = c * FIELD + (FIRST + x) * PITCH
+                        target[at : at + CY] += forced(STEPS - 2 - step, i, c)
+    for c in range(NC):
+        for away, start, extra in WIDE:
+            for source, target, size in (
+                (PITCH - extra, 0, extra),
+                (0, extra, CY + extra),
+            ):
+                if size:
+                    at = c * FIELD + (FIRST - away) * PITCH + source
+                    west = state_3[at : at + size]
+                    at = c * FIELD + (FIRST + CX - 1 + away) * PITCH + source
+                    east = state_3[at : at + size]
+                    at = c * WIDE_ROWS + start + target
+                    out_a[at : at + size] = jnp.where(even, east, west)
+                    out_b[at : at + size] = jnp.where(even, west, east)
+
+
+def interior(core_coef, edge_coef, back_2, back_1, tops, lows, slot_push, out, *scratch):
+    coef, forced, field_2, field_1, forcing = scratch
+    for f in range(5):
+        at = f * FIELD + FIRST * PITCH
+        coef[at : at + CORE] = core_coef[f * CORE : (f + 1) * CORE]
+        for b in (FIRST - 1, FIRST + CX):
+            at = f * FIELD + b * PITCH
+            coef[at : at + PITCH] = edge_coef[at : at + PITCH]
+    for step in range(STEPS):
+        rows = slice(step * CX * CY, (step + 1) * CX * CY)
+        forcing[rows] = jnp.dot(
+            slot_push[...], tops[rows], preferred_element_type=f32
+        ) + jnp.dot(slot_push[...], lows[rows], preferred_element_type=f32)
+
+    def add_forcing(ref, step, columns):
         for c in range(NC):
-            for x in range(CX):
+            for x in columns:
                 at = c * FIELD + (FIRST + x) * PITCH
                 first = step * CX * CY + x * CY
                 value = forcing[first : first + CY, c * 128 : (c + 1) * 128]
@@ -477,52 +585,33 @@
                 else:
                     ref[at : at + CY] += value
 
-    def backward(source, target, low, high):
-        def body(b, carry):
-            at = pl.multiple_of(b * PITCH, 8)
-            k = [
-                coef[pl.ds(at, PITCH)],
-                coef[pl.ds(FIELD + at - PITCH, PITCH)],
-                coef[pl.ds(2 * FIELD + at + PITCH, PITCH)],
-                coef[pl.ds(3 * FIELD + at, PITCH)],
-                coef[pl.ds(4 * FIELD + at, PITCH)],
-            ]
+    def sweep(source, target, low, high):
+        def body(x, carry):
+            at = pl.multiple_of((x + FIRST) * PITCH, 8)
             for c in range(NC):
-                base = c * FIELD + at
-                here = source[pl.ds(base, PITCH)]
-                target[pl.ds(base, PITCH)] = (
-                    k[0] * here
-                    + k[1] * source[pl.ds(base - PITCH, PITCH)]
-                    + k[2] * source[pl.ds(base + PITCH, PITCH)]
-                    + pltpu.roll(k[3] * here, 1, 0)
-                    + pltpu.roll(k[4] * here, PITCH - 1, 0)
-                )
+                value = backward_column(source, c * FIELD + at, coef, at)
+                if target is out:
+                    target[pl.ds(pl.multiple_of(c * CORE + x * PITCH, 8), PITCH)] = value
+                else:
+                    target[pl.ds(c * FIELD + at, PITCH)] = value
             return carry
 
         lax.fori_loop(low, high, body, 0)
 
-    for step in range(STEPS):
-        source, target = buffers[step % 2], buffers[(step + 1) % 2]
-        add_forcing(source, STEPS - 1 - step)
-        backward(source, target, FIRST - 1 - step, FIRST + CX + 1 + step)
-    final = buffers[STEPS % 2]
-
-    for c in range(NC):
-        at = c * FIELD + FIRST * PITCH
-        out_core[c * CORE : (c + 1) * CORE] = final[at : at + CORE]
-        for away, start, extra in WIDE:
-            for source, target, size in (
-                (PITCH - extra, 0, extra),
-                (0, extra, CY + extra),
-            ):
-                if size:
-                    at = c * FIELD + (FIRST - away) * PITCH + source
-                    west = final[at : at + size]
-                    at = c * FIELD + (FIRST + CX - 1 + away) * PITCH + source
-                    east = final[at : at + size]
-                    at = c * WIDE_ROWS + start + target
-                    out_a[at : at + size] = jnp.where(even, east, west)
-                    out_b[at : at + size] = jnp.where(even, west, east)
+    def copy(source, target, columns):
+        for c in range(NC):
+            for x in columns:
+                at = c * FIELD + (FIRST + x) * PITCH
+                target[at : at + PITCH] = source[at : at + PITCH]
+
+    add_forcing(forced, STEPS - 1, range(CX))
+    sweep(forced, field_2, 2, CX - 2)
+    add_forcing(field_2, STEPS - 2, range(2, CX - 2))
+    copy(back_2, field_2, (0, 1, CX - 2, CX - 1))
+    sweep(field_2, field_1, 1, CX - 1)
+    add_forcing(field_1, STEPS - 3, range(1, CX - 1))
+    copy(back_1, field_1, (-1, 0, CX - 1, CX))
+    sweep(field_1, out, 0, CX)
 
 
 def add_x(ny, delta, picks, core, x_a, x_b, *rest):
@@ -665,52 +754,83 @@
     x_a = swap(x_a, "gx", 1)
     x_b = pair_b(x_b, "gx", "gy")
 
-    core, coef, picks, wide, slot_pick, slot_push, beam_pick, columns = call(
+    big = (NC * FIELD, 128)
+    (
+        core,
+        coef,
+        picks,
+        wide,
+        slot_push,
+        beam_pick,
+        columns,
+        state_1,
+        state_2,
+        tally,
+        edge_pick,
+    ) = call(
         lambda *refs: prepare(ny, *refs),
         [
             (NC * CORE, 128),
             (5 * CORE, 128),
             (CORE, total),
             (slots, NC * 128),
-            jax.ShapeDtypeStruct((slots, CX * CY), bf16),
             jax.ShapeDtypeStruct((CX * CY, slots), bf16),
             jax.ShapeDtypeStruct((slots, beam_count), bf16),
             (slots, 8),
+            (NC * CORE, 128),
+            (NC * CORE, 128),
+            (STEPS * slots, 128),
+            jax.ShapeDtypeStruct((slots, 256), bf16),
         ],
         [fine, coefs, control_near, near_tiles, meta, weights, y_a, y_b, *others],
         [
+            pltpu.VMEM((NC * CORE, 128), f32),
             pltpu.VMEM((total * NC, 128), f32),
             pltpu.VMEM((128, 128), f32),
         ],
         flops=3000000,
     )
-
-
-    tops, lows, coef = call(
-        forecast,
+    back_a, back_b, back_2, back_1, edge_coef, tops, lows = call(
+        edges,
         [
-            jax.ShapeDtypeStruct((STEPS * CX * CY, NC * 128), bf16),
-            jax.ShapeDtypeStruct((STEPS * CX * CY, NC * 128), bf16),
+            (X_COEF, 128),
+            (X_COEF, 128),
+            big,
+            big,
             (5 * FIELD, 128),
+            jax.ShapeDtypeStruct((STEPS * slots, NC * 128), bf16),
+            jax.ShapeDtypeStruct((STEPS * slots, NC * 128), bf16),
         ],
-        [core, coef, x_a, x_b],
         [
-            pltpu.VMEM((NC * FIELD, 128), f32),
-            pltpu.VMEM((NC * FIELD, 128), f32),
+            core,
+            coef,
+            state_1,
+            state_2,
+            tally,
+            wide,
+            edge_pick,
+            slot_push,
+            beam_pick,
+            columns,
+            x_a,
+            x_b,
+            *beams,
+        ],
+        [pltpu.VMEM(big, f32)] * 4
+        + [
             pltpu.VMEM((3 * FIELD, 128), f32),
+            pltpu.VMEM((STEPS * 2 * RIM * CY, NC * 128), f32),
         ],
         flops=10000000,
     )
-    back_a, back_b, core = call(
-        main,
-        [(X_COEF, 128), (X_COEF, 128), (NC * CORE, 128)],
-        [coef, tops, lows, wide, slot_pick, slot_push, beam_pick, columns, *beams],
-        [
-            pltpu.VMEM((NC * FIELD, 128), f32),
-            pltpu.VMEM((NC * FIELD, 128), f32),
-            pltpu.VMEM((STEPS * CX * CY, NC * 128), f32),
-        ],
-        flops=20000000,
+    (core,) = call(
+        interior,
+        [(NC * CORE, 128)],
+        [coef, edge_coef, back_2, back_1, tops, lows, slot_push],
+        [pltpu.VMEM((5 * FIELD, 128), f32)]
+        + [pltpu.VMEM(big, f32)] * 3
+        + [pltpu.VMEM((STEPS * CX * CY, NC * 128), f32)],
+        flops=10000000,
     )
     x_a = swap(back_a, "gx", 1)
     x_b = pair_b(back_b, "gx", "gy")

time: 39.2 us -> 35.8 us (0.913); the launches traced: 38.4 us -> 35.4 us
  waiting for transfers between devices: 10.7 us -> 8.24 us
  starting transfers between devices: 16.7 us -> 15.7 us
  Pallas kernels: 10.3 us -> 10.8 us
    ppermute x11, waiting for transfers between devices: 10.7 us -> 8.22 us  [swap(): lax.ppermute(block, axis, [(i, i ^ xor) for i in range(lax.axis_size(axis...]
    ppermute x11, starting transfers between devices: 13.1 us -> 11.5 us  [swap(): lax.ppermute(block, axis, [(i, i ^ xor) for i in range(lax.axis_size(axis...]
    ppermute x1, starting transfers between devices: 0.98 us -> 1.59 us  [ring_b(): return lax.ppermute(block, axis, pairs)]
    pallas_call x7, Pallas kernels: 10.3 us -> 10.8 us  [call(): pl.pallas_call(body, out_shape=shapes, in_specs=in_specs or [VMEM] * len(...]
  transfers between devices with their start and end apart: 15 -> 15, of which waited for: 5 -> 4; matrix products, arithmetic and copies ran while one was open for 0% -> 0% of each run, Pallas kernels for 9% -> 16%
where the time goes in v12:
time: 35.8 us; the launch traced here: 35.4 us
  starting transfers between devices  15.7 us (44%)
  Pallas kernels  10.8 us (30%)
  waiting for transfers between devices  8.24 us (23%)
  between operations  0.72 us (2%)
    ppermute x11, starting transfers between devices, swap(): lax.ppermute(block, axis, [(i, i ^ xor) for i in range(lax.axis_size(axis...  11.5 us
    pallas_call x7, Pallas kernels, call(): pl.pallas_call(body, out_shape=shapes, in_specs=in_specs or [VMEM] * len(...  10.8 us
    ppermute x11, waiting for transfers between devices, swap(): lax.ppermute(block, axis, [(i, i ^ xor) for i in range(lax.axis_size(axis...  8.22 us
    ppermute x3, starting transfers between devices, pair_b(): return lax.ppermute(block, ('gx', 'gy'), pairs)  2.6 us
    ppermute x1, starting transfers between devices, ring_b(): return lax.ppermute(block, axis, pairs)  1.59 us
  transfers between devices with their start and end apart: 15, of which 4 were waited for; matrix products, arithmetic and copies ran while one was open for 0% of the time, Pallas kernels for 16%

profile of v12, /device:TPU:0, one launch (start us, length us, event | category | flops | bytes accessed | tf_op | source)
XLA Modules:
  0.0 35.4 jit_solution(14320996971556539666)
XLA Ops:
  0.6 0.0 copy-start
  0.6 1.4 %shard_map.131 = (f32[320,128]{1,0:T(8,128)S(1)}, f32[304,128]{1,0:T(8,128)S(1)}, f32[4,256,128]{2,1,0:T(8,128)S(1)}, f32[3,256,128]{2,1,0:T(8,128)S(1)}, f32[16...) custom-call(f32[4,256,128]{2,1,0:T(8,128)} %bitcast.16, ...), custom_call_target="tpu_custom_call" | custom-call | flops 1000000 | bytes 944128 | tf_op jit(solution)/shard_map/pallas_call | solution.py:36
  2.1 0.5 %collective-permute-start = (f32[320,128]{1,0:T(8,128)S(1)}, f32[320,128]{1,0:T(8,128)S(1)}, u32[]{:S(2)}, u32[]{:S(2)}) collective-permute-start(f32[320,128]{1,0:T(8,128)S(1)} %get-tuple-element.42), channel_id=1, source_target_pairs={{0,1},{1,0},{2,3},{3,2},{4,5},{5,4},{6,7},{7,6},{8,9},{9,8},{10,11... | collective-permute-start | bytes 491528 | tf_op jit(solution)/shard_map/ppermute | solution.py:48
  2.6 2.6 %collective-permute-start.1 = (f32[304,128]{1,0:T(8,128)S(1)}, f32[304,128]{1,0:T(8,128)S(1)}, u32[]{:S(2)}, u32[]{:S(2)}) collective-permute-start(f32[304,128]{1,0:T(8,128)S(1)} %get-tuple-element.43), channel_id=1, source_target_pairs={{0,4},{1,2},{2,1},{3,7},{4,0},{5,6},{6,5},{7,3},{8,12},{9,10},{10,... | collective-permute-start | bytes 466952 | tf_op jit(solution)/shard_map/ppermute | solution.py:64
  5.2 1.2 %collective-permute-start.3 = (f32[16,128]{1,0:T(8,128)}, f32[16,128]{1,0:T(8,128)S(1)}, u32[]{:S(2)}, u32[]{:S(2)}) collective-permute-start(f32[16,128]{1,0:T(8,128)} %bitcast.22), channel_id=1, source_target_pairs={{0,3},{1,2},{2,1},{3,0},{4,7},{5,6},{6,5},{7,4},{8,11},{9,10},{10,... | collective-permute-start | bytes 24584 | tf_op jit(solution)/shard_map/ppermute | solution.py:48
  6.4 0.5 %collective-permute-start.2 = (f32[16,128]{1,0:T(8,128)}, f32[16,128]{1,0:T(8,128)S(1)}, u32[]{:S(2)}, u32[]{:S(2)}) collective-permute-start(f32[16,128]{1,0:T(8,128)} %bitcast.23), channel_id=1, source_target_pairs={{0,2},{1,3},{2,0},{3,1},{4,6},{5,7},{6,4},{7,5},{8,10},{9,11},{10,... | collective-permute-start | bytes 24584 | tf_op jit(solution)/shard_map/ppermute | solution.py:48
  6.9 1.6 %collective-permute-start.6 = (f32[24,128]{1,0:T(8,128)}, f32[24,128]{1,0:T(8,128)S(1)}, u32[]{:S(2)}, u32[]{:S(2)}) collective-permute-start(f32[24,128]{1,0:T(8,128)} %bitcast.20), channel_id=1, source_target_pairs={{0,8},{4,12},{8,0},{12,4},{16,24},{20,28},{24,16},{28,20},{1,9},{5... | collective-permute-start | bytes 36872 | tf_op jit(solution)/shard_map/ppermute | solution.py:48
  8.5 0.0 collective-permute-done.3.refs_9_.refs_7_
  8.5 1.8 %collective-permute-done.2.refs_8_.refs_6_ = f32[16,128]{1,0:T(8,128)S(1)} collective-permute-done((f32[16,128]{1,0:T(8,128)}, f32[16,128]{1,0:T(8,128)S(1)}, u32[]{:S(2)}, u32[]{:S(2)}) %collective-permute-start.2) | collective-permute-done | bytes 8224 | tf_op jit(solution)/shard_map/ppermute | solution.py:48
  10.3 0.0 collective-permute-done.1.refs_7_.refs_5_
  10.3 0.0 collective-permute-done.refs_6_.refs_4_
  10.3 0.5 %shard_map.133 = (f32[318,128]{1,0:T(8,128)S(1)}, f32[318,128]{1,0:T(8,128)S(1)}) custom-call(f32[4,256,128]{2,1,0:T(8,128)S(1)} %get-tuple-element.38.refs_0_, f32[3,256,128]{2,1,0:T(8,128)S(1)} %get-tuple-element.39.refs_1_, f32[16,128]{1,0:T(8,128)S(1)} %get-tuple-element.37.refs_2_.alpha, f32[16,128]{1,0:T(8,128)S(1)} %get-tuple-element.40.refs_3_, ...), custom_call_target="tpu_custom_call" | custom-call | flops 1000000 | bytes 1269760 | tf_op jit(solution)/shard_map/pallas_call | solution.py:36
  10.8 0.6 %collective-permute-start.4 = (f32[318,128]{1,0:T(8,128)S(1)}, f32[318,128]{1,0:T(8,128)S(1)}, u32[]{:S(2)}, u32[]{:S(2)}) collective-permute-start(f32[318,128]{1,0:T(8,128)S(1)} %get-tuple-element.55), channel_id=1, source_target_pairs={{0,4},{4,0},{8,12},{12,8},{16,20},{20,16},{24,28},{28,24},{1,5},{5... | collective-permute-start | bytes 488456 | tf_op jit(solution)/shard_map/ppermute | solution.py:48
  11.4 0.0 collective-permute-start.5
  11.4 0.0 collective-permute-done.6
  11.4 5.1 %collective-permute-start.9 = (f32[48,128]{1,0:T(8,128)S(1)}, f32[48,128]{1,0:T(8,128)S(1)}, u32[]{:S(2)}, u32[]{:S(2)}) collective-permute-start(f32[48,128]{1,0:T(8,128)S(1)} %constant_dynamic-update-slice_fusion.rest_0_), channel_id=1, source_target_pairs={{0,20},{4,16},{8,28},{12,24},{16,4},{20,0},{24,12},{28,8},{1,21},{... | collective-permute-start | bytes 73736 | tf_op jit(solution)/shard_map/ppermute | solution.py:48
  16.6 0.3 collective-permute-start.8
  16.9 0.3 collective-permute-start.7
  17.2 0.0 copy-done
  17.2 3.1 %shard_map.132 = (f32[1536,128]{1,0:T(8,128)S(1)}, f32[1920,128]{1,0:T(8,128)S(1)}, f32[384,16]{1,0:T(8,128)S(1)}, f32[256,512]{1,0:T(8,128)S(1)}, bf16[256,256]...) custom-call(f32[4,256,128]{2,1,0:T(8,128)S(1)} %get-tuple-element.38, ...), custom_call_target="tpu_custom_call" | custom-call | flops 3000000 | bytes 1802240 | tf_op jit(solution)/shard_map/pallas_call | solution.py:36
  20.3 0.0 collective-permute-done.9.rest_3_
  20.3 1.0 %collective-permute-done.8.rest_2_ = f32[48,128]{1,0:T(8,128)S(1)} collective-permute-done((f32[48,128]{1,0:T(8,128)S(1)}, f32[48,128]{1,0:T(8,128)S(1)}, u32[]{:S(2)}, u32[]{:S(2)}) %collective-permute-start.8) | collective-permute-done | bytes 24608 | tf_op jit(solution)/shard_map/ppermute | solution.py:48
  21.3 0.0 collective-permute-done.7.rest_1_
  21.3 0.0 collective-permute-done.4.x_a
  21.3 0.0 collective-permute-done.5.x_b
  21.3 2.4 %shard_map.134 = (f32[216,128]{1,0:T(8,128)S(1)}, f32[216,128]{1,0:T(8,128)S(1)}, f32[2304,128]{1,0:T(8,128)S(1)}, f32[2304,128]{1,0:T(8,128)S(1)}, f32[2880,128...) custom-call(f32[1536,128]{1,0:T(8,128)S(1)} %get-tuple-element.46.core, ...), custom_call_target="tpu_custom_call" | custom-call | flops 10000000 | bytes 5281792 | tf_op jit(solution)/shard_map/pallas_call | solution.py:36
  23.7 0.8 %collective-permute-start.10 = (f32[216,128]{1,0:T(8,128)S(1)}, f32[216,128]{1,0:T(8,128)S(1)}, u32[]{:S(2)}, u32[]{:S(2)}) collective-permute-start(f32[216,128]{1,0:T(8,128)S(1)} %get-tuple-element.63), channel_id=1, source_target_pairs={{0,4},{4,0},{8,12},{12,8},{16,20},{20,16},{24,28},{28,24},{1,5},{5... | collective-permute-start | bytes 331784 | tf_op jit(solution)/shard_map/ppermute | solution.py:48
  24.6 0.0 collective-permute-start.11
  24.6 1.9 %shard_map.135.refs_2_ = f32[1536,128]{1,0:T(8,128)S(1)} custom-call(f32[1920,128]{1,0:T(8,128)S(1)} %get-tuple-element.45.core_coef, f32[2880,128]{1,0:T(8,128)S(1)} %get-tuple-element.58.edge_coef, f32[2304,128]{1,0:T(8,128)S(1)} %get-tuple-element.59.back_2, f32[2304,128]{1,0:T(8,128)S(1)} %get-tuple-element.60.back_1, ...), custom_call_target="tpu_custom_call" | custom-call | flops 10000000 | bytes 8224768 | tf_op jit(solution)/shard_map/pallas_call | solution.py:36
  26.5 2.0 %collective-permute-done.10.refs_3_ = f32[216,128]{1,0:T(8,128)S(1)} collective-permute-done((f32[216,128]{1,0:T(8,128)S(1)}, f32[216,128]{1,0:T(8,128)S(1)}, u32[]{:S(2)}, u32[]{:S(2)}) %collective-permute-start.10) | collective-permute-done | bytes 110624 | tf_op jit(solution)/shard_map/ppermute | solution.py:48
  28.6 0.0 collective-permute-done.11.refs_4_
  28.6 0.4 %shard_map.136 = (f32[208,128]{1,0:T(8,128)S(1)}, f32[208,128]{1,0:T(8,128)S(1)}, f32[4,256,128]{2,1,0:T(8,128)S(1)}, f32[16,128]{1,0:T(8,128)S(1)}, f32[16,128]{1,0:T(8,128)S(1)}) custom-call(f32[4,256,128]{2,1,0:T(8,128)S(1)} %get-tuple-element.38.refs_0_, f32[384,16]{1,0:T(8,128)S(1)} %get-tuple-element.44.refs_1_, f32[1536,128]{1,0:T(8,128)S(1)} %shard_map.135.refs_2_, ...), custom_call_target="tpu_custom_call" | custom-call | flops 1000000 | bytes 1556480 | tf_op jit(solution)/shard_map/pallas_call | solution.py:36
  29.0 0.0 collective-permute-start.12
  29.0 1.6 %collective-permute-start.13 = (f32[208,128]{1,0:T(8,128)S(1)}, f32[208,128]{1,0:T(8,128)S(1)}, u32[]{:S(2)}, u32[]{:S(2)}) collective-permute-start(f32[208,128]{1,0:T(8,128)S(1)} %get-tuple-element.68), channel_id=1, source_target_pairs={{0,3},{1,2},{2,1},{3,0},{4,7},{5,6},{6,5},{7,4},{8,11},{9,10},{10,... | collective-permute-start | bytes 319496 | tf_op jit(solution)/shard_map/ppermute | solution.py:70
  30.6 0.5 %collective-permute-start.14 = (f32[16,128]{1,0:T(8,128)S(1)}, f32[16,128]{1,0:T(8,128)S(1)}, u32[]{:S(2)}, u32[]{:S(2)}) collective-permute-start(f32[16,128]{1,0:T(8,128)S(1)} %get-tuple-element.69), channel_id=1, source_target_pairs={{0,2},{1,3},{2,0},{3,1},{4,6},{5,7},{6,4},{7,5},{8,10},{9,11},{10,... | collective-permute-start | bytes 24584 | tf_op jit(solution)/shard_map/ppermute | solution.py:48
  31.1 3.4 %collective-permute-done.14.rest_0_ = f32[16,128]{1,0:T(8,128)S(1)} collective-permute-done((f32[16,128]{1,0:T(8,128)S(1)}, f32[16,128]{1,0:T(8,128)S(1)}, u32[]{:S(2)}, u32[]{:S(2)}) %collective-permute-start.14) | collective-permute-done | bytes 8224 | tf_op jit(solution)/shard_map/ppermute | solution.py:48
  34.5 0.0 collective-permute-done.12.y_a
  34.5 0.0 collective-permute-done.13.y_b
  34.5 0.9 %shard_map.137 = (f32[4,256,128]{2,1,0:T(8,128)}, f32[16,128]{1,0:T(8,128)}) custom-call(f32[16,128]{1,0:T(8,128)S(1)} %get-tuple-element.37.refs_2_.alpha, f32[4,256,128]{2,1,0:T(8,128)S(1)} %get-tuple-element.65.near, f32[16,128]{1,0:T(8,128)S(1)} %get-tuple-element.66.sums, f32[208,128]{1,0:T(8,128)S(1)} %collective-permute-done.12.y_a, ...), custom_call_target="tpu_custom_call" | custom-call | flops 1000000 | bytes 761856 | tf_op jit(solution)/shard_map/pallas_call | solution.py:36
  (2 shorter events, 0.0 us)
Async XLA Ops:
  0.6 16.6 %copy-start = (f32[1,1,256,4,128]{4,3,2,1,0:T(4,128)S(1)}, f32[1,1,256,4,128]{4,3,2,1,0:T(4,128)}, u32[]{:S(2)}) copy-start(f32[1,1,256,4,128]{4,3,2,1,0:T(4,128)} %param.22) | copy-start | bytes 1572868
  2.1 8.2 %collective-permute-start = (f32[320,128]{1,0:T(8,128)S(1)}, f32[320,128]{1,0:T(8,128)S(1)}, u32[]{:S(2)}, u32[]{:S(2)}) collective-permute-start(f32[320,128]{1,0:T(8,128)S(1)} %get-tuple-element.42), channel_id=1, source_target_pairs={{0,1},{1,0},{2,3},{3,2},{4,5},{5,4},{6,7},{7,6},{8,9},{9,8},{10,11... | collective-permute-start | bytes 491528 | tf_op jit(solution)/shard_map/ppermute | solution.py:48
  2.6 7.7 %collective-permute-start.1 = (f32[304,128]{1,0:T(8,128)S(1)}, f32[304,128]{1,0:T(8,128)S(1)}, u32[]{:S(2)}, u32[]{:S(2)}) collective-permute-start(f32[304,128]{1,0:T(8,128)S(1)} %get-tuple-element.43), channel_id=1, source_target_pairs={{0,4},{1,2},{2,1},{3,7},{4,0},{5,6},{6,5},{7,3},{8,12},{9,10},{10,... | collective-permute-start | bytes 466952 | tf_op jit(solution)/shard_map/ppermute | solution.py:64
  5.2 3.3 %collective-permute-start.3 = (f32[16,128]{1,0:T(8,128)}, f32[16,128]{1,0:T(8,128)S(1)}, u32[]{:S(2)}, u32[]{:S(2)}) collective-permute-start(f32[16,128]{1,0:T(8,128)} %bitcast.22), channel_id=1, source_target_pairs={{0,3},{1,2},{2,1},{3,0},{4,7},{5,6},{6,5},{7,4},{8,11},{9,10},{10,... | collective-permute-start | bytes 24584 | tf_op jit(solution)/shard_map/ppermute | solution.py:48
  6.4 3.9 %collective-permute-start.2 = (f32[16,128]{1,0:T(8,128)}, f32[16,128]{1,0:T(8,128)S(1)}, u32[]{:S(2)}, u32[]{:S(2)}) collective-permute-start(f32[16,128]{1,0:T(8,128)} %bitcast.23), channel_id=1, source_target_pairs={{0,2},{1,3},{2,0},{3,1},{4,6},{5,7},{6,4},{7,5},{8,10},{9,11},{10,... | collective-permute-start | bytes 24584 | tf_op jit(solution)/shard_map/ppermute | solution.py:48
  6.9 4.5 %collective-permute-start.6 = (f32[24,128]{1,0:T(8,128)}, f32[24,128]{1,0:T(8,128)S(1)}, u32[]{:S(2)}, u32[]{:S(2)}) collective-permute-start(f32[24,128]{1,0:T(8,128)} %bitcast.20), channel_id=1, source_target_pairs={{0,8},{4,12},{8,0},{12,4},{16,24},{20,28},{24,16},{28,20},{1,9},{5... | collective-permute-start | bytes 36872 | tf_op jit(solution)/shard_map/ppermute | solution.py:48
  10.8 10.4 %collective-permute-start.4 = (f32[318,128]{1,0:T(8,128)S(1)}, f32[318,128]{1,0:T(8,128)S(1)}, u32[]{:S(2)}, u32[]{:S(2)}) collective-permute-start(f32[318,128]{1,0:T(8,128)S(1)} %get-tuple-element.55), channel_id=1, source_target_pairs={{0,4},{4,0},{8,12},{12,8},{16,20},{20,16},{24,28},{28,24},{1,5},{5... | collective-permute-start | bytes 488456 | tf_op jit(solution)/shard_map/ppermute | solution.py:48
  11.4 9.9 %collective-permute-start.5 = (f32[318,128]{1,0:T(8,128)S(1)}, f32[318,128]{1,0:T(8,128)S(1)}, u32[]{:S(2)}, u32[]{:S(2)}) collective-permute-start(f32[318,128]{1,0:T(8,128)S(1)} %get-tuple-element.56), channel_id=1, source_target_pairs={{0,1},{4,8},{8,4},{12,16},{16,12},{20,24},{24,20},{28,29},{1,0},{5... | collective-permute-start | bytes 488456 | tf_op jit(solution)/shard_map/ppermute | solution.py:64
  11.4 8.9 %collective-permute-start.9 = (f32[48,128]{1,0:T(8,128)S(1)}, f32[48,128]{1,0:T(8,128)S(1)}, u32[]{:S(2)}, u32[]{:S(2)}) collective-permute-start(f32[48,128]{1,0:T(8,128)S(1)} %constant_dynamic-update-slice_fusion.rest_0_), channel_id=1, source_target_pairs={{0,20},{4,16},{8,28},{12,24},{16,4},{20,0},{24,12},{28,8},{1,21},{... | collective-permute-start | bytes 73736 | tf_op jit(solution)/shard_map/ppermute | solution.py:48
  16.6 4.7 %collective-permute-start.8 = (f32[48,128]{1,0:T(8,128)S(1)}, f32[48,128]{1,0:T(8,128)S(1)}, u32[]{:S(2)}, u32[]{:S(2)}) collective-permute-start(f32[48,128]{1,0:T(8,128)S(1)} %constant_dynamic-update-slice_fusion.rest_0_), channel_id=1, source_target_pairs={{0,16},{4,20},{8,24},{12,28},{16,0},{20,4},{24,8},{28,12},{1,17},{... | collective-permute-start | bytes 73736 | tf_op jit(solution)/shard_map/ppermute | solution.py:48
  16.9 4.4 %collective-permute-start.7 = (f32[48,128]{1,0:T(8,128)S(1)}, f32[48,128]{1,0:T(8,128)S(1)}, u32[]{:S(2)}, u32[]{:S(2)}) collective-permute-start(f32[48,128]{1,0:T(8,128)S(1)} %constant_dynamic-update-slice_fusion.rest_0_), channel_id=1, source_target_pairs={{0,4},{4,0},{8,12},{12,8},{16,20},{20,16},{24,28},{28,24},{1,5},{5... | collective-permute-start | bytes 73736 | tf_op jit(solution)/shard_map/ppermute | solution.py:48
  23.7 4.8 %collective-permute-start.10 = (f32[216,128]{1,0:T(8,128)S(1)}, f32[216,128]{1,0:T(8,128)S(1)}, u32[]{:S(2)}, u32[]{:S(2)}) collective-permute-start(f32[216,128]{1,0:T(8,128)S(1)} %get-tuple-element.63), channel_id=1, source_target_pairs={{0,4},{4,0},{8,12},{12,8},{16,20},{20,16},{24,28},{28,24},{1,5},{5... | collective-permute-start | bytes 331784 | tf_op jit(solution)/shard_map/ppermute | solution.py:48
  24.6 4.0 %collective-permute-start.11 = (f32[216,128]{1,0:T(8,128)S(1)}, f32[216,128]{1,0:T(8,128)S(1)}, u32[]{:S(2)}, u32[]{:S(2)}) collective-permute-start(f32[216,128]{1,0:T(8,128)S(1)} %get-tuple-element.64), channel_id=1, source_target_pairs={{0,1},{4,8},{8,4},{12,16},{16,12},{20,24},{24,20},{28,29},{1,0},{5... | collective-permute-start | bytes 331784 | tf_op jit(solution)/shard_map/ppermute | solution.py:64
  29.0 5.5 %collective-permute-start.12 = (f32[208,128]{1,0:T(8,128)S(1)}, f32[208,128]{1,0:T(8,128)S(1)}, u32[]{:S(2)}, u32[]{:S(2)}) collective-permute-start(f32[208,128]{1,0:T(8,128)S(1)} %get-tuple-element.67), channel_id=1, source_target_pairs={{0,1},{1,0},{2,3},{3,2},{4,5},{5,4},{6,7},{7,6},{8,9},{9,8},{10,11... | collective-permute-start | bytes 319496 | tf_op jit(solution)/shard_map/ppermute | solution.py:48
  29.0 5.5 %collective-permute-start.13 = (f32[208,128]{1,0:T(8,128)S(1)}, f32[208,128]{1,0:T(8,128)S(1)}, u32[]{:S(2)}, u32[]{:S(2)}) collective-permute-start(f32[208,128]{1,0:T(8,128)S(1)} %get-tuple-element.68), channel_id=1, source_target_pairs={{0,3},{1,2},{2,1},{3,0},{4,7},{5,6},{6,5},{7,4},{8,11},{9,10},{10,... | collective-permute-start | bytes 319496 | tf_op jit(solution)/shard_map/ppermute | solution.py:70
  30.6 3.9 %collective-permute-start.14 = (f32[16,128]{1,0:T(8,128)S(1)}, f32[16,128]{1,0:T(8,128)S(1)}, u32[]{:S(2)}, u32[]{:S(2)}) collective-permute-start(f32[16,128]{1,0:T(8,128)S(1)} %get-tuple-element.69), channel_id=1, source_target_pairs={{0,2},{1,3},{2,0},{3,1},{4,6},{5,7},{6,4},{7,5},{8,10},{9,11},{10,... | collective-permute-start | bytes 24584 | tf_op jit(solution)/shard_map/ppermute | solution.py:48

commit v13 on v12

--- a/solution.py
+++ b/solution.py
@@ -232,10 +232,11 @@
     return jnp.concatenate([ref[pl.ds(c, count, stride=NC)] for c in range(NC)], axis=1)
 
 
-def pack_x(ny, delta, coefs, alpha, near_tiles, y_a, y_b, *rest):
+def pack_x(ny, delta, coefs, alpha, near_tiles, _, y_a, y_b, *rest):
     others = rest[: ny - 2]
     out_a, out_b, field, picks, known, tiles = rest[ny - 2 :]
     even, _, _ = place_on("gx")
+    out_b[X_HALO:] = jnp.zeros((8, 128), f32)
     owned = alpha.shape[0] // NC
     gather_known(alpha, y_a, others, known)
     turned = tile_numbers(near_tiles, y_a, y_b, tiles)
@@ -282,46 +283,7 @@
         put(X_COEF + f * SLIM_ROWS, SLIM)
 
 
-def prepare(ny, delta, coefs, alpha, near_tiles, meta, weights, y_a, y_b, *rest):
-    others = rest[: ny - 2]
-    core, coef, picks, wide, slot_push, beam_pick, columns = rest[ny - 2 : ny + 5]
-    state_1, state_2, tally, edge_pick = rest[ny + 5 : ny + 9]
-    state_3, known, tiles = rest[ny + 9 :]
-    owned = alpha.shape[0] // NC
-
-    def fill(ref, base, own, y_base, reach):
-        for x in range(CX):
-            at = base + x * PITCH
-            ref[at : at + CY] = own[x * CY : (x + 1) * CY]
-            ref[at + CY : at + PITCH] = jnp.zeros((PITCH - CY, 128), f32)
-        for away in range(1, reach + 1):
-            north, south = y_sides(y_a, y_b, pl.ds(y_base + (away - 1) * CX, CX))
-            ref[pl.ds(base + CY - 1 + away, CX, stride=PITCH)] = north
-            ref[pl.ds(base + PITCH - away, CX, stride=PITCH)] = south
-
-    for c in range(NC):
-        fill(core, c * CORE, delta.at[c], c * RIM * CX, RIM)
-    for f in range(3):
-        fill(coef, f * CORE, coefs.at[f], Y_COEF + f * INNER * CX, INNER)
-
-    def combine(b, carry):
-        at = pl.multiple_of(b * PITCH, 8)
-        combined = combine_coefs(*[coef[pl.ds(f * CORE + at, PITCH)] for f in range(3)])
-        for f, value in enumerate(combined):
-            coef[pl.ds(f * CORE + at, PITCH)] = value
-        return carry
-
-    lax.fori_loop(0, CX, combine, 0)
-
-    gather_known(alpha, y_a, others, known)
-    turned = tile_numbers(near_tiles, y_a, y_b, tiles)
-    ids = tile_ids(ny, owned)
-    for x in range(CX):
-        picks[x * PITCH : (x + 1) * PITCH] = (turned[:, x : x + 1] == ids).astype(f32)
-    fine = two_part_dot(picks[...].astype(bf16), by_variable(known, ny * owned))
-    for c in range(NC):
-        core[c * CORE : (c + 1) * CORE] += profile_weight * fine[:, c * 128 : (c + 1) * 128]
-
+def one_hots(meta, weights, wide, slot_pick, slot_push, beam_pick, columns, edge_pick):
     slots = meta.shape[1]
     for c in range(NC):
         wide[:, c * 128 : (c + 1) * 128] = weights[pl.ds(c, slots, stride=NC)]
@@ -329,7 +291,7 @@
     turned = jnp.transpose(meta[...])
     columns[...] = turned
     slot_lane = lax.broadcasted_iota(jnp.int32, (slots, CX * CY), 1).astype(f32)
-    slot_pick = (slot_lane == turned[:, 0:1]).astype(f32).astype(bf16)
+    slot_pick[...] = (slot_lane == turned[:, 0:1]).astype(f32).astype(bf16)
     edge_lane = lax.broadcasted_iota(jnp.int32, (slots, 128), 1)
     half = RIM * CY
     place = jnp.where(edge_lane < half, edge_lane, edge_lane + CX * CY - 2 * half)
@@ -342,6 +304,46 @@
     beam_lane = lax.broadcasted_iota(jnp.int32, (slots, per_beam), 1).astype(f32)
     beam_pick[...] = (beam_lane == turned[:, 1:2]).astype(f32).astype(bf16)
 
+
+def prepare(ny, delta, coefs, alpha, near_tiles, columns, slot_pick, wide, y_a, y_b, *rest):
+    others = rest[: ny - 2]
+    core, coef, picks, state_1, state_2, tally, state_3, known, tiles = rest[ny - 2 :]
+    owned = alpha.shape[0] // NC
+
+    def fill(ref, base, own, y_base, reach):
+        for x in range(CX):
+            at = base + x * PITCH
+            ref[at : at + CY] = own[x * CY : (x + 1) * CY]
+            ref[at + CY : at + PITCH] = jnp.zeros((PITCH - CY, 128), f32)
+        for away in range(1, reach + 1):
+            north, south = y_sides(y_a, y_b, pl.ds(y_base + (away - 1) * CX, CX))
+            ref[pl.ds(base + CY - 1 + away, CX, stride=PITCH)] = north
+            ref[pl.ds(base + PITCH - away, CX, stride=PITCH)] = south
+
+    for c in range(NC):
+        fill(core, c * CORE, delta.at[c], c * RIM * CX, RIM)
+    for f in range(3):
+        fill(coef, f * CORE, coefs.at[f], Y_COEF + f * INNER * CX, INNER)
+
+    def combine(b, carry):
+        at = pl.multiple_of(b * PITCH, 8)
+        combined = combine_coefs(*[coef[pl.ds(f * CORE + at, PITCH)] for f in range(3)])
+        for f, value in enumerate(combined):
+            coef[pl.ds(f * CORE + at, PITCH)] = value
+        return carry
+
+    lax.fori_loop(0, CX, combine, 0)
+
+    gather_known(alpha, y_a, others, known)
+    turned = tile_numbers(near_tiles, y_a, y_b, tiles)
+    ids = tile_ids(ny, owned)
+    for x in range(CX):
+        picks[x * PITCH : (x + 1) * PITCH] = (turned[:, x : x + 1] == ids).astype(f32)
+    fine = two_part_dot(picks[...].astype(bf16), by_variable(known, ny * owned))
+    for c in range(NC):
+        core[c * CORE : (c + 1) * CORE] += profile_weight * fine[:, c * 128 : (c + 1) * 128]
+
+    slots = columns.shape[0]
     states = [core, state_1, state_2, state_3]
     for step in range(STEPS):
         source, target = states[step], states[step + 1]
@@ -362,7 +364,7 @@
                 at = c * CORE + x * PITCH
                 pieces.append(target[at : at + CY])
             own.append(jnp.concatenate(pieces + pieces[:1], axis=0))
-        seen = two_part_dot(slot_pick, jnp.concatenate(own, axis=1)) * wide[...]
+        seen = two_part_dot(slot_pick[...], jnp.concatenate(own, axis=1)) * wide[...]
         total = seen[:, 0:128]
         for c in range(1, NC):
             total = total + seen[:, c * 128 : (c + 1) * 128]
@@ -427,6 +429,7 @@
     out_a, out_b, back_2, back_1, coef, tops, lows = rest[-13:-6]
     state_0, state_1, state_2, state_3, raw, forcing = rest[-6:]
     even, _, _ = place_on("gx")
+    out_b[X_COEF:] = jnp.zeros((8, 128), f32)
     slots = columns.shape[0]
 
     def fill(ref, base, x_base, found):
@@ -740,10 +743,22 @@
     beams = jnp.concatenate([near_beams, swap(own_beams, "gx", 2)])
     beams = [beams] + [swap(beams, "gx", xor) for xor in range(1, nx) if xor % 4 < 2]
 
+    wide, slot_pick, slot_push, beam_pick, columns, edge_pick = call(
+        one_hots,
+        [
+            (slots, NC * 128),
+            jax.ShapeDtypeStruct((slots, CX * CY), bf16),
+            jax.ShapeDtypeStruct((CX * CY, slots), bf16),
+            jax.ShapeDtypeStruct((slots, beam_count), bf16),
+            (slots, 8),
+            jax.ShapeDtypeStruct((slots, 256), bf16),
+        ],
+        [meta, weights],
+    )
     x_a, x_b = call(
         lambda *refs: pack_x(ny, *refs),
-        [(X_HALO, 128), (X_HALO, 128)],
-        [fine, coefs, control_near, near_tiles, y_a, y_b, *others],
+        [(X_HALO, 128), (X_HALO + 8, 128)],
+        [fine, coefs, control_near, near_tiles, columns, y_a, y_b, *others],
         [
             pltpu.VMEM((2 * RIM * PITCH, 128), f32),
             pltpu.VMEM((2 * RIM * PITCH, total), f32),
@@ -755,34 +770,17 @@
     x_b = pair_b(x_b, "gx", "gy")
 
     big = (NC * FIELD, 128)
-    (
-        core,
-        coef,
-        picks,
-        wide,
-        slot_push,
-        beam_pick,
-        columns,
-        state_1,
-        state_2,
-        tally,
-        edge_pick,
-    ) = call(
+    core, coef, picks, state_1, state_2, tally = call(
         lambda *refs: prepare(ny, *refs),
         [
             (NC * CORE, 128),
             (5 * CORE, 128),
             (CORE, total),
-            (slots, NC * 128),
-            jax.ShapeDtypeStruct((CX * CY, slots), bf16),
-            jax.ShapeDtypeStruct((slots, beam_count), bf16),
-            (slots, 8),
             (NC * CORE, 128),
             (NC * CORE, 128),
             (STEPS * slots, 128),
-            jax.ShapeDtypeStruct((slots, 256), bf16),
-        ],
-        [fine, coefs, control_near, near_tiles, meta, weights, y_a, y_b, *others],
+        ],
+        [fine, coefs, control_near, near_tiles, columns, slot_pick, wide, y_a, y_b, *others],
         [
             pltpu.VMEM((NC * CORE, 128), f32),
             pltpu.VMEM((total * NC, 128), f32),
@@ -794,7 +792,7 @@
         edges,
         [
             (X_COEF, 128),
-            (X_COEF, 128),
+            (X_COEF + 8, 128),
             big,
             big,
             (5 * FIELD, 128),

time: 35.8 us -> 36.3 us (1.014)
  starting transfers between devices: 15.7 us -> 17.5 us
  waiting for transfers between devices: 8.24 us -> 7.13 us
    ppermute x11, starting transfers between devices: 11.5 us -> 13.2 us  [swap(): lax.ppermute(block, axis, [(i, i ^ xor) for i in range(lax.axis_size(axis...]
    ppermute x11, waiting for transfers between devices: 8.22 us -> 7.11 us  [swap(): lax.ppermute(block, axis, [(i, i ^ xor) for i in range(lax.axis_size(axis...]
    pallas_call x7 -> x8, Pallas kernels: 10.8 us -> 10.8 us  [call(): pl.pallas_call(body, out_shape=shapes, in_specs=in_specs or [VMEM] * len(...]
where the time goes in v13:
time: 36.3 us; the launch traced here: 36.1 us
  starting transfers between devices  17.5 us (48%)
  Pallas kernels  10.8 us (30%)
  waiting for transfers between devices  7.13 us (20%)
  between operations  0.74 us (2%)
    ppermute x11, starting transfers between devices, swap(): lax.ppermute(block, axis, [(i, i ^ xor) for i in range(lax.axis_size(axis...  13.2 us
    pallas_call x8, Pallas kernels, call(): pl.pallas_call(body, out_shape=shapes, in_specs=in_specs or [VMEM] * len(...  10.8 us
    ppermute x11, waiting for transfers between devices, swap(): lax.ppermute(block, axis, [(i, i ^ xor) for i in range(lax.axis_size(axis...  7.11 us
    ppermute x3, starting transfers between devices, pair_b(): return lax.ppermute(block, ('gx', 'gy'), pairs)  2.67 us
    ppermute x1, starting transfers between devices, ring_b(): return lax.ppermute(block, axis, pairs)  1.6 us
  transfers between devices with their start and end apart: 15, of which 4 were waited for; matrix products, arithmetic and copies ran while one was open for 0% of the time, Pallas kernels for 16%

profile of v13, /device:TPU:0, one launch (start us, length us, event | category | flops | bytes accessed | tf_op | source)
XLA Modules:
  0.0 36.1 jit_solution(13502729170609835640)
XLA Ops:
  0.6 0.0 copy-start
  0.6 1.4 %shard_map.131 = (f32[320,128]{1,0:T(8,128)S(1)}, f32[304,128]{1,0:T(8,128)S(1)}, f32[4,256,128]{2,1,0:T(8,128)S(1)}, f32[3,256,128]{2,1,0:T(8,128)S(1)}, f32[16...) custom-call(f32[4,256,128]{2,1,0:T(8,128)} %bitcast.16, ...), custom_call_target="tpu_custom_call" | custom-call | flops 1000000 | bytes 944128 | tf_op jit(solution)/shard_map/pallas_call | solution.py:36
  2.1 0.5 %collective-permute-start = (f32[320,128]{1,0:T(8,128)S(1)}, f32[320,128]{1,0:T(8,128)S(1)}, u32[]{:S(2)}, u32[]{:S(2)}) collective-permute-start(f32[320,128]{1,0:T(8,128)S(1)} %get-tuple-element.46), channel_id=1, source_target_pairs={{0,1},{1,0},{2,3},{3,2},{4,5},{5,4},{6,7},{7,6},{8,9},{9,8},{10,11... | collective-permute-start | bytes 491528 | tf_op jit(solution)/shard_map/ppermute | solution.py:48
  2.6 2.6 %collective-permute-start.1 = (f32[304,128]{1,0:T(8,128)S(1)}, f32[304,128]{1,0:T(8,128)S(1)}, u32[]{:S(2)}, u32[]{:S(2)}) collective-permute-start(f32[304,128]{1,0:T(8,128)S(1)} %get-tuple-element.47), channel_id=1, source_target_pairs={{0,4},{1,2},{2,1},{3,7},{4,0},{5,6},{6,5},{7,3},{8,12},{9,10},{10,... | collective-permute-start | bytes 466952 | tf_op jit(solution)/shard_map/ppermute | solution.py:64
  5.2 1.2 %collective-permute-start.3 = (f32[16,128]{1,0:T(8,128)}, f32[16,128]{1,0:T(8,128)S(1)}, u32[]{:S(2)}, u32[]{:S(2)}) collective-permute-start(f32[16,128]{1,0:T(8,128)} %bitcast.22), channel_id=1, source_target_pairs={{0,3},{1,2},{2,1},{3,0},{4,7},{5,6},{6,5},{7,4},{8,11},{9,10},{10,... | collective-permute-start | bytes 24584 | tf_op jit(solution)/shard_map/ppermute | solution.py:48
  6.4 0.5 %collective-permute-start.2 = (f32[16,128]{1,0:T(8,128)}, f32[16,128]{1,0:T(8,128)S(1)}, u32[]{:S(2)}, u32[]{:S(2)}) collective-permute-start(f32[16,128]{1,0:T(8,128)} %bitcast.23), channel_id=1, source_target_pairs={{0,2},{1,3},{2,0},{3,1},{4,6},{5,7},{6,4},{7,5},{8,10},{9,11},{10,... | collective-permute-start | bytes 24584 | tf_op jit(solution)/shard_map/ppermute | solution.py:48
  6.9 1.6 %collective-permute-start.6 = (f32[24,128]{1,0:T(8,128)}, f32[24,128]{1,0:T(8,128)S(1)}, u32[]{:S(2)}, u32[]{:S(2)}) collective-permute-start(f32[24,128]{1,0:T(8,128)} %bitcast.20), channel_id=1, source_target_pairs={{0,8},{4,12},{8,0},{12,4},{16,24},{20,28},{24,16},{28,20},{1,9},{5... | collective-permute-start | bytes 36872 | tf_op jit(solution)/shard_map/ppermute | solution.py:48
  8.5 0.0 copy-done
  8.5 0.3 shard_map.132
  8.8 0.0 collective-permute-done.3.refs_10_.refs_8_
  8.8 1.5 %collective-permute-done.2.refs_9_.refs_7_ = f32[16,128]{1,0:T(8,128)S(1)} collective-permute-done((f32[16,128]{1,0:T(8,128)}, f32[16,128]{1,0:T(8,128)S(1)}, u32[]{:S(2)}, u32[]{:S(2)}) %collective-permute-start.2) | collective-permute-done | bytes 8224 | tf_op jit(solution)/shard_map/ppermute | solution.py:48
  10.3 0.0 collective-permute-done.1.refs_8_.refs_6_
  10.3 0.0 collective-permute-done.refs_7_.refs_5_
  10.3 0.5 %shard_map.134 = (f32[318,128]{1,0:T(8,128)S(1)}, f32[326,128]{1,0:T(8,128)S(1)}) custom-call(f32[4,256,128]{2,1,0:T(8,128)S(1)} %get-tuple-element.39.refs_0_, f32[3,256,128]{2,1,0:T(8,128)S(1)} %get-tuple-element.40.refs_1_, f32[16,128]{1,0:T(8,128)S(1)} %get-tuple-element.38.refs_2_.alpha, f32[16,128]{1,0:T(8,128)S(1)} %get-tuple-element.41.refs_3_, ...), custom_call_target="tpu_custom_call" | custom-call | flops 1000000 | bytes 1277952 | tf_op jit(solution)/shard_map/pallas_call | solution.py:36
  10.8 0.6 %collective-permute-start.4 = (f32[318,128]{1,0:T(8,128)S(1)}, f32[318,128]{1,0:T(8,128)S(1)}, u32[]{:S(2)}, u32[]{:S(2)}) collective-permute-start(f32[318,128]{1,0:T(8,128)S(1)} %get-tuple-element.57), channel_id=1, source_target_pairs={{0,4},{4,0},{8,12},{12,8},{16,20},{20,16},{24,28},{28,24},{1,5},{5... | collective-permute-start | bytes 488456 | tf_op jit(solution)/shard_map/ppermute | solution.py:48
  11.4 0.0 collective-permute-start.5
  11.4 0.0 collective-permute-done.6
  11.4 5.1 %collective-permute-start.9 = (f32[48,128]{1,0:T(8,128)S(1)}, f32[48,128]{1,0:T(8,128)S(1)}, u32[]{:S(2)}, u32[]{:S(2)}) collective-permute-start(f32[48,128]{1,0:T(8,128)S(1)} %constant_dynamic-update-slice_fusion.rest_0_), channel_id=1, source_target_pairs={{0,20},{4,16},{8,28},{12,24},{16,4},{20,0},{24,12},{28,8},{1,21},{... | collective-permute-start | bytes 73736 | tf_op jit(solution)/shard_map/ppermute | solution.py:48
  16.6 0.3 collective-permute-start.8
  16.9 0.3 collective-permute-start.7
  17.2 2.8 %shard_map.133 = (f32[1536,128]{1,0:T(8,128)S(1)}, f32[1920,128]{1,0:T(8,128)S(1)}, f32[384,16]{1,0:T(8,128)S(1)}, f32[1536,128]{1,0:T(8,128)S(1)}, f32[1536,128]{1,0:T(8,128)S(1)}, /*index=5*/f32[768,128]{1,0:T(8,128)S(1)}) custom-call(f32[4,256,128]{2,1,0:T(8,128)S(1)} %get-tuple-element.39.refs_0_, f32[3,256,128]{2,1,0:T(8,128)S(1)} %get-tuple-element.40.refs_1_, ...), custom_call_target="tpu_custom_call" | custom-call | flops 3000000 | bytes 2064384 | tf_op jit(solution)/shard_map/pallas_call | solution.py:36
  20.1 0.0 collective-permute-done.9.rest_3_
  20.1 1.2 %collective-permute-done.8.rest_2_ = f32[48,128]{1,0:T(8,128)S(1)} collective-permute-done((f32[48,128]{1,0:T(8,128)S(1)}, f32[48,128]{1,0:T(8,128)S(1)}, u32[]{:S(2)}, u32[]{:S(2)}) %collective-permute-start.8) | collective-permute-done | bytes 24608 | tf_op jit(solution)/shard_map/ppermute | solution.py:48
  21.3 0.0 collective-permute-done.7.rest_1_
  21.3 0.0 collective-permute-done.4.x_a
  21.3 0.0 collective-permute-done.5.x_b
  21.3 2.4 %shard_map.135 = (f32[216,128]{1,0:T(8,128)S(1)}, f32[224,128]{1,0:T(8,128)S(1)}, f32[2304,128]{1,0:T(8,128)S(1)}, f32[2304,128]{1,0:T(8,128)S(1)}, f32[2880,128...) custom-call(f32[1536,128]{1,0:T(8,128)S(1)} %get-tuple-element.50.core, ...), custom_call_target="tpu_custom_call" | custom-call | flops 10000000 | bytes 5285888 | tf_op jit(solution)/shard_map/pallas_call | solution.py:36
  23.7 0.1 collective-permute-start.11
  23.8 2.5 %collective-permute-start.10 = (f32[216,128]{1,0:T(8,128)S(1)}, f32[216,128]{1,0:T(8,128)S(1)}, u32[]{:S(2)}, u32[]{:S(2)}) collective-permute-start(f32[216,128]{1,0:T(8,128)S(1)} %get-tuple-element.65), channel_id=1, source_target_pairs={{0,4},{4,0},{8,12},{12,8},{16,20},{20,16},{24,28},{28,24},{1,5},{5... | collective-permute-start | bytes 331784 | tf_op jit(solution)/shard_map/ppermute | solution.py:48
  26.3 1.9 %shard_map.136.refs_2_ = f32[1536,128]{1,0:T(8,128)S(1)} custom-call(f32[1920,128]{1,0:T(8,128)S(1)} %get-tuple-element.49.core_coef, f32[2880,128]{1,0:T(8,128)S(1)} %get-tuple-element.60.edge_coef, f32[2304,128]{1,0:T(8,128)S(1)} %get-tuple-element.61.back_2, f32[2304,128]{1,0:T(8,128)S(1)} %get-tuple-element.62.back_1, ...), custom_call_target="tpu_custom_call" | custom-call | flops 10000000 | bytes 8224768 | tf_op jit(solution)/shard_map/pallas_call | solution.py:36
  28.2 1.0 %collective-permute-done.10.refs_3_ = f32[216,128]{1,0:T(8,128)S(1)} collective-permute-done((f32[216,128]{1,0:T(8,128)S(1)}, f32[216,128]{1,0:T(8,128)S(1)}, u32[]{:S(2)}, u32[]{:S(2)}) %collective-permute-start.10) | collective-permute-done | bytes 110624 | tf_op jit(solution)/shard_map/ppermute | solution.py:48
  29.2 0.0 collective-permute-done.11.refs_4_
  29.2 0.4 %shard_map.137 = (f32[208,128]{1,0:T(8,128)S(1)}, f32[208,128]{1,0:T(8,128)S(1)}, f32[4,256,128]{2,1,0:T(8,128)S(1)}, f32[16,128]{1,0:T(8,128)S(1)}, f32[16,128]{1,0:T(8,128)S(1)}) custom-call(f32[4,256,128]{2,1,0:T(8,128)S(1)} %get-tuple-element.39.refs_0_, f32[384,16]{1,0:T(8,128)S(1)} %get-tuple-element.48.refs_1_, f32[1536,128]{1,0:T(8,128)S(1)} %shard_map.136.refs_2_, ...), custom_call_target="tpu_custom_call" | custom-call | flops 1000000 | bytes 1560576 | tf_op jit(solution)/shard_map/pallas_call | solution.py:36
  29.6 0.0 collective-permute-start.12
  29.6 1.6 %collective-permute-start.13 = (f32[208,128]{1,0:T(8,128)S(1)}, f32[208,128]{1,0:T(8,128)S(1)}, u32[]{:S(2)}, u32[]{:S(2)}) collective-permute-start(f32[208,128]{1,0:T(8,128)S(1)} %get-tuple-element.70), channel_id=1, source_target_pairs={{0,3},{1,2},{2,1},{3,0},{4,7},{5,6},{6,5},{7,4},{8,11},{9,10},{10,... | collective-permute-start | bytes 319496 | tf_op jit(solution)/shard_map/ppermute | solution.py:70
  31.2 0.5 %collective-permute-start.14 = (f32[16,128]{1,0:T(8,128)S(1)}, f32[16,128]{1,0:T(8,128)S(1)}, u32[]{:S(2)}, u32[]{:S(2)}) collective-permute-start(f32[16,128]{1,0:T(8,128)S(1)} %get-tuple-element.71), channel_id=1, source_target_pairs={{0,2},{1,3},{2,0},{3,1},{4,6},{5,7},{6,4},{7,5},{8,10},{9,11},{10,... | collective-permute-start | bytes 24584 | tf_op jit(solution)/shard_map/ppermute | solution.py:48
  31.8 3.4 %collective-permute-done.14.rest_0_ = f32[16,128]{1,0:T(8,128)S(1)} collective-permute-done((f32[16,128]{1,0:T(8,128)S(1)}, f32[16,128]{1,0:T(8,128)S(1)}, u32[]{:S(2)}, u32[]{:S(2)}) %collective-permute-start.14) | collective-permute-done | bytes 8224 | tf_op jit(solution)/shard_map/ppermute | solution.py:48
  35.2 0.0 collective-permute-done.12.y_a
  35.2 0.0 collective-permute-done.13.y_b
  35.2 0.9 %shard_map.138 = (f32[4,256,128]{2,1,0:T(8,128)}, f32[16,128]{1,0:T(8,128)}) custom-call(f32[16,128]{1,0:T(8,128)S(1)} %get-tuple-element.38.refs_2_.alpha, f32[4,256,128]{2,1,0:T(8,128)S(1)} %get-tuple-element.67.near, f32[16,128]{1,0:T(8,128)S(1)} %get-tuple-element.68.sums, f32[208,128]{1,0:T(8,128)S(1)} %collective-permute-done.12.y_a, ...), custom_call_target="tpu_custom_call" | custom-call | flops 1000000 | bytes 761856 | tf_op jit(solution)/shard_map/pallas_call | solution.py:36
  (2 shorter events, 0.0 us)
Async XLA Ops:
  0.6 7.8 %copy-start = (f32[1,1,256,4,128]{4,3,2,1,0:T(4,128)S(1)}, f32[1,1,256,4,128]{4,3,2,1,0:T(4,128)}, u32[]{:S(2)}) copy-start(f32[1,1,256,4,128]{4,3,2,1,0:T(4,128)} %param.22) | copy-start | bytes 1572868
  2.1 8.2 %collective-permute-start = (f32[320,128]{1,0:T(8,128)S(1)}, f32[320,128]{1,0:T(8,128)S(1)}, u32[]{:S(2)}, u32[]{:S(2)}) collective-permute-start(f32[320,128]{1,0:T(8,128)S(1)} %get-tuple-element.46), channel_id=1, source_target_pairs={{0,1},{1,0},{2,3},{3,2},{4,5},{5,4},{6,7},{7,6},{8,9},{9,8},{10,11... | collective-permute-start | bytes 491528 | tf_op jit(solution)/shard_map/ppermute | solution.py:48
  2.6 7.7 %collective-permute-start.1 = (f32[304,128]{1,0:T(8,128)S(1)}, f32[304,128]{1,0:T(8,128)S(1)}, u32[]{:S(2)}, u32[]{:S(2)}) collective-permute-start(f32[304,128]{1,0:T(8,128)S(1)} %get-tuple-element.47), channel_id=1, source_target_pairs={{0,4},{1,2},{2,1},{3,7},{4,0},{5,6},{6,5},{7,3},{8,12},{9,10},{10,... | collective-permute-start | bytes 466952 | tf_op jit(solution)/shard_map/ppermute | solution.py:64
  5.2 3.6 %collective-permute-start.3 = (f32[16,128]{1,0:T(8,128)}, f32[16,128]{1,0:T(8,128)S(1)}, u32[]{:S(2)}, u32[]{:S(2)}) collective-permute-start(f32[16,128]{1,0:T(8,128)} %bitcast.22), channel_id=1, source_target_pairs={{0,3},{1,2},{2,1},{3,0},{4,7},{5,6},{6,5},{7,4},{8,11},{9,10},{10,... | collective-permute-start | bytes 24584 | tf_op jit(solution)/shard_map/ppermute | solution.py:48
  6.4 3.9 %collective-permute-start.2 = (f32[16,128]{1,0:T(8,128)}, f32[16,128]{1,0:T(8,128)S(1)}, u32[]{:S(2)}, u32[]{:S(2)}) collective-permute-start(f32[16,128]{1,0:T(8,128)} %bitcast.23), channel_id=1, source_target_pairs={{0,2},{1,3},{2,0},{3,1},{4,6},{5,7},{6,4},{7,5},{8,10},{9,11},{10,... | collective-permute-start | bytes 24584 | tf_op jit(solution)/shard_map/ppermute | solution.py:48
  6.9 4.5 %collective-permute-start.6 = (f32[24,128]{1,0:T(8,128)}, f32[24,128]{1,0:T(8,128)S(1)}, u32[]{:S(2)}, u32[]{:S(2)}) collective-permute-start(f32[24,128]{1,0:T(8,128)} %bitcast.20), channel_id=1, source_target_pairs={{0,8},{4,12},{8,0},{12,4},{16,24},{20,28},{24,16},{28,20},{1,9},{5... | collective-permute-start | bytes 36872 | tf_op jit(solution)/shard_map/ppermute | solution.py:48
  10.8 10.4 %collective-permute-start.4 = (f32[318,128]{1,0:T(8,128)S(1)}, f32[318,128]{1,0:T(8,128)S(1)}, u32[]{:S(2)}, u32[]{:S(2)}) collective-permute-start(f32[318,128]{1,0:T(8,128)S(1)} %get-tuple-element.57), channel_id=1, source_target_pairs={{0,4},{4,0},{8,12},{12,8},{16,20},{20,16},{24,28},{28,24},{1,5},{5... | collective-permute-start | bytes 488456 | tf_op jit(solution)/shard_map/ppermute | solution.py:48
  11.4 9.9 %collective-permute-start.5 = (f32[326,128]{1,0:T(8,128)S(1)}, f32[326,128]{1,0:T(8,128)S(1)}, u32[]{:S(2)}, u32[]{:S(2)}) collective-permute-start(f32[326,128]{1,0:T(8,128)S(1)} %get-tuple-element.58), channel_id=1, source_target_pairs={{0,1},{4,8},{8,4},{12,16},{16,12},{20,24},{24,20},{28,29},{1,0},{5... | collective-permute-start | bytes 500744 | tf_op jit(solution)/shard_map/ppermute | solution.py:64
  11.4 8.6 %collective-permute-start.9 = (f32[48,128]{1,0:T(8,128)S(1)}, f32[48,128]{1,0:T(8,128)S(1)}, u32[]{:S(2)}, u32[]{:S(2)}) collective-permute-start(f32[48,128]{1,0:T(8,128)S(1)} %constant_dynamic-update-slice_fusion.rest_0_), channel_id=1, source_target_pairs={{0,20},{4,16},{8,28},{12,24},{16,4},{20,0},{24,12},{28,8},{1,21},{... | collective-permute-start | bytes 73736 | tf_op jit(solution)/shard_map/ppermute | solution.py:48
  16.6 4.7 %collective-permute-start.8 = (f32[48,128]{1,0:T(8,128)S(1)}, f32[48,128]{1,0:T(8,128)S(1)}, u32[]{:S(2)}, u32[]{:S(2)}) collective-permute-start(f32[48,128]{1,0:T(8,128)S(1)} %constant_dynamic-update-slice_fusion.rest_0_), channel_id=1, source_target_pairs={{0,16},{4,20},{8,24},{12,28},{16,0},{20,4},{24,8},{28,12},{1,17},{... | collective-permute-start | bytes 73736 | tf_op jit(solution)/shard_map/ppermute | solution.py:48
  16.9 4.4 %collective-permute-start.7 = (f32[48,128]{1,0:T(8,128)S(1)}, f32[48,128]{1,0:T(8,128)S(1)}, u32[]{:S(2)}, u32[]{:S(2)}) collective-permute-start(f32[48,128]{1,0:T(8,128)S(1)} %constant_dynamic-update-slice_fusion.rest_0_), channel_id=1, source_target_pairs={{0,4},{4,0},{8,12},{12,8},{16,20},{20,16},{24,28},{28,24},{1,5},{5... | collective-permute-start | bytes 73736 | tf_op jit(solution)/shard_map/ppermute | solution.py:48
  23.7 5.6 %collective-permute-start.11 = (f32[224,128]{1,0:T(8,128)S(1)}, f32[224,128]{1,0:T(8,128)S(1)}, u32[]{:S(2)}, u32[]{:S(2)}) collective-permute-start(f32[224,128]{1,0:T(8,128)S(1)} %get-tuple-element.66), channel_id=1, source_target_pairs={{0,1},{4,8},{8,4},{12,16},{16,12},{20,24},{24,20},{28,29},{1,0},{5... | collective-permute-start | bytes 344072 | tf_op jit(solution)/shard_map/ppermute | solution.py:64
  23.8 5.5 %collective-permute-start.10 = (f32[216,128]{1,0:T(8,128)S(1)}, f32[216,128]{1,0:T(8,128)S(1)}, u32[]{:S(2)}, u32[]{:S(2)}) collective-permute-start(f32[216,128]{1,0:T(8,128)S(1)} %get-tuple-element.65), channel_id=1, source_target_pairs={{0,4},{4,0},{8,12},{12,8},{16,20},{20,16},{24,28},{28,24},{1,5},{5... | collective-permute-start | bytes 331784 | tf_op jit(solution)/shard_map/ppermute | solution.py:48
  29.6 5.5 %collective-permute-start.12 = (f32[208,128]{1,0:T(8,128)S(1)}, f32[208,128]{1,0:T(8,128)S(1)}, u32[]{:S(2)}, u32[]{:S(2)}) collective-permute-start(f32[208,128]{1,0:T(8,128)S(1)} %get-tuple-element.69), channel_id=1, source_target_pairs={{0,1},{1,0},{2,3},{3,2},{4,5},{5,4},{6,7},{7,6},{8,9},{9,8},{10,11... | collective-permute-start | bytes 319496 | tf_op jit(solution)/shard_map/ppermute | solution.py:48
  29.6 5.5 %collective-permute-start.13 = (f32[208,128]{1,0:T(8,128)S(1)}, f32[208,128]{1,0:T(8,128)S(1)}, u32[]{:S(2)}, u32[]{:S(2)}) collective-permute-start(f32[208,128]{1,0:T(8,128)S(1)} %get-tuple-element.70), channel_id=1, source_target_pairs={{0,3},{1,2},{2,1},{3,0},{4,7},{5,6},{6,5},{7,4},{8,11},{9,10},{10,... | collective-permute-start | bytes 319496 | tf_op jit(solution)/shard_map/ppermute | solution.py:70
  31.2 3.9 %collective-permute-start.14 = (f32[16,128]{1,0:T(8,128)S(1)}, f32[16,128]{1,0:T(8,128)S(1)}, u32[]{:S(2)}, u32[]{:S(2)}) collective-permute-start(f32[16,128]{1,0:T(8,128)S(1)} %get-tuple-element.71), channel_id=1, source_target_pairs={{0,2},{1,3},{2,0},{3,1},{4,6},{5,7},{6,4},{7,5},{8,10},{9,11},{10,... | collective-permute-start | bytes 24584 | tf_op jit(solution)/shard_map/ppermute | solution.py:48

commit v14 on v13

--- a/solution.py
+++ b/solution.py
@@ -175,10 +175,9 @@
     held = BEAM_BITS
     beam = gates[0]
     owner = jnp.bitwise_xor(beam >> held, lax.axis_index("gx"))
-    block = (owner & -4) | ((owner & 1) << 1) | ((owner >> 1) & 1)
     meta[...] = jnp.zeros(meta.shape, f32)
     meta[0:1] = gates[2].astype(f32)
-    meta[1:2] = ((block << held) | (beam & ((1 << held) - 1))).astype(f32)
+    meta[1:2] = ((owner << held) | (beam & ((1 << held) - 1))).astype(f32)
     meta[2:3] = gates[1].astype(f32)
     meta[3:4] = gates[3].astype(f32) * values[...]
 
@@ -236,7 +235,6 @@
     others = rest[: ny - 2]
     out_a, out_b, field, picks, known, tiles = rest[ny - 2 :]
     even, _, _ = place_on("gx")
-    out_b[X_HALO:] = jnp.zeros((8, 128), f32)
     owned = alpha.shape[0] // NC
     gather_known(alpha, y_a, others, known)
     turned = tile_numbers(near_tiles, y_a, y_b, tiles)
@@ -429,7 +427,6 @@
     out_a, out_b, back_2, back_1, coef, tops, lows = rest[-13:-6]
     state_0, state_1, state_2, state_3, raw, forcing = rest[-6:]
     even, _, _ = place_on("gx")
-    out_b[X_COEF:] = jnp.zeros((8, 128), f32)
     slots = columns.shape[0]
 
     def fill(ref, base, x_base, found):
@@ -740,8 +737,8 @@
     y_a = swap(y_a, "gy", 1)
     y_b = pair_b(y_b, "gy", "gx")
     others = [swap(control, "gy", xor) for xor in range(2, ny)]
-    beams = jnp.concatenate([near_beams, swap(own_beams, "gx", 2)])
-    beams = [beams] + [swap(beams, "gx", xor) for xor in range(1, nx) if xor % 4 < 2]
+    beams = jnp.concatenate([near_beams, swap(own_beams, "gx", 1)])
+    beams = [beams] + [swap(beams, "gx", xor) for xor in range(2, nx, 2)]
 
     wide, slot_pick, slot_push, beam_pick, columns, edge_pick = call(
         one_hots,
@@ -757,7 +754,7 @@
     )
     x_a, x_b = call(
         lambda *refs: pack_x(ny, *refs),
-        [(X_HALO, 128), (X_HALO + 8, 128)],
+        [(X_HALO, 128), (X_HALO, 128)],
         [fine, coefs, control_near, near_tiles, columns, y_a, y_b, *others],
         [
             pltpu.VMEM((2 * RIM * PITCH, 128), f32),
@@ -792,7 +789,7 @@
         edges,
         [
             (X_COEF, 128),
-            (X_COEF + 8, 128),
+            (X_COEF, 128),
             big,
             big,
             (5 * FIELD, 128),

time: 36.3 us -> 35.5 us (0.978)
  starting transfers between devices: 17.5 us -> 15.4 us
  waiting for transfers between devices: 7.13 us -> 8.41 us
    ppermute x11, waiting for transfers between devices: 7.11 us -> 8.4 us  [swap(): lax.ppermute(block, axis, [(i, i ^ xor) for i in range(lax.axis_size(axis...]
    ppermute x1, starting transfers between devices: 1.6 us -> 0.59 us  [ring_b(): return lax.ppermute(block, axis, pairs)]
    ppermute x11, starting transfers between devices: 13.2 us -> 12.2 us  [swap(): lax.ppermute(block, axis, [(i, i ^ xor) for i in range(lax.axis_size(axis...]
  transfers between devices with their start and end apart: 15 -> 15, of which waited for: 4 -> 5; matrix products, arithmetic and copies ran while one was open for 0% -> 0% of each run, Pallas kernels for 16% -> 16%
where the time goes in v14:
time: 35.5 us; the launch traced here: 35.4 us
  starting transfers between devices  15.4 us (43%)
  Pallas kernels  10.8 us (30%)
  waiting for transfers between devices  8.41 us (24%)
  between operations  0.72 us (2%)
    ppermute x11, starting transfers between devices, swap(): lax.ppermute(block, axis, [(i, i ^ xor) for i in range(lax.axis_size(axis...  12.2 us
    pallas_call x8, Pallas kernels, call(): pl.pallas_call(body, out_shape=shapes, in_specs=in_specs or [VMEM] * len(...  10.8 us
    ppermute x11, waiting for transfers between devices, swap(): lax.ppermute(block, axis, [(i, i ^ xor) for i in range(lax.axis_size(axis...  8.4 us
    ppermute x3, starting transfers between devices, pair_b(): return lax.ppermute(block, ('gx', 'gy'), pairs)  2.6 us
  transfers between devices with their start and end apart: 15, of which 5 were waited for; matrix products, arithmetic and copies ran while one was open for 0% of the time, Pallas kernels for 16%

profile of v14, /device:TPU:0, one launch (start us, length us, event | category | flops | bytes accessed | tf_op | source)
XLA Modules:
  0.0 35.4 jit_solution(2945227668406184758)
XLA Ops:
  0.6 0.0 copy-start
  0.6 1.4 %shard_map.131 = (f32[320,128]{1,0:T(8,128)S(1)}, f32[304,128]{1,0:T(8,128)S(1)}, f32[4,256,128]{2,1,0:T(8,128)S(1)}, f32[3,256,128]{2,1,0:T(8,128)S(1)}, f32[16...) custom-call(f32[4,256,128]{2,1,0:T(8,128)} %bitcast.16, ...), custom_call_target="tpu_custom_call" | custom-call | flops 1000000 | bytes 944128 | tf_op jit(solution)/shard_map/pallas_call | solution.py:36
  2.1 0.5 %collective-permute-start = (f32[320,128]{1,0:T(8,128)S(1)}, f32[320,128]{1,0:T(8,128)S(1)}, u32[]{:S(2)}, u32[]{:S(2)}) collective-permute-start(f32[320,128]{1,0:T(8,128)S(1)} %get-tuple-element.46), channel_id=1, source_target_pairs={{0,1},{1,0},{2,3},{3,2},{4,5},{5,4},{6,7},{7,6},{8,9},{9,8},{10,11... | collective-permute-start | bytes 491528 | tf_op jit(solution)/shard_map/ppermute | solution.py:48
  2.6 2.6 %collective-permute-start.1 = (f32[304,128]{1,0:T(8,128)S(1)}, f32[304,128]{1,0:T(8,128)S(1)}, u32[]{:S(2)}, u32[]{:S(2)}) collective-permute-start(f32[304,128]{1,0:T(8,128)S(1)} %get-tuple-element.47), channel_id=1, source_target_pairs={{0,4},{1,2},{2,1},{3,7},{4,0},{5,6},{6,5},{7,3},{8,12},{9,10},{10,... | collective-permute-start | bytes 466952 | tf_op jit(solution)/shard_map/ppermute | solution.py:64
  5.2 1.2 %collective-permute-start.3 = (f32[16,128]{1,0:T(8,128)}, f32[16,128]{1,0:T(8,128)S(1)}, u32[]{:S(2)}, u32[]{:S(2)}) collective-permute-start(f32[16,128]{1,0:T(8,128)} %bitcast.22), channel_id=1, source_target_pairs={{0,3},{1,2},{2,1},{3,0},{4,7},{5,6},{6,5},{7,4},{8,11},{9,10},{10,... | collective-permute-start | bytes 24584 | tf_op jit(solution)/shard_map/ppermute | solution.py:48
  6.4 0.5 %collective-permute-start.2 = (f32[16,128]{1,0:T(8,128)}, f32[16,128]{1,0:T(8,128)S(1)}, u32[]{:S(2)}, u32[]{:S(2)}) collective-permute-start(f32[16,128]{1,0:T(8,128)} %bitcast.23), channel_id=1, source_target_pairs={{0,2},{1,3},{2,0},{3,1},{4,6},{5,7},{6,4},{7,5},{8,10},{9,11},{10,... | collective-permute-start | bytes 24584 | tf_op jit(solution)/shard_map/ppermute | solution.py:48
  6.9 1.5 %collective-permute-start.6 = (f32[24,128]{1,0:T(8,128)}, f32[24,128]{1,0:T(8,128)S(1)}, u32[]{:S(2)}, u32[]{:S(2)}) collective-permute-start(f32[24,128]{1,0:T(8,128)} %bitcast.20), channel_id=1, source_target_pairs={{0,4},{4,0},{8,12},{12,8},{16,20},{20,16},{24,28},{28,24},{1,5},{5... | collective-permute-start | bytes 36872 | tf_op jit(solution)/shard_map/ppermute | solution.py:48
  8.4 0.0 copy-done
  8.4 0.3 shard_map.132
  8.7 0.0 collective-permute-done.3.refs_10_.refs_8_
  8.8 1.5 %collective-permute-done.2.refs_9_.refs_7_ = f32[16,128]{1,0:T(8,128)S(1)} collective-permute-done((f32[16,128]{1,0:T(8,128)}, f32[16,128]{1,0:T(8,128)S(1)}, u32[]{:S(2)}, u32[]{:S(2)}) %collective-permute-start.2) | collective-permute-done | bytes 8224 | tf_op jit(solution)/shard_map/ppermute | solution.py:48
  10.3 0.0 collective-permute-done.1.refs_8_.refs_6_
  10.3 0.0 collective-permute-done.refs_7_.refs_5_
  10.3 0.5 %shard_map.134 = (f32[318,128]{1,0:T(8,128)S(1)}, f32[318,128]{1,0:T(8,128)S(1)}) custom-call(f32[4,256,128]{2,1,0:T(8,128)S(1)} %get-tuple-element.39.refs_0_, f32[3,256,128]{2,1,0:T(8,128)S(1)} %get-tuple-element.40.refs_1_, f32[16,128]{1,0:T(8,128)S(1)} %get-tuple-element.38.refs_2_.alpha, f32[16,128]{1,0:T(8,128)S(1)} %get-tuple-element.41.refs_3_, ...), custom_call_target="tpu_custom_call" | custom-call | flops 1000000 | bytes 1277952 | tf_op jit(solution)/shard_map/pallas_call | solution.py:36
  10.8 0.6 %collective-permute-start.4 = (f32[318,128]{1,0:T(8,128)S(1)}, f32[318,128]{1,0:T(8,128)S(1)}, u32[]{:S(2)}, u32[]{:S(2)}) collective-permute-start(f32[318,128]{1,0:T(8,128)S(1)} %get-tuple-element.57), channel_id=1, source_target_pairs={{0,4},{4,0},{8,12},{12,8},{16,20},{20,16},{24,28},{28,24},{1,5},{5... | collective-permute-start | bytes 488456 | tf_op jit(solution)/shard_map/ppermute | solution.py:48
  11.4 0.0 collective-permute-start.5
  11.4 0.0 collective-permute-done.6
  11.4 5.1 %collective-permute-start.9 = (f32[48,128]{1,0:T(8,128)S(1)}, f32[48,128]{1,0:T(8,128)S(1)}, u32[]{:S(2)}, u32[]{:S(2)}) collective-permute-start(f32[48,128]{1,0:T(8,128)S(1)} %constant_dynamic-update-slice_fusion.rest_0_), channel_id=1, source_target_pairs={{0,24},{4,28},{8,16},{12,20},{16,8},{20,12},{24,0},{28,4},{1,25},{... | collective-permute-start | bytes 73736 | tf_op jit(solution)/shard_map/ppermute | solution.py:48
  16.5 0.0 collective-permute-start.8
  16.5 0.6 %collective-permute-start.7 = (f32[48,128]{1,0:T(8,128)S(1)}, f32[48,128]{1,0:T(8,128)S(1)}, u32[]{:S(2)}, u32[]{:S(2)}) collective-permute-start(f32[48,128]{1,0:T(8,128)S(1)} %constant_dynamic-update-slice_fusion.rest_0_), channel_id=1, source_target_pairs={{0,8},{4,12},{8,0},{12,4},{16,24},{20,28},{24,16},{28,20},{1,9},{5... | collective-permute-start | bytes 73736 | tf_op jit(solution)/shard_map/ppermute | solution.py:48
  17.1 2.8 %shard_map.133 = (f32[1536,128]{1,0:T(8,128)S(1)}, f32[1920,128]{1,0:T(8,128)S(1)}, f32[384,16]{1,0:T(8,128)S(1)}, f32[1536,128]{1,0:T(8,128)S(1)}, f32[1536,128]{1,0:T(8,128)S(1)}, /*index=5*/f32[768,128]{1,0:T(8,128)S(1)}) custom-call(f32[4,256,128]{2,1,0:T(8,128)S(1)} %get-tuple-element.39.refs_0_, f32[3,256,128]{2,1,0:T(8,128)S(1)} %get-tuple-element.40.refs_1_, ...), custom_call_target="tpu_custom_call" | custom-call | flops 3000000 | bytes 2064384 | tf_op jit(solution)/shard_map/pallas_call | solution.py:36
  20.0 0.3 collective-permute-done.9.rest_3_
  20.3 0.9 %collective-permute-done.8.rest_2_ = f32[48,128]{1,0:T(8,128)S(1)} collective-permute-done((f32[48,128]{1,0:T(8,128)S(1)}, f32[48,128]{1,0:T(8,128)S(1)}, u32[]{:S(2)}, u32[]{:S(2)}) %collective-permute-start.8) | collective-permute-done | bytes 24608 | tf_op jit(solution)/shard_map/ppermute | solution.py:48
  21.2 0.0 collective-permute-done.7.rest_1_
  21.2 0.0 collective-permute-done.4.x_a
  21.2 0.0 collective-permute-done.5.x_b
  21.2 2.5 %shard_map.135 = (f32[216,128]{1,0:T(8,128)S(1)}, f32[216,128]{1,0:T(8,128)S(1)}, f32[2304,128]{1,0:T(8,128)S(1)}, f32[2304,128]{1,0:T(8,128)S(1)}, f32[2880,128...) custom-call(f32[1536,128]{1,0:T(8,128)S(1)} %get-tuple-element.50.core, ...), custom_call_target="tpu_custom_call" | custom-call | flops 10000000 | bytes 5281792 | tf_op jit(solution)/shard_map/pallas_call | solution.py:36
  23.7 0.6 %collective-permute-start.10 = (f32[216,128]{1,0:T(8,128)S(1)}, f32[216,128]{1,0:T(8,128)S(1)}, u32[]{:S(2)}, u32[]{:S(2)}) collective-permute-start(f32[216,128]{1,0:T(8,128)S(1)} %get-tuple-element.65), channel_id=1, source_target_pairs={{0,4},{4,0},{8,12},{12,8},{16,20},{20,16},{24,28},{28,24},{1,5},{5... | collective-permute-start | bytes 331784 | tf_op jit(solution)/shard_map/ppermute | solution.py:48
  24.3 0.0 collective-permute-start.11
  24.3 1.9 %shard_map.136.refs_2_ = f32[1536,128]{1,0:T(8,128)S(1)} custom-call(f32[1920,128]{1,0:T(8,128)S(1)} %get-tuple-element.49.core_coef, f32[2880,128]{1,0:T(8,128)S(1)} %get-tuple-element.60.edge_coef, f32[2304,128]{1,0:T(8,128)S(1)} %get-tuple-element.61.back_2, f32[2304,128]{1,0:T(8,128)S(1)} %get-tuple-element.62.back_1, ...), custom_call_target="tpu_custom_call" | custom-call | flops 10000000 | bytes 8224768 | tf_op jit(solution)/shard_map/pallas_call | solution.py:36
  26.3 2.2 %collective-permute-done.10.refs_3_ = f32[216,128]{1,0:T(8,128)S(1)} collective-permute-done((f32[216,128]{1,0:T(8,128)S(1)}, f32[216,128]{1,0:T(8,128)S(1)}, u32[]{:S(2)}, u32[]{:S(2)}) %collective-permute-start.10) | collective-permute-done | bytes 110624 | tf_op jit(solution)/shard_map/ppermute | solution.py:48
  28.5 0.0 collective-permute-done.11.refs_4_
  28.5 0.4 %shard_map.137 = (f32[208,128]{1,0:T(8,128)S(1)}, f32[208,128]{1,0:T(8,128)S(1)}, f32[4,256,128]{2,1,0:T(8,128)S(1)}, f32[16,128]{1,0:T(8,128)S(1)}, f32[16,128]{1,0:T(8,128)S(1)}) custom-call(f32[4,256,128]{2,1,0:T(8,128)S(1)} %get-tuple-element.39.refs_0_, f32[384,16]{1,0:T(8,128)S(1)} %get-tuple-element.48.refs_1_, f32[1536,128]{1,0:T(8,128)S(1)} %shard_map.136.refs_2_, ...), custom_call_target="tpu_custom_call" | custom-call | flops 1000000 | bytes 1556480 | tf_op jit(solution)/shard_map/pallas_call | solution.py:36
  28.9 0.0 collective-permute-start.12
  28.9 0.6 %collective-permute-start.13 = (f32[208,128]{1,0:T(8,128)S(1)}, f32[208,128]{1,0:T(8,128)S(1)}, u32[]{:S(2)}, u32[]{:S(2)}) collective-permute-start(f32[208,128]{1,0:T(8,128)S(1)} %get-tuple-element.70), channel_id=1, source_target_pairs={{0,3},{1,2},{2,1},{3,0},{4,7},{5,6},{6,5},{7,4},{8,11},{9,10},{10,... | collective-permute-start | bytes 319496 | tf_op jit(solution)/shard_map/ppermute | solution.py:70
  29.5 1.5 %collective-permute-start.14 = (f32[16,128]{1,0:T(8,128)S(1)}, f32[16,128]{1,0:T(8,128)S(1)}, u32[]{:S(2)}, u32[]{:S(2)}) collective-permute-start(f32[16,128]{1,0:T(8,128)S(1)} %get-tuple-element.71), channel_id=1, source_target_pairs={{0,2},{1,3},{2,0},{3,1},{4,6},{5,7},{6,4},{7,5},{8,10},{9,11},{10,... | collective-permute-start | bytes 24584 | tf_op jit(solution)/shard_map/ppermute | solution.py:48
  31.1 3.4 %collective-permute-done.14.rest_0_ = f32[16,128]{1,0:T(8,128)S(1)} collective-permute-done((f32[16,128]{1,0:T(8,128)S(1)}, f32[16,128]{1,0:T(8,128)S(1)}, u32[]{:S(2)}, u32[]{:S(2)}) %collective-permute-start.14) | collective-permute-done | bytes 8224 | tf_op jit(solution)/shard_map/ppermute | solution.py:48
  34.4 0.0 collective-permute-done.12.y_a
  34.4 0.0 collective-permute-done.13.y_b
  34.4 0.9 %shard_map.138 = (f32[4,256,128]{2,1,0:T(8,128)}, f32[16,128]{1,0:T(8,128)}) custom-call(f32[16,128]{1,0:T(8,128)S(1)} %get-tuple-element.38.refs_2_.alpha, f32[4,256,128]{2,1,0:T(8,128)S(1)} %get-tuple-element.67.near, f32[16,128]{1,0:T(8,128)S(1)} %get-tuple-element.68.sums, f32[208,128]{1,0:T(8,128)S(1)} %collective-permute-done.12.y_a, ...), custom_call_target="tpu_custom_call" | custom-call | flops 1000000 | bytes 761856 | tf_op jit(solution)/shard_map/pallas_call | solution.py:36
  (2 shorter events, 0.0 us)
Async XLA Ops:
  0.6 7.8 %copy-start = (f32[1,1,256,4,128]{4,3,2,1,0:T(4,128)S(1)}, f32[1,1,256,4,128]{4,3,2,1,0:T(4,128)}, u32[]{:S(2)}) copy-start(f32[1,1,256,4,128]{4,3,2,1,0:T(4,128)} %param.22) | copy-start | bytes 1572868
  2.1 8.2 %collective-permute-start = (f32[320,128]{1,0:T(8,128)S(1)}, f32[320,128]{1,0:T(8,128)S(1)}, u32[]{:S(2)}, u32[]{:S(2)}) collective-permute-start(f32[320,128]{1,0:T(8,128)S(1)} %get-tuple-element.46), channel_id=1, source_target_pairs={{0,1},{1,0},{2,3},{3,2},{4,5},{5,4},{6,7},{7,6},{8,9},{9,8},{10,11... | collective-permute-start | bytes 491528 | tf_op jit(solution)/shard_map/ppermute | solution.py:48
  2.6 7.7 %collective-permute-start.1 = (f32[304,128]{1,0:T(8,128)S(1)}, f32[304,128]{1,0:T(8,128)S(1)}, u32[]{:S(2)}, u32[]{:S(2)}) collective-permute-start(f32[304,128]{1,0:T(8,128)S(1)} %get-tuple-element.47), channel_id=1, source_target_pairs={{0,4},{1,2},{2,1},{3,7},{4,0},{5,6},{6,5},{7,3},{8,12},{9,10},{10,... | collective-permute-start | bytes 466952 | tf_op jit(solution)/shard_map/ppermute | solution.py:64
  5.2 3.6 %collective-permute-start.3 = (f32[16,128]{1,0:T(8,128)}, f32[16,128]{1,0:T(8,128)S(1)}, u32[]{:S(2)}, u32[]{:S(2)}) collective-permute-start(f32[16,128]{1,0:T(8,128)} %bitcast.22), channel_id=1, source_target_pairs={{0,3},{1,2},{2,1},{3,0},{4,7},{5,6},{6,5},{7,4},{8,11},{9,10},{10,... | collective-permute-start | bytes 24584 | tf_op jit(solution)/shard_map/ppermute | solution.py:48
  6.4 3.9 %collective-permute-start.2 = (f32[16,128]{1,0:T(8,128)}, f32[16,128]{1,0:T(8,128)S(1)}, u32[]{:S(2)}, u32[]{:S(2)}) collective-permute-start(f32[16,128]{1,0:T(8,128)} %bitcast.23), channel_id=1, source_target_pairs={{0,2},{1,3},{2,0},{3,1},{4,6},{5,7},{6,4},{7,5},{8,10},{9,11},{10,... | collective-permute-start | bytes 24584 | tf_op jit(solution)/shard_map/ppermute | solution.py:48
  6.9 4.5 %collective-permute-start.6 = (f32[24,128]{1,0:T(8,128)}, f32[24,128]{1,0:T(8,128)S(1)}, u32[]{:S(2)}, u32[]{:S(2)}) collective-permute-start(f32[24,128]{1,0:T(8,128)} %bitcast.20), channel_id=1, source_target_pairs={{0,4},{4,0},{8,12},{12,8},{16,20},{20,16},{24,28},{28,24},{1,5},{5... | collective-permute-start | bytes 36872 | tf_op jit(solution)/shard_map/ppermute | solution.py:48
  10.8 10.4 %collective-permute-start.4 = (f32[318,128]{1,0:T(8,128)S(1)}, f32[318,128]{1,0:T(8,128)S(1)}, u32[]{:S(2)}, u32[]{:S(2)}) collective-permute-start(f32[318,128]{1,0:T(8,128)S(1)} %get-tuple-element.57), channel_id=1, source_target_pairs={{0,4},{4,0},{8,12},{12,8},{16,20},{20,16},{24,28},{28,24},{1,5},{5... | collective-permute-start | bytes 488456 | tf_op jit(solution)/shard_map/ppermute | solution.py:48
  11.4 9.8 %collective-permute-start.5 = (f32[318,128]{1,0:T(8,128)S(1)}, f32[318,128]{1,0:T(8,128)S(1)}, u32[]{:S(2)}, u32[]{:S(2)}) collective-permute-start(f32[318,128]{1,0:T(8,128)S(1)} %get-tuple-element.58), channel_id=1, source_target_pairs={{0,1},{4,8},{8,4},{12,16},{16,12},{20,24},{24,20},{28,29},{1,0},{5... | collective-permute-start | bytes 488456 | tf_op jit(solution)/shard_map/ppermute | solution.py:64
  11.4 8.9 %collective-permute-start.9 = (f32[48,128]{1,0:T(8,128)S(1)}, f32[48,128]{1,0:T(8,128)S(1)}, u32[]{:S(2)}, u32[]{:S(2)}) collective-permute-start(f32[48,128]{1,0:T(8,128)S(1)} %constant_dynamic-update-slice_fusion.rest_0_), channel_id=1, source_target_pairs={{0,24},{4,28},{8,16},{12,20},{16,8},{20,12},{24,0},{28,4},{1,25},{... | collective-permute-start | bytes 73736 | tf_op jit(solution)/shard_map/ppermute | solution.py:48
  16.5 4.7 %collective-permute-start.8 = (f32[48,128]{1,0:T(8,128)S(1)}, f32[48,128]{1,0:T(8,128)S(1)}, u32[]{:S(2)}, u32[]{:S(2)}) collective-permute-start(f32[48,128]{1,0:T(8,128)S(1)} %constant_dynamic-update-slice_fusion.rest_0_), channel_id=1, source_target_pairs={{0,16},{4,20},{8,24},{12,28},{16,0},{20,4},{24,8},{28,12},{1,17},{... | collective-permute-start | bytes 73736 | tf_op jit(solution)/shard_map/ppermute | solution.py:48
  16.5 4.7 %collective-permute-start.7 = (f32[48,128]{1,0:T(8,128)S(1)}, f32[48,128]{1,0:T(8,128)S(1)}, u32[]{:S(2)}, u32[]{:S(2)}) collective-permute-start(f32[48,128]{1,0:T(8,128)S(1)} %constant_dynamic-update-slice_fusion.rest_0_), channel_id=1, source_target_pairs={{0,8},{4,12},{8,0},{12,4},{16,24},{20,28},{24,16},{28,20},{1,9},{5... | collective-permute-start | bytes 73736 | tf_op jit(solution)/shard_map/ppermute | solution.py:48
  23.7 4.8 %collective-permute-start.10 = (f32[216,128]{1,0:T(8,128)S(1)}, f32[216,128]{1,0:T(8,128)S(1)}, u32[]{:S(2)}, u32[]{:S(2)}) collective-permute-start(f32[216,128]{1,0:T(8,128)S(1)} %get-tuple-element.65), channel_id=1, source_target_pairs={{0,4},{4,0},{8,12},{12,8},{16,20},{20,16},{24,28},{28,24},{1,5},{5... | collective-permute-start | bytes 331784 | tf_op jit(solution)/shard_map/ppermute | solution.py:48
  24.3 4.2 %collective-permute-start.11 = (f32[216,128]{1,0:T(8,128)S(1)}, f32[216,128]{1,0:T(8,128)S(1)}, u32[]{:S(2)}, u32[]{:S(2)}) collective-permute-start(f32[216,128]{1,0:T(8,128)S(1)} %get-tuple-element.66), channel_id=1, source_target_pairs={{0,1},{4,8},{8,4},{12,16},{16,12},{20,24},{24,20},{28,29},{1,0},{5... | collective-permute-start | bytes 331784 | tf_op jit(solution)/shard_map/ppermute | solution.py:64
  28.9 5.5 %collective-permute-start.12 = (f32[208,128]{1,0:T(8,128)S(1)}, f32[208,128]{1,0:T(8,128)S(1)}, u32[]{:S(2)}, u32[]{:S(2)}) collective-permute-start(f32[208,128]{1,0:T(8,128)S(1)} %get-tuple-element.69), channel_id=1, source_target_pairs={{0,1},{1,0},{2,3},{3,2},{4,5},{5,4},{6,7},{7,6},{8,9},{9,8},{10,11... | collective-permute-start | bytes 319496 | tf_op jit(solution)/shard_map/ppermute | solution.py:48
  28.9 5.5 %collective-permute-start.13 = (f32[208,128]{1,0:T(8,128)S(1)}, f32[208,128]{1,0:T(8,128)S(1)}, u32[]{:S(2)}, u32[]{:S(2)}) collective-permute-start(f32[208,128]{1,0:T(8,128)S(1)} %get-tuple-element.70), channel_id=1, source_target_pairs={{0,3},{1,2},{2,1},{3,0},{4,7},{5,6},{6,5},{7,4},{8,11},{9,10},{10,... | collective-permute-start | bytes 319496 | tf_op jit(solution)/shard_map/ppermute | solution.py:70
  29.5 4.9 %collective-permute-start.14 = (f32[16,128]{1,0:T(8,128)S(1)}, f32[16,128]{1,0:T(8,128)S(1)}, u32[]{:S(2)}, u32[]{:S(2)}) collective-permute-start(f32[16,128]{1,0:T(8,128)S(1)} %get-tuple-element.71), channel_id=1, source_target_pairs={{0,2},{1,3},{2,0},{3,1},{4,6},{5,7},{6,4},{7,5},{8,10},{9,11},{10,... | collective-permute-start | bytes 24584 | tf_op jit(solution)/shard_map/ppermute | solution.py:48

commit v15 on v14

--- a/solution.py
+++ b/solution.py
@@ -98,6 +98,7 @@
 WIDE, WIDE_ROWS = layers(RIM)
 SLIM, SLIM_ROWS = layers(INNER)
 X_COEF = NC * WIDE_ROWS
+CORNERS = NC * 2 * sum(extra for _, _, extra in WIDE)
 X_HALO = X_COEF + 3 * SLIM_ROWS
 
 Y_COEF = NC * RIM * CX
@@ -559,7 +560,9 @@
                     out_b[at : at + size] = jnp.where(even, west, east)
 
 
-def interior(core_coef, edge_coef, back_2, back_1, tops, lows, slot_push, out, *scratch):
+def interior(
+    core_coef, edge_coef, back_2, back_1, tops, lows, slot_push, out, out_a, out_b, *scratch
+):
     coef, forced, field_2, field_1, forcing = scratch
     for f in range(5):
         at = f * FIELD + FIRST * PITCH
@@ -612,6 +615,14 @@
     add_forcing(field_1, STEPS - 3, range(1, CX - 1))
     copy(back_1, field_1, (-1, 0, CX - 1, CX))
     sweep(field_1, out, 0, CX)
+    even, _, _ = place_on("gy")
+    for c in range(NC):
+        for away in range(1, RIM + 1):
+            north = out[pl.ds(c * CORE + CY - 1 + away, CX, stride=PITCH)]
+            south = out[pl.ds(c * CORE + PITCH - away, CX, stride=PITCH)]
+            at = (c * RIM + away - 1) * CX
+            out_a[at : at + CX] = jnp.where(even, north, south)
+            out_b[at : at + CX] = jnp.where(even, south, north)
 
 
 def add_x(ny, delta, picks, core, x_a, x_b, *rest):
@@ -636,13 +647,18 @@
                     field[at : at + size] += west
                     at = c * CORE + (CX - away) * PITCH + target
                     field[at : at + size] += east
-    for c in range(NC):
-        for away in range(1, RIM + 1):
-            north = field[pl.ds(c * CORE + CY - 1 + away, CX, stride=PITCH)]
-            south = field[pl.ds(c * CORE + PITCH - away, CX, stride=PITCH)]
-            at = (c * RIM + away - 1) * CX
-            out_a[at : at + CX] = jnp.where(even, north, south)
-            out_b[at : at + CX] = jnp.where(even, south, north)
+    at = 0
+    for c in range(NC):
+        for away, start, extra in WIDE:
+            if extra:
+                first = c * WIDE_ROWS + start
+                south = x_sides(x_a, x_b, pl.ds(first, extra))
+                north = x_sides(x_a, x_b, pl.ds(first + extra + CY, extra))
+                for side in range(2):
+                    out_a[at : at + extra] = jnp.where(even, north[side], south[side])
+                    out_b[at : at + extra] = jnp.where(even, south[side], north[side])
+                    at += extra
+    for c in range(NC):
         for x in range(CX):
             at = c * CORE + x * PITCH
             here = slice(x * CY, (x + 1) * CY)
@@ -652,27 +668,34 @@
     for c in range(NC):
         sums[pl.ds(c, total, stride=NC)] = tile_sums[:, c * 128 : (c + 1) * 128]
     out_sums[...] = sums[0:rows]
-    out_a[Y_COEF:] = sums[rows : 2 * rows]
+    out_a[CORNERS:] = sums[rows : 2 * rows]
     if merged:
-        out_b[Y_COEF:] = sums[3 * rows : 4 * rows]
+        out_b[CORNERS:] = sums[3 * rows : 4 * rows]
     for s, other in enumerate(out_others):
         other[...] = sums[(2 + s) * rows : (3 + s) * rows]
 
 
-def add_y(alpha, near, sums, y_a, y_b, *rest):
+def add_y(alpha, near, sums, y_a, y_b, small_a, small_b, *rest):
     others = rest[:-2]
     out_delta, out_alpha = rest[-2:]
     out_delta[...] = near[...]
-    for c in range(NC):
-        for away in range(1, RIM + 1):
+    at = 0
+    for c in range(NC):
+        for away, start, extra in WIDE:
             north, south = y_sides(y_a, y_b, pl.ds((c * RIM + away - 1) * CX, CX))
             high = pl.ds(CY - away, CX, stride=CY)
             low = pl.ds(away - 1, CX, stride=CY)
             out_delta[c, high] = out_delta[c, high] + north
             out_delta[c, low] = out_delta[c, low] + south
-    total = sums[...] + y_a[Y_COEF:]
-    if y_b.shape[0] > Y_COEF:
-        total = total + y_b[Y_COEF:]
+            if extra:
+                for x in (away - 1, CX - away):
+                    north, south = y_sides(small_a, small_b, pl.ds(at, extra))
+                    out_delta[c, (x + 1) * CY - extra : (x + 1) * CY] += north
+                    out_delta[c, x * CY : x * CY + extra] += south
+                    at += extra
+    total = sums[...] + small_a[CORNERS:]
+    if small_b.shape[0] > CORNERS:
+        total = total + small_b[CORNERS:]
     for other in others:
         total = total + other[...]
     out_alpha[...] = alpha[...] + profile_weight * total
@@ -818,9 +841,9 @@
         ],
         flops=10000000,
     )
-    (core,) = call(
+    core, rim_a, rim_b = call(
         interior,
-        [(NC * CORE, 128)],
+        [(NC * CORE, 128), (Y_COEF, 128), (Y_COEF, 128)],
         [coef, edge_coef, back_2, back_1, tops, lows, slot_push],
         [pltpu.VMEM((5 * FIELD, 128), f32)]
         + [pltpu.VMEM(big, f32)] * 3
@@ -833,8 +856,8 @@
     back_a, back_b, near, sums, *back = call(
         lambda *refs: add_x(ny, *refs),
         [
-            (Y_COEF + rows, 128),
-            (Y_COEF + (rows if ny == 4 else 0), 128),
+            (CORNERS + rows, 128),
+            (CORNERS + (rows if ny == 4 else 0), 128),
             fine.shape,
             (rows, 128),
         ]
@@ -842,13 +865,15 @@
         [fine, picks, core, x_a, x_b],
         [pltpu.VMEM((NC * CORE, 128), f32), pltpu.VMEM((total * NC, 128), f32)],
     )
-    y_a = swap(back_a, "gy", 1)
-    y_b = ring_b(back_b, "gy")
+    y_a = swap(rim_a, "gy", 1)
+    y_b = pair_b(rim_b, "gy", "gx")
+    small_a = swap(back_a, "gy", 1)
+    small_b = ring_b(back_b, "gy")
     others = [swap(value, "gy", xor) for xor, value in zip(loose, back)]
     grad_delta, grad_alpha = call(
         add_y,
         [fine.shape, control.shape],
-        [control_near, near, sums, y_a, y_b, *others],
+        [control_near, near, sums, y_a, y_b, small_a, small_b, *others],
     )
     return grad_delta.reshape(delta.shape), grad_alpha.reshape(alpha.shape)
 

time: 35.5 us -> 35.3 us (level)
  waiting for transfers between devices: 8.41 us -> 5.63 us
  starting transfers between devices: 15.4 us -> 17.9 us
    ppermute x11 -> x12, waiting for transfers between devices: 8.4 us -> 5.48 us  [swap(): lax.ppermute(block, axis, [(i, i ^ xor) for i in range(lax.axis_size(axis...]
    ppermute x3 -> x4, starting transfers between devices: 2.6 us -> 4.56 us  [pair_b(): return lax.ppermute(block, ('gx', 'gy'), pairs)]
    ppermute x1, starting transfers between devices: 0.59 us -> 1.3 us  [ring_b(): return lax.ppermute(block, axis, pairs)]
    ppermute x11 -> x12, starting transfers between devices: 12.2 us -> 12.1 us  [swap(): lax.ppermute(block, axis, [(i, i ^ xor) for i in range(lax.axis_size(axis...]
  transfers between devices with their start and end apart: 15 -> 17, of which waited for: 5 -> 5; matrix products, arithmetic and copies ran while one was open for 0% -> 0% of each run, Pallas kernels for 16% -> 17%
where the time goes in v15:
time: 35.3 us; the launch traced here: 35.2 us
  starting transfers between devices  17.9 us (51%)
  Pallas kernels  10.9 us (31%)
  waiting for transfers between devices  5.63 us (16%)
  between operations  0.72 us (2%)
    ppermute x12, starting transfers between devices, swap(): lax.ppermute(block, axis, [(i, i ^ xor) for i in range(lax.axis_size(axis...  12.1 us
    pallas_call x8, Pallas kernels, call(): pl.pallas_call(body, out_shape=shapes, in_specs=in_specs or [VMEM] * len(...  10.9 us
    ppermute x12, waiting for transfers between devices, swap(): lax.ppermute(block, axis, [(i, i ^ xor) for i in range(lax.axis_size(axis...  5.48 us
    ppermute x4, starting transfers between devices, pair_b(): return lax.ppermute(block, ('gx', 'gy'), pairs)  4.56 us
    ppermute x1, starting transfers between devices, ring_b(): return lax.ppermute(block, axis, pairs)  1.3 us
  transfers between devices with their start and end apart: 17, of which 5 were waited for; matrix products, arithmetic and copies ran while one was open for 0% of the time, Pallas kernels for 17%

profile of v15, /device:TPU:0, one launch (start us, length us, event | category | flops | bytes accessed | tf_op | source)
XLA Modules:
  0.0 35.2 jit_solution(247315177724068750)
XLA Ops:
  0.6 0.0 copy-start
  0.6 1.4 %shard_map.131 = (f32[320,128]{1,0:T(8,128)S(1)}, f32[304,128]{1,0:T(8,128)S(1)}, f32[4,256,128]{2,1,0:T(8,128)S(1)}, f32[3,256,128]{2,1,0:T(8,128)S(1)}, f32[16...) custom-call(f32[4,256,128]{2,1,0:T(8,128)} %bitcast.16, ...), custom_call_target="tpu_custom_call" | custom-call | flops 1000000 | bytes 944128 | tf_op jit(solution)/shard_map/pallas_call | solution.py:36
  2.1 0.5 %collective-permute-start = (f32[320,128]{1,0:T(8,128)S(1)}, f32[320,128]{1,0:T(8,128)S(1)}, u32[]{:S(2)}, u32[]{:S(2)}) collective-permute-start(f32[320,128]{1,0:T(8,128)S(1)} %get-tuple-element.49), channel_id=1, source_target_pairs={{0,1},{1,0},{2,3},{3,2},{4,5},{5,4},{6,7},{7,6},{8,9},{9,8},{10,11... | collective-permute-start | bytes 491528 | tf_op jit(solution)/shard_map/ppermute | solution.py:48
  2.6 2.6 %collective-permute-start.1 = (f32[304,128]{1,0:T(8,128)S(1)}, f32[304,128]{1,0:T(8,128)S(1)}, u32[]{:S(2)}, u32[]{:S(2)}) collective-permute-start(f32[304,128]{1,0:T(8,128)S(1)} %get-tuple-element.50), channel_id=1, source_target_pairs={{0,4},{1,2},{2,1},{3,7},{4,0},{5,6},{6,5},{7,3},{8,12},{9,10},{10,... | collective-permute-start | bytes 466952 | tf_op jit(solution)/shard_map/ppermute | solution.py:64
  5.2 1.2 %collective-permute-start.3 = (f32[16,128]{1,0:T(8,128)}, f32[16,128]{1,0:T(8,128)S(1)}, u32[]{:S(2)}, u32[]{:S(2)}) collective-permute-start(f32[16,128]{1,0:T(8,128)} %bitcast.22), channel_id=1, source_target_pairs={{0,3},{1,2},{2,1},{3,0},{4,7},{5,6},{6,5},{7,4},{8,11},{9,10},{10,... | collective-permute-start | bytes 24584 | tf_op jit(solution)/shard_map/ppermute | solution.py:48
  6.4 0.5 %collective-permute-start.2 = (f32[16,128]{1,0:T(8,128)}, f32[16,128]{1,0:T(8,128)S(1)}, u32[]{:S(2)}, u32[]{:S(2)}) collective-permute-start(f32[16,128]{1,0:T(8,128)} %bitcast.23), channel_id=1, source_target_pairs={{0,2},{1,3},{2,0},{3,1},{4,6},{5,7},{6,4},{7,5},{8,10},{9,11},{10,... | collective-permute-start | bytes 24584 | tf_op jit(solution)/shard_map/ppermute | solution.py:48
  6.9 1.5 %collective-permute-start.6 = (f32[24,128]{1,0:T(8,128)}, f32[24,128]{1,0:T(8,128)S(1)}, u32[]{:S(2)}, u32[]{:S(2)}) collective-permute-start(f32[24,128]{1,0:T(8,128)} %bitcast.20), channel_id=1, source_target_pairs={{0,4},{4,0},{8,12},{12,8},{16,20},{20,16},{24,28},{28,24},{1,5},{5... | collective-permute-start | bytes 36872 | tf_op jit(solution)/shard_map/ppermute | solution.py:48
  8.4 0.0 copy-done
  8.4 0.3 shard_map.132
  8.7 0.0 collective-permute-done.3.refs_10_.refs_8_
  8.7 1.5 %collective-permute-done.2.refs_9_.refs_7_ = f32[16,128]{1,0:T(8,128)S(1)} collective-permute-done((f32[16,128]{1,0:T(8,128)}, f32[16,128]{1,0:T(8,128)S(1)}, u32[]{:S(2)}, u32[]{:S(2)}) %collective-permute-start.2) | collective-permute-done | bytes 8224 | tf_op jit(solution)/shard_map/ppermute | solution.py:48
  10.3 0.0 collective-permute-done.1.refs_8_.refs_6_
  10.3 0.0 collective-permute-done.refs_7_.refs_5_
  10.3 0.5 %shard_map.134 = (f32[318,128]{1,0:T(8,128)S(1)}, f32[318,128]{1,0:T(8,128)S(1)}) custom-call(f32[4,256,128]{2,1,0:T(8,128)S(1)} %get-tuple-element.42.refs_0_, f32[3,256,128]{2,1,0:T(8,128)S(1)} %get-tuple-element.43.refs_1_, f32[16,128]{1,0:T(8,128)S(1)} %get-tuple-element.41.refs_2_.alpha, f32[16,128]{1,0:T(8,128)S(1)} %get-tuple-element.44.refs_3_, ...), custom_call_target="tpu_custom_call" | custom-call | flops 1000000 | bytes 1277952 | tf_op jit(solution)/shard_map/pallas_call | solution.py:36
  10.8 0.6 %collective-permute-start.4 = (f32[318,128]{1,0:T(8,128)S(1)}, f32[318,128]{1,0:T(8,128)S(1)}, u32[]{:S(2)}, u32[]{:S(2)}) collective-permute-start(f32[318,128]{1,0:T(8,128)S(1)} %get-tuple-element.60), channel_id=1, source_target_pairs={{0,4},{4,0},{8,12},{12,8},{16,20},{20,16},{24,28},{28,24},{1,5},{5... | collective-permute-start | bytes 488456 | tf_op jit(solution)/shard_map/ppermute | solution.py:48
  11.4 0.0 collective-permute-start.5
  11.4 0.0 collective-permute-done.6
  11.4 5.1 %collective-permute-start.9 = (f32[48,128]{1,0:T(8,128)S(1)}, f32[48,128]{1,0:T(8,128)S(1)}, u32[]{:S(2)}, u32[]{:S(2)}) collective-permute-start(f32[48,128]{1,0:T(8,128)S(1)} %constant_dynamic-update-slice_fusion.rest_0_), channel_id=1, source_target_pairs={{0,24},{4,28},{8,16},{12,20},{16,8},{20,12},{24,0},{28,4},{1,25},{... | collective-permute-start | bytes 73736 | tf_op jit(solution)/shard_map/ppermute | solution.py:48
  16.5 0.0 collective-permute-start.8
  16.5 0.6 %collective-permute-start.7 = (f32[48,128]{1,0:T(8,128)S(1)}, f32[48,128]{1,0:T(8,128)S(1)}, u32[]{:S(2)}, u32[]{:S(2)}) collective-permute-start(f32[48,128]{1,0:T(8,128)S(1)} %constant_dynamic-update-slice_fusion.rest_0_), channel_id=1, source_target_pairs={{0,8},{4,12},{8,0},{12,4},{16,24},{20,28},{24,16},{28,20},{1,9},{5... | collective-permute-start | bytes 73736 | tf_op jit(solution)/shard_map/ppermute | solution.py:48
  17.1 2.8 %shard_map.133 = (f32[1536,128]{1,0:T(8,128)S(1)}, f32[1920,128]{1,0:T(8,128)S(1)}, f32[384,16]{1,0:T(8,128)S(1)}, f32[1536,128]{1,0:T(8,128)S(1)}, f32[1536,128]{1,0:T(8,128)S(1)}, /*index=5*/f32[768,128]{1,0:T(8,128)S(1)}) custom-call(f32[4,256,128]{2,1,0:T(8,128)S(1)} %get-tuple-element.42.refs_0_, f32[3,256,128]{2,1,0:T(8,128)S(1)} %get-tuple-element.43.refs_1_, ...), custom_call_target="tpu_custom_call" | custom-call | flops 3000000 | bytes 2064384 | tf_op jit(solution)/shard_map/pallas_call | solution.py:36
  20.0 0.3 collective-permute-done.9.rest_3_
  20.3 0.9 %collective-permute-done.8.rest_2_ = f32[48,128]{1,0:T(8,128)S(1)} collective-permute-done((f32[48,128]{1,0:T(8,128)S(1)}, f32[48,128]{1,0:T(8,128)S(1)}, u32[]{:S(2)}, u32[]{:S(2)}) %collective-permute-start.8) | collective-permute-done | bytes 24608 | tf_op jit(solution)/shard_map/ppermute | solution.py:48
  21.2 0.0 collective-permute-done.7.rest_1_
  21.2 0.0 collective-permute-done.4.x_a
  21.2 0.0 collective-permute-done.5.x_b
  21.2 2.5 %shard_map.135 = (f32[216,128]{1,0:T(8,128)S(1)}, f32[216,128]{1,0:T(8,128)S(1)}, f32[2304,128]{1,0:T(8,128)S(1)}, f32[2304,128]{1,0:T(8,128)S(1)}, f32[2880,128...) custom-call(f32[1536,128]{1,0:T(8,128)S(1)} %get-tuple-element.53.core, ...), custom_call_target="tpu_custom_call" | custom-call | flops 10000000 | bytes 5281792 | tf_op jit(solution)/shard_map/pallas_call | solution.py:36
  23.7 0.6 %collective-permute-start.10 = (f32[216,128]{1,0:T(8,128)S(1)}, f32[216,128]{1,0:T(8,128)S(1)}, u32[]{:S(2)}, u32[]{:S(2)}) collective-permute-start(f32[216,128]{1,0:T(8,128)S(1)} %get-tuple-element.69), channel_id=1, source_target_pairs={{0,4},{4,0},{8,12},{12,8},{16,20},{20,16},{24,28},{28,24},{1,5},{5... | collective-permute-start | bytes 331784 | tf_op jit(solution)/shard_map/ppermute | solution.py:48
  24.3 0.0 collective-permute-start.11
  24.3 2.0 %shard_map.136 = (f32[1536,128]{1,0:T(8,128)S(1)}, f32[192,128]{1,0:T(8,128)S(1)}, f32[192,128]{1,0:T(8,128)S(1)}) custom-call(f32[1920,128]{1,0:T(8,128)S(1)} %get-tuple-element.52.core_coef, f32[2880,128]{1,0:T(8,128)S(1)} %get-tuple-element.63.edge_coef, f32[2304,128]{1,0:T(8,128)S(1)} %get-tuple-element.64.back_2, ...), custom_call_target="tpu_custom_call" | custom-call | flops 10000000 | bytes 8224768 | tf_op jit(solution)/shard_map/pallas_call | solution.py:36
  26.3 0.6 %collective-permute-start.12 = (f32[192,128]{1,0:T(8,128)S(1)}, f32[192,128]{1,0:T(8,128)S(1)}, u32[]{:S(2)}, u32[]{:S(2)}) collective-permute-start(f32[192,128]{1,0:T(8,128)S(1)} %get-tuple-element.73), channel_id=1, source_target_pairs={{0,1},{1,0},{2,3},{3,2},{4,5},{5,4},{6,7},{7,6},{8,9},{9,8},{10,11... | collective-permute-start | bytes 294920 | tf_op jit(solution)/shard_map/ppermute | solution.py:48
  26.9 2.0 %collective-permute-start.13 = (f32[192,128]{1,0:T(8,128)S(1)}, f32[192,128]{1,0:T(8,128)S(1)}, u32[]{:S(2)}, u32[]{:S(2)}) collective-permute-start(f32[192,128]{1,0:T(8,128)S(1)} %get-tuple-element.74), channel_id=1, source_target_pairs={{0,4},{1,2},{2,1},{3,7},{4,0},{5,6},{6,5},{7,3},{8,12},{9,10},{10,... | collective-permute-start | bytes 294920 | tf_op jit(solution)/shard_map/ppermute | solution.py:64
  28.9 0.0 collective-permute-done.10.refs_3_
  28.9 0.0 collective-permute-done.11.refs_4_
  28.9 0.4 %shard_map.137 = (f32[40,128]{1,0:T(8,128)S(1)}, f32[40,128]{1,0:T(8,128)S(1)}, f32[4,256,128]{2,1,0:T(8,128)S(1)}, f32[16,128]{1,0:T(8,128)S(1)}, f32[16,128]{1,0:T(8,128)S(1)}) custom-call(f32[4,256,128]{2,1,0:T(8,128)S(1)} %get-tuple-element.42.refs_0_, f32[384,16]{1,0:T(8,128)S(1)} %get-tuple-element.51.refs_1_, ...), custom_call_target="tpu_custom_call" | custom-call | flops 1000000 | bytes 1556480 | tf_op jit(solution)/shard_map/pallas_call | solution.py:36
  29.2 0.0 collective-permute-start.14
  29.2 1.3 %collective-permute-start.15 = (f32[40,128]{1,0:T(8,128)S(1)}, f32[40,128]{1,0:T(8,128)S(1)}, u32[]{:S(2)}, u32[]{:S(2)}) collective-permute-start(f32[40,128]{1,0:T(8,128)S(1)} %get-tuple-element.76), channel_id=1, source_target_pairs={{0,3},{1,2},{2,1},{3,0},{4,7},{5,6},{6,5},{7,4},{8,11},{9,10},{10,... | collective-permute-start | bytes 61448 | tf_op jit(solution)/shard_map/ppermute | solution.py:70
  30.6 0.8 %collective-permute-start.16 = (f32[16,128]{1,0:T(8,128)S(1)}, f32[16,128]{1,0:T(8,128)S(1)}, u32[]{:S(2)}, u32[]{:S(2)}) collective-permute-start(f32[16,128]{1,0:T(8,128)S(1)} %get-tuple-element.77), channel_id=1, source_target_pairs={{0,2},{1,3},{2,0},{3,1},{4,6},{5,7},{6,4},{7,5},{8,10},{9,11},{10,... | collective-permute-start | bytes 24584 | tf_op jit(solution)/shard_map/ppermute | solution.py:48
  31.4 0.0 collective-permute-done.12.y_a
  31.4 0.1 collective-permute-done.13.y_b
  31.5 2.7 %collective-permute-done.16.rest_0_ = f32[16,128]{1,0:T(8,128)S(1)} collective-permute-done((f32[16,128]{1,0:T(8,128)S(1)}, f32[16,128]{1,0:T(8,128)S(1)}, u32[]{:S(2)}, u32[]{:S(2)}) %collective-permute-start.16) | collective-permute-done | bytes 8224 | tf_op jit(solution)/shard_map/ppermute | solution.py:48
  34.2 0.0 collective-permute-done.14.small_a
  34.2 0.0 collective-permute-done.15.small_b
  34.2 1.0 %shard_map.138 = (f32[4,256,128]{2,1,0:T(8,128)}, f32[16,128]{1,0:T(8,128)}) custom-call(f32[16,128]{1,0:T(8,128)S(1)} %get-tuple-element.41.refs_2_.alpha, f32[4,256,128]{2,1,0:T(8,128)S(1)} %get-tuple-element.71.near, f32[16,128]{1,0:T(8,128)S(1)} %get-tuple-element.72.sums, f32[192,128]{1,0:T(8,128)S(1)} %collective-permute-done.12.y_a, ...), custom_call_target="tpu_custom_call" | custom-call | flops 1000000 | bytes 786432 | tf_op jit(solution)/shard_map/pallas_call | solution.py:36
  (2 shorter events, 0.0 us)
Async XLA Ops:
  0.6 7.8 %copy-start = (f32[1,1,256,4,128]{4,3,2,1,0:T(4,128)S(1)}, f32[1,1,256,4,128]{4,3,2,1,0:T(4,128)}, u32[]{:S(2)}) copy-start(f32[1,1,256,4,128]{4,3,2,1,0:T(4,128)} %param.22) | copy-start | bytes 1572868
  2.1 8.2 %collective-permute-start = (f32[320,128]{1,0:T(8,128)S(1)}, f32[320,128]{1,0:T(8,128)S(1)}, u32[]{:S(2)}, u32[]{:S(2)}) collective-permute-start(f32[320,128]{1,0:T(8,128)S(1)} %get-tuple-element.49), channel_id=1, source_target_pairs={{0,1},{1,0},{2,3},{3,2},{4,5},{5,4},{6,7},{7,6},{8,9},{9,8},{10,11... | collective-permute-start | bytes 491528 | tf_op jit(solution)/shard_map/ppermute | solution.py:48
  2.6 7.7 %collective-permute-start.1 = (f32[304,128]{1,0:T(8,128)S(1)}, f32[304,128]{1,0:T(8,128)S(1)}, u32[]{:S(2)}, u32[]{:S(2)}) collective-permute-start(f32[304,128]{1,0:T(8,128)S(1)} %get-tuple-element.50), channel_id=1, source_target_pairs={{0,4},{1,2},{2,1},{3,7},{4,0},{5,6},{6,5},{7,3},{8,12},{9,10},{10,... | collective-permute-start | bytes 466952 | tf_op jit(solution)/shard_map/ppermute | solution.py:64
  5.2 3.6 %collective-permute-start.3 = (f32[16,128]{1,0:T(8,128)}, f32[16,128]{1,0:T(8,128)S(1)}, u32[]{:S(2)}, u32[]{:S(2)}) collective-permute-start(f32[16,128]{1,0:T(8,128)} %bitcast.22), channel_id=1, source_target_pairs={{0,3},{1,2},{2,1},{3,0},{4,7},{5,6},{6,5},{7,4},{8,11},{9,10},{10,... | collective-permute-start | bytes 24584 | tf_op jit(solution)/shard_map/ppermute | solution.py:48
  6.4 3.9 %collective-permute-start.2 = (f32[16,128]{1,0:T(8,128)}, f32[16,128]{1,0:T(8,128)S(1)}, u32[]{:S(2)}, u32[]{:S(2)}) collective-permute-start(f32[16,128]{1,0:T(8,128)} %bitcast.23), channel_id=1, source_target_pairs={{0,2},{1,3},{2,0},{3,1},{4,6},{5,7},{6,4},{7,5},{8,10},{9,11},{10,... | collective-permute-start | bytes 24584 | tf_op jit(solution)/shard_map/ppermute | solution.py:48
  6.9 4.5 %collective-permute-start.6 = (f32[24,128]{1,0:T(8,128)}, f32[24,128]{1,0:T(8,128)S(1)}, u32[]{:S(2)}, u32[]{:S(2)}) collective-permute-start(f32[24,128]{1,0:T(8,128)} %bitcast.20), channel_id=1, source_target_pairs={{0,4},{4,0},{8,12},{12,8},{16,20},{20,16},{24,28},{28,24},{1,5},{5... | collective-permute-start | bytes 36872 | tf_op jit(solution)/shard_map/ppermute | solution.py:48
  10.8 10.4 %collective-permute-start.4 = (f32[318,128]{1,0:T(8,128)S(1)}, f32[318,128]{1,0:T(8,128)S(1)}, u32[]{:S(2)}, u32[]{:S(2)}) collective-permute-start(f32[318,128]{1,0:T(8,128)S(1)} %get-tuple-element.60), channel_id=1, source_target_pairs={{0,4},{4,0},{8,12},{12,8},{16,20},{20,16},{24,28},{28,24},{1,5},{5... | collective-permute-start | bytes 488456 | tf_op jit(solution)/shard_map/ppermute | solution.py:48
  11.4 9.8 %collective-permute-start.5 = (f32[318,128]{1,0:T(8,128)S(1)}, f32[318,128]{1,0:T(8,128)S(1)}, u32[]{:S(2)}, u32[]{:S(2)}) collective-permute-start(f32[318,128]{1,0:T(8,128)S(1)} %get-tuple-element.61), channel_id=1, source_target_pairs={{0,1},{4,8},{8,4},{12,16},{16,12},{20,24},{24,20},{28,29},{1,0},{5... | collective-permute-start | bytes 488456 | tf_op jit(solution)/shard_map/ppermute | solution.py:64
  11.4 8.9 %collective-permute-start.9 = (f32[48,128]{1,0:T(8,128)S(1)}, f32[48,128]{1,0:T(8,128)S(1)}, u32[]{:S(2)}, u32[]{:S(2)}) collective-permute-start(f32[48,128]{1,0:T(8,128)S(1)} %constant_dynamic-update-slice_fusion.rest_0_), channel_id=1, source_target_pairs={{0,24},{4,28},{8,16},{12,20},{16,8},{20,12},{24,0},{28,4},{1,25},{... | collective-permute-start | bytes 73736 | tf_op jit(solution)/shard_map/ppermute | solution.py:48
  16.5 4.7 %collective-permute-start.8 = (f32[48,128]{1,0:T(8,128)S(1)}, f32[48,128]{1,0:T(8,128)S(1)}, u32[]{:S(2)}, u32[]{:S(2)}) collective-permute-start(f32[48,128]{1,0:T(8,128)S(1)} %constant_dynamic-update-slice_fusion.rest_0_), channel_id=1, source_target_pairs={{0,16},{4,20},{8,24},{12,28},{16,0},{20,4},{24,8},{28,12},{1,17},{... | collective-permute-start | bytes 73736 | tf_op jit(solution)/shard_map/ppermute | solution.py:48
  16.5 4.7 %collective-permute-start.7 = (f32[48,128]{1,0:T(8,128)S(1)}, f32[48,128]{1,0:T(8,128)S(1)}, u32[]{:S(2)}, u32[]{:S(2)}) collective-permute-start(f32[48,128]{1,0:T(8,128)S(1)} %constant_dynamic-update-slice_fusion.rest_0_), channel_id=1, source_target_pairs={{0,8},{4,12},{8,0},{12,4},{16,24},{20,28},{24,16},{28,20},{1,9},{5... | collective-permute-start | bytes 73736 | tf_op jit(solution)/shard_map/ppermute | solution.py:48
  23.7 5.2 %collective-permute-start.10 = (f32[216,128]{1,0:T(8,128)S(1)}, f32[216,128]{1,0:T(8,128)S(1)}, u32[]{:S(2)}, u32[]{:S(2)}) collective-permute-start(f32[216,128]{1,0:T(8,128)S(1)} %get-tuple-element.69), channel_id=1, source_target_pairs={{0,4},{4,0},{8,12},{12,8},{16,20},{20,16},{24,28},{28,24},{1,5},{5... | collective-permute-start | bytes 331784 | tf_op jit(solution)/shard_map/ppermute | solution.py:48
  24.3 4.5 %collective-permute-start.11 = (f32[216,128]{1,0:T(8,128)S(1)}, f32[216,128]{1,0:T(8,128)S(1)}, u32[]{:S(2)}, u32[]{:S(2)}) collective-permute-start(f32[216,128]{1,0:T(8,128)S(1)} %get-tuple-element.70), channel_id=1, source_target_pairs={{0,1},{4,8},{8,4},{12,16},{16,12},{20,24},{24,20},{28,29},{1,0},{5... | collective-permute-start | bytes 331784 | tf_op jit(solution)/shard_map/ppermute | solution.py:64
  26.3 5.1 %collective-permute-start.12 = (f32[192,128]{1,0:T(8,128)S(1)}, f32[192,128]{1,0:T(8,128)S(1)}, u32[]{:S(2)}, u32[]{:S(2)}) collective-permute-start(f32[192,128]{1,0:T(8,128)S(1)} %get-tuple-element.73), channel_id=1, source_target_pairs={{0,1},{1,0},{2,3},{3,2},{4,5},{5,4},{6,7},{7,6},{8,9},{9,8},{10,11... | collective-permute-start | bytes 294920 | tf_op jit(solution)/shard_map/ppermute | solution.py:48
  26.9 4.6 %collective-permute-start.13 = (f32[192,128]{1,0:T(8,128)S(1)}, f32[192,128]{1,0:T(8,128)S(1)}, u32[]{:S(2)}, u32[]{:S(2)}) collective-permute-start(f32[192,128]{1,0:T(8,128)S(1)} %get-tuple-element.74), channel_id=1, source_target_pairs={{0,4},{1,2},{2,1},{3,7},{4,0},{5,6},{6,5},{7,3},{8,12},{9,10},{10,... | collective-permute-start | bytes 294920 | tf_op jit(solution)/shard_map/ppermute | solution.py:64
  29.2 5.0 %collective-permute-start.14 = (f32[40,128]{1,0:T(8,128)S(1)}, f32[40,128]{1,0:T(8,128)S(1)}, u32[]{:S(2)}, u32[]{:S(2)}) collective-permute-start(f32[40,128]{1,0:T(8,128)S(1)} %get-tuple-element.75), channel_id=1, source_target_pairs={{0,1},{1,0},{2,3},{3,2},{4,5},{5,4},{6,7},{7,6},{8,9},{9,8},{10,11... | collective-permute-start | bytes 61448 | tf_op jit(solution)/shard_map/ppermute | solution.py:48
  29.2 5.0 %collective-permute-start.15 = (f32[40,128]{1,0:T(8,128)S(1)}, f32[40,128]{1,0:T(8,128)S(1)}, u32[]{:S(2)}, u32[]{:S(2)}) collective-permute-start(f32[40,128]{1,0:T(8,128)S(1)} %get-tuple-element.76), channel_id=1, source_target_pairs={{0,3},{1,2},{2,1},{3,0},{4,7},{5,6},{6,5},{7,4},{8,11},{9,10},{10,... | collective-permute-start | bytes 61448 | tf_op jit(solution)/shard_map/ppermute | solution.py:70
  30.6 3.7 %collective-permute-start.16 = (f32[16,128]{1,0:T(8,128)S(1)}, f32[16,128]{1,0:T(8,128)S(1)}, u32[]{:S(2)}, u32[]{:S(2)}) collective-permute-start(f32[16,128]{1,0:T(8,128)S(1)} %get-tuple-element.77), channel_id=1, source_target_pairs={{0,2},{1,3},{2,0},{3,1},{4,6},{5,7},{6,4},{7,5},{8,10},{9,11},{10,... | collective-permute-start | bytes 24584 | tf_op jit(solution)/shard_map/ppermute | solution.py:48

commit v16 on v15

--- a/solution.py
+++ b/solution.py
@@ -355,7 +355,7 @@
                 target[pl.ds(base, PITCH)] = forward_column(source, base, k)
             return carry
 
-        lax.fori_loop(step + 1, CX - 1 - step, body, 0)
+        lax.fori_loop(step + 1, CX - 1 - step, body, 0, unroll=2)
         own = []
         for c in range(NC):
             pieces = [jnp.zeros(((step + 1) * CY, 128), f32)]
@@ -417,18 +417,17 @@
     tally,
     wide,
     edge_pick,
-    slot_push,
-    beam_pick,
-    columns,
     x_a,
     x_b,
-    *rest,
+    coef,
+    totals,
+    state_0,
+    state_1,
+    state_2,
+    state_3,
+    raw,
 ):
-    beams = rest[:-13]
-    out_a, out_b, back_2, back_1, coef, tops, lows = rest[-13:-6]
-    state_0, state_1, state_2, state_3, raw, forcing = rest[-6:]
-    even, _, _ = place_on("gx")
-    slots = columns.shape[0]
+    slots = wide.shape[0]
 
     def fill(ref, base, x_base, found):
         for away, start, extra in found:
@@ -470,12 +469,8 @@
         for f, value in enumerate(combine_coefs(*[raw[rows[f]] for f in range(3)])):
             coef[rows[f]] = value
 
-    gate_lane = lax.broadcasted_iota(jnp.int32, (slots, 128), 1).astype(f32)
-    gate_here = gate_lane == columns[:, 2:3]
-    scaled = columns[:, 3:4]
     outer = [*range(RIM), *range(CX - RIM, CX)]
     half = RIM * CY
-    push = jnp.concatenate([slot_push[0:half], slot_push[CX * CY - half :]], axis=0)
     states = [state_0, state_1, state_2, state_3]
     for step in range(STEPS):
         source, target = states[step], states[step + 1]
@@ -500,6 +495,25 @@
             edge_pick[...], jnp.concatenate(parts, axis=1), preferred_element_type=f32
         )
         seen = seen * wide[...]
+        rows = slice(step * slots, (step + 1) * slots)
+        total = tally[rows]
+        for c in range(NC):
+            total = total + seen[:, c * 128 : (c + 1) * 128]
+        totals[rows] = total
+
+
+def push_edges(coef, totals, wide, slot_push, beam_pick, columns, *rest):
+    beams = rest[:-9]
+    out_a, out_b, back_2, back_1, tops, lows, state_0, state_3, forcing = rest[-9:]
+    even, _, _ = place_on("gx")
+    slots = columns.shape[0]
+    gate_lane = lax.broadcasted_iota(jnp.int32, (slots, 128), 1).astype(f32)
+    gate_here = gate_lane == columns[:, 2:3]
+    scaled = columns[:, 3:4]
+    outer = [*range(RIM), *range(CX - RIM, CX)]
+    half = RIM * CY
+    push = jnp.concatenate([slot_push[0:half], slot_push[CX * CY - half :]], axis=0)
+    for step in range(STEPS):
         table = []
         for part in beams:
             for at in range(0, part.shape[0], STEPS * OWN_BEAMS):
@@ -507,9 +521,7 @@
                 table.append(part[first : first + OWN_BEAMS])
         table = two_part_dot(beam_pick[...], jnp.concatenate(table, axis=0))
         rows = slice(step * slots, (step + 1) * slots)
-        total = tally[rows] - jnp.where(gate_here, table, 0.0)
-        for c in range(NC):
-            total = total + seen[:, c * 128 : (c + 1) * 128]
+        total = totals[rows] - jnp.where(gate_here, table, 0.0)
         misfit = scaled * jnp.sum(total, axis=1, keepdims=True)
         top, low = split(misfit * wide[...])
         tops[rows] = top
@@ -599,7 +611,7 @@
                     target[pl.ds(c * FIELD + at, PITCH)] = value
             return carry
 
-        lax.fori_loop(low, high, body, 0)
+        lax.fori_loop(low, high, body, 0, unroll=2)
 
     def copy(source, target, columns):
         for c in range(NC):
@@ -808,35 +820,27 @@
         ],
         flops=3000000,
     )
-    back_a, back_b, back_2, back_1, edge_coef, tops, lows = call(
+    edge_coef, totals = call(
         edges,
+        [(5 * FIELD, 128), (STEPS * slots, 128)],
+        [core, coef, state_1, state_2, tally, wide, edge_pick, x_a, x_b],
+        [pltpu.VMEM(big, f32)] * 4 + [pltpu.VMEM((3 * FIELD, 128), f32)],
+        flops=10000000,
+    )
+    back_a, back_b, back_2, back_1, tops, lows = call(
+        push_edges,
         [
             (X_COEF, 128),
             (X_COEF, 128),
             big,
             big,
-            (5 * FIELD, 128),
             jax.ShapeDtypeStruct((STEPS * slots, NC * 128), bf16),
             jax.ShapeDtypeStruct((STEPS * slots, NC * 128), bf16),
         ],
+        [edge_coef, totals, wide, slot_push, beam_pick, columns, *beams],
         [
-            core,
-            coef,
-            state_1,
-            state_2,
-            tally,
-            wide,
-            edge_pick,
-            slot_push,
-            beam_pick,
-            columns,
-            x_a,
-            x_b,
-            *beams,
-        ],
-        [pltpu.VMEM(big, f32)] * 4
-        + [
-            pltpu.VMEM((3 * FIELD, 128), f32),
+            pltpu.VMEM(big, f32),
+            pltpu.VMEM(big, f32),
             pltpu.VMEM((STEPS * 2 * RIM * CY, NC * 128), f32),
         ],
         flops=10000000,

time: 35.3 us -> 34.6 us (0.980)
  waiting for transfers between devices: 5.63 us -> 4.85 us
  Pallas kernels: 10.9 us -> 10.4 us
  starting transfers between devices: 17.9 us -> 18.4 us
    ppermute x12, waiting for transfers between devices: 5.48 us -> 4.51 us  [swap(): lax.ppermute(block, axis, [(i, i ^ xor) for i in range(lax.axis_size(axis...]
    ppermute x12, starting transfers between devices: 12.1 us -> 12.8 us  [swap(): lax.ppermute(block, axis, [(i, i ^ xor) for i in range(lax.axis_size(axis...]
    pallas_call x8 -> x9, Pallas kernels: 10.9 us -> 10.4 us  [call(): pl.pallas_call(body, out_shape=shapes, in_specs=in_specs or [VMEM] * len(...]
  transfers between devices with their start and end apart: 17 -> 17, of which waited for: 5 -> 4; matrix products, arithmetic and copies ran while one was open for 0% -> 0% of each run, Pallas kernels for 17% -> 19%
where the time goes in v16:
time: 34.6 us; the launch traced here: 34.4 us
  starting transfers between devices  18.4 us (53%)
  Pallas kernels  10.4 us (30%)
  waiting for transfers between devices  4.85 us (14%)
  between operations  0.75 us (2%)
    ppermute x12, starting transfers between devices, swap(): lax.ppermute(block, axis, [(i, i ^ xor) for i in range(lax.axis_size(axis...  12.8 us
    pallas_call x9, Pallas kernels, call(): pl.pallas_call(body, out_shape=shapes, in_specs=in_specs or [VMEM] * len(...  10.4 us
    ppermute x12, waiting for transfers between devices, swap(): lax.ppermute(block, axis, [(i, i ^ xor) for i in range(lax.axis_size(axis...  4.51 us
    ppermute x4, starting transfers between devices, pair_b(): return lax.ppermute(block, ('gx', 'gy'), pairs)  4.35 us
    ppermute x1, starting transfers between devices, ring_b(): return lax.ppermute(block, axis, pairs)  1.25 us
  transfers between devices with their start and end apart: 17, of which 4 were waited for; matrix products, arithmetic and copies ran while one was open for 0% of the time, Pallas kernels for 19%

profile of v16, /device:TPU:0, one launch (start us, length us, event | category | flops | bytes accessed | tf_op | source)
XLA Modules:
  0.0 34.4 jit_solution(1095542601175934582)
XLA Ops:
  0.6 0.0 copy-start
  0.6 1.4 %shard_map.131 = (f32[320,128]{1,0:T(8,128)S(1)}, f32[304,128]{1,0:T(8,128)S(1)}, f32[4,256,128]{2,1,0:T(8,128)S(1)}, f32[3,256,128]{2,1,0:T(8,128)S(1)}, f32[16...) custom-call(f32[4,256,128]{2,1,0:T(8,128)} %bitcast.16, ...), custom_call_target="tpu_custom_call" | custom-call | flops 1000000 | bytes 944128 | tf_op jit(solution)/shard_map/pallas_call | solution.py:36
  2.1 0.5 %collective-permute-start = (f32[320,128]{1,0:T(8,128)S(1)}, f32[320,128]{1,0:T(8,128)S(1)}, u32[]{:S(2)}, u32[]{:S(2)}) collective-permute-start(f32[320,128]{1,0:T(8,128)S(1)} %get-tuple-element.50), channel_id=1, source_target_pairs={{0,1},{1,0},{2,3},{3,2},{4,5},{5,4},{6,7},{7,6},{8,9},{9,8},{10,11... | collective-permute-start | bytes 491528 | tf_op jit(solution)/shard_map/ppermute | solution.py:48
  2.6 2.6 %collective-permute-start.1 = (f32[304,128]{1,0:T(8,128)S(1)}, f32[304,128]{1,0:T(8,128)S(1)}, u32[]{:S(2)}, u32[]{:S(2)}) collective-permute-start(f32[304,128]{1,0:T(8,128)S(1)} %get-tuple-element.51), channel_id=1, source_target_pairs={{0,4},{1,2},{2,1},{3,7},{4,0},{5,6},{6,5},{7,3},{8,12},{9,10},{10,... | collective-permute-start | bytes 466952 | tf_op jit(solution)/shard_map/ppermute | solution.py:64
  5.2 1.2 %collective-permute-start.3 = (f32[16,128]{1,0:T(8,128)}, f32[16,128]{1,0:T(8,128)S(1)}, u32[]{:S(2)}, u32[]{:S(2)}) collective-permute-start(f32[16,128]{1,0:T(8,128)} %bitcast.22), channel_id=1, source_target_pairs={{0,3},{1,2},{2,1},{3,0},{4,7},{5,6},{6,5},{7,4},{8,11},{9,10},{10,... | collective-permute-start | bytes 24584 | tf_op jit(solution)/shard_map/ppermute | solution.py:48
  6.4 0.5 %collective-permute-start.2 = (f32[16,128]{1,0:T(8,128)}, f32[16,128]{1,0:T(8,128)S(1)}, u32[]{:S(2)}, u32[]{:S(2)}) collective-permute-start(f32[16,128]{1,0:T(8,128)} %bitcast.23), channel_id=1, source_target_pairs={{0,2},{1,3},{2,0},{3,1},{4,6},{5,7},{6,4},{7,5},{8,10},{9,11},{10,... | collective-permute-start | bytes 24584 | tf_op jit(solution)/shard_map/ppermute | solution.py:48
  6.9 1.5 %collective-permute-start.6 = (f32[24,128]{1,0:T(8,128)}, f32[24,128]{1,0:T(8,128)S(1)}, u32[]{:S(2)}, u32[]{:S(2)}) collective-permute-start(f32[24,128]{1,0:T(8,128)} %bitcast.20), channel_id=1, source_target_pairs={{0,4},{4,0},{8,12},{12,8},{16,20},{20,16},{24,28},{28,24},{1,5},{5... | collective-permute-start | bytes 36872 | tf_op jit(solution)/shard_map/ppermute | solution.py:48
  8.4 0.0 copy-done
  8.4 0.3 shard_map.132
  8.7 0.0 collective-permute-done.3.refs_10_.refs_8_
  8.7 1.5 %collective-permute-done.2.refs_9_.refs_7_ = f32[16,128]{1,0:T(8,128)S(1)} collective-permute-done((f32[16,128]{1,0:T(8,128)}, f32[16,128]{1,0:T(8,128)S(1)}, u32[]{:S(2)}, u32[]{:S(2)}) %collective-permute-start.2) | collective-permute-done | bytes 8224 | tf_op jit(solution)/shard_map/ppermute | solution.py:48
  10.3 0.0 collective-permute-done.1.refs_8_.refs_6_
  10.3 0.0 collective-permute-done.refs_7_.refs_5_
  10.3 0.5 %shard_map.134 = (f32[318,128]{1,0:T(8,128)S(1)}, f32[318,128]{1,0:T(8,128)S(1)}) custom-call(f32[4,256,128]{2,1,0:T(8,128)S(1)} %get-tuple-element.43.refs_0_, f32[3,256,128]{2,1,0:T(8,128)S(1)} %get-tuple-element.44.refs_1_, f32[16,128]{1,0:T(8,128)S(1)} %get-tuple-element.42.refs_2_.alpha, f32[16,128]{1,0:T(8,128)S(1)} %get-tuple-element.45.refs_3_, ...), custom_call_target="tpu_custom_call" | custom-call | flops 1000000 | bytes 1277952 | tf_op jit(solution)/shard_map/pallas_call | solution.py:36
  10.8 0.6 %collective-permute-start.4 = (f32[318,128]{1,0:T(8,128)S(1)}, f32[318,128]{1,0:T(8,128)S(1)}, u32[]{:S(2)}, u32[]{:S(2)}) collective-permute-start(f32[318,128]{1,0:T(8,128)S(1)} %get-tuple-element.59), channel_id=1, source_target_pairs={{0,4},{4,0},{8,12},{12,8},{16,20},{20,16},{24,28},{28,24},{1,5},{5... | collective-permute-start | bytes 488456 | tf_op jit(solution)/shard_map/ppermute | solution.py:48
  11.4 0.0 collective-permute-start.5
  11.4 0.0 collective-permute-done.6
  11.4 5.1 %collective-permute-start.9 = (f32[48,128]{1,0:T(8,128)S(1)}, f32[48,128]{1,0:T(8,128)S(1)}, u32[]{:S(2)}, u32[]{:S(2)}) collective-permute-start(f32[48,128]{1,0:T(8,128)S(1)} %constant_dynamic-update-slice_fusion.rest_0_), channel_id=1, source_target_pairs={{0,24},{4,28},{8,16},{12,20},{16,8},{20,12},{24,0},{28,4},{1,25},{... | collective-permute-start | bytes 73736 | tf_op jit(solution)/shard_map/ppermute | solution.py:48
  16.5 0.0 collective-permute-start.8
  16.5 0.6 %collective-permute-start.7 = (f32[48,128]{1,0:T(8,128)S(1)}, f32[48,128]{1,0:T(8,128)S(1)}, u32[]{:S(2)}, u32[]{:S(2)}) collective-permute-start(f32[48,128]{1,0:T(8,128)S(1)} %constant_dynamic-update-slice_fusion.rest_0_), channel_id=1, source_target_pairs={{0,8},{4,12},{8,0},{12,4},{16,24},{20,28},{24,16},{28,20},{1,9},{5... | collective-permute-start | bytes 73736 | tf_op jit(solution)/shard_map/ppermute | solution.py:48
  17.1 2.7 %shard_map.133 = (f32[1536,128]{1,0:T(8,128)S(1)}, f32[1920,128]{1,0:T(8,128)S(1)}, f32[384,16]{1,0:T(8,128)S(1)}, f32[1536,128]{1,0:T(8,128)S(1)}, f32[1536,128]{1,0:T(8,128)S(1)}, /*index=5*/f32[768,128]{1,0:T(8,128)S(1)}) custom-call(f32[4,256,128]{2,1,0:T(8,128)S(1)} %get-tuple-element.43.refs_0_, f32[3,256,128]{2,1,0:T(8,128)S(1)} %get-tuple-element.44.refs_1_, ...), custom_call_target="tpu_custom_call" | custom-call | flops 3000000 | bytes 2064384 | tf_op jit(solution)/shard_map/pallas_call | solution.py:36
  19.8 0.0 collective-permute-done.4.x_a
  19.8 0.0 collective-permute-done.5.x_b
  19.9 0.8 %shard_map.135 = (f32[2880,128]{1,0:T(8,128)S(1)}, f32[768,128]{1,0:T(8,128)S(1)}) custom-call(f32[1536,128]{1,0:T(8,128)S(1)} %get-tuple-element.54.core, f32[1920,128]{1,0:T(8,128)S(1)} %get-tuple-element.53.core_coef, f32[1536,128]{1,0:T(8,128)S(1)} %get-tuple-element.55.near_1, f32[1536,128]{1,0:T(8,128)S(1)} %get-tuple-element.56.near_2, ...), custom_call_target="tpu_custom_call" | custom-call | flops 10000000 | bytes 4847616 | tf_op jit(solution)/shard_map/pallas_call | solution.py:36
  20.7 0.0 collective-permute-done.9.rest_3_
  20.7 0.5 %collective-permute-done.8.rest_2_ = f32[48,128]{1,0:T(8,128)S(1)} collective-permute-done((f32[48,128]{1,0:T(8,128)S(1)}, f32[48,128]{1,0:T(8,128)S(1)}, u32[]{:S(2)}, u32[]{:S(2)}) %collective-permute-start.8) | collective-permute-done | bytes 24608 | tf_op jit(solution)/shard_map/ppermute | solution.py:48
  21.2 0.0 collective-permute-done.7.rest_1_
  21.2 1.4 %shard_map.136 = (f32[216,128]{1,0:T(8,128)S(1)}, f32[216,128]{1,0:T(8,128)S(1)}, f32[2304,128]{1,0:T(8,128)S(1)}, f32[2304,128]{1,0:T(8,128)S(1)}, bf16[768,512...) custom-call(f32[2880,128]{1,0:T(8,128)S(1)} %get-tuple-element.61.coef.edge_coef, ...), custom_call_target="tpu_custom_call" | custom-call | flops 10000000 | bytes 2826240 | tf_op jit(solution)/shard_map/pallas_call | solution.py:36
  22.6 1.3 %collective-permute-start.10 = (f32[216,128]{1,0:T(8,128)S(1)}, f32[216,128]{1,0:T(8,128)S(1)}, u32[]{:S(2)}, u32[]{:S(2)}) collective-permute-start(f32[216,128]{1,0:T(8,128)S(1)} %get-tuple-element.71), channel_id=1, source_target_pairs={{0,4},{4,0},{8,12},{12,8},{16,20},{20,16},{24,28},{28,24},{1,5},{5... | collective-permute-start | bytes 331784 | tf_op jit(solution)/shard_map/ppermute | solution.py:48
  24.0 0.0 collective-permute-start.11
  24.0 1.8 %shard_map.137 = (f32[1536,128]{1,0:T(8,128)S(1)}, f32[192,128]{1,0:T(8,128)S(1)}, f32[192,128]{1,0:T(8,128)S(1)}) custom-call(f32[1920,128]{1,0:T(8,128)S(1)} %get-tuple-element.53.core_coef, f32[2880,128]{1,0:T(8,128)S(1)} %get-tuple-element.61.coef.edge_coef, f32[2304,128]{1,0:T(8,128)S(1)} %get-tuple-element.66.back_2, ...), custom_call_target="tpu_custom_call" | custom-call | flops 10000000 | bytes 8224768 | tf_op jit(solution)/shard_map/pallas_call | solution.py:36
  25.8 0.6 %collective-permute-start.12 = (f32[192,128]{1,0:T(8,128)S(1)}, f32[192,128]{1,0:T(8,128)S(1)}, u32[]{:S(2)}, u32[]{:S(2)}) collective-permute-start(f32[192,128]{1,0:T(8,128)S(1)} %get-tuple-element.75), channel_id=1, source_target_pairs={{0,1},{1,0},{2,3},{3,2},{4,5},{5,4},{6,7},{7,6},{8,9},{9,8},{10,11... | collective-permute-start | bytes 294920 | tf_op jit(solution)/shard_map/ppermute | solution.py:48
  26.4 1.8 %collective-permute-start.13 = (f32[192,128]{1,0:T(8,128)S(1)}, f32[192,128]{1,0:T(8,128)S(1)}, u32[]{:S(2)}, u32[]{:S(2)}) collective-permute-start(f32[192,128]{1,0:T(8,128)S(1)} %get-tuple-element.76), channel_id=1, source_target_pairs={{0,4},{1,2},{2,1},{3,7},{4,0},{5,6},{6,5},{7,3},{8,12},{9,10},{10,... | collective-permute-start | bytes 294920 | tf_op jit(solution)/shard_map/ppermute | solution.py:64
  28.1 0.0 collective-permute-done.10.refs_3_
  28.1 0.0 collective-permute-done.11.refs_4_
  28.2 0.4 %shard_map.138 = (f32[40,128]{1,0:T(8,128)S(1)}, f32[40,128]{1,0:T(8,128)S(1)}, f32[4,256,128]{2,1,0:T(8,128)S(1)}, f32[16,128]{1,0:T(8,128)S(1)}, f32[16,128]{1,0:T(8,128)S(1)}) custom-call(f32[4,256,128]{2,1,0:T(8,128)S(1)} %get-tuple-element.43.refs_0_, f32[384,16]{1,0:T(8,128)S(1)} %get-tuple-element.52.refs_1_, ...), custom_call_target="tpu_custom_call" | custom-call | flops 1000000 | bytes 1556480 | tf_op jit(solution)/shard_map/pallas_call | solution.py:36
  28.5 0.0 collective-permute-start.14
  28.5 1.3 %collective-permute-start.15 = (f32[40,128]{1,0:T(8,128)S(1)}, f32[40,128]{1,0:T(8,128)S(1)}, u32[]{:S(2)}, u32[]{:S(2)}) collective-permute-start(f32[40,128]{1,0:T(8,128)S(1)} %get-tuple-element.78), channel_id=1, source_target_pairs={{0,3},{1,2},{2,1},{3,0},{4,7},{5,6},{6,5},{7,4},{8,11},{9,10},{10,... | collective-permute-start | bytes 61448 | tf_op jit(solution)/shard_map/ppermute | solution.py:70
  29.8 0.9 %collective-permute-start.16 = (f32[16,128]{1,0:T(8,128)S(1)}, f32[16,128]{1,0:T(8,128)S(1)}, u32[]{:S(2)}, u32[]{:S(2)}) collective-permute-start(f32[16,128]{1,0:T(8,128)S(1)} %get-tuple-element.79), channel_id=1, source_target_pairs={{0,2},{1,3},{2,0},{3,1},{4,6},{5,7},{6,4},{7,5},{8,10},{9,11},{10,... | collective-permute-start | bytes 24584 | tf_op jit(solution)/shard_map/ppermute | solution.py:48
  30.7 0.0 collective-permute-done.12.y_a
  30.7 0.3 collective-permute-done.13.y_b
  31.0 2.4 %collective-permute-done.16.rest_0_ = f32[16,128]{1,0:T(8,128)S(1)} collective-permute-done((f32[16,128]{1,0:T(8,128)S(1)}, f32[16,128]{1,0:T(8,128)S(1)}, u32[]{:S(2)}, u32[]{:S(2)}) %collective-permute-start.16) | collective-permute-done | bytes 8224 | tf_op jit(solution)/shard_map/ppermute | solution.py:48
  33.4 0.0 collective-permute-done.14.small_a
  33.4 0.0 collective-permute-done.15.small_b
  33.4 1.0 %shard_map.139 = (f32[4,256,128]{2,1,0:T(8,128)}, f32[16,128]{1,0:T(8,128)}) custom-call(f32[16,128]{1,0:T(8,128)S(1)} %get-tuple-element.42.refs_2_.alpha, f32[4,256,128]{2,1,0:T(8,128)S(1)} %get-tuple-element.73.near, f32[16,128]{1,0:T(8,128)S(1)} %get-tuple-element.74.sums, f32[192,128]{1,0:T(8,128)S(1)} %collective-permute-done.12.y_a, ...), custom_call_target="tpu_custom_call" | custom-call | flops 1000000 | bytes 786432 | tf_op jit(solution)/shard_map/pallas_call | solution.py:36
  (2 shorter events, 0.0 us)
Async XLA Ops:
  0.6 7.8 %copy-start = (f32[1,1,256,4,128]{4,3,2,1,0:T(4,128)S(1)}, f32[1,1,256,4,128]{4,3,2,1,0:T(4,128)}, u32[]{:S(2)}) copy-start(f32[1,1,256,4,128]{4,3,2,1,0:T(4,128)} %param.22) | copy-start | bytes 1572868
  2.1 8.2 %collective-permute-start = (f32[320,128]{1,0:T(8,128)S(1)}, f32[320,128]{1,0:T(8,128)S(1)}, u32[]{:S(2)}, u32[]{:S(2)}) collective-permute-start(f32[320,128]{1,0:T(8,128)S(1)} %get-tuple-element.50), channel_id=1, source_target_pairs={{0,1},{1,0},{2,3},{3,2},{4,5},{5,4},{6,7},{7,6},{8,9},{9,8},{10,11... | collective-permute-start | bytes 491528 | tf_op jit(solution)/shard_map/ppermute | solution.py:48
  2.6 7.7 %collective-permute-start.1 = (f32[304,128]{1,0:T(8,128)S(1)}, f32[304,128]{1,0:T(8,128)S(1)}, u32[]{:S(2)}, u32[]{:S(2)}) collective-permute-start(f32[304,128]{1,0:T(8,128)S(1)} %get-tuple-element.51), channel_id=1, source_target_pairs={{0,4},{1,2},{2,1},{3,7},{4,0},{5,6},{6,5},{7,3},{8,12},{9,10},{10,... | collective-permute-start | bytes 466952 | tf_op jit(solution)/shard_map/ppermute | solution.py:64
  5.2 3.6 %collective-permute-start.3 = (f32[16,128]{1,0:T(8,128)}, f32[16,128]{1,0:T(8,128)S(1)}, u32[]{:S(2)}, u32[]{:S(2)}) collective-permute-start(f32[16,128]{1,0:T(8,128)} %bitcast.22), channel_id=1, source_target_pairs={{0,3},{1,2},{2,1},{3,0},{4,7},{5,6},{6,5},{7,4},{8,11},{9,10},{10,... | collective-permute-start | bytes 24584 | tf_op jit(solution)/shard_map/ppermute | solution.py:48
  6.4 3.9 %collective-permute-start.2 = (f32[16,128]{1,0:T(8,128)}, f32[16,128]{1,0:T(8,128)S(1)}, u32[]{:S(2)}, u32[]{:S(2)}) collective-permute-start(f32[16,128]{1,0:T(8,128)} %bitcast.23), channel_id=1, source_target_pairs={{0,2},{1,3},{2,0},{3,1},{4,6},{5,7},{6,4},{7,5},{8,10},{9,11},{10,... | collective-permute-start | bytes 24584 | tf_op jit(solution)/shard_map/ppermute | solution.py:48
  6.9 4.5 %collective-permute-start.6 = (f32[24,128]{1,0:T(8,128)}, f32[24,128]{1,0:T(8,128)S(1)}, u32[]{:S(2)}, u32[]{:S(2)}) collective-permute-start(f32[24,128]{1,0:T(8,128)} %bitcast.20), channel_id=1, source_target_pairs={{0,4},{4,0},{8,12},{12,8},{16,20},{20,16},{24,28},{28,24},{1,5},{5... | collective-permute-start | bytes 36872 | tf_op jit(solution)/shard_map/ppermute | solution.py:48
  10.8 9.0 %collective-permute-start.4 = (f32[318,128]{1,0:T(8,128)S(1)}, f32[318,128]{1,0:T(8,128)S(1)}, u32[]{:S(2)}, u32[]{:S(2)}) collective-permute-start(f32[318,128]{1,0:T(8,128)S(1)} %get-tuple-element.59), channel_id=1, source_target_pairs={{0,4},{4,0},{8,12},{12,8},{16,20},{20,16},{24,28},{28,24},{1,5},{5... | collective-permute-start | bytes 488456 | tf_op jit(solution)/shard_map/ppermute | solution.py:48
  11.4 8.4 %collective-permute-start.5 = (f32[318,128]{1,0:T(8,128)S(1)}, f32[318,128]{1,0:T(8,128)S(1)}, u32[]{:S(2)}, u32[]{:S(2)}) collective-permute-start(f32[318,128]{1,0:T(8,128)S(1)} %get-tuple-element.60), channel_id=1, source_target_pairs={{0,1},{4,8},{8,4},{12,16},{16,12},{20,24},{24,20},{28,29},{1,0},{5... | collective-permute-start | bytes 488456 | tf_op jit(solution)/shard_map/ppermute | solution.py:64
  11.4 9.3 %collective-permute-start.9 = (f32[48,128]{1,0:T(8,128)S(1)}, f32[48,128]{1,0:T(8,128)S(1)}, u32[]{:S(2)}, u32[]{:S(2)}) collective-permute-start(f32[48,128]{1,0:T(8,128)S(1)} %constant_dynamic-update-slice_fusion.rest_0_), channel_id=1, source_target_pairs={{0,24},{4,28},{8,16},{12,20},{16,8},{20,12},{24,0},{28,4},{1,25},{... | collective-permute-start | bytes 73736 | tf_op jit(solution)/shard_map/ppermute | solution.py:48
  16.5 4.7 %collective-permute-start.8 = (f32[48,128]{1,0:T(8,128)S(1)}, f32[48,128]{1,0:T(8,128)S(1)}, u32[]{:S(2)}, u32[]{:S(2)}) collective-permute-start(f32[48,128]{1,0:T(8,128)S(1)} %constant_dynamic-update-slice_fusion.rest_0_), channel_id=1, source_target_pairs={{0,16},{4,20},{8,24},{12,28},{16,0},{20,4},{24,8},{28,12},{1,17},{... | collective-permute-start | bytes 73736 | tf_op jit(solution)/shard_map/ppermute | solution.py:48
  16.5 4.7 %collective-permute-start.7 = (f32[48,128]{1,0:T(8,128)S(1)}, f32[48,128]{1,0:T(8,128)S(1)}, u32[]{:S(2)}, u32[]{:S(2)}) collective-permute-start(f32[48,128]{1,0:T(8,128)S(1)} %constant_dynamic-update-slice_fusion.rest_0_), channel_id=1, source_target_pairs={{0,8},{4,12},{8,0},{12,4},{16,24},{20,28},{24,16},{28,20},{1,9},{5... | collective-permute-start | bytes 73736 | tf_op jit(solution)/shard_map/ppermute | solution.py:48
  22.6 5.5 %collective-permute-start.10 = (f32[216,128]{1,0:T(8,128)S(1)}, f32[216,128]{1,0:T(8,128)S(1)}, u32[]{:S(2)}, u32[]{:S(2)}) collective-permute-start(f32[216,128]{1,0:T(8,128)S(1)} %get-tuple-element.71), channel_id=1, source_target_pairs={{0,4},{4,0},{8,12},{12,8},{16,20},{20,16},{24,28},{28,24},{1,5},{5... | collective-permute-start | bytes 331784 | tf_op jit(solution)/shard_map/ppermute | solution.py:48
  24.0 4.2 %collective-permute-start.11 = (f32[216,128]{1,0:T(8,128)S(1)}, f32[216,128]{1,0:T(8,128)S(1)}, u32[]{:S(2)}, u32[]{:S(2)}) collective-permute-start(f32[216,128]{1,0:T(8,128)S(1)} %get-tuple-element.72), channel_id=1, source_target_pairs={{0,1},{4,8},{8,4},{12,16},{16,12},{20,24},{24,20},{28,29},{1,0},{5... | collective-permute-start | bytes 331784 | tf_op jit(solution)/shard_map/ppermute | solution.py:64
  25.8 4.9 %collective-permute-start.12 = (f32[192,128]{1,0:T(8,128)S(1)}, f32[192,128]{1,0:T(8,128)S(1)}, u32[]{:S(2)}, u32[]{:S(2)}) collective-permute-start(f32[192,128]{1,0:T(8,128)S(1)} %get-tuple-element.75), channel_id=1, source_target_pairs={{0,1},{1,0},{2,3},{3,2},{4,5},{5,4},{6,7},{7,6},{8,9},{9,8},{10,11... | collective-permute-start | bytes 294920 | tf_op jit(solution)/shard_map/ppermute | solution.py:48
  26.4 4.6 %collective-permute-start.13 = (f32[192,128]{1,0:T(8,128)S(1)}, f32[192,128]{1,0:T(8,128)S(1)}, u32[]{:S(2)}, u32[]{:S(2)}) collective-permute-start(f32[192,128]{1,0:T(8,128)S(1)} %get-tuple-element.76), channel_id=1, source_target_pairs={{0,4},{1,2},{2,1},{3,7},{4,0},{5,6},{6,5},{7,3},{8,12},{9,10},{10,... | collective-permute-start | bytes 294920 | tf_op jit(solution)/shard_map/ppermute | solution.py:64
  28.5 4.9 %collective-permute-start.14 = (f32[40,128]{1,0:T(8,128)S(1)}, f32[40,128]{1,0:T(8,128)S(1)}, u32[]{:S(2)}, u32[]{:S(2)}) collective-permute-start(f32[40,128]{1,0:T(8,128)S(1)} %get-tuple-element.77), channel_id=1, source_target_pairs={{0,1},{1,0},{2,3},{3,2},{4,5},{5,4},{6,7},{7,6},{8,9},{9,8},{10,11... | collective-permute-start | bytes 61448 | tf_op jit(solution)/shard_map/ppermute | solution.py:48
  28.5 4.9 %collective-permute-start.15 = (f32[40,128]{1,0:T(8,128)S(1)}, f32[40,128]{1,0:T(8,128)S(1)}, u32[]{:S(2)}, u32[]{:S(2)}) collective-permute-start(f32[40,128]{1,0:T(8,128)S(1)} %get-tuple-element.78), channel_id=1, source_target_pairs={{0,3},{1,2},{2,1},{3,0},{4,7},{5,6},{6,5},{7,4},{8,11},{9,10},{10,... | collective-permute-start | bytes 61448 | tf_op jit(solution)/shard_map/ppermute | solution.py:70
  29.8 3.7 %collective-permute-start.16 = (f32[16,128]{1,0:T(8,128)S(1)}, f32[16,128]{1,0:T(8,128)S(1)}, u32[]{:S(2)}, u32[]{:S(2)}) collective-permute-start(f32[16,128]{1,0:T(8,128)S(1)} %get-tuple-element.79), channel_id=1, source_target_pairs={{0,2},{1,3},{2,0},{3,1},{4,6},{5,7},{6,4},{7,5},{8,10},{9,11},{10,... | collective-permute-start | bytes 24584 | tf_op jit(solution)/shard_map/ppermute | solution.py:48

commit v17 on v16

--- a/solution.py
+++ b/solution.py
@@ -27,7 +27,9 @@
 HBM = pl.BlockSpec(memory_space=pltpu.HBM)
 
 
-def call(body, outs, ins, scratch=(), in_specs=None, flops=1000000, limit=40 * 2**20):
+def call(
+    body, outs, ins, scratch=(), in_specs=None, out_specs=None, flops=1000000, limit=40 * 2**20
+):
     shapes = [
         out if isinstance(out, jax.ShapeDtypeStruct) else jax.ShapeDtypeStruct(out, f32)
         for out in outs
@@ -37,7 +39,7 @@
         body,
         out_shape=shapes,
         in_specs=in_specs or [VMEM] * len(ins),
-        out_specs=[VMEM] * len(shapes),
+        out_specs=out_specs or [VMEM] * len(shapes),
         scratch_shapes=list(scratch),
         compiler_params=pltpu.CompilerParams(vmem_limit_bytes=limit),
         cost_estimate=pl.CostEstimate(flops=flops, bytes_accessed=size, transcendentals=0),
@@ -153,7 +155,7 @@
     ]
     for move in moves:
         move.start()
-    for move in moves:
+    for move in moves[1:]:
         move.wait()
 
     def put(at, field, away):
@@ -162,9 +164,6 @@
         out_a[at : at + CX] = jnp.where(even, north, south)
         out_b[at : at + CX] = jnp.where(even, south, north)
 
-    for c in range(NC):
-        for away in range(1, RIM + 1):
-            put((c * RIM + away - 1) * CX, fine.at[c], away)
     for f in range(3):
         for away in range(1, INNER + 1):
             put(Y_COEF + (f * INNER + away - 1) * CX, coefs.at[f], away)
@@ -181,6 +180,10 @@
     meta[1:2] = ((owner << held) | (beam & ((1 << held) - 1))).astype(f32)
     meta[2:3] = gates[1].astype(f32)
     meta[3:4] = gates[3].astype(f32) * values[...]
+    moves[0].wait()
+    for c in range(NC):
+        for away in range(1, RIM + 1):
+            put((c * RIM + away - 1) * CX, fine.at[c], away)
 
 
 def y_sides(got_a, got_b, rows, fill=0.0):
@@ -355,7 +358,7 @@
                 target[pl.ds(base, PITCH)] = forward_column(source, base, k)
             return carry
 
-        lax.fori_loop(step + 1, CX - 1 - step, body, 0, unroll=2)
+        lax.fori_loop(step + 1, CX - 1 - step, body, 0, unroll=True)
         own = []
         for c in range(NC):
             pieces = [jnp.zeros(((step + 1) * CY, 128), f32)]
@@ -573,9 +576,22 @@
 
 
 def interior(
-    core_coef, edge_coef, back_2, back_1, tops, lows, slot_push, out, out_a, out_b, *scratch
+    core_coef,
+    edge_coef,
+    back_2,
+    back_1,
+    tops,
+    lows,
+    slot_push,
+    picks,
+    out,
+    out_a,
+    out_b,
+    out_picks,
+    *scratch,
 ):
     coef, forced, field_2, field_1, forcing = scratch
+    out_picks[...] = jnp.transpose(picks[...]).astype(bf16)
     for f in range(5):
         at = f * FIELD + FIRST * PITCH
         coef[at : at + CORE] = core_coef[f * CORE : (f + 1) * CORE]
@@ -611,7 +627,7 @@
                     target[pl.ds(c * FIELD + at, PITCH)] = value
             return carry
 
-        lax.fori_loop(low, high, body, 0, unroll=2)
+        lax.fori_loop(low, high, body, 0, unroll=True)
 
     def copy(source, target, columns):
         for c in range(NC):
@@ -643,7 +659,7 @@
     merged = ny == 4
     field, sums = rest[-2:]
     even, _, _ = place_on("gy")
-    total = picks.shape[1]
+    total = picks.shape[0]
     rows = total * NC // ny
     field[...] = core[...]
     for c in range(NC):
@@ -676,7 +692,7 @@
             here = slice(x * CY, (x + 1) * CY)
             out_near[c, here] = delta[c, here] + field[at : at + CY]
     adjoint = jnp.concatenate([field[c * CORE : (c + 1) * CORE] for c in range(NC)], axis=1)
-    tile_sums = two_part_dot(jnp.transpose(picks[...]).astype(bf16), adjoint)
+    tile_sums = two_part_dot(picks[...], adjoint)
     for c in range(NC):
         sums[pl.ds(c, total, stride=NC)] = tile_sums[:, c * 128 : (c + 1) * 128]
     out_sums[...] = sums[0:rows]
@@ -688,11 +704,12 @@
 
 
 def add_y(alpha, near, sums, y_a, y_b, small_a, small_b, *rest):
-    others = rest[:-2]
-    out_delta, out_alpha = rest[-2:]
-    out_delta[...] = near[...]
+    others = rest[:-4]
+    result, out_alpha, out_delta, sems = rest[-4:]
+    moves = []
     at = 0
     for c in range(NC):
+        out_delta[c] = near[c]
         for away, start, extra in WIDE:
             north, south = y_sides(y_a, y_b, pl.ds((c * RIM + away - 1) * CX, CX))
             high = pl.ds(CY - away, CX, stride=CY)
@@ -705,12 +722,17 @@
                     out_delta[c, (x + 1) * CY - extra : (x + 1) * CY] += north
                     out_delta[c, x * CY : x * CY + extra] += south
                     at += extra
+        move = pltpu.make_async_copy(out_delta.at[c], result.at[c], sems.at[c])
+        move.start()
+        moves.append(move)
     total = sums[...] + small_a[CORNERS:]
     if small_b.shape[0] > CORNERS:
         total = total + small_b[CORNERS:]
     for other in others:
         total = total + other[...]
     out_alpha[...] = alpha[...] + profile_weight * total
+    for move in moves:
+        move.wait()
 
 
 def on_device(
@@ -845,10 +867,15 @@
         ],
         flops=10000000,
     )
-    core, rim_a, rim_b = call(
+    core, rim_a, rim_b, picks = call(
         interior,
-        [(NC * CORE, 128), (Y_COEF, 128), (Y_COEF, 128)],
-        [coef, edge_coef, back_2, back_1, tops, lows, slot_push],
+        [
+            (NC * CORE, 128),
+            (Y_COEF, 128),
+            (Y_COEF, 128),
+            jax.ShapeDtypeStruct((total, CORE), bf16),
+        ],
+        [coef, edge_coef, back_2, back_1, tops, lows, slot_push, picks],
         [pltpu.VMEM((5 * FIELD, 128), f32)]
         + [pltpu.VMEM(big, f32)] * 3
         + [pltpu.VMEM((STEPS * CX * CY, NC * 128), f32)],
@@ -878,6 +905,8 @@
         add_y,
         [fine.shape, control.shape],
         [control_near, near, sums, y_a, y_b, small_a, small_b, *others],
+        [pltpu.VMEM(fine.shape, f32), pltpu.SemaphoreType.DMA((NC,))],
+        out_specs=[HBM, VMEM],
     )
     return grad_delta.reshape(delta.shape), grad_alpha.reshape(alpha.shape)
 

time: 34.6 us -> 34.5 us (level)
    ppermute x4, starting transfers between devices: 4.35 us -> 4.92 us  [pair_b(): return lax.ppermute(block, ('gx', 'gy'), pairs)]
    ppermute x12, waiting for transfers between devices: 4.51 us -> 5.01 us  [swap(): lax.ppermute(block, axis, [(i, i ^ xor) for i in range(lax.axis_size(axis...]
    ppermute x1, starting transfers between devices: 1.25 us -> 0.89 us  [ring_b(): return lax.ppermute(block, axis, pairs)]
  transfers between devices with their start and end apart: 17 -> 17, of which waited for: 4 -> 5; matrix products, arithmetic and copies ran while one was open for 0% -> 0% of each run, Pallas kernels for 19% -> 17%
where the time goes in v17:
time: 34.5 us; the launch traced here: 34.4 us
  starting transfers between devices  18.4 us (53%)
  Pallas kernels  10.1 us (29%)
  waiting for transfers between devices  5.08 us (15%)
  between operations  0.74 us (2%)
    ppermute x12, starting transfers between devices, swap(): lax.ppermute(block, axis, [(i, i ^ xor) for i in range(lax.axis_size(axis...  12.6 us
    pallas_call x9, Pallas kernels, call(): pl.pallas_call(body, out_shape=shapes, in_specs=in_specs or [VMEM] * len(...  10.1 us
    ppermute x12, waiting for transfers between devices, swap(): lax.ppermute(block, axis, [(i, i ^ xor) for i in range(lax.axis_size(axis...  5.01 us
    ppermute x4, starting transfers between devices, pair_b(): return lax.ppermute(block, ('gx', 'gy'), pairs)  4.92 us
    ppermute x1, starting transfers between devices, ring_b(): return lax.ppermute(block, axis, pairs)  0.89 us
  transfers between devices with their start and end apart: 17, of which 5 were waited for; matrix products, arithmetic and copies ran while one was open for 0% of the time, Pallas kernels for 17%

profile of v17, /device:TPU:0, one launch (start us, length us, event | category | flops | bytes accessed | tf_op | source)
XLA Modules:
  0.0 34.4 jit_solution(3662531966134623433)
XLA Ops:
  0.6 0.0 copy-start
  0.6 1.4 %shard_map.131 = (f32[320,128]{1,0:T(8,128)S(1)}, f32[304,128]{1,0:T(8,128)S(1)}, f32[4,256,128]{2,1,0:T(8,128)S(1)}, f32[3,256,128]{2,1,0:T(8,128)S(1)}, f32[16...) custom-call(f32[4,256,128]{2,1,0:T(8,128)} %bitcast.16, ...), custom_call_target="tpu_custom_call" | custom-call | flops 1000000 | bytes 944128 | tf_op jit(solution)/shard_map/pallas_call | solution.py:38
  2.1 0.5 %collective-permute-start = (f32[320,128]{1,0:T(8,128)S(1)}, f32[320,128]{1,0:T(8,128)S(1)}, u32[]{:S(2)}, u32[]{:S(2)}) collective-permute-start(f32[320,128]{1,0:T(8,128)S(1)} %get-tuple-element.51), channel_id=1, source_target_pairs={{0,1},{1,0},{2,3},{3,2},{4,5},{5,4},{6,7},{7,6},{8,9},{9,8},{10,11... | collective-permute-start | bytes 491528 | tf_op jit(solution)/shard_map/ppermute | solution.py:50
  2.6 2.6 %collective-permute-start.1 = (f32[304,128]{1,0:T(8,128)S(1)}, f32[304,128]{1,0:T(8,128)S(1)}, u32[]{:S(2)}, u32[]{:S(2)}) collective-permute-start(f32[304,128]{1,0:T(8,128)S(1)} %get-tuple-element.52), channel_id=1, source_target_pairs={{0,4},{1,2},{2,1},{3,7},{4,0},{5,6},{6,5},{7,3},{8,12},{9,10},{10,... | collective-permute-start | bytes 466952 | tf_op jit(solution)/shard_map/ppermute | solution.py:66
  5.2 1.2 %collective-permute-start.3 = (f32[16,128]{1,0:T(8,128)}, f32[16,128]{1,0:T(8,128)S(1)}, u32[]{:S(2)}, u32[]{:S(2)}) collective-permute-start(f32[16,128]{1,0:T(8,128)} %bitcast.22), channel_id=1, source_target_pairs={{0,3},{1,2},{2,1},{3,0},{4,7},{5,6},{6,5},{7,4},{8,11},{9,10},{10,... | collective-permute-start | bytes 24584 | tf_op jit(solution)/shard_map/ppermute | solution.py:50
  6.4 0.5 %collective-permute-start.2 = (f32[16,128]{1,0:T(8,128)}, f32[16,128]{1,0:T(8,128)S(1)}, u32[]{:S(2)}, u32[]{:S(2)}) collective-permute-start(f32[16,128]{1,0:T(8,128)} %bitcast.23), channel_id=1, source_target_pairs={{0,2},{1,3},{2,0},{3,1},{4,6},{5,7},{6,4},{7,5},{8,10},{9,11},{10,... | collective-permute-start | bytes 24584 | tf_op jit(solution)/shard_map/ppermute | solution.py:50
  6.9 1.5 %collective-permute-start.6 = (f32[24,128]{1,0:T(8,128)}, f32[24,128]{1,0:T(8,128)S(1)}, u32[]{:S(2)}, u32[]{:S(2)}) collective-permute-start(f32[24,128]{1,0:T(8,128)} %bitcast.20), channel_id=1, source_target_pairs={{0,4},{4,0},{8,12},{12,8},{16,20},{20,16},{24,28},{28,24},{1,5},{5... | collective-permute-start | bytes 36872 | tf_op jit(solution)/shard_map/ppermute | solution.py:50
  8.4 0.0 copy-done
  8.4 0.3 shard_map.132
  8.7 0.0 collective-permute-done.3.refs_10_.refs_8_
  8.8 1.5 %collective-permute-done.2.refs_9_.refs_7_ = f32[16,128]{1,0:T(8,128)S(1)} collective-permute-done((f32[16,128]{1,0:T(8,128)}, f32[16,128]{1,0:T(8,128)S(1)}, u32[]{:S(2)}, u32[]{:S(2)}) %collective-permute-start.2) | collective-permute-done | bytes 8224 | tf_op jit(solution)/shard_map/ppermute | solution.py:50
  10.3 0.0 collective-permute-done.1.refs_8_.refs_6_
  10.3 0.0 collective-permute-done.refs_7_.refs_5_
  10.3 0.5 %shard_map.134 = (f32[318,128]{1,0:T(8,128)S(1)}, f32[318,128]{1,0:T(8,128)S(1)}) custom-call(f32[4,256,128]{2,1,0:T(8,128)S(1)} %get-tuple-element.44.refs_0_, f32[3,256,128]{2,1,0:T(8,128)S(1)} %get-tuple-element.45.refs_1_, f32[16,128]{1,0:T(8,128)S(1)} %get-tuple-element.43.refs_2_.alpha, f32[16,128]{1,0:T(8,128)S(1)} %get-tuple-element.46.refs_3_, ...), custom_call_target="tpu_custom_call" | custom-call | flops 1000000 | bytes 1277952 | tf_op jit(solution)/shard_map/pallas_call | solution.py:38
  10.8 0.6 %collective-permute-start.4 = (f32[318,128]{1,0:T(8,128)S(1)}, f32[318,128]{1,0:T(8,128)S(1)}, u32[]{:S(2)}, u32[]{:S(2)}) collective-permute-start(f32[318,128]{1,0:T(8,128)S(1)} %get-tuple-element.59), channel_id=1, source_target_pairs={{0,4},{4,0},{8,12},{12,8},{16,20},{20,16},{24,28},{28,24},{1,5},{5... | collective-permute-start | bytes 488456 | tf_op jit(solution)/shard_map/ppermute | solution.py:50
  11.4 0.0 collective-permute-start.5
  11.4 0.0 collective-permute-done.6
  11.4 5.1 %collective-permute-start.9 = (f32[48,128]{1,0:T(8,128)S(1)}, f32[48,128]{1,0:T(8,128)S(1)}, u32[]{:S(2)}, u32[]{:S(2)}) collective-permute-start(f32[48,128]{1,0:T(8,128)S(1)} %constant_dynamic-update-slice_fusion.rest_0_), channel_id=1, source_target_pairs={{0,24},{4,28},{8,16},{12,20},{16,8},{20,12},{24,0},{28,4},{1,25},{... | collective-permute-start | bytes 73736 | tf_op jit(solution)/shard_map/ppermute | solution.py:50
  16.5 0.0 collective-permute-start.8
  16.5 0.6 %collective-permute-start.7 = (f32[48,128]{1,0:T(8,128)S(1)}, f32[48,128]{1,0:T(8,128)S(1)}, u32[]{:S(2)}, u32[]{:S(2)}) collective-permute-start(f32[48,128]{1,0:T(8,128)S(1)} %constant_dynamic-update-slice_fusion.rest_0_), channel_id=1, source_target_pairs={{0,8},{4,12},{8,0},{12,4},{16,24},{20,28},{24,16},{28,20},{1,9},{5... | collective-permute-start | bytes 73736 | tf_op jit(solution)/shard_map/ppermute | solution.py:50
  17.1 2.1 %shard_map.133 = (f32[1536,128]{1,0:T(8,128)S(1)}, f32[1920,128]{1,0:T(8,128)S(1)}, f32[384,16]{1,0:T(8,128)S(1)}, f32[1536,128]{1,0:T(8,128)S(1)}, f32[1536,128]{1,0:T(8,128)S(1)}, /*index=5*/f32[768,128]{1,0:T(8,128)S(1)}) custom-call(f32[4,256,128]{2,1,0:T(8,128)S(1)} %get-tuple-element.44.refs_0_, f32[3,256,128]{2,1,0:T(8,128)S(1)} %get-tuple-element.45.refs_1_, ...), custom_call_target="tpu_custom_call" | custom-call | flops 3000000 | bytes 2064384 | tf_op jit(solution)/shard_map/pallas_call | solution.py:38
  19.3 0.0 collective-permute-done.4.x_a
  19.3 0.0 collective-permute-done.5.x_b
  19.3 0.8 %shard_map.135 = (f32[2880,128]{1,0:T(8,128)S(1)}, f32[768,128]{1,0:T(8,128)S(1)}) custom-call(f32[1536,128]{1,0:T(8,128)S(1)} %get-tuple-element.54.core, f32[1920,128]{1,0:T(8,128)S(1)} %get-tuple-element.53.core_coef, f32[1536,128]{1,0:T(8,128)S(1)} %get-tuple-element.55.near_1, f32[1536,128]{1,0:T(8,128)S(1)} %get-tuple-element.56.near_2, ...), custom_call_target="tpu_custom_call" | custom-call | flops 10000000 | bytes 4847616 | tf_op jit(solution)/shard_map/pallas_call | solution.py:38
  20.1 0.2 collective-permute-done.9.rest_3_
  20.3 0.9 %collective-permute-done.8.rest_2_ = f32[48,128]{1,0:T(8,128)S(1)} collective-permute-done((f32[48,128]{1,0:T(8,128)S(1)}, f32[48,128]{1,0:T(8,128)S(1)}, u32[]{:S(2)}, u32[]{:S(2)}) %collective-permute-start.8) | collective-permute-done | bytes 24608 | tf_op jit(solution)/shard_map/ppermute | solution.py:50
  21.2 0.0 collective-permute-done.7.rest_1_
  21.2 1.4 %shard_map.136 = (f32[216,128]{1,0:T(8,128)S(1)}, f32[216,128]{1,0:T(8,128)S(1)}, f32[2304,128]{1,0:T(8,128)S(1)}, f32[2304,128]{1,0:T(8,128)S(1)}, bf16[768,512...) custom-call(f32[2880,128]{1,0:T(8,128)S(1)} %get-tuple-element.61.coef.edge_coef, ...), custom_call_target="tpu_custom_call" | custom-call | flops 10000000 | bytes 2826240 | tf_op jit(solution)/shard_map/pallas_call | solution.py:38
  22.7 0.8 %collective-permute-start.10 = (f32[216,128]{1,0:T(8,128)S(1)}, f32[216,128]{1,0:T(8,128)S(1)}, u32[]{:S(2)}, u32[]{:S(2)}) collective-permute-start(f32[216,128]{1,0:T(8,128)S(1)} %get-tuple-element.73), channel_id=1, source_target_pairs={{0,4},{4,0},{8,12},{12,8},{16,20},{20,16},{24,28},{28,24},{1,5},{5... | collective-permute-start | bytes 331784 | tf_op jit(solution)/shard_map/ppermute | solution.py:50
  23.4 0.0 collective-permute-start.11
  23.4 1.6 %shard_map.137 = (f32[1536,128]{1,0:T(8,128)S(1)}, f32[192,128]{1,0:T(8,128)S(1)}, f32[192,128]{1,0:T(8,128)S(1)}, bf16[16,384]{1,0:T(8,128)(2,1)S(1)}) custom-call(f32[1920,128]{1,0:T(8,128)S(1)} %get-tuple-element.53.core_coef, f32[2880,128]{1,0:T(8,128)S(1)} %get-tuple-element.61.coef.edge_coef, f32[2304,128]{1,0:T(8,128)S(1)} %get-tuple-element.66.back_2, ...), custom_call_target="tpu_custom_call" | custom-call | flops 10000000 | bytes 8249344 | tf_op jit(solution)/shard_map/pallas_call | solution.py:38
  25.1 0.6 %collective-permute-start.12 = (f32[192,128]{1,0:T(8,128)S(1)}, f32[192,128]{1,0:T(8,128)S(1)}, u32[]{:S(2)}, u32[]{:S(2)}) collective-permute-start(f32[192,128]{1,0:T(8,128)S(1)} %get-tuple-element.77), channel_id=1, source_target_pairs={{0,1},{1,0},{2,3},{3,2},{4,5},{5,4},{6,7},{7,6},{8,9},{9,8},{10,11... | collective-permute-start | bytes 294920 | tf_op jit(solution)/shard_map/ppermute | solution.py:50
  25.6 2.3 %collective-permute-start.13 = (f32[192,128]{1,0:T(8,128)S(1)}, f32[192,128]{1,0:T(8,128)S(1)}, u32[]{:S(2)}, u32[]{:S(2)}) collective-permute-start(f32[192,128]{1,0:T(8,128)S(1)} %get-tuple-element.78), channel_id=1, source_target_pairs={{0,4},{1,2},{2,1},{3,7},{4,0},{5,6},{6,5},{7,3},{8,12},{9,10},{10,... | collective-permute-start | bytes 294920 | tf_op jit(solution)/shard_map/ppermute | solution.py:66
  28.0 0.0 collective-permute-done.10.refs_3_
  28.0 0.0 collective-permute-done.11.refs_4_
  28.0 0.4 %shard_map.138 = (f32[40,128]{1,0:T(8,128)S(1)}, f32[40,128]{1,0:T(8,128)S(1)}, f32[4,256,128]{2,1,0:T(8,128)S(1)}, f32[16,128]{1,0:T(8,128)S(1)}, f32[16,128]{1,0:T(8,128)S(1)}) custom-call(f32[4,256,128]{2,1,0:T(8,128)S(1)} %get-tuple-element.44.refs_0_, bf16[16,384]{1,0:T(8,128)(2,1)S(1)} %get-tuple-element.71.refs_1_, ...), custom_call_target="tpu_custom_call" | custom-call | flops 1000000 | bytes 1556480 | tf_op jit(solution)/shard_map/pallas_call | solution.py:38
  28.4 0.0 collective-permute-start.14
  28.4 0.9 %collective-permute-start.15 = (f32[40,128]{1,0:T(8,128)S(1)}, f32[40,128]{1,0:T(8,128)S(1)}, u32[]{:S(2)}, u32[]{:S(2)}) collective-permute-start(f32[40,128]{1,0:T(8,128)S(1)} %get-tuple-element.80), channel_id=1, source_target_pairs={{0,3},{1,2},{2,1},{3,0},{4,7},{5,6},{6,5},{7,4},{8,11},{9,10},{10,... | collective-permute-start | bytes 61448 | tf_op jit(solution)/shard_map/ppermute | solution.py:72
  29.3 1.2 %collective-permute-start.16 = (f32[16,128]{1,0:T(8,128)S(1)}, f32[16,128]{1,0:T(8,128)S(1)}, u32[]{:S(2)}, u32[]{:S(2)}) collective-permute-start(f32[16,128]{1,0:T(8,128)S(1)} %get-tuple-element.81), channel_id=1, source_target_pairs={{0,2},{1,3},{2,0},{3,1},{4,6},{5,7},{6,4},{7,5},{8,10},{9,11},{10,... | collective-permute-start | bytes 24584 | tf_op jit(solution)/shard_map/ppermute | solution.py:50
  30.5 0.0 collective-permute-done.12.y_a
  30.5 0.1 collective-permute-done.13.y_b
  30.6 2.3 %collective-permute-done.16.rest_0_ = f32[16,128]{1,0:T(8,128)S(1)} collective-permute-done((f32[16,128]{1,0:T(8,128)S(1)}, f32[16,128]{1,0:T(8,128)S(1)}, u32[]{:S(2)}, u32[]{:S(2)}) %collective-permute-start.16) | collective-permute-done | bytes 8224 | tf_op jit(solution)/shard_map/ppermute | solution.py:50
  32.9 0.0 collective-permute-done.14.small_a
  32.9 0.0 collective-permute-done.15.small_b
  32.9 1.5 %shard_map.139 = (f32[4,256,128]{2,1,0:T(8,128)}, f32[16,128]{1,0:T(8,128)}) custom-call(f32[16,128]{1,0:T(8,128)S(1)} %get-tuple-element.43.refs_2_.alpha, f32[4,256,128]{2,1,0:T(8,128)S(1)} %get-tuple-element.75.near, f32[16,128]{1,0:T(8,128)S(1)} %get-tuple-element.76.sums, f32[192,128]{1,0:T(8,128)S(1)} %collective-permute-done.12.y_a, ...), custom_call_target="tpu_custom_call" | custom-call | flops 1000000 | bytes 786432 | tf_op jit(solution)/shard_map/pallas_call | solution.py:38
  (2 shorter events, 0.0 us)
Async XLA Ops:
  0.6 7.8 %copy-start = (f32[1,1,256,4,128]{4,3,2,1,0:T(4,128)S(1)}, f32[1,1,256,4,128]{4,3,2,1,0:T(4,128)}, u32[]{:S(2)}) copy-start(f32[1,1,256,4,128]{4,3,2,1,0:T(4,128)} %param.22) | copy-start | bytes 1572868
  2.1 8.2 %collective-permute-start = (f32[320,128]{1,0:T(8,128)S(1)}, f32[320,128]{1,0:T(8,128)S(1)}, u32[]{:S(2)}, u32[]{:S(2)}) collective-permute-start(f32[320,128]{1,0:T(8,128)S(1)} %get-tuple-element.51), channel_id=1, source_target_pairs={{0,1},{1,0},{2,3},{3,2},{4,5},{5,4},{6,7},{7,6},{8,9},{9,8},{10,11... | collective-permute-start | bytes 491528 | tf_op jit(solution)/shard_map/ppermute | solution.py:50
  2.6 7.7 %collective-permute-start.1 = (f32[304,128]{1,0:T(8,128)S(1)}, f32[304,128]{1,0:T(8,128)S(1)}, u32[]{:S(2)}, u32[]{:S(2)}) collective-permute-start(f32[304,128]{1,0:T(8,128)S(1)} %get-tuple-element.52), channel_id=1, source_target_pairs={{0,4},{1,2},{2,1},{3,7},{4,0},{5,6},{6,5},{7,3},{8,12},{9,10},{10,... | collective-permute-start | bytes 466952 | tf_op jit(solution)/shard_map/ppermute | solution.py:66
  5.2 3.6 %collective-permute-start.3 = (f32[16,128]{1,0:T(8,128)}, f32[16,128]{1,0:T(8,128)S(1)}, u32[]{:S(2)}, u32[]{:S(2)}) collective-permute-start(f32[16,128]{1,0:T(8,128)} %bitcast.22), channel_id=1, source_target_pairs={{0,3},{1,2},{2,1},{3,0},{4,7},{5,6},{6,5},{7,4},{8,11},{9,10},{10,... | collective-permute-start | bytes 24584 | tf_op jit(solution)/shard_map/ppermute | solution.py:50
  6.4 3.9 %collective-permute-start.2 = (f32[16,128]{1,0:T(8,128)}, f32[16,128]{1,0:T(8,128)S(1)}, u32[]{:S(2)}, u32[]{:S(2)}) collective-permute-start(f32[16,128]{1,0:T(8,128)} %bitcast.23), channel_id=1, source_target_pairs={{0,2},{1,3},{2,0},{3,1},{4,6},{5,7},{6,4},{7,5},{8,10},{9,11},{10,... | collective-permute-start | bytes 24584 | tf_op jit(solution)/shard_map/ppermute | solution.py:50
  6.9 4.5 %collective-permute-start.6 = (f32[24,128]{1,0:T(8,128)}, f32[24,128]{1,0:T(8,128)S(1)}, u32[]{:S(2)}, u32[]{:S(2)}) collective-permute-start(f32[24,128]{1,0:T(8,128)} %bitcast.20), channel_id=1, source_target_pairs={{0,4},{4,0},{8,12},{12,8},{16,20},{20,16},{24,28},{28,24},{1,5},{5... | collective-permute-start | bytes 36872 | tf_op jit(solution)/shard_map/ppermute | solution.py:50
  10.8 8.4 %collective-permute-start.4 = (f32[318,128]{1,0:T(8,128)S(1)}, f32[318,128]{1,0:T(8,128)S(1)}, u32[]{:S(2)}, u32[]{:S(2)}) collective-permute-start(f32[318,128]{1,0:T(8,128)S(1)} %get-tuple-element.59), channel_id=1, source_target_pairs={{0,4},{4,0},{8,12},{12,8},{16,20},{20,16},{24,28},{28,24},{1,5},{5... | collective-permute-start | bytes 488456 | tf_op jit(solution)/shard_map/ppermute | solution.py:50
  11.4 7.9 %collective-permute-start.5 = (f32[318,128]{1,0:T(8,128)S(1)}, f32[318,128]{1,0:T(8,128)S(1)}, u32[]{:S(2)}, u32[]{:S(2)}) collective-permute-start(f32[318,128]{1,0:T(8,128)S(1)} %get-tuple-element.60), channel_id=1, source_target_pairs={{0,1},{4,8},{8,4},{12,16},{16,12},{20,24},{24,20},{28,29},{1,0},{5... | collective-permute-start | bytes 488456 | tf_op jit(solution)/shard_map/ppermute | solution.py:66
  11.4 8.9 %collective-permute-start.9 = (f32[48,128]{1,0:T(8,128)S(1)}, f32[48,128]{1,0:T(8,128)S(1)}, u32[]{:S(2)}, u32[]{:S(2)}) collective-permute-start(f32[48,128]{1,0:T(8,128)S(1)} %constant_dynamic-update-slice_fusion.rest_0_), channel_id=1, source_target_pairs={{0,24},{4,28},{8,16},{12,20},{16,8},{20,12},{24,0},{28,4},{1,25},{... | collective-permute-start | bytes 73736 | tf_op jit(solution)/shard_map/ppermute | solution.py:50
  16.5 4.7 %collective-permute-start.8 = (f32[48,128]{1,0:T(8,128)S(1)}, f32[48,128]{1,0:T(8,128)S(1)}, u32[]{:S(2)}, u32[]{:S(2)}) collective-permute-start(f32[48,128]{1,0:T(8,128)S(1)} %constant_dynamic-update-slice_fusion.rest_0_), channel_id=1, source_target_pairs={{0,16},{4,20},{8,24},{12,28},{16,0},{20,4},{24,8},{28,12},{1,17},{... | collective-permute-start | bytes 73736 | tf_op jit(solution)/shard_map/ppermute | solution.py:50
  16.5 4.7 %collective-permute-start.7 = (f32[48,128]{1,0:T(8,128)S(1)}, f32[48,128]{1,0:T(8,128)S(1)}, u32[]{:S(2)}, u32[]{:S(2)}) collective-permute-start(f32[48,128]{1,0:T(8,128)S(1)} %constant_dynamic-update-slice_fusion.rest_0_), channel_id=1, source_target_pairs={{0,8},{4,12},{8,0},{12,4},{16,24},{20,28},{24,16},{28,20},{1,9},{5... | collective-permute-start | bytes 73736 | tf_op jit(solution)/shard_map/ppermute | solution.py:50
  22.7 5.3 %collective-permute-start.10 = (f32[216,128]{1,0:T(8,128)S(1)}, f32[216,128]{1,0:T(8,128)S(1)}, u32[]{:S(2)}, u32[]{:S(2)}) collective-permute-start(f32[216,128]{1,0:T(8,128)S(1)} %get-tuple-element.73), channel_id=1, source_target_pairs={{0,4},{4,0},{8,12},{12,8},{16,20},{20,16},{24,28},{28,24},{1,5},{5... | collective-permute-start | bytes 331784 | tf_op jit(solution)/shard_map/ppermute | solution.py:50
  23.4 4.5 %collective-permute-start.11 = (f32[216,128]{1,0:T(8,128)S(1)}, f32[216,128]{1,0:T(8,128)S(1)}, u32[]{:S(2)}, u32[]{:S(2)}) collective-permute-start(f32[216,128]{1,0:T(8,128)S(1)} %get-tuple-element.74), channel_id=1, source_target_pairs={{0,1},{4,8},{8,4},{12,16},{16,12},{20,24},{24,20},{28,29},{1,0},{5... | collective-permute-start | bytes 331784 | tf_op jit(solution)/shard_map/ppermute | solution.py:66
  25.1 5.4 %collective-permute-start.12 = (f32[192,128]{1,0:T(8,128)S(1)}, f32[192,128]{1,0:T(8,128)S(1)}, u32[]{:S(2)}, u32[]{:S(2)}) collective-permute-start(f32[192,128]{1,0:T(8,128)S(1)} %get-tuple-element.77), channel_id=1, source_target_pairs={{0,1},{1,0},{2,3},{3,2},{4,5},{5,4},{6,7},{7,6},{8,9},{9,8},{10,11... | collective-permute-start | bytes 294920 | tf_op jit(solution)/shard_map/ppermute | solution.py:50
  25.6 4.9 %collective-permute-start.13 = (f32[192,128]{1,0:T(8,128)S(1)}, f32[192,128]{1,0:T(8,128)S(1)}, u32[]{:S(2)}, u32[]{:S(2)}) collective-permute-start(f32[192,128]{1,0:T(8,128)S(1)} %get-tuple-element.78), channel_id=1, source_target_pairs={{0,4},{1,2},{2,1},{3,7},{4,0},{5,6},{6,5},{7,3},{8,12},{9,10},{10,... | collective-permute-start | bytes 294920 | tf_op jit(solution)/shard_map/ppermute | solution.py:66
  28.4 4.6 %collective-permute-start.14 = (f32[40,128]{1,0:T(8,128)S(1)}, f32[40,128]{1,0:T(8,128)S(1)}, u32[]{:S(2)}, u32[]{:S(2)}) collective-permute-start(f32[40,128]{1,0:T(8,128)S(1)} %get-tuple-element.79), channel_id=1, source_target_pairs={{0,1},{1,0},{2,3},{3,2},{4,5},{5,4},{6,7},{7,6},{8,9},{9,8},{10,11... | collective-permute-start | bytes 61448 | tf_op jit(solution)/shard_map/ppermute | solution.py:50
  28.4 4.6 %collective-permute-start.15 = (f32[40,128]{1,0:T(8,128)S(1)}, f32[40,128]{1,0:T(8,128)S(1)}, u32[]{:S(2)}, u32[]{:S(2)}) collective-permute-start(f32[40,128]{1,0:T(8,128)S(1)} %get-tuple-element.80), channel_id=1, source_target_pairs={{0,3},{1,2},{2,1},{3,0},{4,7},{5,6},{6,5},{7,4},{8,11},{9,10},{10,... | collective-permute-start | bytes 61448 | tf_op jit(solution)/shard_map/ppermute | solution.py:72
  29.3 3.7 %collective-permute-start.16 = (f32[16,128]{1,0:T(8,128)S(1)}, f32[16,128]{1,0:T(8,128)S(1)}, u32[]{:S(2)}, u32[]{:S(2)}) collective-permute-start(f32[16,128]{1,0:T(8,128)S(1)} %get-tuple-element.81), channel_id=1, source_target_pairs={{0,2},{1,3},{2,0},{3,1},{4,6},{5,7},{6,4},{7,5},{8,10},{9,11},{10,... | collective-permute-start | bytes 24584 | tf_op jit(solution)/shard_map/ppermute | solution.py:50

commit v18 on v17

--- a/solution.py
+++ b/solution.py
@@ -27,9 +27,7 @@
 HBM = pl.BlockSpec(memory_space=pltpu.HBM)
 
 
-def call(
-    body, outs, ins, scratch=(), in_specs=None, out_specs=None, flops=1000000, limit=40 * 2**20
-):
+def call(body, outs, ins, scratch=(), in_specs=None, flops=1000000, limit=40 * 2**20):
     shapes = [
         out if isinstance(out, jax.ShapeDtypeStruct) else jax.ShapeDtypeStruct(out, f32)
         for out in outs
@@ -39,7 +37,7 @@
         body,
         out_shape=shapes,
         in_specs=in_specs or [VMEM] * len(ins),
-        out_specs=out_specs or [VMEM] * len(shapes),
+        out_specs=[VMEM] * len(shapes),
         scratch_shapes=list(scratch),
         compiler_params=pltpu.CompilerParams(vmem_limit_bytes=limit),
         cost_estimate=pl.CostEstimate(flops=flops, bytes_accessed=size, transcendentals=0),
@@ -334,7 +332,7 @@
             coef[pl.ds(f * CORE + at, PITCH)] = value
         return carry
 
-    lax.fori_loop(0, CX, combine, 0)
+    lax.fori_loop(0, CX, combine, 0, unroll=True)
 
     gather_known(alpha, y_a, others, known)
     turned = tile_numbers(near_tiles, y_a, y_b, tiles)
@@ -704,12 +702,11 @@
 
 
 def add_y(alpha, near, sums, y_a, y_b, small_a, small_b, *rest):
-    others = rest[:-4]
-    result, out_alpha, out_delta, sems = rest[-4:]
-    moves = []
+    others = rest[:-2]
+    out_delta, out_alpha = rest[-2:]
+    out_delta[...] = near[...]
     at = 0
     for c in range(NC):
-        out_delta[c] = near[c]
         for away, start, extra in WIDE:
             north, south = y_sides(y_a, y_b, pl.ds((c * RIM + away - 1) * CX, CX))
             high = pl.ds(CY - away, CX, stride=CY)
@@ -722,17 +719,12 @@
                     out_delta[c, (x + 1) * CY - extra : (x + 1) * CY] += north
                     out_delta[c, x * CY : x * CY + extra] += south
                     at += extra
-        move = pltpu.make_async_copy(out_delta.at[c], result.at[c], sems.at[c])
-        move.start()
-        moves.append(move)
     total = sums[...] + small_a[CORNERS:]
     if small_b.shape[0] > CORNERS:
         total = total + small_b[CORNERS:]
     for other in others:
         total = total + other[...]
     out_alpha[...] = alpha[...] + profile_weight * total
-    for move in moves:
-        move.wait()
 
 
 def on_device(
@@ -905,8 +897,6 @@
         add_y,
         [fine.shape, control.shape],
         [control_near, near, sums, y_a, y_b, small_a, small_b, *others],
-        [pltpu.VMEM(fine.shape, f32), pltpu.SemaphoreType.DMA((NC,))],
-        out_specs=[HBM, VMEM],
     )
     return grad_delta.reshape(delta.shape), grad_alpha.reshape(alpha.shape)
 

time: 34.5 us -> 34 us (0.986)
  Pallas kernels: 10.1 us -> 9.44 us
    pallas_call x9, Pallas kernels: 10.1 us -> 9.44 us  [call(): pl.pallas_call(body, out_shape=shapes, in_specs=in_specs or [VMEM] * len(...]
where the time goes in v18:
time: 34 us; the launch traced here: 33.9 us
  starting transfers between devices  18.4 us (54%)
  Pallas kernels  9.44 us (28%)
  waiting for transfers between devices  5.26 us (15%)
  between operations  0.74 us (2%)
    ppermute x12, starting transfers between devices, swap(): lax.ppermute(block, axis, [(i, i ^ xor) for i in range(lax.axis_size(axis...  12.5 us
    pallas_call x9, Pallas kernels, call(): pl.pallas_call(body, out_shape=shapes, in_specs=in_specs or [VMEM] * len(...  9.44 us
    ppermute x12, waiting for transfers between devices, swap(): lax.ppermute(block, axis, [(i, i ^ xor) for i in range(lax.axis_size(axis...  5.2 us
    ppermute x4, starting transfers between devices, pair_b(): return lax.ppermute(block, ('gx', 'gy'), pairs)  5.09 us
    ppermute x1, starting transfers between devices, ring_b(): return lax.ppermute(block, axis, pairs)  0.89 us
  transfers between devices with their start and end apart: 17, of which 5 were waited for; matrix products, arithmetic and copies ran while one was open for 0% of the time, Pallas kernels for 17%

profile of v18, /device:TPU:0, one launch (start us, length us, event | category | flops | bytes accessed | tf_op | source)
XLA Modules:
  0.0 33.9 jit_solution(809851557737213602)
XLA Ops:
  0.6 0.0 copy-start
  0.6 1.4 %shard_map.131 = (f32[320,128]{1,0:T(8,128)S(1)}, f32[304,128]{1,0:T(8,128)S(1)}, f32[4,256,128]{2,1,0:T(8,128)S(1)}, f32[3,256,128]{2,1,0:T(8,128)S(1)}, f32[16...) custom-call(f32[4,256,128]{2,1,0:T(8,128)} %bitcast.16, ...), custom_call_target="tpu_custom_call" | custom-call | flops 1000000 | bytes 944128 | tf_op jit(solution)/shard_map/pallas_call | solution.py:36
  2.1 0.5 %collective-permute-start = (f32[320,128]{1,0:T(8,128)S(1)}, f32[320,128]{1,0:T(8,128)S(1)}, u32[]{:S(2)}, u32[]{:S(2)}) collective-permute-start(f32[320,128]{1,0:T(8,128)S(1)} %get-tuple-element.51), channel_id=1, source_target_pairs={{0,1},{1,0},{2,3},{3,2},{4,5},{5,4},{6,7},{7,6},{8,9},{9,8},{10,11... | collective-permute-start | bytes 491528 | tf_op jit(solution)/shard_map/ppermute | solution.py:48
  2.6 2.6 %collective-permute-start.1 = (f32[304,128]{1,0:T(8,128)S(1)}, f32[304,128]{1,0:T(8,128)S(1)}, u32[]{:S(2)}, u32[]{:S(2)}) collective-permute-start(f32[304,128]{1,0:T(8,128)S(1)} %get-tuple-element.52), channel_id=1, source_target_pairs={{0,4},{1,2},{2,1},{3,7},{4,0},{5,6},{6,5},{7,3},{8,12},{9,10},{10,... | collective-permute-start | bytes 466952 | tf_op jit(solution)/shard_map/ppermute | solution.py:64
  5.2 1.2 %collective-permute-start.3 = (f32[16,128]{1,0:T(8,128)}, f32[16,128]{1,0:T(8,128)S(1)}, u32[]{:S(2)}, u32[]{:S(2)}) collective-permute-start(f32[16,128]{1,0:T(8,128)} %bitcast.22), channel_id=1, source_target_pairs={{0,3},{1,2},{2,1},{3,0},{4,7},{5,6},{6,5},{7,4},{8,11},{9,10},{10,... | collective-permute-start | bytes 24584 | tf_op jit(solution)/shard_map/ppermute | solution.py:48
  6.4 0.5 %collective-permute-start.2 = (f32[16,128]{1,0:T(8,128)}, f32[16,128]{1,0:T(8,128)S(1)}, u32[]{:S(2)}, u32[]{:S(2)}) collective-permute-start(f32[16,128]{1,0:T(8,128)} %bitcast.23), channel_id=1, source_target_pairs={{0,2},{1,3},{2,0},{3,1},{4,6},{5,7},{6,4},{7,5},{8,10},{9,11},{10,... | collective-permute-start | bytes 24584 | tf_op jit(solution)/shard_map/ppermute | solution.py:48
  6.9 1.5 %collective-permute-start.6 = (f32[24,128]{1,0:T(8,128)}, f32[24,128]{1,0:T(8,128)S(1)}, u32[]{:S(2)}, u32[]{:S(2)}) collective-permute-start(f32[24,128]{1,0:T(8,128)} %bitcast.20), channel_id=1, source_target_pairs={{0,4},{4,0},{8,12},{12,8},{16,20},{20,16},{24,28},{28,24},{1,5},{5... | collective-permute-start | bytes 36872 | tf_op jit(solution)/shard_map/ppermute | solution.py:48
  8.4 0.0 copy-done
  8.4 0.3 shard_map.132
  8.7 0.0 collective-permute-done.3.refs_10_.refs_8_
  8.8 1.5 %collective-permute-done.2.refs_9_.refs_7_ = f32[16,128]{1,0:T(8,128)S(1)} collective-permute-done((f32[16,128]{1,0:T(8,128)}, f32[16,128]{1,0:T(8,128)S(1)}, u32[]{:S(2)}, u32[]{:S(2)}) %collective-permute-start.2) | collective-permute-done | bytes 8224 | tf_op jit(solution)/shard_map/ppermute | solution.py:48
  10.3 0.0 collective-permute-done.1.refs_8_.refs_6_
  10.3 0.0 collective-permute-done.refs_7_.refs_5_
  10.3 0.5 %shard_map.134 = (f32[318,128]{1,0:T(8,128)S(1)}, f32[318,128]{1,0:T(8,128)S(1)}) custom-call(f32[4,256,128]{2,1,0:T(8,128)S(1)} %get-tuple-element.44.refs_0_, f32[3,256,128]{2,1,0:T(8,128)S(1)} %get-tuple-element.45.refs_1_, f32[16,128]{1,0:T(8,128)S(1)} %get-tuple-element.43.refs_2_.alpha, f32[16,128]{1,0:T(8,128)S(1)} %get-tuple-element.46.refs_3_, ...), custom_call_target="tpu_custom_call" | custom-call | flops 1000000 | bytes 1277952 | tf_op jit(solution)/shard_map/pallas_call | solution.py:36
  10.8 0.6 %collective-permute-start.4 = (f32[318,128]{1,0:T(8,128)S(1)}, f32[318,128]{1,0:T(8,128)S(1)}, u32[]{:S(2)}, u32[]{:S(2)}) collective-permute-start(f32[318,128]{1,0:T(8,128)S(1)} %get-tuple-element.59), channel_id=1, source_target_pairs={{0,4},{4,0},{8,12},{12,8},{16,20},{20,16},{24,28},{28,24},{1,5},{5... | collective-permute-start | bytes 488456 | tf_op jit(solution)/shard_map/ppermute | solution.py:48
  11.4 0.0 collective-permute-start.5
  11.4 0.0 collective-permute-done.6
  11.4 5.1 %collective-permute-start.9 = (f32[48,128]{1,0:T(8,128)S(1)}, f32[48,128]{1,0:T(8,128)S(1)}, u32[]{:S(2)}, u32[]{:S(2)}) collective-permute-start(f32[48,128]{1,0:T(8,128)S(1)} %constant_dynamic-update-slice_fusion.rest_0_), channel_id=1, source_target_pairs={{0,24},{4,28},{8,16},{12,20},{16,8},{20,12},{24,0},{28,4},{1,25},{... | collective-permute-start | bytes 73736 | tf_op jit(solution)/shard_map/ppermute | solution.py:48
  16.5 0.0 collective-permute-start.8
  16.5 0.6 %collective-permute-start.7 = (f32[48,128]{1,0:T(8,128)S(1)}, f32[48,128]{1,0:T(8,128)S(1)}, u32[]{:S(2)}, u32[]{:S(2)}) collective-permute-start(f32[48,128]{1,0:T(8,128)S(1)} %constant_dynamic-update-slice_fusion.rest_0_), channel_id=1, source_target_pairs={{0,8},{4,12},{8,0},{12,4},{16,24},{20,28},{24,16},{28,20},{1,9},{5... | collective-permute-start | bytes 73736 | tf_op jit(solution)/shard_map/ppermute | solution.py:48
  17.1 1.9 %shard_map.133 = (f32[1536,128]{1,0:T(8,128)S(1)}, f32[1920,128]{1,0:T(8,128)S(1)}, f32[384,16]{1,0:T(8,128)S(1)}, f32[1536,128]{1,0:T(8,128)S(1)}, f32[1536,128]{1,0:T(8,128)S(1)}, /*index=5*/f32[768,128]{1,0:T(8,128)S(1)}) custom-call(f32[4,256,128]{2,1,0:T(8,128)S(1)} %get-tuple-element.44.refs_0_, f32[3,256,128]{2,1,0:T(8,128)S(1)} %get-tuple-element.45.refs_1_, ...), custom_call_target="tpu_custom_call" | custom-call | flops 3000000 | bytes 2064384 | tf_op jit(solution)/shard_map/pallas_call | solution.py:36
  19.1 0.0 collective-permute-done.4.x_a
  19.1 0.0 collective-permute-done.5.x_b
  19.1 0.8 %shard_map.135 = (f32[2880,128]{1,0:T(8,128)S(1)}, f32[768,128]{1,0:T(8,128)S(1)}) custom-call(f32[1536,128]{1,0:T(8,128)S(1)} %get-tuple-element.54.core, f32[1920,128]{1,0:T(8,128)S(1)} %get-tuple-element.53.core_coef, f32[1536,128]{1,0:T(8,128)S(1)} %get-tuple-element.55.near_1, f32[1536,128]{1,0:T(8,128)S(1)} %get-tuple-element.56.near_2, ...), custom_call_target="tpu_custom_call" | custom-call | flops 10000000 | bytes 4847616 | tf_op jit(solution)/shard_map/pallas_call | solution.py:36
  19.9 0.4 %collective-permute-done.9.rest_3_ = f32[48,128]{1,0:T(8,128)S(1)} collective-permute-done((f32[48,128]{1,0:T(8,128)S(1)}, f32[48,128]{1,0:T(8,128)S(1)}, u32[]{:S(2)}, u32[]{:S(2)}) %collective-permute-start.9) | collective-permute-done | bytes 24608 | tf_op jit(solution)/shard_map/ppermute | solution.py:48
  20.3 0.9 %collective-permute-done.8.rest_2_ = f32[48,128]{1,0:T(8,128)S(1)} collective-permute-done((f32[48,128]{1,0:T(8,128)S(1)}, f32[48,128]{1,0:T(8,128)S(1)}, u32[]{:S(2)}, u32[]{:S(2)}) %collective-permute-start.8) | collective-permute-done | bytes 24608 | tf_op jit(solution)/shard_map/ppermute | solution.py:48
  21.2 0.0 collective-permute-done.7.rest_1_
  21.2 1.4 %shard_map.136 = (f32[216,128]{1,0:T(8,128)S(1)}, f32[216,128]{1,0:T(8,128)S(1)}, f32[2304,128]{1,0:T(8,128)S(1)}, f32[2304,128]{1,0:T(8,128)S(1)}, bf16[768,512...) custom-call(f32[2880,128]{1,0:T(8,128)S(1)} %get-tuple-element.61.coef.edge_coef, ...), custom_call_target="tpu_custom_call" | custom-call | flops 10000000 | bytes 2826240 | tf_op jit(solution)/shard_map/pallas_call | solution.py:36
  22.7 0.6 %collective-permute-start.10 = (f32[216,128]{1,0:T(8,128)S(1)}, f32[216,128]{1,0:T(8,128)S(1)}, u32[]{:S(2)}, u32[]{:S(2)}) collective-permute-start(f32[216,128]{1,0:T(8,128)S(1)} %get-tuple-element.73), channel_id=1, source_target_pairs={{0,4},{4,0},{8,12},{12,8},{16,20},{20,16},{24,28},{28,24},{1,5},{5... | collective-permute-start | bytes 331784 | tf_op jit(solution)/shard_map/ppermute | solution.py:48
  23.3 0.0 collective-permute-start.11
  23.3 1.6 %shard_map.137 = (f32[1536,128]{1,0:T(8,128)S(1)}, f32[192,128]{1,0:T(8,128)S(1)}, f32[192,128]{1,0:T(8,128)S(1)}, bf16[16,384]{1,0:T(8,128)(2,1)S(1)}) custom-call(f32[1920,128]{1,0:T(8,128)S(1)} %get-tuple-element.53.core_coef, f32[2880,128]{1,0:T(8,128)S(1)} %get-tuple-element.61.coef.edge_coef, f32[2304,128]{1,0:T(8,128)S(1)} %get-tuple-element.66.back_2, ...), custom_call_target="tpu_custom_call" | custom-call | flops 10000000 | bytes 8249344 | tf_op jit(solution)/shard_map/pallas_call | solution.py:36
  24.9 0.6 %collective-permute-start.12 = (f32[192,128]{1,0:T(8,128)S(1)}, f32[192,128]{1,0:T(8,128)S(1)}, u32[]{:S(2)}, u32[]{:S(2)}) collective-permute-start(f32[192,128]{1,0:T(8,128)S(1)} %get-tuple-element.77), channel_id=1, source_target_pairs={{0,1},{1,0},{2,3},{3,2},{4,5},{5,4},{6,7},{7,6},{8,9},{9,8},{10,11... | collective-permute-start | bytes 294920 | tf_op jit(solution)/shard_map/ppermute | solution.py:48
  25.5 2.5 %collective-permute-start.13 = (f32[192,128]{1,0:T(8,128)S(1)}, f32[192,128]{1,0:T(8,128)S(1)}, u32[]{:S(2)}, u32[]{:S(2)}) collective-permute-start(f32[192,128]{1,0:T(8,128)S(1)} %get-tuple-element.78), channel_id=1, source_target_pairs={{0,4},{1,2},{2,1},{3,7},{4,0},{5,6},{6,5},{7,3},{8,12},{9,10},{10,... | collective-permute-start | bytes 294920 | tf_op jit(solution)/shard_map/ppermute | solution.py:64
  28.0 0.0 collective-permute-done.10.refs_3_
  28.0 0.0 collective-permute-done.11.refs_4_
  28.0 0.4 %shard_map.138 = (f32[40,128]{1,0:T(8,128)S(1)}, f32[40,128]{1,0:T(8,128)S(1)}, f32[4,256,128]{2,1,0:T(8,128)S(1)}, f32[16,128]{1,0:T(8,128)S(1)}, f32[16,128]{1,0:T(8,128)S(1)}) custom-call(f32[4,256,128]{2,1,0:T(8,128)S(1)} %get-tuple-element.44.refs_0_, bf16[16,384]{1,0:T(8,128)(2,1)S(1)} %get-tuple-element.71.refs_1_, ...), custom_call_target="tpu_custom_call" | custom-call | flops 1000000 | bytes 1556480 | tf_op jit(solution)/shard_map/pallas_call | solution.py:36
  28.4 0.0 collective-permute-start.14
  28.4 0.9 %collective-permute-start.15 = (f32[40,128]{1,0:T(8,128)S(1)}, f32[40,128]{1,0:T(8,128)S(1)}, u32[]{:S(2)}, u32[]{:S(2)}) collective-permute-start(f32[40,128]{1,0:T(8,128)S(1)} %get-tuple-element.80), channel_id=1, source_target_pairs={{0,3},{1,2},{2,1},{3,0},{4,7},{5,6},{6,5},{7,4},{8,11},{9,10},{10,... | collective-permute-start | bytes 61448 | tf_op jit(solution)/shard_map/ppermute | solution.py:70
  29.3 1.2 %collective-permute-start.16 = (f32[16,128]{1,0:T(8,128)S(1)}, f32[16,128]{1,0:T(8,128)S(1)}, u32[]{:S(2)}, u32[]{:S(2)}) collective-permute-start(f32[16,128]{1,0:T(8,128)S(1)} %get-tuple-element.81), channel_id=1, source_target_pairs={{0,2},{1,3},{2,0},{3,1},{4,6},{5,7},{6,4},{7,5},{8,10},{9,11},{10,... | collective-permute-start | bytes 24584 | tf_op jit(solution)/shard_map/ppermute | solution.py:48
  30.5 0.0 collective-permute-done.12.y_a
  30.5 0.1 collective-permute-done.13.y_b
  30.6 2.3 %collective-permute-done.16.rest_0_ = f32[16,128]{1,0:T(8,128)S(1)} collective-permute-done((f32[16,128]{1,0:T(8,128)S(1)}, f32[16,128]{1,0:T(8,128)S(1)}, u32[]{:S(2)}, u32[]{:S(2)}) %collective-permute-start.16) | collective-permute-done | bytes 8224 | tf_op jit(solution)/shard_map/ppermute | solution.py:48
  32.9 0.0 collective-permute-done.14.small_a
  32.9 0.0 collective-permute-done.15.small_b
  32.9 1.0 %shard_map.139 = (f32[4,256,128]{2,1,0:T(8,128)}, f32[16,128]{1,0:T(8,128)}) custom-call(f32[16,128]{1,0:T(8,128)S(1)} %get-tuple-element.43.refs_2_.alpha, f32[4,256,128]{2,1,0:T(8,128)S(1)} %get-tuple-element.75.near, f32[16,128]{1,0:T(8,128)S(1)} %get-tuple-element.76.sums, f32[192,128]{1,0:T(8,128)S(1)} %collective-permute-done.12.y_a, ...), custom_call_target="tpu_custom_call" | custom-call | flops 1000000 | bytes 786432 | tf_op jit(solution)/shard_map/pallas_call | solution.py:36
  (2 shorter events, 0.0 us)
Async XLA Ops:
  0.6 7.8 %copy-start = (f32[1,1,256,4,128]{4,3,2,1,0:T(4,128)S(1)}, f32[1,1,256,4,128]{4,3,2,1,0:T(4,128)}, u32[]{:S(2)}) copy-start(f32[1,1,256,4,128]{4,3,2,1,0:T(4,128)} %param.22) | copy-start | bytes 1572868
  2.1 8.2 %collective-permute-start = (f32[320,128]{1,0:T(8,128)S(1)}, f32[320,128]{1,0:T(8,128)S(1)}, u32[]{:S(2)}, u32[]{:S(2)}) collective-permute-start(f32[320,128]{1,0:T(8,128)S(1)} %get-tuple-element.51), channel_id=1, source_target_pairs={{0,1},{1,0},{2,3},{3,2},{4,5},{5,4},{6,7},{7,6},{8,9},{9,8},{10,11... | collective-permute-start | bytes 491528 | tf_op jit(solution)/shard_map/ppermute | solution.py:48
  2.6 7.7 %collective-permute-start.1 = (f32[304,128]{1,0:T(8,128)S(1)}, f32[304,128]{1,0:T(8,128)S(1)}, u32[]{:S(2)}, u32[]{:S(2)}) collective-permute-start(f32[304,128]{1,0:T(8,128)S(1)} %get-tuple-element.52), channel_id=1, source_target_pairs={{0,4},{1,2},{2,1},{3,7},{4,0},{5,6},{6,5},{7,3},{8,12},{9,10},{10,... | collective-permute-start | bytes 466952 | tf_op jit(solution)/shard_map/ppermute | solution.py:64
  5.2 3.6 %collective-permute-start.3 = (f32[16,128]{1,0:T(8,128)}, f32[16,128]{1,0:T(8,128)S(1)}, u32[]{:S(2)}, u32[]{:S(2)}) collective-permute-start(f32[16,128]{1,0:T(8,128)} %bitcast.22), channel_id=1, source_target_pairs={{0,3},{1,2},{2,1},{3,0},{4,7},{5,6},{6,5},{7,4},{8,11},{9,10},{10,... | collective-permute-start | bytes 24584 | tf_op jit(solution)/shard_map/ppermute | solution.py:48
  6.4 3.9 %collective-permute-start.2 = (f32[16,128]{1,0:T(8,128)}, f32[16,128]{1,0:T(8,128)S(1)}, u32[]{:S(2)}, u32[]{:S(2)}) collective-permute-start(f32[16,128]{1,0:T(8,128)} %bitcast.23), channel_id=1, source_target_pairs={{0,2},{1,3},{2,0},{3,1},{4,6},{5,7},{6,4},{7,5},{8,10},{9,11},{10,... | collective-permute-start | bytes 24584 | tf_op jit(solution)/shard_map/ppermute | solution.py:48
  6.9 4.5 %collective-permute-start.6 = (f32[24,128]{1,0:T(8,128)}, f32[24,128]{1,0:T(8,128)S(1)}, u32[]{:S(2)}, u32[]{:S(2)}) collective-permute-start(f32[24,128]{1,0:T(8,128)} %bitcast.20), channel_id=1, source_target_pairs={{0,4},{4,0},{8,12},{12,8},{16,20},{20,16},{24,28},{28,24},{1,5},{5... | collective-permute-start | bytes 36872 | tf_op jit(solution)/shard_map/ppermute | solution.py:48
  10.8 8.2 %collective-permute-start.4 = (f32[318,128]{1,0:T(8,128)S(1)}, f32[318,128]{1,0:T(8,128)S(1)}, u32[]{:S(2)}, u32[]{:S(2)}) collective-permute-start(f32[318,128]{1,0:T(8,128)S(1)} %get-tuple-element.59), channel_id=1, source_target_pairs={{0,4},{4,0},{8,12},{12,8},{16,20},{20,16},{24,28},{28,24},{1,5},{5... | collective-permute-start | bytes 488456 | tf_op jit(solution)/shard_map/ppermute | solution.py:48
  11.4 7.7 %collective-permute-start.5 = (f32[318,128]{1,0:T(8,128)S(1)}, f32[318,128]{1,0:T(8,128)S(1)}, u32[]{:S(2)}, u32[]{:S(2)}) collective-permute-start(f32[318,128]{1,0:T(8,128)S(1)} %get-tuple-element.60), channel_id=1, source_target_pairs={{0,1},{4,8},{8,4},{12,16},{16,12},{20,24},{24,20},{28,29},{1,0},{5... | collective-permute-start | bytes 488456 | tf_op jit(solution)/shard_map/ppermute | solution.py:64
  11.4 8.9 %collective-permute-start.9 = (f32[48,128]{1,0:T(8,128)S(1)}, f32[48,128]{1,0:T(8,128)S(1)}, u32[]{:S(2)}, u32[]{:S(2)}) collective-permute-start(f32[48,128]{1,0:T(8,128)S(1)} %constant_dynamic-update-slice_fusion.rest_0_), channel_id=1, source_target_pairs={{0,24},{4,28},{8,16},{12,20},{16,8},{20,12},{24,0},{28,4},{1,25},{... | collective-permute-start | bytes 73736 | tf_op jit(solution)/shard_map/ppermute | solution.py:48
  16.5 4.7 %collective-permute-start.8 = (f32[48,128]{1,0:T(8,128)S(1)}, f32[48,128]{1,0:T(8,128)S(1)}, u32[]{:S(2)}, u32[]{:S(2)}) collective-permute-start(f32[48,128]{1,0:T(8,128)S(1)} %constant_dynamic-update-slice_fusion.rest_0_), channel_id=1, source_target_pairs={{0,16},{4,20},{8,24},{12,28},{16,0},{20,4},{24,8},{28,12},{1,17},{... | collective-permute-start | bytes 73736 | tf_op jit(solution)/shard_map/ppermute | solution.py:48
  16.5 4.7 %collective-permute-start.7 = (f32[48,128]{1,0:T(8,128)S(1)}, f32[48,128]{1,0:T(8,128)S(1)}, u32[]{:S(2)}, u32[]{:S(2)}) collective-permute-start(f32[48,128]{1,0:T(8,128)S(1)} %constant_dynamic-update-slice_fusion.rest_0_), channel_id=1, source_target_pairs={{0,8},{4,12},{8,0},{12,4},{16,24},{20,28},{24,16},{28,20},{1,9},{5... | collective-permute-start | bytes 73736 | tf_op jit(solution)/shard_map/ppermute | solution.py:48
  22.7 5.3 %collective-permute-start.10 = (f32[216,128]{1,0:T(8,128)S(1)}, f32[216,128]{1,0:T(8,128)S(1)}, u32[]{:S(2)}, u32[]{:S(2)}) collective-permute-start(f32[216,128]{1,0:T(8,128)S(1)} %get-tuple-element.73), channel_id=1, source_target_pairs={{0,4},{4,0},{8,12},{12,8},{16,20},{20,16},{24,28},{28,24},{1,5},{5... | collective-permute-start | bytes 331784 | tf_op jit(solution)/shard_map/ppermute | solution.py:48
  23.3 4.7 %collective-permute-start.11 = (f32[216,128]{1,0:T(8,128)S(1)}, f32[216,128]{1,0:T(8,128)S(1)}, u32[]{:S(2)}, u32[]{:S(2)}) collective-permute-start(f32[216,128]{1,0:T(8,128)S(1)} %get-tuple-element.74), channel_id=1, source_target_pairs={{0,1},{4,8},{8,4},{12,16},{16,12},{20,24},{24,20},{28,29},{1,0},{5... | collective-permute-start | bytes 331784 | tf_op jit(solution)/shard_map/ppermute | solution.py:64
  24.9 5.6 %collective-permute-start.12 = (f32[192,128]{1,0:T(8,128)S(1)}, f32[192,128]{1,0:T(8,128)S(1)}, u32[]{:S(2)}, u32[]{:S(2)}) collective-permute-start(f32[192,128]{1,0:T(8,128)S(1)} %get-tuple-element.77), channel_id=1, source_target_pairs={{0,1},{1,0},{2,3},{3,2},{4,5},{5,4},{6,7},{7,6},{8,9},{9,8},{10,11... | collective-permute-start | bytes 294920 | tf_op jit(solution)/shard_map/ppermute | solution.py:48
  25.5 5.1 %collective-permute-start.13 = (f32[192,128]{1,0:T(8,128)S(1)}, f32[192,128]{1,0:T(8,128)S(1)}, u32[]{:S(2)}, u32[]{:S(2)}) collective-permute-start(f32[192,128]{1,0:T(8,128)S(1)} %get-tuple-element.78), channel_id=1, source_target_pairs={{0,4},{1,2},{2,1},{3,7},{4,0},{5,6},{6,5},{7,3},{8,12},{9,10},{10,... | collective-permute-start | bytes 294920 | tf_op jit(solution)/shard_map/ppermute | solution.py:64
  28.4 4.6 %collective-permute-start.14 = (f32[40,128]{1,0:T(8,128)S(1)}, f32[40,128]{1,0:T(8,128)S(1)}, u32[]{:S(2)}, u32[]{:S(2)}) collective-permute-start(f32[40,128]{1,0:T(8,128)S(1)} %get-tuple-element.79), channel_id=1, source_target_pairs={{0,1},{1,0},{2,3},{3,2},{4,5},{5,4},{6,7},{7,6},{8,9},{9,8},{10,11... | collective-permute-start | bytes 61448 | tf_op jit(solution)/shard_map/ppermute | solution.py:48
  28.4 4.6 %collective-permute-start.15 = (f32[40,128]{1,0:T(8,128)S(1)}, f32[40,128]{1,0:T(8,128)S(1)}, u32[]{:S(2)}, u32[]{:S(2)}) collective-permute-start(f32[40,128]{1,0:T(8,128)S(1)} %get-tuple-element.80), channel_id=1, source_target_pairs={{0,3},{1,2},{2,1},{3,0},{4,7},{5,6},{6,5},{7,4},{8,11},{9,10},{10,... | collective-permute-start | bytes 61448 | tf_op jit(solution)/shard_map/ppermute | solution.py:70
  29.3 3.7 %collective-permute-start.16 = (f32[16,128]{1,0:T(8,128)S(1)}, f32[16,128]{1,0:T(8,128)S(1)}, u32[]{:S(2)}, u32[]{:S(2)}) collective-permute-start(f32[16,128]{1,0:T(8,128)S(1)} %get-tuple-element.81), channel_id=1, source_target_pairs={{0,2},{1,3},{2,0},{3,1},{4,6},{5,7},{6,4},{7,5},{8,10},{9,11},{10,... | collective-permute-start | bytes 24584 | tf_op jit(solution)/shard_map/ppermute | solution.py:48

commit v19 on v18

--- a/solution.py
+++ b/solution.py
@@ -175,6 +175,8 @@
     owner = jnp.bitwise_xor(beam >> held, lax.axis_index("gx"))
     meta[...] = jnp.zeros(meta.shape, f32)
     meta[0:1] = gates[2].astype(f32)
+    half = lax.axis_size("gx") // 2
+    owner = (((half - (owner >> 1)) & (half - 1)) << 1) | (owner & 1)
     meta[1:2] = ((owner << held) | (beam & ((1 << held) - 1))).astype(f32)
     meta[2:3] = gates[1].astype(f32)
     meta[3:4] = gates[3].astype(f32) * values[...]
@@ -787,7 +789,7 @@
     y_b = pair_b(y_b, "gy", "gx")
     others = [swap(control, "gy", xor) for xor in range(2, ny)]
     beams = jnp.concatenate([near_beams, swap(own_beams, "gx", 1)])
-    beams = [beams] + [swap(beams, "gx", xor) for xor in range(2, nx, 2)]
+    beams = [beams] + [swap(beams, "gx", xor) for xor in range(nx - 2, 0, -2)]
 
     wide, slot_pick, slot_push, beam_pick, columns, edge_pick = call(
         one_hots,

time: 34 us -> 34.8 us (1.024)
  waiting for transfers between devices: 5.26 us -> 7.43 us
  starting transfers between devices: 18.4 us -> 16.9 us
    ppermute x12, waiting for transfers between devices: 5.2 us -> 7.42 us  [swap(): lax.ppermute(block, axis, [(i, i ^ xor) for i in range(lax.axis_size(axis...]
    ppermute x4, starting transfers between devices: 5.09 us -> 4.06 us  [pair_b(): return lax.ppermute(block, ('gx', 'gy'), pairs)]
  transfers between devices with their start and end apart: 17 -> 17, of which waited for: 5 -> 4; matrix products, arithmetic and copies ran while one was open for 0% -> 0% of each run, Pallas kernels for 17% -> 16%
where the time goes in v19:
time: 34.8 us; the launch traced here: 34.6 us
  starting transfers between devices  16.9 us (49%)
  Pallas kernels  9.45 us (27%)
  waiting for transfers between devices  7.43 us (21%)
  between operations  0.76 us (2%)
    ppermute x12, starting transfers between devices, swap(): lax.ppermute(block, axis, [(i, i ^ xor) for i in range(lax.axis_size(axis...  12.3 us
    pallas_call x9, Pallas kernels, call(): pl.pallas_call(body, out_shape=shapes, in_specs=in_specs or [VMEM] * len(...  9.45 us
    ppermute x12, waiting for transfers between devices, swap(): lax.ppermute(block, axis, [(i, i ^ xor) for i in range(lax.axis_size(axis...  7.42 us
    ppermute x4, starting transfers between devices, pair_b(): return lax.ppermute(block, ('gx', 'gy'), pairs)  4.06 us
  transfers between devices with their start and end apart: 17, of which 4 were waited for; matrix products, arithmetic and copies ran while one was open for 0% of the time, Pallas kernels for 16%

profile of v19, /device:TPU:0, one launch (start us, length us, event | category | flops | bytes accessed | tf_op | source)
XLA Modules:
  0.0 34.6 jit_solution(3276254531061350677)
XLA Ops:
  0.6 0.0 copy-start
  0.6 1.4 %shard_map.131 = (f32[320,128]{1,0:T(8,128)S(1)}, f32[304,128]{1,0:T(8,128)S(1)}, f32[4,256,128]{2,1,0:T(8,128)S(1)}, f32[3,256,128]{2,1,0:T(8,128)S(1)}, f32[16...) custom-call(f32[4,256,128]{2,1,0:T(8,128)} %bitcast.16, ...), custom_call_target="tpu_custom_call" | custom-call | flops 1000000 | bytes 944128 | tf_op jit(solution)/shard_map/pallas_call | solution.py:36
  2.1 0.5 %collective-permute-start = (f32[320,128]{1,0:T(8,128)S(1)}, f32[320,128]{1,0:T(8,128)S(1)}, u32[]{:S(2)}, u32[]{:S(2)}) collective-permute-start(f32[320,128]{1,0:T(8,128)S(1)} %get-tuple-element.51), channel_id=1, source_target_pairs={{0,1},{1,0},{2,3},{3,2},{4,5},{5,4},{6,7},{7,6},{8,9},{9,8},{10,11... | collective-permute-start | bytes 491528 | tf_op jit(solution)/shard_map/ppermute | solution.py:48
  2.6 2.6 %collective-permute-start.1 = (f32[304,128]{1,0:T(8,128)S(1)}, f32[304,128]{1,0:T(8,128)S(1)}, u32[]{:S(2)}, u32[]{:S(2)}) collective-permute-start(f32[304,128]{1,0:T(8,128)S(1)} %get-tuple-element.52), channel_id=1, source_target_pairs={{0,4},{1,2},{2,1},{3,7},{4,0},{5,6},{6,5},{7,3},{8,12},{9,10},{10,... | collective-permute-start | bytes 466952 | tf_op jit(solution)/shard_map/ppermute | solution.py:64
  5.2 1.2 %collective-permute-start.3 = (f32[16,128]{1,0:T(8,128)}, f32[16,128]{1,0:T(8,128)S(1)}, u32[]{:S(2)}, u32[]{:S(2)}) collective-permute-start(f32[16,128]{1,0:T(8,128)} %bitcast.22), channel_id=1, source_target_pairs={{0,3},{1,2},{2,1},{3,0},{4,7},{5,6},{6,5},{7,4},{8,11},{9,10},{10,... | collective-permute-start | bytes 24584 | tf_op jit(solution)/shard_map/ppermute | solution.py:48
  6.4 0.5 %collective-permute-start.2 = (f32[16,128]{1,0:T(8,128)}, f32[16,128]{1,0:T(8,128)S(1)}, u32[]{:S(2)}, u32[]{:S(2)}) collective-permute-start(f32[16,128]{1,0:T(8,128)} %bitcast.23), channel_id=1, source_target_pairs={{0,2},{1,3},{2,0},{3,1},{4,6},{5,7},{6,4},{7,5},{8,10},{9,11},{10,... | collective-permute-start | bytes 24584 | tf_op jit(solution)/shard_map/ppermute | solution.py:48
  6.9 1.5 %collective-permute-start.6 = (f32[24,128]{1,0:T(8,128)}, f32[24,128]{1,0:T(8,128)S(1)}, u32[]{:S(2)}, u32[]{:S(2)}) collective-permute-start(f32[24,128]{1,0:T(8,128)} %bitcast.20), channel_id=1, source_target_pairs={{0,4},{4,0},{8,12},{12,8},{16,20},{20,16},{24,28},{28,24},{1,5},{5... | collective-permute-start | bytes 36872 | tf_op jit(solution)/shard_map/ppermute | solution.py:48
  8.4 0.0 copy-done
  8.4 0.3 shard_map.132
  8.7 0.0 collective-permute-done.3.refs_10_.refs_8_
  8.8 1.5 %collective-permute-done.2.refs_9_.refs_7_ = f32[16,128]{1,0:T(8,128)S(1)} collective-permute-done((f32[16,128]{1,0:T(8,128)}, f32[16,128]{1,0:T(8,128)S(1)}, u32[]{:S(2)}, u32[]{:S(2)}) %collective-permute-start.2) | collective-permute-done | bytes 8224 | tf_op jit(solution)/shard_map/ppermute | solution.py:48
  10.3 0.0 collective-permute-done.1.refs_8_.refs_6_
  10.3 0.0 collective-permute-done.refs_7_.refs_5_
  10.3 0.5 %shard_map.134 = (f32[318,128]{1,0:T(8,128)S(1)}, f32[318,128]{1,0:T(8,128)S(1)}) custom-call(f32[4,256,128]{2,1,0:T(8,128)S(1)} %get-tuple-element.44.refs_0_, f32[3,256,128]{2,1,0:T(8,128)S(1)} %get-tuple-element.45.refs_1_, f32[16,128]{1,0:T(8,128)S(1)} %get-tuple-element.43.refs_2_.alpha, f32[16,128]{1,0:T(8,128)S(1)} %get-tuple-element.46.refs_3_, ...), custom_call_target="tpu_custom_call" | custom-call | flops 1000000 | bytes 1277952 | tf_op jit(solution)/shard_map/pallas_call | solution.py:36
  10.9 0.6 %collective-permute-start.4 = (f32[318,128]{1,0:T(8,128)S(1)}, f32[318,128]{1,0:T(8,128)S(1)}, u32[]{:S(2)}, u32[]{:S(2)}) collective-permute-start(f32[318,128]{1,0:T(8,128)S(1)} %get-tuple-element.59), channel_id=1, source_target_pairs={{0,4},{4,0},{8,12},{12,8},{16,20},{20,16},{24,28},{28,24},{1,5},{5... | collective-permute-start | bytes 488456 | tf_op jit(solution)/shard_map/ppermute | solution.py:48
  11.4 0.0 collective-permute-start.5
  11.4 0.0 collective-permute-done.6
  11.4 3.0 %collective-permute-start.9 = (f32[48,128]{1,0:T(8,128)S(1)}, f32[48,128]{1,0:T(8,128)S(1)}, u32[]{:S(2)}, u32[]{:S(2)}) collective-permute-start(f32[48,128]{1,0:T(8,128)S(1)} %constant_dynamic-update-slice_fusion.rest_0_), channel_id=1, source_target_pairs={{0,8},{4,12},{8,0},{12,4},{16,24},{20,28},{24,16},{28,20},{1,9},{5... | collective-permute-start | bytes 73736 | tf_op jit(solution)/shard_map/ppermute | solution.py:48
  14.5 2.6 %collective-permute-start.8 = (f32[48,128]{1,0:T(8,128)S(1)}, f32[48,128]{1,0:T(8,128)S(1)}, u32[]{:S(2)}, u32[]{:S(2)}) collective-permute-start(f32[48,128]{1,0:T(8,128)S(1)} %constant_dynamic-update-slice_fusion.rest_0_), channel_id=1, source_target_pairs={{0,16},{4,20},{8,24},{12,28},{16,0},{20,4},{24,8},{28,12},{1,17},{... | collective-permute-start | bytes 73736 | tf_op jit(solution)/shard_map/ppermute | solution.py:48
  17.1 0.0 collective-permute-start.7
  17.1 1.9 %shard_map.133 = (f32[1536,128]{1,0:T(8,128)S(1)}, f32[1920,128]{1,0:T(8,128)S(1)}, f32[384,16]{1,0:T(8,128)S(1)}, f32[1536,128]{1,0:T(8,128)S(1)}, f32[1536,128]{1,0:T(8,128)S(1)}, /*index=5*/f32[768,128]{1,0:T(8,128)S(1)}) custom-call(f32[4,256,128]{2,1,0:T(8,128)S(1)} %get-tuple-element.44.refs_0_, f32[3,256,128]{2,1,0:T(8,128)S(1)} %get-tuple-element.45.refs_1_, ...), custom_call_target="tpu_custom_call" | custom-call | flops 3000000 | bytes 2064384 | tf_op jit(solution)/shard_map/pallas_call | solution.py:36
  19.0 0.0 collective-permute-done.4.x_a
  19.0 0.0 collective-permute-done.5.x_b
  19.0 0.8 %shard_map.135 = (f32[2880,128]{1,0:T(8,128)S(1)}, f32[768,128]{1,0:T(8,128)S(1)}) custom-call(f32[1536,128]{1,0:T(8,128)S(1)} %get-tuple-element.54.core, f32[1920,128]{1,0:T(8,128)S(1)} %get-tuple-element.53.core_coef, f32[1536,128]{1,0:T(8,128)S(1)} %get-tuple-element.55.near_1, f32[1536,128]{1,0:T(8,128)S(1)} %get-tuple-element.56.near_2, ...), custom_call_target="tpu_custom_call" | custom-call | flops 10000000 | bytes 4847616 | tf_op jit(solution)/shard_map/pallas_call | solution.py:36
  19.9 0.0 collective-permute-done.9.rest_3_
  19.9 0.0 collective-permute-done.8.rest_2_
  19.9 2.8 %collective-permute-done.7.rest_1_ = f32[48,128]{1,0:T(8,128)S(1)} collective-permute-done((f32[48,128]{1,0:T(8,128)S(1)}, f32[48,128]{1,0:T(8,128)S(1)}, u32[]{:S(2)}, u32[]{:S(2)}) %collective-permute-start.7) | collective-permute-done | bytes 24608 | tf_op jit(solution)/shard_map/ppermute | solution.py:48
  22.7 1.4 %shard_map.136 = (f32[216,128]{1,0:T(8,128)S(1)}, f32[216,128]{1,0:T(8,128)S(1)}, f32[2304,128]{1,0:T(8,128)S(1)}, f32[2304,128]{1,0:T(8,128)S(1)}, bf16[768,512...) custom-call(f32[2880,128]{1,0:T(8,128)S(1)} %get-tuple-element.61.coef.edge_coef, ...), custom_call_target="tpu_custom_call" | custom-call | flops 10000000 | bytes 2826240 | tf_op jit(solution)/shard_map/pallas_call | solution.py:36
  24.1 0.2 collective-permute-start.10
  24.3 0.0 collective-permute-start.11
  24.3 1.6 %shard_map.137 = (f32[1536,128]{1,0:T(8,128)S(1)}, f32[192,128]{1,0:T(8,128)S(1)}, f32[192,128]{1,0:T(8,128)S(1)}, bf16[16,384]{1,0:T(8,128)(2,1)S(1)}) custom-call(f32[1920,128]{1,0:T(8,128)S(1)} %get-tuple-element.53.core_coef, f32[2880,128]{1,0:T(8,128)S(1)} %get-tuple-element.61.coef.edge_coef, f32[2304,128]{1,0:T(8,128)S(1)} %get-tuple-element.66.back_2, ...), custom_call_target="tpu_custom_call" | custom-call | flops 10000000 | bytes 8249344 | tf_op jit(solution)/shard_map/pallas_call | solution.py:36
  26.0 0.6 %collective-permute-start.12 = (f32[192,128]{1,0:T(8,128)S(1)}, f32[192,128]{1,0:T(8,128)S(1)}, u32[]{:S(2)}, u32[]{:S(2)}) collective-permute-start(f32[192,128]{1,0:T(8,128)S(1)} %get-tuple-element.77), channel_id=1, source_target_pairs={{0,1},{1,0},{2,3},{3,2},{4,5},{5,4},{6,7},{7,6},{8,9},{9,8},{10,11... | collective-permute-start | bytes 294920 | tf_op jit(solution)/shard_map/ppermute | solution.py:48
  26.5 1.5 %collective-permute-start.13 = (f32[192,128]{1,0:T(8,128)S(1)}, f32[192,128]{1,0:T(8,128)S(1)}, u32[]{:S(2)}, u32[]{:S(2)}) collective-permute-start(f32[192,128]{1,0:T(8,128)S(1)} %get-tuple-element.78), channel_id=1, source_target_pairs={{0,4},{1,2},{2,1},{3,7},{4,0},{5,6},{6,5},{7,3},{8,12},{9,10},{10,... | collective-permute-start | bytes 294920 | tf_op jit(solution)/shard_map/ppermute | solution.py:64
  28.0 1.0 %collective-permute-done.10.refs_3_ = f32[216,128]{1,0:T(8,128)S(1)} collective-permute-done((f32[216,128]{1,0:T(8,128)S(1)}, f32[216,128]{1,0:T(8,128)S(1)}, u32[]{:S(2)}, u32[]{:S(2)}) %collective-permute-start.10) | collective-permute-done | bytes 110624 | tf_op jit(solution)/shard_map/ppermute | solution.py:48
  29.0 0.0 collective-permute-done.11.refs_4_
  29.0 0.4 %shard_map.138 = (f32[40,128]{1,0:T(8,128)S(1)}, f32[40,128]{1,0:T(8,128)S(1)}, f32[4,256,128]{2,1,0:T(8,128)S(1)}, f32[16,128]{1,0:T(8,128)S(1)}, f32[16,128]{1,0:T(8,128)S(1)}) custom-call(f32[4,256,128]{2,1,0:T(8,128)S(1)} %get-tuple-element.44.refs_0_, bf16[16,384]{1,0:T(8,128)(2,1)S(1)} %get-tuple-element.71.refs_1_, ...), custom_call_target="tpu_custom_call" | custom-call | flops 1000000 | bytes 1556480 | tf_op jit(solution)/shard_map/pallas_call | solution.py:36
  29.3 0.0 collective-permute-start.14
  29.3 0.6 %collective-permute-start.15 = (f32[40,128]{1,0:T(8,128)S(1)}, f32[40,128]{1,0:T(8,128)S(1)}, u32[]{:S(2)}, u32[]{:S(2)}) collective-permute-start(f32[40,128]{1,0:T(8,128)S(1)} %get-tuple-element.80), channel_id=1, source_target_pairs={{0,3},{1,2},{2,1},{3,0},{4,7},{5,6},{6,5},{7,4},{8,11},{9,10},{10,... | collective-permute-start | bytes 61448 | tf_op jit(solution)/shard_map/ppermute | solution.py:70
  29.9 1.6 %collective-permute-start.16 = (f32[16,128]{1,0:T(8,128)S(1)}, f32[16,128]{1,0:T(8,128)S(1)}, u32[]{:S(2)}, u32[]{:S(2)}) collective-permute-start(f32[16,128]{1,0:T(8,128)S(1)} %get-tuple-element.81), channel_id=1, source_target_pairs={{0,2},{1,3},{2,0},{3,1},{4,6},{5,7},{6,4},{7,5},{8,10},{9,11},{10,... | collective-permute-start | bytes 24584 | tf_op jit(solution)/shard_map/ppermute | solution.py:48
  31.5 0.0 collective-permute-done.12.y_a
  31.5 0.0 collective-permute-done.13.y_b
  31.5 2.1 %collective-permute-done.16.rest_0_ = f32[16,128]{1,0:T(8,128)S(1)} collective-permute-done((f32[16,128]{1,0:T(8,128)S(1)}, f32[16,128]{1,0:T(8,128)S(1)}, u32[]{:S(2)}, u32[]{:S(2)}) %collective-permute-start.16) | collective-permute-done | bytes 8224 | tf_op jit(solution)/shard_map/ppermute | solution.py:48
  33.6 0.0 collective-permute-done.14.small_a
  33.6 0.0 collective-permute-done.15.small_b
  33.6 1.0 %shard_map.139 = (f32[4,256,128]{2,1,0:T(8,128)}, f32[16,128]{1,0:T(8,128)}) custom-call(f32[16,128]{1,0:T(8,128)S(1)} %get-tuple-element.43.refs_2_.alpha, f32[4,256,128]{2,1,0:T(8,128)S(1)} %get-tuple-element.75.near, f32[16,128]{1,0:T(8,128)S(1)} %get-tuple-element.76.sums, f32[192,128]{1,0:T(8,128)S(1)} %collective-permute-done.12.y_a, ...), custom_call_target="tpu_custom_call" | custom-call | flops 1000000 | bytes 786432 | tf_op jit(solution)/shard_map/pallas_call | solution.py:36
  (2 shorter events, 0.0 us)
Async XLA Ops:
  0.6 7.8 %copy-start = (f32[1,1,256,4,128]{4,3,2,1,0:T(4,128)S(1)}, f32[1,1,256,4,128]{4,3,2,1,0:T(4,128)}, u32[]{:S(2)}) copy-start(f32[1,1,256,4,128]{4,3,2,1,0:T(4,128)} %param.22) | copy-start | bytes 1572868
  2.1 8.2 %collective-permute-start = (f32[320,128]{1,0:T(8,128)S(1)}, f32[320,128]{1,0:T(8,128)S(1)}, u32[]{:S(2)}, u32[]{:S(2)}) collective-permute-start(f32[320,128]{1,0:T(8,128)S(1)} %get-tuple-element.51), channel_id=1, source_target_pairs={{0,1},{1,0},{2,3},{3,2},{4,5},{5,4},{6,7},{7,6},{8,9},{9,8},{10,11... | collective-permute-start | bytes 491528 | tf_op jit(solution)/shard_map/ppermute | solution.py:48
  2.6 7.7 %collective-permute-start.1 = (f32[304,128]{1,0:T(8,128)S(1)}, f32[304,128]{1,0:T(8,128)S(1)}, u32[]{:S(2)}, u32[]{:S(2)}) collective-permute-start(f32[304,128]{1,0:T(8,128)S(1)} %get-tuple-element.52), channel_id=1, source_target_pairs={{0,4},{1,2},{2,1},{3,7},{4,0},{5,6},{6,5},{7,3},{8,12},{9,10},{10,... | collective-permute-start | bytes 466952 | tf_op jit(solution)/shard_map/ppermute | solution.py:64
  5.2 3.6 %collective-permute-start.3 = (f32[16,128]{1,0:T(8,128)}, f32[16,128]{1,0:T(8,128)S(1)}, u32[]{:S(2)}, u32[]{:S(2)}) collective-permute-start(f32[16,128]{1,0:T(8,128)} %bitcast.22), channel_id=1, source_target_pairs={{0,3},{1,2},{2,1},{3,0},{4,7},{5,6},{6,5},{7,4},{8,11},{9,10},{10,... | collective-permute-start | bytes 24584 | tf_op jit(solution)/shard_map/ppermute | solution.py:48
  6.4 3.9 %collective-permute-start.2 = (f32[16,128]{1,0:T(8,128)}, f32[16,128]{1,0:T(8,128)S(1)}, u32[]{:S(2)}, u32[]{:S(2)}) collective-permute-start(f32[16,128]{1,0:T(8,128)} %bitcast.23), channel_id=1, source_target_pairs={{0,2},{1,3},{2,0},{3,1},{4,6},{5,7},{6,4},{7,5},{8,10},{9,11},{10,... | collective-permute-start | bytes 24584 | tf_op jit(solution)/shard_map/ppermute | solution.py:48
  6.9 4.5 %collective-permute-start.6 = (f32[24,128]{1,0:T(8,128)}, f32[24,128]{1,0:T(8,128)S(1)}, u32[]{:S(2)}, u32[]{:S(2)}) collective-permute-start(f32[24,128]{1,0:T(8,128)} %bitcast.20), channel_id=1, source_target_pairs={{0,4},{4,0},{8,12},{12,8},{16,20},{20,16},{24,28},{28,24},{1,5},{5... | collective-permute-start | bytes 36872 | tf_op jit(solution)/shard_map/ppermute | solution.py:48
  10.9 8.2 %collective-permute-start.4 = (f32[318,128]{1,0:T(8,128)S(1)}, f32[318,128]{1,0:T(8,128)S(1)}, u32[]{:S(2)}, u32[]{:S(2)}) collective-permute-start(f32[318,128]{1,0:T(8,128)S(1)} %get-tuple-element.59), channel_id=1, source_target_pairs={{0,4},{4,0},{8,12},{12,8},{16,20},{20,16},{24,28},{28,24},{1,5},{5... | collective-permute-start | bytes 488456 | tf_op jit(solution)/shard_map/ppermute | solution.py:48
  11.4 7.6 %collective-permute-start.5 = (f32[318,128]{1,0:T(8,128)S(1)}, f32[318,128]{1,0:T(8,128)S(1)}, u32[]{:S(2)}, u32[]{:S(2)}) collective-permute-start(f32[318,128]{1,0:T(8,128)S(1)} %get-tuple-element.60), channel_id=1, source_target_pairs={{0,1},{4,8},{8,4},{12,16},{16,12},{20,24},{24,20},{28,29},{1,0},{5... | collective-permute-start | bytes 488456 | tf_op jit(solution)/shard_map/ppermute | solution.py:64
  11.4 8.4 %collective-permute-start.9 = (f32[48,128]{1,0:T(8,128)S(1)}, f32[48,128]{1,0:T(8,128)S(1)}, u32[]{:S(2)}, u32[]{:S(2)}) collective-permute-start(f32[48,128]{1,0:T(8,128)S(1)} %constant_dynamic-update-slice_fusion.rest_0_), channel_id=1, source_target_pairs={{0,8},{4,12},{8,0},{12,4},{16,24},{20,28},{24,16},{28,20},{1,9},{5... | collective-permute-start | bytes 73736 | tf_op jit(solution)/shard_map/ppermute | solution.py:48
  14.5 5.4 %collective-permute-start.8 = (f32[48,128]{1,0:T(8,128)S(1)}, f32[48,128]{1,0:T(8,128)S(1)}, u32[]{:S(2)}, u32[]{:S(2)}) collective-permute-start(f32[48,128]{1,0:T(8,128)S(1)} %constant_dynamic-update-slice_fusion.rest_0_), channel_id=1, source_target_pairs={{0,16},{4,20},{8,24},{12,28},{16,0},{20,4},{24,8},{28,12},{1,17},{... | collective-permute-start | bytes 73736 | tf_op jit(solution)/shard_map/ppermute | solution.py:48
  17.1 5.6 %collective-permute-start.7 = (f32[48,128]{1,0:T(8,128)S(1)}, f32[48,128]{1,0:T(8,128)S(1)}, u32[]{:S(2)}, u32[]{:S(2)}) collective-permute-start(f32[48,128]{1,0:T(8,128)S(1)} %constant_dynamic-update-slice_fusion.rest_0_), channel_id=1, source_target_pairs={{0,24},{4,28},{8,16},{12,20},{16,8},{20,12},{24,0},{28,4},{1,25},{... | collective-permute-start | bytes 73736 | tf_op jit(solution)/shard_map/ppermute | solution.py:48
  24.1 4.8 %collective-permute-start.10 = (f32[216,128]{1,0:T(8,128)S(1)}, f32[216,128]{1,0:T(8,128)S(1)}, u32[]{:S(2)}, u32[]{:S(2)}) collective-permute-start(f32[216,128]{1,0:T(8,128)S(1)} %get-tuple-element.73), channel_id=1, source_target_pairs={{0,4},{4,0},{8,12},{12,8},{16,20},{20,16},{24,28},{28,24},{1,5},{5... | collective-permute-start | bytes 331784 | tf_op jit(solution)/shard_map/ppermute | solution.py:48
  24.3 4.6 %collective-permute-start.11 = (f32[216,128]{1,0:T(8,128)S(1)}, f32[216,128]{1,0:T(8,128)S(1)}, u32[]{:S(2)}, u32[]{:S(2)}) collective-permute-start(f32[216,128]{1,0:T(8,128)S(1)} %get-tuple-element.74), channel_id=1, source_target_pairs={{0,1},{4,8},{8,4},{12,16},{16,12},{20,24},{24,20},{28,29},{1,0},{5... | collective-permute-start | bytes 331784 | tf_op jit(solution)/shard_map/ppermute | solution.py:64
  26.0 5.5 %collective-permute-start.12 = (f32[192,128]{1,0:T(8,128)S(1)}, f32[192,128]{1,0:T(8,128)S(1)}, u32[]{:S(2)}, u32[]{:S(2)}) collective-permute-start(f32[192,128]{1,0:T(8,128)S(1)} %get-tuple-element.77), channel_id=1, source_target_pairs={{0,1},{1,0},{2,3},{3,2},{4,5},{5,4},{6,7},{7,6},{8,9},{9,8},{10,11... | collective-permute-start | bytes 294920 | tf_op jit(solution)/shard_map/ppermute | solution.py:48
  26.5 5.0 %collective-permute-start.13 = (f32[192,128]{1,0:T(8,128)S(1)}, f32[192,128]{1,0:T(8,128)S(1)}, u32[]{:S(2)}, u32[]{:S(2)}) collective-permute-start(f32[192,128]{1,0:T(8,128)S(1)} %get-tuple-element.78), channel_id=1, source_target_pairs={{0,4},{1,2},{2,1},{3,7},{4,0},{5,6},{6,5},{7,3},{8,12},{9,10},{10,... | collective-permute-start | bytes 294920 | tf_op jit(solution)/shard_map/ppermute | solution.py:64
  29.3 4.2 %collective-permute-start.14 = (f32[40,128]{1,0:T(8,128)S(1)}, f32[40,128]{1,0:T(8,128)S(1)}, u32[]{:S(2)}, u32[]{:S(2)}) collective-permute-start(f32[40,128]{1,0:T(8,128)S(1)} %get-tuple-element.79), channel_id=1, source_target_pairs={{0,1},{1,0},{2,3},{3,2},{4,5},{5,4},{6,7},{7,6},{8,9},{9,8},{10,11... | collective-permute-start | bytes 61448 | tf_op jit(solution)/shard_map/ppermute | solution.py:48
  29.3 4.2 %collective-permute-start.15 = (f32[40,128]{1,0:T(8,128)S(1)}, f32[40,128]{1,0:T(8,128)S(1)}, u32[]{:S(2)}, u32[]{:S(2)}) collective-permute-start(f32[40,128]{1,0:T(8,128)S(1)} %get-tuple-element.80), channel_id=1, source_target_pairs={{0,3},{1,2},{2,1},{3,0},{4,7},{5,6},{6,5},{7,4},{8,11},{9,10},{10,... | collective-permute-start | bytes 61448 | tf_op jit(solution)/shard_map/ppermute | solution.py:70
  29.9 3.7 %collective-permute-start.16 = (f32[16,128]{1,0:T(8,128)S(1)}, f32[16,128]{1,0:T(8,128)S(1)}, u32[]{:S(2)}, u32[]{:S(2)}) collective-permute-start(f32[16,128]{1,0:T(8,128)S(1)} %get-tuple-element.81), channel_id=1, source_target_pairs={{0,2},{1,3},{2,0},{3,1},{4,6},{5,7},{6,4},{7,5},{8,10},{9,11},{10,... | collective-permute-start | bytes 24584 | tf_op jit(solution)/shard_map/ppermute | solution.py:48
